TPU v7x, 32 devices: a whole 2x2x4 slice. The times are simulated.
32 devices in a mesh: aa: 8 (over z, core), ba: 4 (over y, x).
Axes of the slice: x: 2, y: 2, z: 4, core: 2. Of those that a mesh axis runs over, the one named last changes fastest.
Arguments:
- right_sides: bfloat16 [32768, 512], P(('aa', 'ba')), may hold values from -6 to 6
- point_order: int32 [32, 1024], P(('aa', 'ba')), may hold values from 0 to 1023, each once within a row
- skeleton: int32 [32, 128], P(('aa', 'ba')), may hold values from 0 to 1023, as said below
- leaf_inverse: bfloat16 [32768, 1024], P(('aa', 'ba')), may hold values from -1 to 3.5
- leaf_basis: bfloat16 [32768, 128], P(('aa', 'ba')), may hold values from -0.1875 to 0.1875
- group_core: bfloat16 [4096, 512], P(('aa', 'ba')), may hold values from -1 to 2, as said below
- transfer: float32 [4096, 128], P(('aa', 'ba')), may hold values from -0.5 to 0.5
- top_core: bfloat16 [1024, 1024], P(('aa', 'ba')), may hold values from -1 to 2
Outputs:
- solution: bfloat16 [32768, 512], P(('aa', 'ba'))
Inputs may be any that keep to these rules, and one draw needn't show every extreme that they name: `skeleton`: each row holds 128 different indices in increasing order. `group_core`: each group's block of 512 rows is symmetric.
All inputs are finite; a program needn't handle non-finite values.
Results may differ from a plain program's by a relative error of at most 0.014.
Values may be sent and summed in bfloat16 or wider, within the bound.
No kernel may reach another device: no remote copies, remote signals or barrier semaphores. Data moves between devices by JAX's collectives and lax.ppermute only.
A program may use at most 64 MiB of HBM per device.

v0:
```python
import jax
import jax.numpy as jnp
from jax import lax
from jax.sharding import PartitionSpec as P


def shards(
    right_sides, point_order, skeleton, leaf_inverse, leaf_basis, group_core, transfer, top_core
):
    ordering = point_order[0]
    skel_rows = skeleton[0]
    rows_matrix = lax.all_gather(top_core, "ba", axis=0, tiled=True)
    ordered = jnp.take(right_sides, ordering, axis=0)
    applied = jnp.dot(leaf_inverse, ordered, preferred_element_type=jnp.float32)
    applied_low = applied.astype(jnp.bfloat16)
    coeffs = jnp.einsum("lr,lc->rc", leaf_basis, applied_low, preferred_element_type=jnp.float32)
    coeffs = coeffs + jnp.take(applied, skel_rows, axis=0)
    coeff_low = coeffs.astype(jnp.bfloat16)
    level_one = jnp.dot(
        group_core,
        lax.all_gather(coeff_low, "ba", axis=0, tiled=True),
        preferred_element_type=jnp.float32,
    )
    remainder = coeffs - level_one
    partial_value = jnp.einsum("rs,rc->sc", transfer, remainder, precision=lax.Precision.HIGHEST)
    group_coeffs = lax.psum(partial_value.astype(jnp.bfloat16), "ba")
    folded = jnp.dot(
        rows_matrix,
        lax.all_gather(group_coeffs, "aa", axis=0, tiled=True),
        preferred_element_type=jnp.float32,
    )
    correction = level_one + jnp.einsum(
        "rs,sc->rc", transfer, folded, precision=lax.Precision.HIGHEST
    )
    expanded = jnp.dot(
        leaf_basis, correction.astype(jnp.bfloat16), preferred_element_type=jnp.float32
    )
    expanded = expanded.at[skel_rows].add(correction)
    solved = applied - jnp.dot(
        leaf_inverse, expanded.astype(jnp.bfloat16), preferred_element_type=jnp.float32
    )
    placed = jnp.zeros(solved.shape, jnp.bfloat16)
    return placed.at[ordering].set(solved.astype(jnp.bfloat16))


def solution(mesh):
    in_specs = (
        P(("aa", "ba"), None),
        P(("aa", "ba"), None),
        P(("aa", "ba"), None),
        P(("aa", "ba"), None),
        P(("aa", "ba"), None),
        P(("aa", "ba"), None),
        P(("aa", "ba"), None),
        P(("aa", "ba"), None),
    )
    out_specs = P(("aa", "ba"), None)
    return jax.shard_map(shards, mesh=mesh, in_specs=in_specs, out_specs=out_specs, check_vma=False)
```

profile of v0, /device:TPU:0, one launch (start us, length us, event | category | flops | bytes accessed | tf_op | source)
XLA Modules:
  0.0 133.4 jit_solution(4892154499209558779)
XLA Ops:
  6.5 0.0 copy-start
  6.5 0.0 all-reduce.2.cloned.1.call-start
  6.5 0.8 fusion.13
  7.3 0.7 compare_and_fusion.1
  8.0 0.7 compare_select_fusion
  8.7 0.7 compare_and_fusion
  9.4 5.4 %gather_fusion = bf16[1024,512]{1,0:T(8,128)(2,1)S(1)} fusion(bf16[1024,512]{1,0:T(8,128)(2,1)} %param.8, s32[1024]{0:T(1024)S(1)} %broadcast_clamp_fusion), kind=kCustom, calls=%fused_computation | custom fusion | bytes 2101248 | tf_op jit(solution)/shard_map/jit(_take)/gather | solution.py:13
  14.8 0.0 copy-done
  14.8 2.9 %convolution_bitcast_fusion = f32[1024,512]{0,1:T(8,128)} fusion(bf16[1024,1024]{1,0:T(8,128)(2,1)S(1)} %copy-done, bf16[1024,512]{1,0:T(8,128)(2,1)S(1)} %gather_fusion, pred[1024]{0:T(1024)(128)(4,1)S(1)} %compare_and_fusion), kind=kOutput, calls=%fused_computation.6 | convolution fusion | flops 1074266112 | bytes 5243904 | tf_op jit(solution)/shard_map/dot_general | solution.py:14
  17.7 2.9 %copy.13 = f32[1024,512]{1,0:T(8,128)} copy(f32[1024,512]{0,1:T(8,128)} %convolution_bitcast_fusion) | data formatting | bytes 4194304 | tf_op jit(solution)/shard_map/dot_general | solution.py:14
  20.6 0.0 copy-start.1
  20.6 2.5 %gather_fusion.1 = f32[128,512]{1,0:T(8,128)S(1)} fusion(f32[1024,512]{1,0:T(8,128)} %copy.13, s32[1024]{0:T(1024)S(1)} %pad_clamp_fusion), kind=kCustom, calls=%fused_computation.1 | custom fusion | bytes 524800 | tf_op jit(solution)/shard_map/jit(_take)/gather | solution.py:17
  23.1 0.0 copy-start.3
  23.1 0.1 copy.14
  23.2 0.0 copy-done.1
  23.2 0.0 copy-start.2
  23.3 0.0 copy-start.4
  23.3 2.1 %fusion.15 = (bf16[128,512]{0,1:T(8,128)(2,1)S(1)}, f32[128,512]{0,1:T(8,128)S(1)}) fusion(f32[128,512]{0,1:T(8,128)S(1)} %copy.14, pred[128]{0:T(512)(128)(4,1)S(1)} %compare_and_fusion.1, bf16[1024,128]{1,0:T(8,128)(2,1)S(1)} %copy-done.1, f32[1024,512]{0,1:T(8,128)} %convolution_bitcast_fusion), kind=kOutput, calls=%fused_computation.34 | convolution fusion | flops 134938624 | bytes 3014784 | tf_op jit(solution)/shard_map/lr,lc->rc/dot_general | solution.py:16
  25.3 11.5 %all_gather.9 = bf16[512,512]{0,1:T(8,128)(2,1)S(1)} all-gather(bf16[128,512]{0,1:T(8,128)(2,1)S(1)} %get-tuple-element.5), channel_id=1, replica_groups=mesh['aa'=8,'ba'=4] {'ba'}, dimensions={0}, use_global_device_ids=true | all-gather | bytes 655360 | tf_op jit(solution)/shard_map/all_gather | solution.py:21
  36.8 0.0 copy-done.3
  36.8 0.3 convolution_bitcast_fusion.2
  37.1 0.0 copy-done.2
  37.2 1.0 fusion.3
  38.2 0.0 all-reduce.2.cloned.1.call-update
  38.2 0.0 all-gather.2.cloned.1.call-start
  38.3 42.4 %all-reduce.2.cloned.1.call-done = bf16[128,512]{0,1:T(8,128)(2,1)} async-done(((bf16[128,512]{0,1:T(8,128)(2,1)}), bf16[128,512]{0,1:T(8,128)(2,1)}) %all-reduce.2.cloned.1.call-update) | async-done | bytes 131088 | tf_op jit(solution)/shard_map/psum | solution.py:26
  80.7 0.0 all-gather.2.cloned.1.call-update
  80.7 0.0 copy-done.4
  80.7 9.2 %all_gather.11 = bf16[128,1024]{1,0:T(8,128)(2,1)S(1)} all-gather(bf16[32,1024]{1,0:T(8,128)(2,1)S(1)} %copy-done.4), channel_id=1, replica_groups=mesh['aa'=8,'ba'=4] {'ba'}, dimensions={0}, use_global_device_ids=true | all-gather | bytes 327680 | tf_op jit(solution)/shard_map/all_gather | solution.py:12
  89.9 16.4 %all-gather.2.cloned.1.call-done = bf16[1024,512]{0,1:T(8,128)(2,1)} async-done(((bf16[128,512]{0,1:T(8,128)(2,1)}), bf16[1024,512]{0,1:T(8,128)(2,1)}) %all-gather.2.cloned.1.call-update) | async-done | bytes 1048592 | tf_op jit(solution)/shard_map/all_gather | solution.py:29
  106.3 1.7 %fusion.16 = f32[512,128]{1,0:T(8,128)S(1)} fusion(bf16[1024,512]{0,1:T(8,128)(2,1)} %all-gather.2.cloned.1.call-done, bf16[128,1024]{1,0:T(8,128)(2,1)S(1)} %all_gather.11), kind=kOutput, calls=%fused_computation.35 | convolution fusion | flops 134217728 | bytes 1572864 | tf_op jit(solution)/shard_map/dot_general | solution.py:27
  108.0 0.4 fusion.1
  108.4 0.1 copy.15
  108.5 1.7 %convolution_bitcast_fusion.1 = f32[1024,512]{1,0:T(8,128)} fusion(bf16[1024,128]{1,0:T(8,128)(2,1)S(1)} %copy-done.1, f32[128,512]{0,1:T(8,128)S(1)} %fusion.1), kind=kOutput, calls=%fused_computation.7 | convolution fusion | flops 134283264 | bytes 2621440 | tf_op jit(solution)/shard_map/dot_general | solution.py:35
  110.3 4.2 %scatter_fusion = f32[1024,512]{1,0:T(8,128)} fusion(f32[1024,512]{1,0:T(8,128)} %convolution_bitcast_fusion.1, s32[128]{0:T(128)S(1)} %fusion.13, f32[128,512]{1,0:T(8,128)S(1)} %copy.15), kind=kCustom, calls=%fused_computation.2 | custom fusion | flops 65536 | bytes 786944 | tf_op jit(solution)/shard_map/scatter-add | solution.py:38
  114.4 4.5 %fusion = bf16[1024,512]{0,1:T(8,128)(2,1)} fusion(f32[1024,512]{0,1:T(8,128)} %convolution_bitcast_fusion, bf16[1024,1024]{1,0:T(8,128)(2,1)S(1)} %copy-done, f32[1024,512]{1,0:T(8,128)} %scatter_fusion), kind=kOutput, calls=%fused_computation.5 | convolution fusion | flops 1075314688 | bytes 7340032 | tf_op jit(solution)/shard_map/dot_general | solution.py:39
  118.9 1.5 %copy.16 = bf16[1024,512]{1,0:T(8,128)(2,1)S(1)} copy(bf16[1024,512]{0,1:T(8,128)(2,1)} %fusion) | data formatting | bytes 2097152 | tf_op jit(solution)/shard_map/convert_element_type | solution.py:43
  120.4 6.1 %scatter_custom_fusion.1 = bf16[1024,512]{1,0:T(8,128)(2,1)} fusion(s32[1024]{0:T(1024)S(1)} %bitcast.44, bf16[1024,512]{1,0:T(8,128)(2,1)S(1)} %copy.16, bf16[]{:T(256)} %constant.18.clone.1), kind=kCustom, calls=%fused_computation.20 | custom fusion | bytes 1048578 | tf_op jit(solution)/shard_map/scatter | solution.py:43
  (2 shorter events, 0.0 us)
Async XLA Ops:
  6.5 8.2 %copy-start = (bf16[1024,1024]{1,0:T(8,128)(2,1)S(1)}, bf16[1024,1024]{1,0:T(8,128)(2,1)}, u32[]{:S(2)}) copy-start(bf16[1024,1024]{1,0:T(8,128)(2,1)} %param.11) | copy-start | bytes 6291460
  6.5 74.1 %all-reduce.2.cloned.1.call-start = ((), (), s32[]{:S(2)}) async-start(), calls=%async_computation | async-start | bytes 262144 | tf_op jit(solution)/shard_map/psum | solution.py:26
  20.6 2.7 %copy-start.1 = (bf16[1024,128]{1,0:T(8,128)(2,1)S(1)}, bf16[1024,128]{1,0:T(8,128)(2,1)}, u32[]{:S(2)}) copy-start(bf16[1024,128]{1,0:T(8,128)(2,1)} %param.12) | copy-start | bytes 786436
  23.1 13.7 %copy-start.3 = (bf16[128,512]{1,0:T(8,128)(2,1)S(1)}, bf16[128,512]{1,0:T(8,128)(2,1)}, u32[]{:S(2)}) copy-start(bf16[128,512]{1,0:T(8,128)(2,1)} %param.13) | copy-start | bytes 393220
  23.2 13.9 %copy-start.2 = (f32[128,128]{1,0:T(8,128)S(1)}, f32[128,128]{1,0:T(8,128)}, u32[]{:S(2)}) copy-start(f32[128,128]{1,0:T(8,128)} %param.14) | copy-start | bytes 196612
  23.3 57.4 %copy-start.4 = (bf16[32,1024]{1,0:T(8,128)(2,1)S(1)}, bf16[32,1024]{1,0:T(8,128)(2,1)}, u32[]{:S(2)}) copy-start(bf16[32,1024]{1,0:T(8,128)(2,1)} %param.15) | copy-start | bytes 196612
  38.2 68.1 %all-gather.2.cloned.1.call-start = ((), (), s32[]{:S(2)}) async-start(), calls=%async_computation.1 | async-start | bytes 1179648 | tf_op jit(solution)/shard_map/all_gather | solution.py:29
Sparse Core Ops, SparseCore 0:
  38.3 42.2 all-reduce.1
  82.3 23.9 all-gather.1
where the time goes:
time: 134 us; the launch traced here: 133 us
  waiting for transfers between devices  58.8 us (44%)
  blocking collectives  20.7 us (15%)
  local copies, waits for them, and re-layouts  18.6 us (14%)
  matrix products  14.6 us (11%)
  between operations  13.5 us (10%)
  other arithmetic  7.04 us (5%)
    psum x1, waiting for transfers between devices, shards(): group_coeffs = lax.psum(partial_value.astype(jnp.bfloat16), 'ba')  42.4 us
    all_gather x1, waiting for transfers between devices, shards(): lax.all_gather(group_coeffs, 'aa', axis=0, tiled=True)  16.4 us
    all_gather x1, blocking collectives, shards(): lax.all_gather(coeff_low, 'ba', axis=0, tiled=True)  11.5 us
    all_gather x1, blocking collectives, shards(): rows_matrix = lax.all_gather(top_core, 'ba', axis=0, tiled=True)  9.24 us
    scatter x1, local copies, waits for them, and re-layouts, shards(): return placed.at[ordering].set(solved.astype(jnp.bfloat16))  6.08 us
    gather x1, local copies, waits for them, and re-layouts, shards(): ordered = jnp.take(right_sides, ordering, axis=0)  5.35 us
    dot_general x1, matrix products, shards(): jnp.dot(leaf_inverse, expanded.astype(jnp.bfloat16), preferred_element_ty...  4.5 us
    scatter-add x1, other arithmetic, shards(): expanded = expanded.at[skel_rows].add(correction)  4.18 us
  transfers between devices with their start and end apart: 2, of which 2 were waited for; matrix products, arithmetic and copies ran while one was open for 0% of the time, Pallas kernels for 0%

commit v1 on v0

v1 whole, which is shorter than its diff:
```python
import functools

import jax
import jax.numpy as jnp
from jax import lax
from jax.experimental import pallas as pl
from jax.experimental.pallas import tpu as pltpu
from jax.sharding import PartitionSpec as P

BF = jnp.bfloat16
F32 = jnp.float32
NN = (((1,), (0,)), ((), ()))
NT = (((1,), (1,)), ((), ()))
TN = (((0,), (0,)), ((), ()))


def dot(a, b, dims=NN):
    return lax.dot_general(a, b, dims, preferred_element_type=F32)


def partners(n, k):
    half = (n - 2) // 2
    return [(k - 1 + j) % (n - 1) + 1 for j in range(1, half + 1)]


def column_of(row, count):
    wide = jnp.broadcast_to(row.astype(F32), (count, row.shape[1]))
    return wide.T.astype(jnp.int32)


def order_rows(order, size):
    return jnp.where(
        lax.broadcasted_iota(jnp.int32, (size, size), 0) == order, 1.0, 0.0
    ).astype(BF)


def basis_pair(skel, basis):
    points, rank = basis.shape
    ones = jnp.where(
        lax.broadcasted_iota(jnp.int32, (points, rank), 0) == skel, 1.0, 0.0
    ).astype(BF)
    return jnp.concatenate([basis, ones], axis=1)


def front_kernel(n, order_ref, skel_ref, sides_ref, inverse_ref, basis_ref, core_ref, transfer_ref, top_ref, *rest):
    messages, (own_ref, held, coeffs, sems) = rest[: n - 1], rest[n - 1 :]
    me = lax.axis_index("ba")
    points, rank = basis_ref.shape
    pieces = sems.shape[0]
    rows = points // pieces
    copies = [
        pltpu.make_async_copy(
            inverse_ref.at[pl.ds(j * rows, rows)], held.at[pl.ds(j * rows, rows)], sems.at[j]
        )
        for j in range(pieces)
    ]
    for copy in copies:
        copy.start()
    share = own_ref.shape[0]
    transfer = transfer_ref[...].astype(BF)
    groups = top_ref.shape[1] // rank
    top = top_ref[...].astype(F32)
    top = jnp.concatenate([top[:, g * rank : (g + 1) * rank] for g in range(groups)], axis=0).astype(BF)
    for k in range(1, n):
        out = messages[k - 1]
        at = share
        out[at : at + rank, :] = transfer
        at += rank
        for m in [k] + partners(n, k):
            block = me ^ (k ^ m)
            out[at : at + rank, :] = core_ref[:, pl.ds(pl.multiple_of(block * rank, rank), rank)]
            at += rank
        out[at:, :] = top
    placed = order_rows(order_ref[...], points)
    pair = basis_pair(skel_ref[...], basis_ref[...])
    both = None
    for j, copy in enumerate(copies):
        copy.wait()
        part = dot(pair[j * rows : (j + 1) * rows], held[j * rows : (j + 1) * rows, :], TN)
        both = part if both is None else both + part
    up = (both[:rank] + both[rank:]).astype(BF)
    up = dot(up, placed, NT).astype(BF)
    coeffs[...] = dot(up, sides_ref[...]).T.astype(BF)
    own_ref[...] = coeffs[pl.ds(pl.multiple_of(me * share, share), share), :]
    for k in range(1, n):
        messages[k - 1][0:share, :] = coeffs[pl.ds(pl.multiple_of((me ^ k) * share, share), share), :]


def leaf_kernel(order_ref, skel_ref, sides_ref, inverse_ref, basis_ref, applied_ref, down_ref):
    points, rank = basis_ref.shape
    order = order_ref[...]
    column = column_of(order, 128)
    lanes = lax.broadcasted_iota(jnp.int32, (points, 128), 1)
    gather = jnp.concatenate(
        [jnp.where(column == lanes + j * 128, 1.0, 0.0).astype(BF) for j in range(points // 128)], axis=1
    )
    ordered = dot(gather, sides_ref[...]).astype(BF)
    applied = dot(inverse_ref[...], ordered).astype(BF)
    placed = order_rows(order, points)
    applied_ref[...] = dot(placed, applied).astype(BF)
    both = dot(inverse_ref[...], basis_pair(skel_ref[...], basis_ref[...]))
    down = (both[:, :rank] + both[:, rank:]).astype(BF)
    down_ref[...] = dot(placed, down).astype(BF)


def group_kernel(n, own_ref, core_ref, transfer_ref, *rest):
    messages, (level_ref, group_ref) = rest[: n - 1], rest[n - 1 :]
    me = lax.axis_index("ba")
    share, rank = own_ref.shape
    core = {}
    for m in range(n):
        core[0, m] = core_ref[:, pl.ds(pl.multiple_of((me ^ m) * rank, rank), rank)]
    for k in range(1, n):
        at = share + rank
        for m in [k] + partners(n, k):
            core[k, m] = messages[k - 1][at : at + rank, :]
            at += rank
    coeffs = [own_ref[...]] + [msg[0:share, :] for msg in messages]
    transfers = [transfer_ref[...].astype(BF)] + [msg[share : share + rank, :] for msg in messages]
    total = None
    for k in range(n):
        level = None
        for m in range(n):
            term = dot(coeffs[m], core[m, k]) if (m, k) in core else dot(coeffs[m], core[k, m], NT)
            level = term if level is None else level + term
        level_ref[:, k * rank : (k + 1) * rank] = level
        rest_of = (coeffs[k].astype(F32) - level).astype(BF)
        term = dot(rest_of, transfers[k])
        total = term if total is None else total + term
    group_ref[...] = total.astype(BF)


def top_rows_kernel(n, groups, top_ref, transfer_ref, *rest):
    messages, (rows_ref, transfers_ref, held) = rest[: n - 1], rest[n - 1 :]
    me = lax.axis_index("ba")
    mine = lax.axis_index("aa")
    rank = transfer_ref.shape[0]
    part = top_ref.shape[0]
    transfers_ref[0:rank, :] = transfer_ref[...].astype(BF)
    held[pl.ds(pl.multiple_of(me * part, part), part), :] = top_ref[...].astype(F32)
    for k in range(1, n):
        msg = messages[k - 1]
        share = msg.shape[0] - (groups * part + rank * (2 + len(partners(n, k))))
        transfers_ref[k * rank : (k + 1) * rank, :] = msg[share : share + rank, :]
        tail = msg[msg.shape[0] - groups * part :, :].astype(F32)
        for g in range(groups):
            held[pl.ds(pl.multiple_of((me ^ k) * part, part), part), g * rank : (g + 1) * rank] = tail[
                g * part : (g + 1) * part
            ]
    for m in range(groups):
        rows_ref[:, m * rank : (m + 1) * rank] = held[
            :, pl.ds(pl.multiple_of((mine ^ m) * rank, rank), rank)
        ].astype(BF)


def top_kernel(n, groups, rows_ref, transfers_ref, level_ref, *rest):
    pieces, outs = rest[:groups], rest[groups:]
    rank = transfers_ref.shape[1]
    stacked = jnp.concatenate([piece[...] for piece in pieces], axis=1)
    top = dot(stacked, rows_ref[...], NT).astype(BF)
    correction = (level_ref[...] + dot(top, transfers_ref[...], NT)).astype(BF)
    for k in range(n):
        outs[k][...] = correction[:, k * rank : (k + 1) * rank]


def final_kernel(n, applied_ref, down_ref, *rest):
    pieces, (out_ref, correction) = rest[:n], rest[n:]
    me = lax.axis_index("ba")
    share = pieces[0].shape[0]
    for k in range(n):
        correction[pl.ds(pl.multiple_of((me ^ k) * share, share), share), :] = pieces[k][...]
    out_ref[...] = (applied_ref[...].astype(F32) - dot(down_ref[...], correction[...], NT)).astype(BF)


def shape(dims, kind=BF):
    return jax.ShapeDtypeStruct(dims, kind)


def call(body, outs, in_specs=None, scratch=(), flops=0, moved=0):
    limit = pltpu.CompilerParams(vmem_limit_bytes=48 * 1024 * 1024)
    extra = {} if in_specs is None else {"in_specs": in_specs}
    return pl.pallas_call(
        body,
        out_shape=outs,
        scratch_shapes=list(scratch),
        compiler_params=limit,
        cost_estimate=pl.CostEstimate(flops=flops, bytes_accessed=moved, transcendentals=0),
        **extra,
    )


def shards(n, groups, sides, order, skel, inverse, basis, core, transfer, top):
    points, cols = sides.shape
    rank = basis.shape[1]
    share = cols // n
    part = top.shape[0]
    vmem = pl.BlockSpec(memory_space=pltpu.VMEM)
    sizes = [share + rank * (2 + len(partners(n, k))) + groups * part for k in range(1, n)]
    front = call(
        functools.partial(front_kernel, n),
        [shape((size, rank)) for size in sizes] + [shape((share, rank))],
        in_specs=[vmem, vmem, vmem, pl.BlockSpec(memory_space=pl.ANY)] + [vmem] * 4,
        scratch=[
            pltpu.VMEM((points, points), BF),
            pltpu.VMEM((cols, rank), BF),
            pltpu.SemaphoreType.DMA((2,)),
        ],
        flops=2 * rank * points * (3 * points + cols),
        moved=2 * points * (points + cols + rank),
    )(order, skel, sides, inverse, basis, core, transfer, top)
    own = front[n - 1]
    received = [
        lax.ppermute(front[k - 1], "ba", [(i, i ^ k) for i in range(n)]) for k in range(1, n)
    ]
    applied, down = call(
        leaf_kernel,
        [shape((points, cols)), shape((points, rank))],
        flops=2 * points * points * (3 * cols + 3 * rank),
        moved=2 * points * (points + 2 * cols + 2 * rank),
    )(order, skel, sides, inverse, basis)
    level, group = call(
        functools.partial(group_kernel, n),
        [shape((share, n * rank), F32), shape((share, rank))],
        flops=2 * share * n * rank * (n + 1) * rank,
        moved=4 * share * n * rank,
    )(own, core, transfer, *received)
    rows, transfers = call(
        functools.partial(top_rows_kernel, n, groups),
        [shape((rank, groups * rank)), shape((n * rank, rank))],
        scratch=[pltpu.VMEM((rank, groups * rank), F32)],
        moved=4 * rank * groups * rank,
    )(top, transfer, *received)
    pieces = {0: group}
    for m in range(2, groups, 2):
        pieces[m] = lax.ppermute(group, "aa", [(i, i ^ m) for i in range(groups)])
    for m in range(0, groups, 2):
        pieces[m + 1] = lax.ppermute(pieces[m], "aa", [(i, i ^ 1) for i in range(groups)])
    corrections = call(
        functools.partial(top_kernel, n, groups),
        [shape((share, rank))] * n,
        flops=2 * share * rank * (groups + n) * rank,
        moved=4 * share * n * rank,
    )(rows, transfers, level, *[pieces[m] for m in range(groups)])
    back = [corrections[0]] + [
        lax.ppermute(corrections[k], "ba", [(i, i ^ k) for i in range(n)]) for k in range(1, n)
    ]
    return call(
        functools.partial(final_kernel, n),
        shape((points, cols)),
        scratch=[pltpu.VMEM((cols, rank), BF)],
        flops=2 * points * cols * rank,
        moved=4 * points * cols,
    )(applied, down, *back)


def solution(mesh):
    spec = P(("aa", "ba"), None)
    return jax.shard_map(
        functools.partial(shards, mesh.shape["ba"], mesh.shape["aa"]),
        mesh=mesh,
        in_specs=(spec,) * 8,
        out_specs=spec,
        check_vma=False,
    )
```

time: 134 us -> 45.8 us (0.34)
  waiting for transfers between devices: 58.8 us -> 13.8 us
  blocking collectives: 20.7 us -> 0 us
  matrix products: 14.6 us -> 0 us
  between operations: 13.5 us -> 0.13 us
  starting transfers between devices: 0.04 us -> 13.1 us
  local copies, waits for them, and re-layouts: 18.6 us -> 7.71 us
  Pallas kernels: 0 us -> 10.7 us
  other arithmetic: 7.04 us -> 0 us
    psum x1 -> x0, waiting for transfers between devices: 42.4 us -> none  [shards(): group_coeffs = lax.psum(partial_value.astype(jnp.bfloat16), 'ba')]
    all_gather x2 -> x0, blocking collectives: 20.7 us -> none  [the longest x1 11.5 us: shards(): lax.all_gather(coeff_low, 'ba', axis=0, tiled=True)]
    all_gather x1 -> x0, waiting for transfers between devices: 16.4 us -> none  [shards(): lax.all_gather(group_coeffs, 'aa', axis=0, tiled=True)]
    dot_general x8 -> x0, matrix products: 14.6 us -> none  [the longest x1 4.5 us: shards(): jnp.dot(leaf_inverse, expanded.astype(jnp.bfloat16), preferred_element_ty...]
    ppermute x0 -> x13, waiting for transfers between devices: none -> 13.8 us  [the longest x3 9.02 us: shards(): lax.ppermute(front[k - 1], 'ba', [(i, i ^ k) for i in range(n)])]
    ppermute x0 -> x13, starting transfers between devices: none -> 13.1 us  [the longest x3 4.55 us: shards(): lax.ppermute(front[k - 1], 'ba', [(i, i ^ k) for i in range(n)])]
    pallas_call x0 -> x6, Pallas kernels: none -> 10.7 us  [the longest x1 5.55 us: shards(): call(leaf_kernel, [shape((points, cols)), shape((points, rank))], flops=2...]
    gather x3 -> x0, local copies, waits for them, and re-layouts: 7.98 us -> none  [the longest x1 5.35 us: shards(): ordered = jnp.take(right_sides, ordering, axis=0)]
  transfers between devices with their start and end apart: 2 -> 13, of which waited for: 2 -> 6; matrix products, arithmetic and copies ran while one was open for 0% -> 0% of each run, Pallas kernels for 0% -> 12%
where the time goes in v1:
time: 45.8 us; the launch traced here: 45.4 us
  waiting for transfers between devices  13.8 us (30%)
  starting transfers between devices  13.1 us (29%)
  Pallas kernels  10.7 us (23%)
  local copies, waits for them, and re-layouts  7.71 us (17%)
    ppermute x3, waiting for transfers between devices, shards(): lax.ppermute(front[k - 1], 'ba', [(i, i ^ k) for i in range(n)])  9.02 us
    unnamed x24, local copies, waits for them, and re-layouts  7.71 us
    pallas_call x1, Pallas kernels, shards(): call(leaf_kernel, [shape((points, cols)), shape((points, rank))], flops=2...  5.55 us
    ppermute x3, starting transfers between devices, shards(): lax.ppermute(front[k - 1], 'ba', [(i, i ^ k) for i in range(n)])  4.55 us
    ppermute x3, starting transfers between devices, shards(): pieces[m] = lax.ppermute(group, 'aa', [(i, i ^ m) for i in range(groups)])  4.45 us
    ppermute x3, waiting for transfers between devices, shards(): pieces[m] = lax.ppermute(group, 'aa', [(i, i ^ m) for i in range(groups)])  4.02 us
    ppermute x3, starting transfers between devices, shards(): lax.ppermute(corrections[k], 'ba', [(i, i ^ k) for i in range(n)])  3.55 us
    pallas_call x1, Pallas kernels, shards(): call(functools.partial(front_kernel, n), [shape((size, rank)) for size in...  2.51 us
  transfers between devices with their start and end apart: 13, of which 6 were waited for; matrix products, arithmetic and copies ran while one was open for 0% of the time, Pallas kernels for 12%

profile of v1, /device:TPU:0, one launch (start us, length us, event | category | flops | bytes accessed | tf_op | source)
XLA Modules:
  0.0 45.4 jit_solution(507364782948319384)
XLA Ops:
  0.0 0.0 copy-start
  0.0 1.6 %copy-done = bf16[1024,1024]{1,0:T(8,128)(2,1)S(1)} copy-done((bf16[1024,1024]{1,0:T(8,128)(2,1)S(1)}, bf16[1024,1024]{1,0:T(8,128)(2,1)}, u32[]{:S(2)}) %copy-start) | copy-done | bytes 2097176
  1.6 1.2 %copy-done.2 = bf16[1024,512]{1,0:T(8,128)(2,1)S(1)} copy-done((bf16[1024,512]{1,0:T(8,128)(2,1)S(1)}, bf16[1024,512]{1,0:T(8,128)(2,1)}, u32[]{:S(2)}) %copy-start.2) | copy-done | bytes 1048600
  2.8 0.8 %copy-done.4 = f32[128,128]{1,0:T(8,128)S(1)} copy-done((f32[128,128]{1,0:T(8,128)S(1)}, f32[128,128]{1,0:T(8,128)}, u32[]{:S(2)}) %copy-start.4) | copy-done | bytes 65560
  3.7 0.9 %copy-done.5 = bf16[128,512]{1,0:T(8,128)(2,1)S(1)} copy-done((bf16[128,512]{1,0:T(8,128)(2,1)S(1)}, bf16[128,512]{1,0:T(8,128)(2,1)}, u32[]{:S(2)}) %copy-start.5) | copy-done | bytes 131096
  4.6 0.8 %copy-done.6 = bf16[32,1024]{1,0:T(8,128)(2,1)S(1)} copy-done((bf16[32,1024]{1,0:T(8,128)(2,1)S(1)}, bf16[32,1024]{1,0:T(8,128)(2,1)}, u32[]{:S(2)}) %copy-start.6) | copy-done | bytes 65560
  5.4 0.9 %copy-done.7 = bf16[1024,128]{1,0:T(8,128)(2,1)S(1)} copy-done((bf16[1024,128]{1,0:T(8,128)(2,1)S(1)}, bf16[1024,128]{1,0:T(8,128)(2,1)}, u32[]{:S(2)}) %copy-start.7) | copy-done | bytes 262168
  6.4 0.7 %copy-done.8 = s32[1,1024]{1,0:T(1,128)S(1)} copy-done((s32[1,1024]{1,0:T(1,128)S(1)}, s32[1,1024]{1,0:T(1,128)}, u32[]{:S(2)}) %copy-start.8) | copy-done | bytes 4120
  7.0 0.7 %copy-done.10 = s32[1,128]{1,0:T(1,128)S(1)} copy-done((s32[1,128]{1,0:T(1,128)S(1)}, s32[1,128]{1,0:T(1,128)}, u32[]{:S(2)}) %copy-start.10) | copy-done | bytes 536
  7.7 2.5 %shard_map.83 = (bf16[768,128]{1,0:T(8,128)(2,1)S(1)}, bf16[768,128]{1,0:T(8,128)(2,1)S(1)}, bf16[768,128]{1,0:T(8,128)(2,1)S(1)}, bf16[128,128]{1,0:T(8,128)(2,1)S(1)}) custom-call(s32[1,1024]{1,0:T(1,128)S(1)} %copy-done.8, s32[1,128]{1,0:T(1,128)S(1)} %copy-done.10, bf16[1024,512]{1,0:T(8,128)(2,1)S(1)} %copy-done.2, bf16[1024,1024]{1,0:T(8,128)(2,1)S(1)} %copy-done, ...), custom_call_target="tpu_custom_call" | custom-call | flops 939524096 | bytes 3407872 | tf_op jit(solution)/shard_map/pallas_call | solution.py:199
  10.2 0.0 copy-start.1
  10.2 0.0 copy-start.9
  10.2 0.0 copy-start.11
  10.3 3.0 %collective-permute-start = (bf16[768,128]{1,0:T(8,128)(2,1)S(1)}, bf16[768,128]{1,0:T(8,128)(2,1)S(1)}, u32[]{:S(2)}, u32[]{:S(2)}) collective-permute-start(bf16[768,128]{1,0:T(8,128)(2,1)S(1)} %get-tuple-element.21), channel_id=1, source_target_pairs={{0,1},{1,0},{2,3},{3,2},{4,5},{5,4},{6,7},{7,6},{8,9},{9,8},{10,11... | collective-permute-start | bytes 589832 | tf_op jit(solution)/shard_map/ppermute | solution.py:213
  13.3 1.5 %collective-permute-start.1 = (bf16[768,128]{1,0:T(8,128)(2,1)S(1)}, bf16[768,128]{1,0:T(8,128)(2,1)S(1)}, u32[]{:S(2)}, u32[]{:S(2)}) collective-permute-start(bf16[768,128]{1,0:T(8,128)(2,1)S(1)} %get-tuple-element.22), channel_id=1, source_target_pairs={{0,2},{1,3},{2,0},{3,1},{4,6},{5,7},{6,4},{7,5},{8,10},{9,11},{10,... | collective-permute-start | bytes 589832 | tf_op jit(solution)/shard_map/ppermute | solution.py:213
  14.8 0.0 collective-permute-start.2
  14.8 4.2 %collective-permute-done.rest_0_ = bf16[768,128]{1,0:T(8,128)(2,1)S(1)} collective-permute-done((bf16[768,128]{1,0:T(8,128)(2,1)S(1)}, bf16[768,128]{1,0:T(8,128)(2,1)S(1)}, u32[]{:S(2)}, u32[]{:S(2)}) %collective-permute-start) | collective-permute-done | bytes 196640 | tf_op jit(solution)/shard_map/ppermute | solution.py:213
  19.0 4.8 %collective-permute-done.1.rest_1_ = bf16[768,128]{1,0:T(8,128)(2,1)S(1)} collective-permute-done((bf16[768,128]{1,0:T(8,128)(2,1)S(1)}, bf16[768,128]{1,0:T(8,128)(2,1)S(1)}, u32[]{:S(2)}, u32[]{:S(2)}) %collective-permute-start.1) | collective-permute-done | bytes 196640 | tf_op jit(solution)/shard_map/ppermute | solution.py:213
  23.8 0.0 collective-permute-done.2.rest_2_
  23.8 0.7 %shard_map.85 = (f32[128,512]{1,0:T(8,128)S(1)}, bf16[128,128]{1,0:T(8,128)(2,1)S(1)}) custom-call(bf16[128,128]{1,0:T(8,128)(2,1)S(1)} %get-tuple-element.26.own_ref, bf16[128,512]{1,0:T(8,128)(2,1)S(1)} %copy-done.5, f32[128,128]{1,0:T(8,128)S(1)} %copy-done.4, bf16[768,128]{1,0:T(8,128)(2,1)S(1)} %collective-permute-done.rest_0_, ...), custom_call_target="tpu_custom_call" | custom-call | flops 83886080 | bytes 262144 | tf_op jit(solution)/shard_map/pallas_call | solution.py:221
  24.5 3.7 %collective-permute-start.8 = (bf16[128,128]{1,0:T(8,128)(2,1)S(1)}, bf16[128,128]{1,0:T(8,128)(2,1)S(1)}, u32[]{:S(2)}, u32[]{:S(2)}) collective-permute-start(bf16[128,128]{1,0:T(8,128)(2,1)S(1)} %get-tuple-element.28.rest_0_), channel_id=1, source_target_pairs={{0,24},{4,28},{8,16},{12,20},{16,8},{20,12},{24,0},{28,4},{1,25},{... | collective-permute-start | bytes 98312 | tf_op jit(solution)/shard_map/ppermute | solution.py:235
  28.2 0.0 collective-permute-start.6
  28.2 0.8 %collective-permute-start.4 = (bf16[128,128]{1,0:T(8,128)(2,1)S(1)}, bf16[128,128]{1,0:T(8,128)(2,1)S(1)}, u32[]{:S(2)}, u32[]{:S(2)}) collective-permute-start(bf16[128,128]{1,0:T(8,128)(2,1)S(1)} %get-tuple-element.28.rest_0_), channel_id=1, source_target_pairs={{0,8},{4,12},{8,0},{12,4},{16,24},{20,28},{24,16},{28,20},{1,9},{5... | collective-permute-start | bytes 98312 | tf_op jit(solution)/shard_map/ppermute | solution.py:235
  29.0 0.0 collective-permute-start.3
  29.0 1.3 %collective-permute-done.8.rest_6_ = bf16[128,128]{1,0:T(8,128)(2,1)S(1)} collective-permute-done((bf16[128,128]{1,0:T(8,128)(2,1)S(1)}, bf16[128,128]{1,0:T(8,128)(2,1)S(1)}, u32[]{:S(2)}, u32[]{:S(2)}) %collective-permute-start.8) | collective-permute-done | bytes 32800 | tf_op jit(solution)/shard_map/ppermute | solution.py:235
  30.3 0.0 collective-permute-start.9
  30.3 2.7 %collective-permute-done.6.rest_4_ = bf16[128,128]{1,0:T(8,128)(2,1)S(1)} collective-permute-done((bf16[128,128]{1,0:T(8,128)(2,1)S(1)}, bf16[128,128]{1,0:T(8,128)(2,1)S(1)}, u32[]{:S(2)}, u32[]{:S(2)}) %collective-permute-start.6) | collective-permute-done | bytes 32800 | tf_op jit(solution)/shard_map/ppermute | solution.py:235
  33.0 0.0 collective-permute-start.7
  33.0 0.0 collective-permute-done.4.rest_2_
  33.0 0.5 %collective-permute-start.5 = (bf16[128,128]{1,0:T(8,128)(2,1)S(1)}, bf16[128,128]{1,0:T(8,128)(2,1)S(1)}, u32[]{:S(2)}, u32[]{:S(2)}) collective-permute-start(bf16[128,128]{1,0:T(8,128)(2,1)S(1)} %collective-permute-done.4.rest_2_), channel_id=1, source_target_pairs={{0,4},{4,0},{8,12},{12,8},{16,20},{20,16},{24,28},{28,24},{1,5},{5... | collective-permute-start | bytes 98312 | tf_op jit(solution)/shard_map/ppermute | solution.py:237
  33.5 0.1 shard_map.84
  33.7 0.0 collective-permute-done.3.rest_1_
  33.7 0.0 collective-permute-done.9.rest_7_
  33.7 0.5 %collective-permute-done.7.rest_5_ = bf16[128,128]{1,0:T(8,128)(2,1)S(1)} collective-permute-done((bf16[128,128]{1,0:T(8,128)(2,1)S(1)}, bf16[128,128]{1,0:T(8,128)(2,1)S(1)}, u32[]{:S(2)}, u32[]{:S(2)}) %collective-permute-start.7) | collective-permute-done | bytes 32800 | tf_op jit(solution)/shard_map/ppermute | solution.py:237
  34.2 0.2 collective-permute-done.5.rest_3_
  34.4 0.4 shard_map.86
  34.8 1.3 %collective-permute-start.10 = (bf16[128,128]{1,0:T(8,128)(2,1)S(1)}, bf16[128,128]{1,0:T(8,128)(2,1)S(1)}, u32[]{:S(2)}, u32[]{:S(2)}) collective-permute-start(bf16[128,128]{1,0:T(8,128)(2,1)S(1)} %get-tuple-element.30), channel_id=1, source_target_pairs={{0,1},{1,0},{2,3},{3,2},{4,5},{5,4},{6,7},{7,6},{8,9},{9,8},{10,11... | collective-permute-start | bytes 98312 | tf_op jit(solution)/shard_map/ppermute | solution.py:245
  36.1 0.8 %collective-permute-start.11 = (bf16[128,128]{1,0:T(8,128)(2,1)S(1)}, bf16[128,128]{1,0:T(8,128)(2,1)S(1)}, u32[]{:S(2)}, u32[]{:S(2)}) collective-permute-start(bf16[128,128]{1,0:T(8,128)(2,1)S(1)} %get-tuple-element.31), channel_id=1, source_target_pairs={{0,2},{1,3},{2,0},{3,1},{4,6},{5,7},{6,4},{7,5},{8,10},{9,11},{10,... | collective-permute-start | bytes 98312 | tf_op jit(solution)/shard_map/ppermute | solution.py:245
  36.9 1.4 %collective-permute-start.12 = (bf16[128,128]{1,0:T(8,128)(2,1)S(1)}, bf16[128,128]{1,0:T(8,128)(2,1)S(1)}, u32[]{:S(2)}, u32[]{:S(2)}) collective-permute-start(bf16[128,128]{1,0:T(8,128)(2,1)S(1)} %get-tuple-element.32), channel_id=1, source_target_pairs={{0,3},{1,2},{2,1},{3,0},{4,7},{5,6},{6,5},{7,4},{8,11},{9,10},{10,... | collective-permute-start | bytes 98312 | tf_op jit(solution)/shard_map/ppermute | solution.py:245
  38.4 0.0 copy-done.3
  38.4 0.0 copy-done.1
  38.4 0.0 copy-done.9
  38.4 0.0 copy-done.11
  38.4 5.6 %shard_map.82 = (bf16[1024,512]{1,0:T(8,128)(2,1)S(1)}, bf16[1024,128]{1,0:T(8,128)(2,1)S(1)}) custom-call(s32[1,1024]{1,0:T(1,128)S(1)} %copy-done.9, s32[1,128]{1,0:T(1,128)S(1)} %copy-done.11, bf16[1024,512]{1,0:T(8,128)(2,1)S(1)} %copy-done.3, bf16[1024,1024]{1,0:T(8,128)(2,1)S(1)} %copy-done.1, bf16[1024,128]{1,0:T(8,128)(2,1)S(1)} %copy-done.7), custom_call_target="tpu_custom_call" | custom-call | flops 4026531840 | bytes 4718592 | tf_op jit(solution)/shard_map/pallas_call | solution.py:215
  43.9 0.0 collective-permute-done.10.rest_1_
  44.0 0.0 collective-permute-done.11.rest_2_
  44.0 0.0 collective-permute-done.12.rest_3_
  44.0 1.4 %shard_map.87 = bf16[1024,512]{1,0:T(8,128)(2,1)} custom-call(bf16[1024,512]{1,0:T(8,128)(2,1)S(1)} %get-tuple-element.19.applied_ref, bf16[1024,128]{1,0:T(8,128)(2,1)S(1)} %get-tuple-element.20.down_ref, bf16[128,128]{1,0:T(8,128)(2,1)S(1)} %get-tuple-element.29.rest_0_, bf16[128,128]{1,0:T(8,128)(2,1)S(1)} %collective-permute-done.10.rest_1_, ...), custom_call_target="tpu_custom_call" | custom-call | flops 134217728 | bytes 2097152 | tf_op jit(solution)/shard_map/pallas_call | solution.py:247
  (8 shorter events, 0.0 us)
Async XLA Ops:
  0.0 1.6 %copy-start = (bf16[1024,1024]{1,0:T(8,128)(2,1)S(1)}, bf16[1024,1024]{1,0:T(8,128)(2,1)}, u32[]{:S(2)}) copy-start(bf16[1024,1024]{1,0:T(8,128)(2,1)} %inverse_ref.3) | copy-start | bytes 6291460
  1.6 1.2 %copy-start.2 = (bf16[1024,512]{1,0:T(8,128)(2,1)S(1)}, bf16[1024,512]{1,0:T(8,128)(2,1)}, u32[]{:S(2)}) copy-start(bf16[1024,512]{1,0:T(8,128)(2,1)} %sides_ref.3) | copy-start | bytes 3145732
  2.8 0.8 %copy-start.4 = (f32[128,128]{1,0:T(8,128)S(1)}, f32[128,128]{1,0:T(8,128)}, u32[]{:S(2)}) copy-start(f32[128,128]{1,0:T(8,128)} %transfer_ref.5) | copy-start | bytes 196612
  3.7 0.9 %copy-start.5 = (bf16[128,512]{1,0:T(8,128)(2,1)S(1)}, bf16[128,512]{1,0:T(8,128)(2,1)}, u32[]{:S(2)}) copy-start(bf16[128,512]{1,0:T(8,128)(2,1)} %core_ref.3) | copy-start | bytes 393220
  4.6 0.8 %copy-start.6 = (bf16[32,1024]{1,0:T(8,128)(2,1)S(1)}, bf16[32,1024]{1,0:T(8,128)(2,1)}, u32[]{:S(2)}) copy-start(bf16[32,1024]{1,0:T(8,128)(2,1)} %top_ref.3) | copy-start | bytes 196612
  5.4 0.9 %copy-start.7 = (bf16[1024,128]{1,0:T(8,128)(2,1)S(1)}, bf16[1024,128]{1,0:T(8,128)(2,1)}, u32[]{:S(2)}) copy-start(bf16[1024,128]{1,0:T(8,128)(2,1)} %basis_ref.3) | copy-start | bytes 786436
  6.4 0.7 %copy-start.8 = (s32[1,1024]{1,0:T(1,128)S(1)}, s32[1,1024]{1,0:T(1,128)}, u32[]{:S(2)}) copy-start(s32[1,1024]{1,0:T(1,128)} %order_ref.3) | copy-start | bytes 12292
  7.0 0.7 %copy-start.10 = (s32[1,128]{1,0:T(1,128)S(1)}, s32[1,128]{1,0:T(1,128)}, u32[]{:S(2)}) copy-start(s32[1,128]{1,0:T(1,128)} %skel_ref.3) | copy-start | bytes 1540
  7.7 30.7 %copy-start.3 = (bf16[1024,512]{1,0:T(8,128)(2,1)S(1)}, bf16[1024,512]{1,0:T(8,128)(2,1)}, u32[]{:S(2)}) copy-start(bf16[1024,512]{1,0:T(8,128)(2,1)} %sides_ref.3) | copy-start | bytes 3145732
  10.2 28.2 %copy-start.1 = (bf16[1024,1024]{1,0:T(8,128)(2,1)S(1)}, bf16[1024,1024]{1,0:T(8,128)(2,1)}, u32[]{:S(2)}) copy-start(bf16[1024,1024]{1,0:T(8,128)(2,1)} %inverse_ref.3) | copy-start | bytes 6291460
  10.2 28.2 %copy-start.9 = (s32[1,1024]{1,0:T(1,128)S(1)}, s32[1,1024]{1,0:T(1,128)}, u32[]{:S(2)}) copy-start(s32[1,1024]{1,0:T(1,128)} %order_ref.3) | copy-start | bytes 12292
  10.2 28.1 %copy-start.11 = (s32[1,128]{1,0:T(1,128)S(1)}, s32[1,128]{1,0:T(1,128)}, u32[]{:S(2)}) copy-start(s32[1,128]{1,0:T(1,128)} %skel_ref.3) | copy-start | bytes 1540
  10.3 8.7 %collective-permute-start = (bf16[768,128]{1,0:T(8,128)(2,1)S(1)}, bf16[768,128]{1,0:T(8,128)(2,1)S(1)}, u32[]{:S(2)}, u32[]{:S(2)}) collective-permute-start(bf16[768,128]{1,0:T(8,128)(2,1)S(1)} %get-tuple-element.21), channel_id=1, source_target_pairs={{0,1},{1,0},{2,3},{3,2},{4,5},{5,4},{6,7},{7,6},{8,9},{9,8},{10,11... | collective-permute-start | bytes 589832 | tf_op jit(solution)/shard_map/ppermute | solution.py:213
  13.3 10.6 %collective-permute-start.1 = (bf16[768,128]{1,0:T(8,128)(2,1)S(1)}, bf16[768,128]{1,0:T(8,128)(2,1)S(1)}, u32[]{:S(2)}, u32[]{:S(2)}) collective-permute-start(bf16[768,128]{1,0:T(8,128)(2,1)S(1)} %get-tuple-element.22), channel_id=1, source_target_pairs={{0,2},{1,3},{2,0},{3,1},{4,6},{5,7},{6,4},{7,5},{8,10},{9,11},{10,... | collective-permute-start | bytes 589832 | tf_op jit(solution)/shard_map/ppermute | solution.py:213
  14.8 9.1 %collective-permute-start.2 = (bf16[768,128]{1,0:T(8,128)(2,1)S(1)}, bf16[768,128]{1,0:T(8,128)(2,1)S(1)}, u32[]{:S(2)}, u32[]{:S(2)}) collective-permute-start(bf16[768,128]{1,0:T(8,128)(2,1)S(1)} %get-tuple-element.23), channel_id=1, source_target_pairs={{0,3},{1,2},{2,1},{3,0},{4,7},{5,6},{6,5},{7,4},{8,11},{9,10},{10,... | collective-permute-start | bytes 589832 | tf_op jit(solution)/shard_map/ppermute | solution.py:213
  24.5 5.8 %collective-permute-start.8 = (bf16[128,128]{1,0:T(8,128)(2,1)S(1)}, bf16[128,128]{1,0:T(8,128)(2,1)S(1)}, u32[]{:S(2)}, u32[]{:S(2)}) collective-permute-start(bf16[128,128]{1,0:T(8,128)(2,1)S(1)} %get-tuple-element.28.rest_0_), channel_id=1, source_target_pairs={{0,24},{4,28},{8,16},{12,20},{16,8},{20,12},{24,0},{28,4},{1,25},{... | collective-permute-start | bytes 98312 | tf_op jit(solution)/shard_map/ppermute | solution.py:235
  28.2 4.8 %collective-permute-start.6 = (bf16[128,128]{1,0:T(8,128)(2,1)S(1)}, bf16[128,128]{1,0:T(8,128)(2,1)S(1)}, u32[]{:S(2)}, u32[]{:S(2)}) collective-permute-start(bf16[128,128]{1,0:T(8,128)(2,1)S(1)} %get-tuple-element.28.rest_0_), channel_id=1, source_target_pairs={{0,16},{4,20},{8,24},{12,28},{16,0},{20,4},{24,8},{28,12},{1,17},{... | collective-permute-start | bytes 98312 | tf_op jit(solution)/shard_map/ppermute | solution.py:235
  28.2 4.8 %collective-permute-start.4 = (bf16[128,128]{1,0:T(8,128)(2,1)S(1)}, bf16[128,128]{1,0:T(8,128)(2,1)S(1)}, u32[]{:S(2)}, u32[]{:S(2)}) collective-permute-start(bf16[128,128]{1,0:T(8,128)(2,1)S(1)} %get-tuple-element.28.rest_0_), channel_id=1, source_target_pairs={{0,8},{4,12},{8,0},{12,4},{16,24},{20,28},{24,16},{28,20},{1,9},{5... | collective-permute-start | bytes 98312 | tf_op jit(solution)/shard_map/ppermute | solution.py:235
  29.0 4.7 %collective-permute-start.3 = (bf16[128,128]{1,0:T(8,128)(2,1)S(1)}, bf16[128,128]{1,0:T(8,128)(2,1)S(1)}, u32[]{:S(2)}, u32[]{:S(2)}) collective-permute-start(bf16[128,128]{1,0:T(8,128)(2,1)S(1)} %get-tuple-element.28.rest_0_), channel_id=1, source_target_pairs={{0,4},{4,0},{8,12},{12,8},{16,20},{20,16},{24,28},{28,24},{1,5},{5... | collective-permute-start | bytes 98312 | tf_op jit(solution)/shard_map/ppermute | solution.py:237
  30.3 3.3 %collective-permute-start.9 = (bf16[128,128]{1,0:T(8,128)(2,1)S(1)}, bf16[128,128]{1,0:T(8,128)(2,1)S(1)}, u32[]{:S(2)}, u32[]{:S(2)}) collective-permute-start(bf16[128,128]{1,0:T(8,128)(2,1)S(1)} %collective-permute-done.8.rest_6_), channel_id=1, source_target_pairs={{0,4},{4,0},{8,12},{12,8},{16,20},{20,16},{24,28},{28,24},{1,5},{5... | collective-permute-start | bytes 98312 | tf_op jit(solution)/shard_map/ppermute | solution.py:237
  33.0 1.2 %collective-permute-start.7 = (bf16[128,128]{1,0:T(8,128)(2,1)S(1)}, bf16[128,128]{1,0:T(8,128)(2,1)S(1)}, u32[]{:S(2)}, u32[]{:S(2)}) collective-permute-start(bf16[128,128]{1,0:T(8,128)(2,1)S(1)} %collective-permute-done.6.rest_4_), channel_id=1, source_target_pairs={{0,4},{4,0},{8,12},{12,8},{16,20},{20,16},{24,28},{28,24},{1,5},{5... | collective-permute-start | bytes 98312 | tf_op jit(solution)/shard_map/ppermute | solution.py:237
  33.0 1.4 %collective-permute-start.5 = (bf16[128,128]{1,0:T(8,128)(2,1)S(1)}, bf16[128,128]{1,0:T(8,128)(2,1)S(1)}, u32[]{:S(2)}, u32[]{:S(2)}) collective-permute-start(bf16[128,128]{1,0:T(8,128)(2,1)S(1)} %collective-permute-done.4.rest_2_), channel_id=1, source_target_pairs={{0,4},{4,0},{8,12},{12,8},{16,20},{20,16},{24,28},{28,24},{1,5},{5... | collective-permute-start | bytes 98312 | tf_op jit(solution)/shard_map/ppermute | solution.py:237
  34.8 9.1 %collective-permute-start.10 = (bf16[128,128]{1,0:T(8,128)(2,1)S(1)}, bf16[128,128]{1,0:T(8,128)(2,1)S(1)}, u32[]{:S(2)}, u32[]{:S(2)}) collective-permute-start(bf16[128,128]{1,0:T(8,128)(2,1)S(1)} %get-tuple-element.30), channel_id=1, source_target_pairs={{0,1},{1,0},{2,3},{3,2},{4,5},{5,4},{6,7},{7,6},{8,9},{9,8},{10,11... | collective-permute-start | bytes 98312 | tf_op jit(solution)/shard_map/ppermute | solution.py:245
  36.1 7.8 %collective-permute-start.11 = (bf16[128,128]{1,0:T(8,128)(2,1)S(1)}, bf16[128,128]{1,0:T(8,128)(2,1)S(1)}, u32[]{:S(2)}, u32[]{:S(2)}) collective-permute-start(bf16[128,128]{1,0:T(8,128)(2,1)S(1)} %get-tuple-element.31), channel_id=1, source_target_pairs={{0,2},{1,3},{2,0},{3,1},{4,6},{5,7},{6,4},{7,5},{8,10},{9,11},{10,... | collective-permute-start | bytes 98312 | tf_op jit(solution)/shard_map/ppermute | solution.py:245
  36.9 7.0 %collective-permute-start.12 = (bf16[128,128]{1,0:T(8,128)(2,1)S(1)}, bf16[128,128]{1,0:T(8,128)(2,1)S(1)}, u32[]{:S(2)}, u32[]{:S(2)}) collective-permute-start(bf16[128,128]{1,0:T(8,128)(2,1)S(1)} %get-tuple-element.32), channel_id=1, source_target_pairs={{0,3},{1,2},{2,1},{3,0},{4,7},{5,6},{6,5},{7,4},{8,11},{9,10},{10,... | collective-permute-start | bytes 98312 | tf_op jit(solution)/shard_map/ppermute | solution.py:245

commit v2 on v1

v2 whole, which is shorter than its diff:
```python
import functools

import jax
import jax.numpy as jnp
from jax import lax
from jax.experimental import pallas as pl
from jax.experimental.pallas import tpu as pltpu
from jax.sharding import PartitionSpec as P

BF = jnp.bfloat16
F32 = jnp.float32
NN = (((1,), (0,)), ((), ()))
NT = (((1,), (1,)), ((), ()))
TN = (((0,), (0,)), ((), ()))


def dot(a, b, dims=NN):
    return lax.dot_general(a, b, dims, preferred_element_type=F32)


def partners(n, k):
    half = (n - 2) // 2
    return [(k - 1 + j) % (n - 1) + 1 for j in range(1, half + 1)]


def column_of(row, count):
    wide = jnp.broadcast_to(row.astype(F32), (count, row.shape[1]))
    return wide.T.astype(jnp.int32)


def order_rows(order, size):
    return jnp.where(
        lax.broadcasted_iota(jnp.int32, (size, size), 0) == order, 1.0, 0.0
    ).astype(BF)


def basis_pair(skel, basis):
    points, rank = basis.shape
    ones = jnp.where(
        lax.broadcasted_iota(jnp.int32, (points, rank), 0) == skel, 1.0, 0.0
    ).astype(BF)
    return jnp.concatenate([basis, ones], axis=1)


def fetch(sources, sems):
    copies = [pltpu.make_async_copy(src, dst, sems.at[j]) for j, (src, dst) in enumerate(sources)]
    for copy in copies:
        copy.start()
    return copies


def pieces_of(ref, count):
    rows = ref.shape[0] // count
    return [ref.at[pl.ds(j * rows, rows)] for j in range(count)]


PIECES = 4


def front_kernel(n, order_hbm, skel_hbm, sides_hbm, inverse_hbm, basis_hbm, core_hbm, transfer_hbm, top_hbm, *rest):
    messages, (own_ref, top_ref, order_ref, skel_ref, sides_ref, inverse_ref, basis_ref, core_ref, transfer_ref, coeffs, sems) = (
        rest[: n - 1],
        rest[n - 1 :],
    )
    me = lax.axis_index("ba")
    points, rank = basis_ref.shape
    rows = points // PIECES
    copies = fetch(
        [(skel_hbm, skel_ref), (basis_hbm, basis_ref), (order_hbm, order_ref)]
        + list(zip(pieces_of(inverse_hbm, PIECES), pieces_of(inverse_ref, PIECES)))
        + [(sides_hbm, sides_ref), (core_hbm, core_ref), (transfer_hbm, transfer_ref), (top_hbm, top_ref)],
        sems,
    )
    share = coeffs.shape[0] // n
    for copy in copies[:3]:
        copy.wait()
    pair = basis_pair(skel_ref[...], basis_ref[...])
    placed = order_rows(order_ref[...], points)
    both = None
    for j in range(PIECES):
        copies[3 + j].wait()
        part = dot(pair[j * rows : (j + 1) * rows], inverse_ref[j * rows : (j + 1) * rows, :], TN)
        both = part if both is None else both + part
    up = (both[:rank] + both[rank:]).astype(BF)
    up = dot(up, placed, NT).astype(BF)
    for copy in copies[3 + PIECES :]:
        copy.wait()
    coeffs[...] = dot(up, sides_ref[...]).T.astype(BF)
    transfer = transfer_ref[...].astype(BF)

    def block(m):
        return core_ref[:, pl.ds(pl.multiple_of((me ^ m) * rank, rank), rank)]

    for k in range(n):
        out = own_ref if k == 0 else messages[k - 1]
        out[0:share, :] = coeffs[pl.ds(pl.multiple_of((me ^ k) * share, share), share), :]
        out[share : share + rank, :] = transfer
        at = share + rank
        for m in range(n) if k == 0 else [0] + [k ^ m for m in partners(n, k)]:
            out[at : at + rank, :] = block(m)
            at += rank


def applied_kernel(order_hbm, sides_hbm, inverse_hbm, after, applied_ref, order_ref, sides_ref, inverse_ref, sems):
    del after
    points = sides_ref.shape[0]
    rows = points // PIECES
    copies = fetch(
        [(order_hbm, order_ref), (sides_hbm, sides_ref)]
        + list(zip(pieces_of(inverse_hbm, PIECES), pieces_of(inverse_ref, PIECES))),
        sems,
    )
    copies[0].wait()
    order = order_ref[...]
    column = column_of(order, 128)
    lanes = lax.broadcasted_iota(jnp.int32, (points, 128), 1)
    gather = jnp.concatenate(
        [jnp.where(column == lanes + j * 128, 1.0, 0.0).astype(BF) for j in range(points // 128)], axis=1
    )
    copies[1].wait()
    ordered = dot(gather, sides_ref[...]).astype(BF)
    parts = []
    for j in range(PIECES):
        copies[2 + j].wait()
        parts.append(dot(inverse_ref[j * rows : (j + 1) * rows, :], ordered).astype(BF))
    applied_ref[...] = dot(order_rows(order, points), jnp.concatenate(parts, axis=0)).astype(BF)


def down_kernel(order_hbm, skel_hbm, inverse_hbm, basis_hbm, after, down_ref, order_ref, skel_ref, inverse_ref, basis_ref, sems):
    del after
    points, rank = basis_ref.shape
    rows = points // PIECES
    copies = fetch(
        [(order_hbm, order_ref), (skel_hbm, skel_ref), (basis_hbm, basis_ref)]
        + list(zip(pieces_of(inverse_hbm, PIECES), pieces_of(inverse_ref, PIECES))),
        sems,
    )
    for copy in copies[:3]:
        copy.wait()
    pair = basis_pair(skel_ref[...], basis_ref[...])
    placed = order_rows(order_ref[...], points)
    parts = []
    for j in range(PIECES):
        copies[3 + j].wait()
        both = dot(inverse_ref[j * rows : (j + 1) * rows, :], pair)
        parts.append((both[:, :rank] + both[:, rank:]).astype(BF))
    down_ref[...] = dot(placed, jnp.concatenate(parts, axis=0)).astype(BF)


def group_kernel(n, rank, after, top_ref, own_ref, *rest):
    del after
    messages, (level_ref, group_ref, top_out) = rest[: n - 1], rest[n - 1 :]
    share = level_ref.shape[0]
    core = {}
    for k in range(n):
        at = share + rank
        for m in range(n) if k == 0 else [k] + partners(n, k):
            core[k, m] = own_ref[at : at + rank, :] if k == 0 else messages[k - 1][at : at + rank, :]
            at += rank
    coeffs = [msg[0:share, :] for msg in (own_ref,) + messages]
    transfers = [msg[share : share + rank, :] for msg in (own_ref,) + messages]
    total = None
    for k in range(n):
        level = None
        for m in range(n):
            term = dot(coeffs[m], core[m, k]) if (m, k) in core else dot(coeffs[m], core[k, m], NT)
            level = term if level is None else level + term
        level_ref[:, k * rank : (k + 1) * rank] = level
        rest_of = (coeffs[k].astype(F32) - level).astype(BF)
        term = dot(rest_of, transfers[k])
        total = term if total is None else total + term
    group_ref[...] = total.astype(BF)
    top_out[...] = top_ref[...]


def top_rows_kernel(n, groups, *rest):
    tops, (rows_ref, held) = rest[:n], rest[n:]
    me = lax.axis_index("ba")
    mine = lax.axis_index("aa")
    part = tops[0].shape[0]
    rank = rows_ref.shape[0]
    for k in range(n):
        held[pl.ds(pl.multiple_of((me ^ k) * part, part), part), :] = tops[k][...].astype(F32)
    for m in range(groups):
        rows_ref[:, m * rank : (m + 1) * rank] = held[
            :, pl.ds(pl.multiple_of((mine ^ m) * rank, rank), rank)
        ].astype(BF)


def top_kernel(n, groups, rows_ref, level_ref, *rest):
    messages, pieces, outs = rest[:n], rest[n : n + groups], rest[n + groups :]
    share = level_ref.shape[0]
    rank = rows_ref.shape[0]
    stacked = jnp.concatenate([piece[...] for piece in pieces], axis=1)
    top = dot(stacked, rows_ref[...], NT).astype(BF)
    transfers = jnp.concatenate([msg[share : share + rank, :] for msg in messages], axis=0)
    correction = (level_ref[...] + dot(top, transfers, NT)).astype(BF)
    for k in range(n):
        outs[k][...] = correction[:, k * rank : (k + 1) * rank]


def final_kernel(n, applied_ref, down_ref, *rest):
    pieces, (out_hbm, correction, out_ref, sems) = rest[:n], rest[n:]
    me = lax.axis_index("ba")
    share = pieces[0].shape[0]
    for k in range(n):
        correction[pl.ds(pl.multiple_of((me ^ k) * share, share), share), :] = pieces[k][...]
    rows = out_ref.shape[0] // PIECES
    copies = []
    for j, (src, dst) in enumerate(zip(pieces_of(out_ref, PIECES), pieces_of(out_hbm, PIECES))):
        at = slice(j * rows, (j + 1) * rows)
        out_ref[at, :] = (
            applied_ref[at, :].astype(F32) - dot(down_ref[at, :], correction[...], NT)
        ).astype(BF)
        copies.append(pltpu.make_async_copy(src, dst, sems.at[j]))
        copies[-1].start()
    for copy in copies:
        copy.wait()


def shape(dims, kind=BF):
    return jax.ShapeDtypeStruct(dims, kind)


def call(body, outs, in_specs, out_specs=None, scratch=(), flops=0, moved=0):
    return pl.pallas_call(
        body,
        out_shape=outs,
        in_specs=in_specs,
        scratch_shapes=list(scratch),
        compiler_params=pltpu.CompilerParams(vmem_limit_bytes=48 * 1024 * 1024),
        cost_estimate=pl.CostEstimate(flops=flops, bytes_accessed=moved, transcendentals=0),
        **({} if out_specs is None else {"out_specs": out_specs}),
    )


def shards(n, groups, sides, order, skel, inverse, basis, core, transfer, top):
    points, cols = sides.shape
    rank = basis.shape[1]
    share = cols // n
    vmem = pl.BlockSpec(memory_space=pltpu.VMEM)
    hbm = pl.BlockSpec(memory_space=pltpu.HBM)
    unread = pl.BlockSpec(memory_space=pl.ANY)

    def like(array):
        return pltpu.VMEM(array.shape, array.dtype)

    def swap(array, axis, k):
        size = {"aa": groups, "ba": n}[axis]
        return lax.ppermute(array, axis, [(i, i ^ k) for i in range(size)])

    sizes = [share + rank * (2 + len(partners(n, k))) for k in range(1, n)] + [share + rank * (n + 1)]
    *messages, own, top_held = call(
        functools.partial(front_kernel, n),
        [shape((size, rank)) for size in sizes] + [shape(top.shape)],
        [hbm] * 8,
        scratch=[like(x) for x in (order, skel, sides, inverse, basis, core, transfer)]
        + [pltpu.VMEM((cols, rank), BF), pltpu.SemaphoreType.DMA((7 + PIECES,))],
        flops=2 * rank * points * (3 * points + cols),
        moved=2 * points * (points + cols + rank),
    )(order, skel, sides, inverse, basis, core, transfer, top)
    received = [swap(messages[k - 1], "ba", k) for k in range(1, n)]
    applied = call(
        applied_kernel,
        shape((points, cols)),
        [hbm] * 3 + [unread],
        scratch=[like(x) for x in (order, sides, inverse)] + [pltpu.SemaphoreType.DMA((2 + PIECES,))],
        flops=2 * points * points * 3 * cols,
        moved=2 * points * (points + 2 * cols),
    )(order, sides, inverse, own)
    level, group, top_held = call(
        functools.partial(group_kernel, n, rank),
        [shape((share, n * rank), F32), shape((share, rank)), shape(top.shape)],
        [unread] + [vmem] * (n + 1),
        flops=2 * share * n * rank * (n + 1) * rank,
        moved=4 * share * n * rank,
    )(applied, top_held, own, *received)
    pieces = {0: group}
    for m in range(2, groups, 2):
        pieces[m] = swap(group, "aa", m)
    tops = [top_held] + [swap(top_held, "ba", k) for k in range(1, n)]
    for m in range(0, groups, 2):
        pieces[m + 1] = swap(pieces[m], "aa", 1)
    rows = call(
        functools.partial(top_rows_kernel, n, groups),
        shape((rank, groups * rank)),
        [vmem] * n,
        scratch=[pltpu.VMEM((rank, groups * rank), F32)],
        moved=4 * rank * groups * rank,
    )(*tops)
    corrections = call(
        functools.partial(top_kernel, n, groups),
        [shape((share, rank))] * n,
        [vmem] * (2 + n + groups),
        flops=2 * share * rank * (groups + n) * rank,
        moved=4 * share * n * rank,
    )(rows, level, own, *received, *[pieces[m] for m in range(groups)])
    back = [corrections[0]] + [swap(corrections[k], "ba", k) for k in range(1, n)]
    down = call(
        down_kernel,
        shape((points, rank)),
        [hbm] * 4 + [unread],
        scratch=[like(x) for x in (order, skel, inverse, basis)] + [pltpu.SemaphoreType.DMA((3 + PIECES,))],
        flops=2 * points * points * 3 * rank,
        moved=2 * points * (points + 2 * rank),
    )(order, skel, inverse, basis, corrections[0])
    return call(
        functools.partial(final_kernel, n),
        shape((points, cols)),
        [vmem] * (2 + n),
        out_specs=hbm,
        scratch=[pltpu.VMEM((cols, rank), BF), pltpu.VMEM((points, cols), BF), pltpu.SemaphoreType.DMA((PIECES,))],
        flops=2 * points * cols * rank,
        moved=4 * points * cols,
    )(applied, down, *back)


def solution(mesh):
    spec = P(("aa", "ba"), None)
    return jax.shard_map(
        functools.partial(shards, mesh.shape["ba"], mesh.shape["aa"]),
        mesh=mesh,
        in_specs=(spec,) * 8,
        out_specs=spec,
        check_vma=False,
    )
```

time: 45.8 us -> 43.8 us (0.956)
  waiting for transfers between devices: 13.8 us -> 4.9 us
  starting transfers between devices: 13.1 us -> 16.8 us
  Pallas kernels: 10.7 us -> 13.8 us
    ppermute x13 -> x16, waiting for transfers between devices: 13.8 us -> 4.9 us  [swap(): return lax.ppermute(array, axis, [(i, i ^ k) for i in range(size)])]
    ppermute x13 -> x16, starting transfers between devices: 13.1 us -> 16.8 us  [swap(): return lax.ppermute(array, axis, [(i, i ^ k) for i in range(size)])]
    pallas_call x4 -> x5, Pallas kernels: 7.8 us -> 10.1 us  [the longest x1 4.91 us: shards(): call(applied_kernel, shape((points, cols)), [hbm] * 3 + [unread], scratch...]
    pallas_call x1, Pallas kernels: 2.51 us -> 3.33 us  [shards(): call(functools.partial(front_kernel, n), [shape((size, rank)) for size in...]
  transfers between devices with their start and end apart: 13 -> 16, of which waited for: 6 -> 6; matrix products, arithmetic and copies ran while one was open for 0% -> 0% of each run, Pallas kernels for 12% -> 19%
where the time goes in v2:
time: 43.8 us; the launch traced here: 43.4 us
  starting transfers between devices  16.8 us (38%)
  Pallas kernels  13.8 us (32%)
  local copies, waits for them, and re-layouts  7.71 us (18%)
  waiting for transfers between devices  4.9 us (11%)
    ppermute x16, starting transfers between devices, swap(): return lax.ppermute(array, axis, [(i, i ^ k) for i in range(size)])  16.8 us
    unnamed x24, local copies, waits for them, and re-layouts  7.71 us
    pallas_call x1, Pallas kernels, shards(): call(applied_kernel, shape((points, cols)), [hbm] * 3 + [unread], scratch...  4.91 us
    ppermute x16, waiting for transfers between devices, swap(): return lax.ppermute(array, axis, [(i, i ^ k) for i in range(size)])  4.9 us
    pallas_call x1, Pallas kernels, shards(): call(functools.partial(front_kernel, n), [shape((size, rank)) for size in...  3.33 us
    pallas_call x1, Pallas kernels, shards(): call(down_kernel, shape((points, rank)), [hbm] * 4 + [unread], scratch=[l...  3.1 us
    pallas_call x1, Pallas kernels, shards(): call(functools.partial(final_kernel, n), shape((points, cols)), [vmem] *...  1.25 us
  transfers between devices with their start and end apart: 16, of which 6 were waited for; matrix products, arithmetic and copies ran while one was open for 0% of the time, Pallas kernels for 19%

profile of v2, /device:TPU:0, one launch (start us, length us, event | category | flops | bytes accessed | tf_op | source)
XLA Modules:
  0.0 43.4 jit_solution(14858669218379086441)
XLA Ops:
  0.0 1.6 %copy-done = bf16[1024,1024]{1,0:T(8,128)(2,1)S(1)} copy-done((bf16[1024,1024]{1,0:T(8,128)(2,1)S(1)}, bf16[1024,1024]{1,0:T(8,128)(2,1)}, u32[]{:S(2)}) %copy-start) | copy-done | bytes 2097176
  1.6 1.2 %copy-done.2 = bf16[1024,512]{1,0:T(8,128)(2,1)S(1)} copy-done((bf16[1024,512]{1,0:T(8,128)(2,1)S(1)}, bf16[1024,512]{1,0:T(8,128)(2,1)}, u32[]{:S(2)}) %copy-start.2) | copy-done | bytes 1048600
  2.8 0.9 %copy-done.3 = bf16[1024,128]{1,0:T(8,128)(2,1)S(1)} copy-done((bf16[1024,128]{1,0:T(8,128)(2,1)S(1)}, bf16[1024,128]{1,0:T(8,128)(2,1)}, u32[]{:S(2)}) %copy-start.3) | copy-done | bytes 262168
  3.8 0.9 %copy-done.5 = bf16[128,512]{1,0:T(8,128)(2,1)S(1)} copy-done((bf16[128,512]{1,0:T(8,128)(2,1)S(1)}, bf16[128,512]{1,0:T(8,128)(2,1)}, u32[]{:S(2)}) %copy-start.5) | copy-done | bytes 131096
  4.7 0.8 %copy-done.6 = f32[128,128]{1,0:T(8,128)S(1)} copy-done((f32[128,128]{1,0:T(8,128)S(1)}, f32[128,128]{1,0:T(8,128)}, u32[]{:S(2)}) %copy-start.6) | copy-done | bytes 65560
  5.5 0.8 %copy-done.7 = bf16[32,1024]{1,0:T(8,128)(2,1)S(1)} copy-done((bf16[32,1024]{1,0:T(8,128)(2,1)S(1)}, bf16[32,1024]{1,0:T(8,128)(2,1)}, u32[]{:S(2)}) %copy-start.7) | copy-done | bytes 65560
  6.4 0.7 %copy-done.8 = s32[1,1024]{1,0:T(1,128)S(1)} copy-done((s32[1,1024]{1,0:T(1,128)S(1)}, s32[1,1024]{1,0:T(1,128)}, u32[]{:S(2)}) %copy-start.8) | copy-done | bytes 4120
  7.0 0.7 %copy-done.10 = s32[1,128]{1,0:T(1,128)S(1)} copy-done((s32[1,128]{1,0:T(1,128)S(1)}, s32[1,128]{1,0:T(1,128)}, u32[]{:S(2)}) %copy-start.10) | copy-done | bytes 536
  7.7 3.3 %shard_map.82 = (bf16[512,128]{1,0:T(8,128)(2,1)S(1)}, bf16[512,128]{1,0:T(8,128)(2,1)S(1)}, bf16[512,128]{1,0:T(8,128)(2,1)S(1)}, bf16[768,128]{1,0:T(8,128)(2,1)S(1)}, bf16[32,1024]{1,0:T(8,128)(2,1)S(1)}) custom-call(s32[1,1024]{1,0:T(1,128)S(1)} %copy-done.8, s32[1,128]{1,0:T(1,128)S(1)} %copy-done.10, bf16[1024,512]{1,0:T(8,128)(2,1)S(1)} %copy-done.2, ...), custom_call_target="tpu_custom_call" | custom-call | flops 939524096 | bytes 3407872 | tf_op jit(solution)/shard_map/pallas_call | solution.py:253
  11.0 3.0 %collective-permute-start = (bf16[512,128]{1,0:T(8,128)(2,1)S(1)}, bf16[512,128]{1,0:T(8,128)(2,1)S(1)}, u32[]{:S(2)}, u32[]{:S(2)}) collective-permute-start(bf16[512,128]{1,0:T(8,128)(2,1)S(1)} %get-tuple-element.19), channel_id=1, source_target_pairs={{0,1},{1,0},{2,3},{3,2},{4,5},{5,4},{6,7},{7,6},{8,9},{9,8},{10,11... | collective-permute-start | bytes 393224 | tf_op jit(solution)/shard_map/ppermute | solution.py:250
  14.0 1.5 %collective-permute-start.1 = (bf16[512,128]{1,0:T(8,128)(2,1)S(1)}, bf16[512,128]{1,0:T(8,128)(2,1)S(1)}, u32[]{:S(2)}, u32[]{:S(2)}) collective-permute-start(bf16[512,128]{1,0:T(8,128)(2,1)S(1)} %get-tuple-element.20), channel_id=1, source_target_pairs={{0,2},{1,3},{2,0},{3,1},{4,6},{5,7},{6,4},{7,5},{8,10},{9,11},{10,... | collective-permute-start | bytes 393224 | tf_op jit(solution)/shard_map/ppermute | solution.py:250
  15.6 0.0 collective-permute-start.2
  15.6 4.9 %shard_map.83.after.applied_ref = bf16[1024,512]{1,0:T(8,128)(2,1)S(1)} custom-call(s32[1,1024]{1,0:T(1,128)S(1)} %copy-done.8, bf16[1024,512]{1,0:T(8,128)(2,1)S(1)} %copy-done.2, bf16[1024,1024]{1,0:T(8,128)(2,1)S(1)} %copy-done.1, bf16[768,128]{1,0:T(8,128)(2,1)S(1)} %get-tuple-element.17.after.own_ref.rest_0_), custom_call_target="tpu_custom_call" | custom-call | flops 3221225472 | bytes 4194304 | tf_op jit(solution)/shard_map/pallas_call | solution.py:263
  20.5 0.0 copy-start.4
  20.5 0.0 copy-start.9
  20.5 0.0 copy-start.11
  20.5 0.0 collective-permute-done.rest_0_.rest_1_
  20.6 1.3 %collective-permute-done.1.rest_1_.rest_2_ = bf16[512,128]{1,0:T(8,128)(2,1)S(1)} collective-permute-done((bf16[512,128]{1,0:T(8,128)(2,1)S(1)}, bf16[512,128]{1,0:T(8,128)(2,1)S(1)}, u32[]{:S(2)}, u32[]{:S(2)}) %collective-permute-start.1) | collective-permute-done | bytes 131104 | tf_op jit(solution)/shard_map/ppermute | solution.py:250
  21.8 0.0 collective-permute-done.2.rest_2_.rest_3_
  21.8 0.7 %shard_map.84 = (f32[128,512]{1,0:T(8,128)S(1)}, bf16[128,128]{1,0:T(8,128)(2,1)S(1)}, bf16[32,1024]{1,0:T(8,128)(2,1)S(1)}) custom-call(bf16[1024,512]{1,0:T(8,128)(2,1)S(1)} %shard_map.83.after.applied_ref, bf16[32,1024]{1,0:T(8,128)(2,1)S(1)} %get-tuple-element.18.top_ref, bf16[768,128]{1,0:T(8,128)(2,1)S(1)} %get-tuple-element.17.after.own_ref.rest_0_, ...), custom_call_target="tpu_custom_call" | custom-call | flops 83886080 | bytes 262144 | tf_op jit(solution)/shard_map/pallas_call | solution.py:271
  22.5 2.7 %collective-permute-start.9 = (bf16[128,128]{1,0:T(8,128)(2,1)S(1)}, bf16[128,128]{1,0:T(8,128)(2,1)S(1)}, u32[]{:S(2)}, u32[]{:S(2)}) collective-permute-start(bf16[128,128]{1,0:T(8,128)(2,1)S(1)} %get-tuple-element.24.rest_4_), channel_id=1, source_target_pairs={{0,16},{4,20},{8,24},{12,28},{16,0},{20,4},{24,8},{28,12},{1,17},{... | collective-permute-start | bytes 98312 | tf_op jit(solution)/shard_map/ppermute | solution.py:250
  25.2 1.2 %collective-permute-start.3 = (bf16[32,1024]{1,0:T(8,128)(2,1)S(1)}, bf16[32,1024]{1,0:T(8,128)(2,1)S(1)}, u32[]{:S(2)}, u32[]{:S(2)}) collective-permute-start(bf16[32,1024]{1,0:T(8,128)(2,1)S(1)} %get-tuple-element.22.rest_0_), channel_id=1, source_target_pairs={{0,1},{1,0},{2,3},{3,2},{4,5},{5,4},{6,7},{7,6},{8,9},{9,8},{10,11... | collective-permute-start | bytes 196616 | tf_op jit(solution)/shard_map/ppermute | solution.py:250
  26.4 1.0 %collective-permute-start.4 = (bf16[32,1024]{1,0:T(8,128)(2,1)S(1)}, bf16[32,1024]{1,0:T(8,128)(2,1)S(1)}, u32[]{:S(2)}, u32[]{:S(2)}) collective-permute-start(bf16[32,1024]{1,0:T(8,128)(2,1)S(1)} %get-tuple-element.22.rest_0_), channel_id=1, source_target_pairs={{0,2},{1,3},{2,0},{3,1},{4,6},{5,7},{6,4},{7,5},{8,10},{9,11},{10,... | collective-permute-start | bytes 196616 | tf_op jit(solution)/shard_map/ppermute | solution.py:250
  27.4 1.3 %collective-permute-start.11 = (bf16[128,128]{1,0:T(8,128)(2,1)S(1)}, bf16[128,128]{1,0:T(8,128)(2,1)S(1)}, u32[]{:S(2)}, u32[]{:S(2)}) collective-permute-start(bf16[128,128]{1,0:T(8,128)(2,1)S(1)} %get-tuple-element.24.rest_4_), channel_id=1, source_target_pairs={{0,24},{4,28},{8,16},{12,20},{16,8},{20,12},{24,0},{28,4},{1,25},{... | collective-permute-start | bytes 98312 | tf_op jit(solution)/shard_map/ppermute | solution.py:250
  28.8 0.2 collective-permute-start.7
  29.0 0.0 collective-permute-done.9.rest_8_
  29.0 1.3 %collective-permute-start.5 = (bf16[32,1024]{1,0:T(8,128)(2,1)S(1)}, bf16[32,1024]{1,0:T(8,128)(2,1)S(1)}, u32[]{:S(2)}, u32[]{:S(2)}) collective-permute-start(bf16[32,1024]{1,0:T(8,128)(2,1)S(1)} %get-tuple-element.22.rest_0_), channel_id=1, source_target_pairs={{0,3},{1,2},{2,1},{3,0},{4,7},{5,6},{6,5},{7,4},{8,11},{9,10},{10,... | collective-permute-start | bytes 196616 | tf_op jit(solution)/shard_map/ppermute | solution.py:250
  30.3 2.9 %collective-permute-done.11.rest_10_ = bf16[128,128]{1,0:T(8,128)(2,1)S(1)} collective-permute-done((bf16[128,128]{1,0:T(8,128)(2,1)S(1)}, bf16[128,128]{1,0:T(8,128)(2,1)S(1)}, u32[]{:S(2)}, u32[]{:S(2)}) %collective-permute-start.11) | collective-permute-done | bytes 32800 | tf_op jit(solution)/shard_map/ppermute | solution.py:250
  33.1 0.0 collective-permute-start.6
  33.1 0.0 collective-permute-done.7.rest_6_
  33.1 0.5 %collective-permute-start.10 = (bf16[128,128]{1,0:T(8,128)(2,1)S(1)}, bf16[128,128]{1,0:T(8,128)(2,1)S(1)}, u32[]{:S(2)}, u32[]{:S(2)}) collective-permute-start(bf16[128,128]{1,0:T(8,128)(2,1)S(1)} %collective-permute-done.9.rest_8_), channel_id=1, source_target_pairs={{0,4},{4,0},{8,12},{12,8},{16,20},{20,16},{24,28},{28,24},{1,5},{5... | collective-permute-start | bytes 98312 | tf_op jit(solution)/shard_map/ppermute | solution.py:250
  33.6 0.0 collective-permute-done.3.rest_1_
  33.7 0.1 collective-permute-start.12
  33.7 0.0 collective-permute-done.4.rest_2_
  33.7 0.4 %collective-permute-start.8 = (bf16[128,128]{1,0:T(8,128)(2,1)S(1)}, bf16[128,128]{1,0:T(8,128)(2,1)S(1)}, u32[]{:S(2)}, u32[]{:S(2)}) collective-permute-start(bf16[128,128]{1,0:T(8,128)(2,1)S(1)} %collective-permute-done.7.rest_6_), channel_id=1, source_target_pairs={{0,4},{4,0},{8,12},{12,8},{16,20},{20,16},{24,28},{28,24},{1,5},{5... | collective-permute-start | bytes 98312 | tf_op jit(solution)/shard_map/ppermute | solution.py:250
  34.2 0.1 shard_map.85.rows_ref
  34.3 0.1 collective-permute-done.6.rest_5_
  34.3 0.2 collective-permute-done.10.rest_9_
  34.5 0.4 collective-permute-done.12.rest_11_
  34.9 0.2 collective-permute-done.8.rest_7_
  35.0 0.4 shard_map.86
  35.5 1.4 %collective-permute-start.13 = (bf16[128,128]{1,0:T(8,128)(2,1)S(1)}, bf16[128,128]{1,0:T(8,128)(2,1)S(1)}, u32[]{:S(2)}, u32[]{:S(2)}) collective-permute-start(bf16[128,128]{1,0:T(8,128)(2,1)S(1)} %get-tuple-element.26), channel_id=1, source_target_pairs={{0,1},{1,0},{2,3},{3,2},{4,5},{5,4},{6,7},{7,6},{8,9},{9,8},{10,11... | collective-permute-start | bytes 98312 | tf_op jit(solution)/shard_map/ppermute | solution.py:250
  36.8 0.5 %collective-permute-start.14 = (bf16[128,128]{1,0:T(8,128)(2,1)S(1)}, bf16[128,128]{1,0:T(8,128)(2,1)S(1)}, u32[]{:S(2)}, u32[]{:S(2)}) collective-permute-start(bf16[128,128]{1,0:T(8,128)(2,1)S(1)} %get-tuple-element.27), channel_id=1, source_target_pairs={{0,2},{1,3},{2,0},{3,1},{4,6},{5,7},{6,4},{7,5},{8,10},{9,11},{10,... | collective-permute-start | bytes 98312 | tf_op jit(solution)/shard_map/ppermute | solution.py:250
  37.3 1.7 %collective-permute-start.15 = (bf16[128,128]{1,0:T(8,128)(2,1)S(1)}, bf16[128,128]{1,0:T(8,128)(2,1)S(1)}, u32[]{:S(2)}, u32[]{:S(2)}) collective-permute-start(bf16[128,128]{1,0:T(8,128)(2,1)S(1)} %get-tuple-element.28), channel_id=1, source_target_pairs={{0,3},{1,2},{2,1},{3,0},{4,7},{5,6},{6,5},{7,4},{8,11},{9,10},{10,... | collective-permute-start | bytes 98312 | tf_op jit(solution)/shard_map/ppermute | solution.py:250
  39.0 3.1 %shard_map.87.down_ref = bf16[1024,128]{1,0:T(8,128)(2,1)S(1)} custom-call(s32[1,1024]{1,0:T(1,128)S(1)} %copy-done.9, s32[1,128]{1,0:T(1,128)S(1)} %copy-done.11, bf16[1024,1024]{1,0:T(8,128)(2,1)S(1)} %copy-done.1, bf16[1024,128]{1,0:T(8,128)(2,1)S(1)} %copy-done.4, bf16[128,128]{1,0:T(8,128)(2,1)S(1)} %get-tuple-element.25.after.rest_0_), custom_call_target="tpu_custom_call" | custom-call | flops 805306368 | bytes 2621440 | tf_op jit(solution)/shard_map/pallas_call | solution.py:299
  42.1 0.0 collective-permute-done.14.rest_2_
  42.2 0.0 collective-permute-done.15.rest_3_
  42.2 1.2 %shard_map.88 = bf16[1024,512]{1,0:T(8,128)(2,1)} custom-call(bf16[1024,512]{1,0:T(8,128)(2,1)S(1)} %shard_map.83.after.applied_ref, bf16[1024,128]{1,0:T(8,128)(2,1)S(1)} %shard_map.87.down_ref, bf16[128,128]{1,0:T(8,128)(2,1)S(1)} %get-tuple-element.25.after.rest_0_, bf16[128,128]{1,0:T(8,128)(2,1)S(1)} %collective-permute-done.13.rest_1_, ...), custom_call_target="tpu_custom_call" | custom-call | flops 134217728 | bytes 2097152 | tf_op jit(solution)/shard_map/pallas_call | solution.py:307
  (15 shorter events, 0.0 us)
Async XLA Ops:
  0.0 1.6 %copy-start = (bf16[1024,1024]{1,0:T(8,128)(2,1)S(1)}, bf16[1024,1024]{1,0:T(8,128)(2,1)}, u32[]{:S(2)}) copy-start(bf16[1024,1024]{1,0:T(8,128)(2,1)} %inverse_hbm.5) | copy-start | bytes 6291460
  1.6 1.2 %copy-start.2 = (bf16[1024,512]{1,0:T(8,128)(2,1)S(1)}, bf16[1024,512]{1,0:T(8,128)(2,1)}, u32[]{:S(2)}) copy-start(bf16[1024,512]{1,0:T(8,128)(2,1)} %sides_hbm.3) | copy-start | bytes 3145732
  2.8 0.9 %copy-start.3 = (bf16[1024,128]{1,0:T(8,128)(2,1)S(1)}, bf16[1024,128]{1,0:T(8,128)(2,1)}, u32[]{:S(2)}) copy-start(bf16[1024,128]{1,0:T(8,128)(2,1)} %basis_hbm.3) | copy-start | bytes 786436
  3.8 0.9 %copy-start.5 = (bf16[128,512]{1,0:T(8,128)(2,1)S(1)}, bf16[128,512]{1,0:T(8,128)(2,1)}, u32[]{:S(2)}) copy-start(bf16[128,512]{1,0:T(8,128)(2,1)} %core_hbm.1) | copy-start | bytes 393220
  4.7 0.8 %copy-start.6 = (f32[128,128]{1,0:T(8,128)S(1)}, f32[128,128]{1,0:T(8,128)}, u32[]{:S(2)}) copy-start(f32[128,128]{1,0:T(8,128)} %transfer_hbm.1) | copy-start | bytes 196612
  5.5 0.8 %copy-start.7 = (bf16[32,1024]{1,0:T(8,128)(2,1)S(1)}, bf16[32,1024]{1,0:T(8,128)(2,1)}, u32[]{:S(2)}) copy-start(bf16[32,1024]{1,0:T(8,128)(2,1)} %top_hbm.1) | copy-start | bytes 196612
  6.4 0.7 %copy-start.8 = (s32[1,1024]{1,0:T(1,128)S(1)}, s32[1,1024]{1,0:T(1,128)}, u32[]{:S(2)}) copy-start(s32[1,1024]{1,0:T(1,128)} %order_hbm.5) | copy-start | bytes 12292
  7.0 0.7 %copy-start.10 = (s32[1,128]{1,0:T(1,128)S(1)}, s32[1,128]{1,0:T(1,128)}, u32[]{:S(2)}) copy-start(s32[1,128]{1,0:T(1,128)} %skel_hbm.3) | copy-start | bytes 1540
  7.7 7.9 %copy-start.1 = (bf16[1024,1024]{1,0:T(8,128)(2,1)S(1)}, bf16[1024,1024]{1,0:T(8,128)(2,1)}, u32[]{:S(2)}) copy-start(bf16[1024,1024]{1,0:T(8,128)(2,1)} %inverse_hbm.5) | copy-start | bytes 6291460
  11.0 9.5 %collective-permute-start = (bf16[512,128]{1,0:T(8,128)(2,1)S(1)}, bf16[512,128]{1,0:T(8,128)(2,1)S(1)}, u32[]{:S(2)}, u32[]{:S(2)}) collective-permute-start(bf16[512,128]{1,0:T(8,128)(2,1)S(1)} %get-tuple-element.19), channel_id=1, source_target_pairs={{0,1},{1,0},{2,3},{3,2},{4,5},{5,4},{6,7},{7,6},{8,9},{9,8},{10,11... | collective-permute-start | bytes 393224 | tf_op jit(solution)/shard_map/ppermute | solution.py:250
  14.0 7.8 %collective-permute-start.1 = (bf16[512,128]{1,0:T(8,128)(2,1)S(1)}, bf16[512,128]{1,0:T(8,128)(2,1)S(1)}, u32[]{:S(2)}, u32[]{:S(2)}) collective-permute-start(bf16[512,128]{1,0:T(8,128)(2,1)S(1)} %get-tuple-element.20), channel_id=1, source_target_pairs={{0,2},{1,3},{2,0},{3,1},{4,6},{5,7},{6,4},{7,5},{8,10},{9,11},{10,... | collective-permute-start | bytes 393224 | tf_op jit(solution)/shard_map/ppermute | solution.py:250
  15.6 6.3 %collective-permute-start.2 = (bf16[512,128]{1,0:T(8,128)(2,1)S(1)}, bf16[512,128]{1,0:T(8,128)(2,1)S(1)}, u32[]{:S(2)}, u32[]{:S(2)}) collective-permute-start(bf16[512,128]{1,0:T(8,128)(2,1)S(1)} %get-tuple-element.21), channel_id=1, source_target_pairs={{0,3},{1,2},{2,1},{3,0},{4,7},{5,6},{6,5},{7,4},{8,11},{9,10},{10,... | collective-permute-start | bytes 393224 | tf_op jit(solution)/shard_map/ppermute | solution.py:250
  20.5 18.5 %copy-start.4 = (bf16[1024,128]{1,0:T(8,128)(2,1)S(1)}, bf16[1024,128]{1,0:T(8,128)(2,1)}, u32[]{:S(2)}) copy-start(bf16[1024,128]{1,0:T(8,128)(2,1)} %basis_hbm.3) | copy-start | bytes 786436
  20.5 18.5 %copy-start.9 = (s32[1,1024]{1,0:T(1,128)S(1)}, s32[1,1024]{1,0:T(1,128)}, u32[]{:S(2)}) copy-start(s32[1,1024]{1,0:T(1,128)} %order_hbm.5) | copy-start | bytes 12292
  20.5 18.5 %copy-start.11 = (s32[1,128]{1,0:T(1,128)S(1)}, s32[1,128]{1,0:T(1,128)}, u32[]{:S(2)}) copy-start(s32[1,128]{1,0:T(1,128)} %skel_hbm.3) | copy-start | bytes 1540
  22.5 6.5 %collective-permute-start.9 = (bf16[128,128]{1,0:T(8,128)(2,1)S(1)}, bf16[128,128]{1,0:T(8,128)(2,1)S(1)}, u32[]{:S(2)}, u32[]{:S(2)}) collective-permute-start(bf16[128,128]{1,0:T(8,128)(2,1)S(1)} %get-tuple-element.24.rest_4_), channel_id=1, source_target_pairs={{0,16},{4,20},{8,24},{12,28},{16,0},{20,4},{24,8},{28,12},{1,17},{... | collective-permute-start | bytes 98312 | tf_op jit(solution)/shard_map/ppermute | solution.py:250
  25.2 8.5 %collective-permute-start.3 = (bf16[32,1024]{1,0:T(8,128)(2,1)S(1)}, bf16[32,1024]{1,0:T(8,128)(2,1)S(1)}, u32[]{:S(2)}, u32[]{:S(2)}) collective-permute-start(bf16[32,1024]{1,0:T(8,128)(2,1)S(1)} %get-tuple-element.22.rest_0_), channel_id=1, source_target_pairs={{0,1},{1,0},{2,3},{3,2},{4,5},{5,4},{6,7},{7,6},{8,9},{9,8},{10,11... | collective-permute-start | bytes 196616 | tf_op jit(solution)/shard_map/ppermute | solution.py:250
  26.4 7.3 %collective-permute-start.4 = (bf16[32,1024]{1,0:T(8,128)(2,1)S(1)}, bf16[32,1024]{1,0:T(8,128)(2,1)S(1)}, u32[]{:S(2)}, u32[]{:S(2)}) collective-permute-start(bf16[32,1024]{1,0:T(8,128)(2,1)S(1)} %get-tuple-element.22.rest_0_), channel_id=1, source_target_pairs={{0,2},{1,3},{2,0},{3,1},{4,6},{5,7},{6,4},{7,5},{8,10},{9,11},{10,... | collective-permute-start | bytes 196616 | tf_op jit(solution)/shard_map/ppermute | solution.py:250
  27.4 5.7 %collective-permute-start.11 = (bf16[128,128]{1,0:T(8,128)(2,1)S(1)}, bf16[128,128]{1,0:T(8,128)(2,1)S(1)}, u32[]{:S(2)}, u32[]{:S(2)}) collective-permute-start(bf16[128,128]{1,0:T(8,128)(2,1)S(1)} %get-tuple-element.24.rest_4_), channel_id=1, source_target_pairs={{0,24},{4,28},{8,16},{12,20},{16,8},{20,12},{24,0},{28,4},{1,25},{... | collective-permute-start | bytes 98312 | tf_op jit(solution)/shard_map/ppermute | solution.py:250
  28.8 4.4 %collective-permute-start.7 = (bf16[128,128]{1,0:T(8,128)(2,1)S(1)}, bf16[128,128]{1,0:T(8,128)(2,1)S(1)}, u32[]{:S(2)}, u32[]{:S(2)}) collective-permute-start(bf16[128,128]{1,0:T(8,128)(2,1)S(1)} %get-tuple-element.24.rest_4_), channel_id=1, source_target_pairs={{0,8},{4,12},{8,0},{12,4},{16,24},{20,28},{24,16},{28,20},{1,9},{5... | collective-permute-start | bytes 98312 | tf_op jit(solution)/shard_map/ppermute | solution.py:250
  29.0 5.2 %collective-permute-start.5 = (bf16[32,1024]{1,0:T(8,128)(2,1)S(1)}, bf16[32,1024]{1,0:T(8,128)(2,1)S(1)}, u32[]{:S(2)}, u32[]{:S(2)}) collective-permute-start(bf16[32,1024]{1,0:T(8,128)(2,1)S(1)} %get-tuple-element.22.rest_0_), channel_id=1, source_target_pairs={{0,3},{1,2},{2,1},{3,0},{4,7},{5,6},{6,5},{7,4},{8,11},{9,10},{10,... | collective-permute-start | bytes 196616 | tf_op jit(solution)/shard_map/ppermute | solution.py:250
  33.1 1.2 %collective-permute-start.6 = (bf16[128,128]{1,0:T(8,128)(2,1)S(1)}, bf16[128,128]{1,0:T(8,128)(2,1)S(1)}, u32[]{:S(2)}, u32[]{:S(2)}) collective-permute-start(bf16[128,128]{1,0:T(8,128)(2,1)S(1)} %get-tuple-element.24.rest_4_), channel_id=1, source_target_pairs={{0,4},{4,0},{8,12},{12,8},{16,20},{20,16},{24,28},{28,24},{1,5},{5... | collective-permute-start | bytes 98312 | tf_op jit(solution)/shard_map/ppermute | solution.py:250
  33.1 1.4 %collective-permute-start.10 = (bf16[128,128]{1,0:T(8,128)(2,1)S(1)}, bf16[128,128]{1,0:T(8,128)(2,1)S(1)}, u32[]{:S(2)}, u32[]{:S(2)}) collective-permute-start(bf16[128,128]{1,0:T(8,128)(2,1)S(1)} %collective-permute-done.9.rest_8_), channel_id=1, source_target_pairs={{0,4},{4,0},{8,12},{12,8},{16,20},{20,16},{24,28},{28,24},{1,5},{5... | collective-permute-start | bytes 98312 | tf_op jit(solution)/shard_map/ppermute | solution.py:250
  33.7 1.2 %collective-permute-start.12 = (bf16[128,128]{1,0:T(8,128)(2,1)S(1)}, bf16[128,128]{1,0:T(8,128)(2,1)S(1)}, u32[]{:S(2)}, u32[]{:S(2)}) collective-permute-start(bf16[128,128]{1,0:T(8,128)(2,1)S(1)} %collective-permute-done.11.rest_10_), channel_id=1, source_target_pairs={{0,4},{4,0},{8,12},{12,8},{16,20},{20,16},{24,28},{28,24},{1,5},{5... | collective-permute-start | bytes 98312 | tf_op jit(solution)/shard_map/ppermute | solution.py:250
  33.7 1.3 %collective-permute-start.8 = (bf16[128,128]{1,0:T(8,128)(2,1)S(1)}, bf16[128,128]{1,0:T(8,128)(2,1)S(1)}, u32[]{:S(2)}, u32[]{:S(2)}) collective-permute-start(bf16[128,128]{1,0:T(8,128)(2,1)S(1)} %collective-permute-done.7.rest_6_), channel_id=1, source_target_pairs={{0,4},{4,0},{8,12},{12,8},{16,20},{20,16},{24,28},{28,24},{1,5},{5... | collective-permute-start | bytes 98312 | tf_op jit(solution)/shard_map/ppermute | solution.py:250
  35.5 6.7 %collective-permute-start.13 = (bf16[128,128]{1,0:T(8,128)(2,1)S(1)}, bf16[128,128]{1,0:T(8,128)(2,1)S(1)}, u32[]{:S(2)}, u32[]{:S(2)}) collective-permute-start(bf16[128,128]{1,0:T(8,128)(2,1)S(1)} %get-tuple-element.26), channel_id=1, source_target_pairs={{0,1},{1,0},{2,3},{3,2},{4,5},{5,4},{6,7},{7,6},{8,9},{9,8},{10,11... | collective-permute-start | bytes 98312 | tf_op jit(solution)/shard_map/ppermute | solution.py:250
  36.8 5.3 %collective-permute-start.14 = (bf16[128,128]{1,0:T(8,128)(2,1)S(1)}, bf16[128,128]{1,0:T(8,128)(2,1)S(1)}, u32[]{:S(2)}, u32[]{:S(2)}) collective-permute-start(bf16[128,128]{1,0:T(8,128)(2,1)S(1)} %get-tuple-element.27), channel_id=1, source_target_pairs={{0,2},{1,3},{2,0},{3,1},{4,6},{5,7},{6,4},{7,5},{8,10},{9,11},{10,... | collective-permute-start | bytes 98312 | tf_op jit(solution)/shard_map/ppermute | solution.py:250
  37.3 4.8 %collective-permute-start.15 = (bf16[128,128]{1,0:T(8,128)(2,1)S(1)}, bf16[128,128]{1,0:T(8,128)(2,1)S(1)}, u32[]{:S(2)}, u32[]{:S(2)}) collective-permute-start(bf16[128,128]{1,0:T(8,128)(2,1)S(1)} %get-tuple-element.28), channel_id=1, source_target_pairs={{0,3},{1,2},{2,1},{3,0},{4,7},{5,6},{6,5},{7,4},{8,11},{9,10},{10,... | collective-permute-start | bytes 98312 | tf_op jit(solution)/shard_map/ppermute | solution.py:250

commit v3 on v2

--- a/solution.py
+++ b/solution.py
@@ -57,11 +57,12 @@
 PIECES = 4
 
 
-def front_kernel(n, order_hbm, skel_hbm, sides_hbm, inverse_hbm, basis_hbm, core_hbm, transfer_hbm, top_hbm, *rest):
-    messages, (own_ref, top_ref, order_ref, skel_ref, sides_ref, inverse_ref, basis_ref, core_ref, transfer_ref, coeffs, sems) = (
-        rest[: n - 1],
-        rest[n - 1 :],
-    )
+def front_kernel(
+    n, order_hbm, skel_hbm, sides_hbm, inverse_hbm, basis_hbm, core_hbm, transfer_hbm, top_hbm, *rest
+):
+    messages, own_ref = rest[: n - 1], rest[n - 1]
+    sides_ref, inverse_ref, placed_ref, pair_ref = rest[n : n + 4]
+    order_ref, skel_ref, basis_ref, core_ref, transfer_ref, top_ref, coeffs, sems = rest[n + 4 :]
     me = lax.axis_index("ba")
     points, rank = basis_ref.shape
     rows = points // PIECES
@@ -74,19 +75,23 @@
     share = coeffs.shape[0] // n
     for copy in copies[:3]:
         copy.wait()
-    pair = basis_pair(skel_ref[...], basis_ref[...])
-    placed = order_rows(order_ref[...], points)
+    pair_ref[...] = basis_pair(skel_ref[...], basis_ref[...])
+    placed_ref[...] = order_rows(order_ref[...], points)
     both = None
     for j in range(PIECES):
         copies[3 + j].wait()
-        part = dot(pair[j * rows : (j + 1) * rows], inverse_ref[j * rows : (j + 1) * rows, :], TN)
+        at = slice(j * rows, (j + 1) * rows)
+        part = dot(pair_ref[at, :], inverse_ref[at, :], TN)
         both = part if both is None else both + part
     up = (both[:rank] + both[rank:]).astype(BF)
-    up = dot(up, placed, NT).astype(BF)
+    up = dot(up, placed_ref[...], NT).astype(BF)
     for copy in copies[3 + PIECES :]:
         copy.wait()
     coeffs[...] = dot(up, sides_ref[...]).T.astype(BF)
     transfer = transfer_ref[...].astype(BF)
+    groups = top_ref.shape[1] // rank
+    top = top_ref[...].astype(F32)
+    top = jnp.concatenate([top[:, g * rank : (g + 1) * rank] for g in range(groups)], axis=0).astype(BF)
 
     def block(m):
         return core_ref[:, pl.ds(pl.multiple_of((me ^ m) * rank, rank), rank)]
@@ -99,57 +104,28 @@
         for m in range(n) if k == 0 else [0] + [k ^ m for m in partners(n, k)]:
             out[at : at + rank, :] = block(m)
             at += rank
-
-
-def applied_kernel(order_hbm, sides_hbm, inverse_hbm, after, applied_ref, order_ref, sides_ref, inverse_ref, sems):
-    del after
-    points = sides_ref.shape[0]
-    rows = points // PIECES
-    copies = fetch(
-        [(order_hbm, order_ref), (sides_hbm, sides_ref)]
-        + list(zip(pieces_of(inverse_hbm, PIECES), pieces_of(inverse_ref, PIECES))),
-        sems,
-    )
-    copies[0].wait()
-    order = order_ref[...]
-    column = column_of(order, 128)
+        out[at:, :] = top
+
+
+def leaf_kernel(order_ref, sides_ref, inverse_ref, placed_ref, pair_ref, applied_ref, down_ref):
+    points, cols = sides_ref.shape
+    rank = down_ref.shape[1]
+    column = column_of(order_ref[...], 128)
     lanes = lax.broadcasted_iota(jnp.int32, (points, 128), 1)
     gather = jnp.concatenate(
         [jnp.where(column == lanes + j * 128, 1.0, 0.0).astype(BF) for j in range(points // 128)], axis=1
     )
-    copies[1].wait()
     ordered = dot(gather, sides_ref[...]).astype(BF)
-    parts = []
-    for j in range(PIECES):
-        copies[2 + j].wait()
-        parts.append(dot(inverse_ref[j * rows : (j + 1) * rows, :], ordered).astype(BF))
-    applied_ref[...] = dot(order_rows(order, points), jnp.concatenate(parts, axis=0)).astype(BF)
-
-
-def down_kernel(order_hbm, skel_hbm, inverse_hbm, basis_hbm, after, down_ref, order_ref, skel_ref, inverse_ref, basis_ref, sems):
+    applied = dot(inverse_ref[...], ordered).astype(BF)
+    both = dot(inverse_ref[...], pair_ref[...])
+    down = (both[:, :rank] + both[:, rank:]).astype(BF)
+    applied_ref[...] = dot(placed_ref[...], applied).astype(BF)
+    down_ref[...] = dot(placed_ref[...], down).astype(BF)
+
+
+def group_kernel(n, rank, after, own_ref, *rest):
     del after
-    points, rank = basis_ref.shape
-    rows = points // PIECES
-    copies = fetch(
-        [(order_hbm, order_ref), (skel_hbm, skel_ref), (basis_hbm, basis_ref)]
-        + list(zip(pieces_of(inverse_hbm, PIECES), pieces_of(inverse_ref, PIECES))),
-        sems,
-    )
-    for copy in copies[:3]:
-        copy.wait()
-    pair = basis_pair(skel_ref[...], basis_ref[...])
-    placed = order_rows(order_ref[...], points)
-    parts = []
-    for j in range(PIECES):
-        copies[3 + j].wait()
-        both = dot(inverse_ref[j * rows : (j + 1) * rows, :], pair)
-        parts.append((both[:, :rank] + both[:, rank:]).astype(BF))
-    down_ref[...] = dot(placed, jnp.concatenate(parts, axis=0)).astype(BF)
-
-
-def group_kernel(n, rank, after, top_ref, own_ref, *rest):
-    del after
-    messages, (level_ref, group_ref, top_out) = rest[: n - 1], rest[n - 1 :]
+    messages, (level_ref, group_ref) = rest[: n - 1], rest[n - 1 :]
     share = level_ref.shape[0]
     core = {}
     for k in range(n):
@@ -170,17 +146,20 @@
         term = dot(rest_of, transfers[k])
         total = term if total is None else total + term
     group_ref[...] = total.astype(BF)
-    top_out[...] = top_ref[...]
 
 
 def top_rows_kernel(n, groups, *rest):
-    tops, (rows_ref, held) = rest[:n], rest[n:]
+    messages, (rows_ref, held) = rest[:n], rest[n:]
     me = lax.axis_index("ba")
     mine = lax.axis_index("aa")
-    part = tops[0].shape[0]
     rank = rows_ref.shape[0]
-    for k in range(n):
-        held[pl.ds(pl.multiple_of((me ^ k) * part, part), part), :] = tops[k][...].astype(F32)
+    part = rank // n
+    for k in range(n):
+        tail = messages[k][messages[k].shape[0] - groups * part :, :].astype(F32)
+        for g in range(groups):
+            held[pl.ds(pl.multiple_of((me ^ k) * part, part), part), g * rank : (g + 1) * rank] = tail[
+                g * part : (g + 1) * part
+            ]
     for m in range(groups):
         rows_ref[:, m * rank : (m + 1) * rank] = held[
             :, pl.ds(pl.multiple_of((mine ^ m) * rank, rank), rank)
@@ -222,13 +201,13 @@
     return jax.ShapeDtypeStruct(dims, kind)
 
 
-def call(body, outs, in_specs, out_specs=None, scratch=(), flops=0, moved=0):
+def call(body, outs, in_specs, out_specs=None, scratch=(), flops=0, moved=0, limit=32):
     return pl.pallas_call(
         body,
         out_shape=outs,
         in_specs=in_specs,
         scratch_shapes=list(scratch),
-        compiler_params=pltpu.CompilerParams(vmem_limit_bytes=48 * 1024 * 1024),
+        compiler_params=pltpu.CompilerParams(vmem_limit_bytes=limit * 1024 * 1024),
         cost_estimate=pl.CostEstimate(flops=flops, bytes_accessed=moved, transcendentals=0),
         **({} if out_specs is None else {"out_specs": out_specs}),
     )
@@ -242,6 +221,9 @@
     hbm = pl.BlockSpec(memory_space=pltpu.HBM)
     unread = pl.BlockSpec(memory_space=pl.ANY)
 
+    def far(*arrays):
+        return [pltpu.with_memory_space_constraint(x, pltpu.HBM) for x in arrays]
+
     def like(array):
         return pltpu.VMEM(array.shape, array.dtype)
 
@@ -249,36 +231,36 @@
         size = {"aa": groups, "ba": n}[axis]
         return lax.ppermute(array, axis, [(i, i ^ k) for i in range(size)])
 
-    sizes = [share + rank * (2 + len(partners(n, k))) for k in range(1, n)] + [share + rank * (n + 1)]
-    *messages, own, top_held = call(
+    tail = rank + groups * top.shape[0]
+    sizes = [share + rank * (1 + len(partners(n, k))) + tail for k in range(1, n)] + [share + rank * n + tail]
+    *messages, own, sides_held, inverse_held, placed, pair = call(
         functools.partial(front_kernel, n),
-        [shape((size, rank)) for size in sizes] + [shape(top.shape)],
+        [shape((size, rank)) for size in sizes]
+        + [shape(sides.shape), shape(inverse.shape), shape((points, points)), shape((points, 2 * rank))],
         [hbm] * 8,
-        scratch=[like(x) for x in (order, skel, sides, inverse, basis, core, transfer)]
+        scratch=[like(x) for x in (order, skel, basis, core, transfer, top)]
         + [pltpu.VMEM((cols, rank), BF), pltpu.SemaphoreType.DMA((7 + PIECES,))],
         flops=2 * rank * points * (3 * points + cols),
         moved=2 * points * (points + cols + rank),
-    )(order, skel, sides, inverse, basis, core, transfer, top)
+    )(*far(order, skel, sides, inverse, basis, core, transfer, top))
     received = [swap(messages[k - 1], "ba", k) for k in range(1, n)]
-    applied = call(
-        applied_kernel,
-        shape((points, cols)),
-        [hbm] * 3 + [unread],
-        scratch=[like(x) for x in (order, sides, inverse)] + [pltpu.SemaphoreType.DMA((2 + PIECES,))],
-        flops=2 * points * points * 3 * cols,
+    applied, down = call(
+        leaf_kernel,
+        [shape((points, cols)), shape((points, rank))],
+        [vmem] * 5,
+        flops=2 * points * points * 3 * (cols + rank),
         moved=2 * points * (points + 2 * cols),
-    )(order, sides, inverse, own)
-    level, group, top_held = call(
+    )(order, sides_held, inverse_held, placed, pair)
+    level, group = call(
         functools.partial(group_kernel, n, rank),
-        [shape((share, n * rank), F32), shape((share, rank)), shape(top.shape)],
-        [unread] + [vmem] * (n + 1),
+        [shape((share, n * rank), F32), shape((share, rank))],
+        [unread] + [vmem] * n,
         flops=2 * share * n * rank * (n + 1) * rank,
         moved=4 * share * n * rank,
-    )(applied, top_held, own, *received)
+    )(down, own, *received)
     pieces = {0: group}
     for m in range(2, groups, 2):
         pieces[m] = swap(group, "aa", m)
-    tops = [top_held] + [swap(top_held, "ba", k) for k in range(1, n)]
     for m in range(0, groups, 2):
         pieces[m + 1] = swap(pieces[m], "aa", 1)
     rows = call(
@@ -287,7 +269,7 @@
         [vmem] * n,
         scratch=[pltpu.VMEM((rank, groups * rank), F32)],
         moved=4 * rank * groups * rank,
-    )(*tops)
+    )(own, *received)
     corrections = call(
         functools.partial(top_kernel, n, groups),
         [shape((share, rank))] * n,
@@ -296,14 +278,6 @@
         moved=4 * share * n * rank,
     )(rows, level, own, *received, *[pieces[m] for m in range(groups)])
     back = [corrections[0]] + [swap(corrections[k], "ba", k) for k in range(1, n)]
-    down = call(
-        down_kernel,
-        shape((points, rank)),
-        [hbm] * 4 + [unread],
-        scratch=[like(x) for x in (order, skel, inverse, basis)] + [pltpu.SemaphoreType.DMA((3 + PIECES,))],
-        flops=2 * points * points * 3 * rank,
-        moved=2 * points * (points + 2 * rank),
-    )(order, skel, inverse, basis, corrections[0])
     return call(
         functools.partial(final_kernel, n),
         shape((points, cols)),

time: 43.8 us -> 36.5 us (0.83)
  local copies, waits for them, and re-layouts: 7.71 us -> 0.01 us
  waiting for transfers between devices: 4.9 us -> 12.6 us
  starting transfers between devices: 16.8 us -> 13.1 us
  Pallas kernels: 13.8 us -> 10.6 us
    unnamed x24 -> x2, local copies, waits for them, and re-layouts: 7.71 us -> 0.01 us
    ppermute x16 -> x13, waiting for transfers between devices: 4.9 us -> 12.6 us  [swap(): return lax.ppermute(array, axis, [(i, i ^ k) for i in range(size)])]
    ppermute x16 -> x13, starting transfers between devices: 16.8 us -> 13.1 us  [swap(): return lax.ppermute(array, axis, [(i, i ^ k) for i in range(size)])]
    pallas_call x2 -> x1, Pallas kernels: 8.02 us -> 4.56 us  [shards(): call(leaf_kernel, [shape((points, cols)), shape((points, rank))], [vmem]...]
  transfers between devices with their start and end apart: 16 -> 13, of which waited for: 6 -> 8; matrix products, arithmetic and copies ran while one was open for 0% -> 0% of each run, Pallas kernels for 19% -> 13%
where the time goes in v3:
time: 36.5 us; the launch traced here: 36.4 us
  starting transfers between devices  13.1 us (36%)
  waiting for transfers between devices  12.6 us (35%)
  Pallas kernels  10.6 us (29%)
    ppermute x13, starting transfers between devices, swap(): return lax.ppermute(array, axis, [(i, i ^ k) for i in range(size)])  13.1 us
    ppermute x13, waiting for transfers between devices, swap(): return lax.ppermute(array, axis, [(i, i ^ k) for i in range(size)])  12.6 us
    pallas_call x1, Pallas kernels, shards(): call(leaf_kernel, [shape((points, cols)), shape((points, rank))], [vmem]...  4.56 us
    pallas_call x1, Pallas kernels, shards(): call(functools.partial(front_kernel, n), [shape((size, rank)) for size in...  3.63 us
    pallas_call x1, Pallas kernels, shards(): call(functools.partial(final_kernel, n), shape((points, cols)), [vmem] *...  1.24 us
  transfers between devices with their start and end apart: 13, of which 8 were waited for; matrix products, arithmetic and copies ran while one was open for 0% of the time, Pallas kernels for 13%

profile of v3, /device:TPU:0, one launch (start us, length us, event | category | flops | bytes accessed | tf_op | source)
XLA Modules:
  0.0 36.4 jit_solution(17310251767127046547)
XLA Ops:
  0.0 0.0 copy-start
  0.0 3.6 %shard_map.82 = (bf16[768,128]{1,0:T(8,128)(2,1)S(1)}, bf16[768,128]{1,0:T(8,128)(2,1)S(1)}, bf16[768,128]{1,0:T(8,128)(2,1)S(1)}, bf16[1024,128]{1,0:T(8,128)(2...) custom-call(s32[1,1024]{1,0:T(1,128)} %order_ref.1, ...), custom_call_target="tpu_custom_call" | custom-call | flops 939524096 | bytes 3407872 | tf_op jit(solution)/shard_map/pallas_call | solution.py:236
  3.6 3.0 %collective-permute-start = (bf16[768,128]{1,0:T(8,128)(2,1)S(1)}, bf16[768,128]{1,0:T(8,128)(2,1)S(1)}, u32[]{:S(2)}, u32[]{:S(2)}) collective-permute-start(bf16[768,128]{1,0:T(8,128)(2,1)S(1)} %get-tuple-element.28), channel_id=1, source_target_pairs={{0,1},{1,0},{2,3},{3,2},{4,5},{5,4},{6,7},{7,6},{8,9},{9,8},{10,11... | collective-permute-start | bytes 589832 | tf_op jit(solution)/shard_map/ppermute | solution.py:232
  6.7 1.5 %collective-permute-start.1 = (bf16[768,128]{1,0:T(8,128)(2,1)S(1)}, bf16[768,128]{1,0:T(8,128)(2,1)S(1)}, u32[]{:S(2)}, u32[]{:S(2)}) collective-permute-start(bf16[768,128]{1,0:T(8,128)(2,1)S(1)} %get-tuple-element.29), channel_id=1, source_target_pairs={{0,2},{1,3},{2,0},{3,1},{4,6},{5,7},{6,4},{7,5},{8,10},{9,11},{10,... | collective-permute-start | bytes 589832 | tf_op jit(solution)/shard_map/ppermute | solution.py:232
  8.2 0.0 collective-permute-start.2
  8.2 0.0 copy-done
  8.2 4.6 %shard_map.83 = (bf16[1024,512]{1,0:T(8,128)(2,1)S(1)}, bf16[1024,128]{1,0:T(8,128)(2,1)S(1)}) custom-call(s32[1,1024]{1,0:T(1,128)S(1)} %copy-done, bf16[1024,512]{1,0:T(8,128)(2,1)S(1)} %get-tuple-element.21.sides_ref, bf16[1024,1024]{1,0:T(8,128)(2,1)S(1)} %get-tuple-element.22.inverse_ref, bf16[1024,1024]{1,0:T(8,128)(2,1)S(1)} %get-tuple-element.23.placed_ref, ...), custom_call_target="tpu_custom_call" | custom-call | flops 4026531840 | bytes 4194304 | tf_op jit(solution)/shard_map/pallas_call | solution.py:247
  12.8 0.0 collective-permute-done.rest_1_.rest_0_
  12.8 4.4 %collective-permute-done.1.rest_2_.rest_1_ = bf16[768,128]{1,0:T(8,128)(2,1)S(1)} collective-permute-done((bf16[768,128]{1,0:T(8,128)(2,1)S(1)}, bf16[768,128]{1,0:T(8,128)(2,1)S(1)}, u32[]{:S(2)}, u32[]{:S(2)}) %collective-permute-start.1) | collective-permute-done | bytes 196640 | tf_op jit(solution)/shard_map/ppermute | solution.py:232
  17.2 0.0 collective-permute-done.2.rest_3_.rest_2_
  17.2 0.7 %shard_map.85 = (f32[128,512]{1,0:T(8,128)S(1)}, bf16[128,128]{1,0:T(8,128)(2,1)S(1)}) custom-call(bf16[1024,128]{1,0:T(8,128)(2,1)S(1)} %get-tuple-element.26.after.down_ref, bf16[1024,128]{1,0:T(8,128)(2,1)S(1)} %get-tuple-element.27.rest_0_.own_ref, bf16[768,128]{1,0:T(8,128)(2,1)S(1)} %collective-permute-done.rest_1_.rest_0_, ...), custom_call_target="tpu_custom_call" | custom-call | flops 83886080 | bytes 262144 | tf_op jit(solution)/shard_map/pallas_call | solution.py:254
  17.9 3.7 %collective-permute-start.8 = (bf16[128,128]{1,0:T(8,128)(2,1)S(1)}, bf16[128,128]{1,0:T(8,128)(2,1)S(1)}, u32[]{:S(2)}, u32[]{:S(2)}) collective-permute-start(bf16[128,128]{1,0:T(8,128)(2,1)S(1)} %get-tuple-element.32.rest_4_), channel_id=1, source_target_pairs={{0,24},{4,28},{8,16},{12,20},{16,8},{20,12},{24,0},{28,4},{1,25},{... | collective-permute-start | bytes 98312 | tf_op jit(solution)/shard_map/ppermute | solution.py:232
  21.6 0.0 collective-permute-start.6
  21.6 0.8 %collective-permute-start.4 = (bf16[128,128]{1,0:T(8,128)(2,1)S(1)}, bf16[128,128]{1,0:T(8,128)(2,1)S(1)}, u32[]{:S(2)}, u32[]{:S(2)}) collective-permute-start(bf16[128,128]{1,0:T(8,128)(2,1)S(1)} %get-tuple-element.32.rest_4_), channel_id=1, source_target_pairs={{0,8},{4,12},{8,0},{12,4},{16,24},{20,28},{24,16},{28,20},{1,9},{5... | collective-permute-start | bytes 98312 | tf_op jit(solution)/shard_map/ppermute | solution.py:232
  22.4 0.0 collective-permute-start.3
  22.4 1.3 %collective-permute-done.8.rest_10_ = bf16[128,128]{1,0:T(8,128)(2,1)S(1)} collective-permute-done((bf16[128,128]{1,0:T(8,128)(2,1)S(1)}, bf16[128,128]{1,0:T(8,128)(2,1)S(1)}, u32[]{:S(2)}, u32[]{:S(2)}) %collective-permute-start.8) | collective-permute-done | bytes 32800 | tf_op jit(solution)/shard_map/ppermute | solution.py:232
  23.7 0.0 collective-permute-start.9
  23.7 2.7 %collective-permute-done.6.rest_8_ = bf16[128,128]{1,0:T(8,128)(2,1)S(1)} collective-permute-done((bf16[128,128]{1,0:T(8,128)(2,1)S(1)}, bf16[128,128]{1,0:T(8,128)(2,1)S(1)}, u32[]{:S(2)}, u32[]{:S(2)}) %collective-permute-start.6) | collective-permute-done | bytes 32800 | tf_op jit(solution)/shard_map/ppermute | solution.py:232
  26.4 0.0 collective-permute-start.7
  26.4 0.0 collective-permute-done.4.rest_6_
  26.4 0.5 %collective-permute-start.5 = (bf16[128,128]{1,0:T(8,128)(2,1)S(1)}, bf16[128,128]{1,0:T(8,128)(2,1)S(1)}, u32[]{:S(2)}, u32[]{:S(2)}) collective-permute-start(bf16[128,128]{1,0:T(8,128)(2,1)S(1)} %collective-permute-done.4.rest_6_), channel_id=1, source_target_pairs={{0,4},{4,0},{8,12},{12,8},{16,20},{20,16},{24,28},{28,24},{1,5},{5... | collective-permute-start | bytes 98312 | tf_op jit(solution)/shard_map/ppermute | solution.py:232
  26.9 0.1 shard_map.84.rows_ref
  27.0 0.0 collective-permute-done.3.rest_5_
  27.0 0.0 collective-permute-done.9.rest_11_
  27.0 0.6 %collective-permute-done.7.rest_9_ = bf16[128,128]{1,0:T(8,128)(2,1)S(1)} collective-permute-done((bf16[128,128]{1,0:T(8,128)(2,1)S(1)}, bf16[128,128]{1,0:T(8,128)(2,1)S(1)}, u32[]{:S(2)}, u32[]{:S(2)}) %collective-permute-start.7) | collective-permute-done | bytes 32800 | tf_op jit(solution)/shard_map/ppermute | solution.py:232
  27.6 0.2 collective-permute-done.5.rest_7_
  27.8 0.4 %shard_map.86 = (bf16[128,128]{1,0:T(8,128)(2,1)S(1)}, bf16[128,128]{1,0:T(8,128)(2,1)S(1)}, bf16[128,128]{1,0:T(8,128)(2,1)S(1)}, bf16[128,128]{1,0:T(8,128)(2,1)S(1)}) custom-call(bf16[128,1024]{1,0:T(8,128)(2,1)S(1)} %shard_map.84.rows_ref, f32[128,512]{1,0:T(8,128)S(1)} %get-tuple-element.31.level_ref, ...), custom_call_target="tpu_custom_call" | custom-call | flops 50331648 | bytes 262144 | tf_op jit(solution)/shard_map/pallas_call | solution.py:273
  28.2 1.3 %collective-permute-start.10 = (bf16[128,128]{1,0:T(8,128)(2,1)S(1)}, bf16[128,128]{1,0:T(8,128)(2,1)S(1)}, u32[]{:S(2)}, u32[]{:S(2)}) collective-permute-start(bf16[128,128]{1,0:T(8,128)(2,1)S(1)} %get-tuple-element.34), channel_id=1, source_target_pairs={{0,1},{1,0},{2,3},{3,2},{4,5},{5,4},{6,7},{7,6},{8,9},{9,8},{10,11... | collective-permute-start | bytes 98312 | tf_op jit(solution)/shard_map/ppermute | solution.py:232
  29.5 0.8 %collective-permute-start.11 = (bf16[128,128]{1,0:T(8,128)(2,1)S(1)}, bf16[128,128]{1,0:T(8,128)(2,1)S(1)}, u32[]{:S(2)}, u32[]{:S(2)}) collective-permute-start(bf16[128,128]{1,0:T(8,128)(2,1)S(1)} %get-tuple-element.35), channel_id=1, source_target_pairs={{0,2},{1,3},{2,0},{3,1},{4,6},{5,7},{6,4},{7,5},{8,10},{9,11},{10,... | collective-permute-start | bytes 98312 | tf_op jit(solution)/shard_map/ppermute | solution.py:232
  30.3 1.4 %collective-permute-start.12 = (bf16[128,128]{1,0:T(8,128)(2,1)S(1)}, bf16[128,128]{1,0:T(8,128)(2,1)S(1)}, u32[]{:S(2)}, u32[]{:S(2)}) collective-permute-start(bf16[128,128]{1,0:T(8,128)(2,1)S(1)} %get-tuple-element.36), channel_id=1, source_target_pairs={{0,3},{1,2},{2,1},{3,0},{4,7},{5,6},{6,5},{7,4},{8,11},{9,10},{10,... | collective-permute-start | bytes 98312 | tf_op jit(solution)/shard_map/ppermute | solution.py:232
  31.7 0.4 %collective-permute-done.10.rest_1_ = bf16[128,128]{1,0:T(8,128)(2,1)S(1)} collective-permute-done((bf16[128,128]{1,0:T(8,128)(2,1)S(1)}, bf16[128,128]{1,0:T(8,128)(2,1)S(1)}, u32[]{:S(2)}, u32[]{:S(2)}) %collective-permute-start.10) | collective-permute-done | bytes 32800 | tf_op jit(solution)/shard_map/ppermute | solution.py:232
  32.2 1.3 %collective-permute-done.11.rest_2_ = bf16[128,128]{1,0:T(8,128)(2,1)S(1)} collective-permute-done((bf16[128,128]{1,0:T(8,128)(2,1)S(1)}, bf16[128,128]{1,0:T(8,128)(2,1)S(1)}, u32[]{:S(2)}, u32[]{:S(2)}) %collective-permute-start.11) | collective-permute-done | bytes 32800 | tf_op jit(solution)/shard_map/ppermute | solution.py:232
  33.4 1.7 %collective-permute-done.12.rest_3_ = bf16[128,128]{1,0:T(8,128)(2,1)S(1)} collective-permute-done((bf16[128,128]{1,0:T(8,128)(2,1)S(1)}, bf16[128,128]{1,0:T(8,128)(2,1)S(1)}, u32[]{:S(2)}, u32[]{:S(2)}) %collective-permute-start.12) | collective-permute-done | bytes 32800 | tf_op jit(solution)/shard_map/ppermute | solution.py:232
  35.1 1.2 %shard_map.87 = bf16[1024,512]{1,0:T(8,128)(2,1)} custom-call(bf16[1024,512]{1,0:T(8,128)(2,1)S(1)} %get-tuple-element.25.applied_ref, bf16[1024,128]{1,0:T(8,128)(2,1)S(1)} %get-tuple-element.26.after.down_ref, bf16[128,128]{1,0:T(8,128)(2,1)S(1)} %get-tuple-element.33.rest_0_, bf16[128,128]{1,0:T(8,128)(2,1)S(1)} %collective-permute-done.10.rest_1_, ...), custom_call_target="tpu_custom_call" | custom-call | flops 134217728 | bytes 2097152 | tf_op jit(solution)/shard_map/pallas_call | solution.py:281
Async XLA Ops:
  0.0 8.2 %copy-start = (s32[1,1024]{1,0:T(1,128)S(1)}, s32[1,1024]{1,0:T(1,128)}, u32[]{:S(2)}) copy-start(s32[1,1024]{1,0:T(1,128)} %order_ref.1) | copy-start | bytes 12292
  3.6 9.1 %collective-permute-start = (bf16[768,128]{1,0:T(8,128)(2,1)S(1)}, bf16[768,128]{1,0:T(8,128)(2,1)S(1)}, u32[]{:S(2)}, u32[]{:S(2)}) collective-permute-start(bf16[768,128]{1,0:T(8,128)(2,1)S(1)} %get-tuple-element.28), channel_id=1, source_target_pairs={{0,1},{1,0},{2,3},{3,2},{4,5},{5,4},{6,7},{7,6},{8,9},{9,8},{10,11... | collective-permute-start | bytes 589832 | tf_op jit(solution)/shard_map/ppermute | solution.py:232
  6.7 10.6 %collective-permute-start.1 = (bf16[768,128]{1,0:T(8,128)(2,1)S(1)}, bf16[768,128]{1,0:T(8,128)(2,1)S(1)}, u32[]{:S(2)}, u32[]{:S(2)}) collective-permute-start(bf16[768,128]{1,0:T(8,128)(2,1)S(1)} %get-tuple-element.29), channel_id=1, source_target_pairs={{0,2},{1,3},{2,0},{3,1},{4,6},{5,7},{6,4},{7,5},{8,10},{9,11},{10,... | collective-permute-start | bytes 589832 | tf_op jit(solution)/shard_map/ppermute | solution.py:232
  8.2 9.1 %collective-permute-start.2 = (bf16[768,128]{1,0:T(8,128)(2,1)S(1)}, bf16[768,128]{1,0:T(8,128)(2,1)S(1)}, u32[]{:S(2)}, u32[]{:S(2)}) collective-permute-start(bf16[768,128]{1,0:T(8,128)(2,1)S(1)} %get-tuple-element.30), channel_id=1, source_target_pairs={{0,3},{1,2},{2,1},{3,0},{4,7},{5,6},{6,5},{7,4},{8,11},{9,10},{10,... | collective-permute-start | bytes 589832 | tf_op jit(solution)/shard_map/ppermute | solution.py:232
  17.9 5.8 %collective-permute-start.8 = (bf16[128,128]{1,0:T(8,128)(2,1)S(1)}, bf16[128,128]{1,0:T(8,128)(2,1)S(1)}, u32[]{:S(2)}, u32[]{:S(2)}) collective-permute-start(bf16[128,128]{1,0:T(8,128)(2,1)S(1)} %get-tuple-element.32.rest_4_), channel_id=1, source_target_pairs={{0,24},{4,28},{8,16},{12,20},{16,8},{20,12},{24,0},{28,4},{1,25},{... | collective-permute-start | bytes 98312 | tf_op jit(solution)/shard_map/ppermute | solution.py:232
  21.6 4.8 %collective-permute-start.6 = (bf16[128,128]{1,0:T(8,128)(2,1)S(1)}, bf16[128,128]{1,0:T(8,128)(2,1)S(1)}, u32[]{:S(2)}, u32[]{:S(2)}) collective-permute-start(bf16[128,128]{1,0:T(8,128)(2,1)S(1)} %get-tuple-element.32.rest_4_), channel_id=1, source_target_pairs={{0,16},{4,20},{8,24},{12,28},{16,0},{20,4},{24,8},{28,12},{1,17},{... | collective-permute-start | bytes 98312 | tf_op jit(solution)/shard_map/ppermute | solution.py:232
  21.6 4.8 %collective-permute-start.4 = (bf16[128,128]{1,0:T(8,128)(2,1)S(1)}, bf16[128,128]{1,0:T(8,128)(2,1)S(1)}, u32[]{:S(2)}, u32[]{:S(2)}) collective-permute-start(bf16[128,128]{1,0:T(8,128)(2,1)S(1)} %get-tuple-element.32.rest_4_), channel_id=1, source_target_pairs={{0,8},{4,12},{8,0},{12,4},{16,24},{20,28},{24,16},{28,20},{1,9},{5... | collective-permute-start | bytes 98312 | tf_op jit(solution)/shard_map/ppermute | solution.py:232
  22.4 4.7 %collective-permute-start.3 = (bf16[128,128]{1,0:T(8,128)(2,1)S(1)}, bf16[128,128]{1,0:T(8,128)(2,1)S(1)}, u32[]{:S(2)}, u32[]{:S(2)}) collective-permute-start(bf16[128,128]{1,0:T(8,128)(2,1)S(1)} %get-tuple-element.32.rest_4_), channel_id=1, source_target_pairs={{0,4},{4,0},{8,12},{12,8},{16,20},{20,16},{24,28},{28,24},{1,5},{5... | collective-permute-start | bytes 98312 | tf_op jit(solution)/shard_map/ppermute | solution.py:232
  23.7 3.3 %collective-permute-start.9 = (bf16[128,128]{1,0:T(8,128)(2,1)S(1)}, bf16[128,128]{1,0:T(8,128)(2,1)S(1)}, u32[]{:S(2)}, u32[]{:S(2)}) collective-permute-start(bf16[128,128]{1,0:T(8,128)(2,1)S(1)} %collective-permute-done.8.rest_10_), channel_id=1, source_target_pairs={{0,4},{4,0},{8,12},{12,8},{16,20},{20,16},{24,28},{28,24},{1,5},{5... | collective-permute-start | bytes 98312 | tf_op jit(solution)/shard_map/ppermute | solution.py:232
  26.4 1.2 %collective-permute-start.7 = (bf16[128,128]{1,0:T(8,128)(2,1)S(1)}, bf16[128,128]{1,0:T(8,128)(2,1)S(1)}, u32[]{:S(2)}, u32[]{:S(2)}) collective-permute-start(bf16[128,128]{1,0:T(8,128)(2,1)S(1)} %collective-permute-done.6.rest_8_), channel_id=1, source_target_pairs={{0,4},{4,0},{8,12},{12,8},{16,20},{20,16},{24,28},{28,24},{1,5},{5... | collective-permute-start | bytes 98312 | tf_op jit(solution)/shard_map/ppermute | solution.py:232
  26.4 1.4 %collective-permute-start.5 = (bf16[128,128]{1,0:T(8,128)(2,1)S(1)}, bf16[128,128]{1,0:T(8,128)(2,1)S(1)}, u32[]{:S(2)}, u32[]{:S(2)}) collective-permute-start(bf16[128,128]{1,0:T(8,128)(2,1)S(1)} %collective-permute-done.4.rest_6_), channel_id=1, source_target_pairs={{0,4},{4,0},{8,12},{12,8},{16,20},{20,16},{24,28},{28,24},{1,5},{5... | collective-permute-start | bytes 98312 | tf_op jit(solution)/shard_map/ppermute | solution.py:232
  28.2 4.0 %collective-permute-start.10 = (bf16[128,128]{1,0:T(8,128)(2,1)S(1)}, bf16[128,128]{1,0:T(8,128)(2,1)S(1)}, u32[]{:S(2)}, u32[]{:S(2)}) collective-permute-start(bf16[128,128]{1,0:T(8,128)(2,1)S(1)} %get-tuple-element.34), channel_id=1, source_target_pairs={{0,1},{1,0},{2,3},{3,2},{4,5},{5,4},{6,7},{7,6},{8,9},{9,8},{10,11... | collective-permute-start | bytes 98312 | tf_op jit(solution)/shard_map/ppermute | solution.py:232
  29.5 3.9 %collective-permute-start.11 = (bf16[128,128]{1,0:T(8,128)(2,1)S(1)}, bf16[128,128]{1,0:T(8,128)(2,1)S(1)}, u32[]{:S(2)}, u32[]{:S(2)}) collective-permute-start(bf16[128,128]{1,0:T(8,128)(2,1)S(1)} %get-tuple-element.35), channel_id=1, source_target_pairs={{0,2},{1,3},{2,0},{3,1},{4,6},{5,7},{6,4},{7,5},{8,10},{9,11},{10,... | collective-permute-start | bytes 98312 | tf_op jit(solution)/shard_map/ppermute | solution.py:232
  30.3 4.8 %collective-permute-start.12 = (bf16[128,128]{1,0:T(8,128)(2,1)S(1)}, bf16[128,128]{1,0:T(8,128)(2,1)S(1)}, u32[]{:S(2)}, u32[]{:S(2)}) collective-permute-start(bf16[128,128]{1,0:T(8,128)(2,1)S(1)} %get-tuple-element.36), channel_id=1, source_target_pairs={{0,3},{1,2},{2,1},{3,0},{4,7},{5,6},{6,5},{7,4},{8,11},{9,10},{10,... | collective-permute-start | bytes 98312 | tf_op jit(solution)/shard_map/ppermute | solution.py:232

commit v4 on v3

--- a/solution.py
+++ b/solution.py
@@ -34,6 +34,14 @@
     ).astype(BF)
 
 
+def order_columns(order, size):
+    column = column_of(order, 128)
+    lanes = lax.broadcasted_iota(jnp.int32, (size, 128), 1)
+    return jnp.concatenate(
+        [jnp.where(column == lanes + j * 128, 1.0, 0.0).astype(BF) for j in range(size // 128)], axis=1
+    )
+
+
 def basis_pair(skel, basis):
     points, rank = basis.shape
     ones = jnp.where(
@@ -61,8 +69,8 @@
     n, order_hbm, skel_hbm, sides_hbm, inverse_hbm, basis_hbm, core_hbm, transfer_hbm, top_hbm, *rest
 ):
     messages, own_ref = rest[: n - 1], rest[n - 1]
-    sides_ref, inverse_ref, placed_ref, pair_ref = rest[n : n + 4]
-    order_ref, skel_ref, basis_ref, core_ref, transfer_ref, top_ref, coeffs, sems = rest[n + 4 :]
+    sides_ref, inverse_ref, gather_ref, placed_ref, pair_ref, top_ref = rest[n : n + 6]
+    order_ref, skel_ref, basis_ref, core_ref, transfer_ref, coeffs, sems = rest[n + 6 :]
     me = lax.axis_index("ba")
     points, rank = basis_ref.shape
     rows = points // PIECES
@@ -76,6 +84,7 @@
     for copy in copies[:3]:
         copy.wait()
     pair_ref[...] = basis_pair(skel_ref[...], basis_ref[...])
+    gather_ref[...] = order_columns(order_ref[...], points)
     placed_ref[...] = order_rows(order_ref[...], points)
     both = None
     for j in range(PIECES):
@@ -84,14 +93,11 @@
         part = dot(pair_ref[at, :], inverse_ref[at, :], TN)
         both = part if both is None else both + part
     up = (both[:rank] + both[rank:]).astype(BF)
-    up = dot(up, placed_ref[...], NT).astype(BF)
+    up = dot(up, gather_ref[...]).astype(BF)
     for copy in copies[3 + PIECES :]:
         copy.wait()
     coeffs[...] = dot(up, sides_ref[...]).T.astype(BF)
     transfer = transfer_ref[...].astype(BF)
-    groups = top_ref.shape[1] // rank
-    top = top_ref[...].astype(F32)
-    top = jnp.concatenate([top[:, g * rank : (g + 1) * rank] for g in range(groups)], axis=0).astype(BF)
 
     def block(m):
         return core_ref[:, pl.ds(pl.multiple_of((me ^ m) * rank, rank), rank)]
@@ -104,22 +110,20 @@
         for m in range(n) if k == 0 else [0] + [k ^ m for m in partners(n, k)]:
             out[at : at + rank, :] = block(m)
             at += rank
-        out[at:, :] = top
-
-
-def leaf_kernel(order_ref, sides_ref, inverse_ref, placed_ref, pair_ref, applied_ref, down_ref):
-    points, cols = sides_ref.shape
+
+
+def applied_kernel(sides_ref, inverse_ref, gather_ref, top_ref, applied_ref, top_out):
+    ordered = dot(gather_ref[...], sides_ref[...]).astype(BF)
+    applied_ref[...] = dot(inverse_ref[...], ordered).astype(BF)
+    top_out[...] = top_ref[...]
+
+
+def down_kernel(inverse_ref, placed_ref, pair_ref, applied_ref, after, applied_out, down_ref):
+    del after
     rank = down_ref.shape[1]
-    column = column_of(order_ref[...], 128)
-    lanes = lax.broadcasted_iota(jnp.int32, (points, 128), 1)
-    gather = jnp.concatenate(
-        [jnp.where(column == lanes + j * 128, 1.0, 0.0).astype(BF) for j in range(points // 128)], axis=1
-    )
-    ordered = dot(gather, sides_ref[...]).astype(BF)
-    applied = dot(inverse_ref[...], ordered).astype(BF)
     both = dot(inverse_ref[...], pair_ref[...])
     down = (both[:, :rank] + both[:, rank:]).astype(BF)
-    applied_ref[...] = dot(placed_ref[...], applied).astype(BF)
+    applied_out[...] = dot(placed_ref[...], applied_ref[...]).astype(BF)
     down_ref[...] = dot(placed_ref[...], down).astype(BF)
 
 
@@ -149,17 +153,13 @@
 
 
 def top_rows_kernel(n, groups, *rest):
-    messages, (rows_ref, held) = rest[:n], rest[n:]
+    tops, (rows_ref, held) = rest[:n], rest[n:]
     me = lax.axis_index("ba")
     mine = lax.axis_index("aa")
+    part = tops[0].shape[0]
     rank = rows_ref.shape[0]
-    part = rank // n
-    for k in range(n):
-        tail = messages[k][messages[k].shape[0] - groups * part :, :].astype(F32)
-        for g in range(groups):
-            held[pl.ds(pl.multiple_of((me ^ k) * part, part), part), g * rank : (g + 1) * rank] = tail[
-                g * part : (g + 1) * part
-            ]
+    for k in range(n):
+        held[pl.ds(pl.multiple_of((me ^ k) * part, part), part), :] = tops[k][...].astype(F32)
     for m in range(groups):
         rows_ref[:, m * rank : (m + 1) * rank] = held[
             :, pl.ds(pl.multiple_of((mine ^ m) * rank, rank), rank)
@@ -231,33 +231,35 @@
         size = {"aa": groups, "ba": n}[axis]
         return lax.ppermute(array, axis, [(i, i ^ k) for i in range(size)])
 
-    tail = rank + groups * top.shape[0]
-    sizes = [share + rank * (1 + len(partners(n, k))) + tail for k in range(1, n)] + [share + rank * n + tail]
-    *messages, own, sides_held, inverse_held, placed, pair = call(
+    sizes = [share + rank * (2 + len(partners(n, k))) for k in range(1, n)] + [share + rank * (n + 1)]
+    *messages, own, sides_held, inverse_held, gather, placed, pair, top_held = call(
         functools.partial(front_kernel, n),
         [shape((size, rank)) for size in sizes]
-        + [shape(sides.shape), shape(inverse.shape), shape((points, points)), shape((points, 2 * rank))],
+        + [shape(sides.shape), shape(inverse.shape)]
+        + [shape((points, points))] * 2
+        + [shape((points, 2 * rank)), shape(top.shape)],
         [hbm] * 8,
-        scratch=[like(x) for x in (order, skel, basis, core, transfer, top)]
+        scratch=[like(x) for x in (order, skel, basis, core, transfer)]
         + [pltpu.VMEM((cols, rank), BF), pltpu.SemaphoreType.DMA((7 + PIECES,))],
         flops=2 * rank * points * (3 * points + cols),
         moved=2 * points * (points + cols + rank),
     )(*far(order, skel, sides, inverse, basis, core, transfer, top))
     received = [swap(messages[k - 1], "ba", k) for k in range(1, n)]
-    applied, down = call(
-        leaf_kernel,
-        [shape((points, cols)), shape((points, rank))],
-        [vmem] * 5,
-        flops=2 * points * points * 3 * (cols + rank),
+    applied, top_held = call(
+        applied_kernel,
+        [shape((points, cols)), shape(top.shape)],
+        [vmem] * 4,
+        flops=4 * points * points * cols,
         moved=2 * points * (points + 2 * cols),
-    )(order, sides_held, inverse_held, placed, pair)
+    )(sides_held, inverse_held, gather, top_held)
+    tops = [top_held] + [swap(top_held, "ba", k) for k in range(1, n)]
     level, group = call(
         functools.partial(group_kernel, n, rank),
         [shape((share, n * rank), F32), shape((share, rank))],
         [unread] + [vmem] * n,
         flops=2 * share * n * rank * (n + 1) * rank,
         moved=4 * share * n * rank,
-    )(down, own, *received)
+    )(applied, own, *received)
     pieces = {0: group}
     for m in range(2, groups, 2):
         pieces[m] = swap(group, "aa", m)
@@ -269,7 +271,7 @@
         [vmem] * n,
         scratch=[pltpu.VMEM((rank, groups * rank), F32)],
         moved=4 * rank * groups * rank,
-    )(own, *received)
+    )(*tops)
     corrections = call(
         functools.partial(top_kernel, n, groups),
         [shape((share, rank))] * n,
@@ -278,6 +280,13 @@
         moved=4 * share * n * rank,
     )(rows, level, own, *received, *[pieces[m] for m in range(groups)])
     back = [corrections[0]] + [swap(corrections[k], "ba", k) for k in range(1, n)]
+    applied, down = call(
+        down_kernel,
+        [shape((points, cols)), shape((points, rank))],
+        [vmem] * 4 + [unread],
+        flops=2 * points * points * (3 * rank + cols),
+        moved=2 * points * (points + 2 * cols),
+    )(inverse_held, placed, pair, applied, corrections[0])
     return call(
         functools.partial(final_kernel, n),
         shape((points, cols)),

time: 36.5 us -> 36 us (0.986)
  waiting for transfers between devices: 12.6 us -> 6.9 us
  starting transfers between devices: 13.1 us -> 17.5 us
  Pallas kernels: 10.6 us -> 11.4 us
    ppermute x13 -> x16, waiting for transfers between devices: 12.6 us -> 6.9 us  [swap(): return lax.ppermute(array, axis, [(i, i ^ k) for i in range(size)])]
    ppermute x13 -> x16, starting transfers between devices: 13.1 us -> 17.5 us  [swap(): return lax.ppermute(array, axis, [(i, i ^ k) for i in range(size)])]
    pallas_call x1, Pallas kernels: 3.63 us -> 4.27 us  [shards(): call(functools.partial(front_kernel, n), [shape((size, rank)) for size in...]
    pallas_call x1 -> x2, Pallas kernels: 4.56 us -> 4.64 us  [the longest x1 2.32 us: shards(): call(applied_kernel, [shape((points, cols)), shape(top.shape)], [vmem] *...]
  transfers between devices with their start and end apart: 13 -> 16, of which waited for: 8 -> 6; matrix products, arithmetic and copies ran while one was open for 0% -> 0% of each run, Pallas kernels for 13% -> 15%
where the time goes in v4:
time: 36 us; the launch traced here: 35.9 us
  starting transfers between devices  17.5 us (49%)
  Pallas kernels  11.4 us (32%)
  waiting for transfers between devices  6.9 us (19%)
    ppermute x16, starting transfers between devices, swap(): return lax.ppermute(array, axis, [(i, i ^ k) for i in range(size)])  17.5 us
    ppermute x16, waiting for transfers between devices, swap(): return lax.ppermute(array, axis, [(i, i ^ k) for i in range(size)])  6.9 us
    pallas_call x1, Pallas kernels, shards(): call(functools.partial(front_kernel, n), [shape((size, rank)) for size in...  4.27 us
    pallas_call x1, Pallas kernels, shards(): call(applied_kernel, [shape((points, cols)), shape(top.shape)], [vmem] *...  2.32 us
    pallas_call x1, Pallas kernels, shards(): call(down_kernel, [shape((points, cols)), shape((points, rank))], [vmem]...  2.32 us
    pallas_call x1, Pallas kernels, shards(): call(functools.partial(final_kernel, n), shape((points, cols)), [vmem] *...  1.24 us
  transfers between devices with their start and end apart: 16, of which 6 were waited for; matrix products, arithmetic and copies ran while one was open for 0% of the time, Pallas kernels for 15%

profile of v4, /device:TPU:0, one launch (start us, length us, event | category | flops | bytes accessed | tf_op | source)
XLA Modules:
  0.0 35.9 jit_solution(15291194454855346350)
XLA Ops:
  0.0 4.3 %shard_map.82 = (bf16[512,128]{1,0:T(8,128)(2,1)S(1)}, bf16[512,128]{1,0:T(8,128)(2,1)S(1)}, bf16[512,128]{1,0:T(8,128)(2,1)S(1)}, bf16[768,128]{1,0:T(8,128)(2,...) custom-call(s32[1,1024]{1,0:T(1,128)} %order_hbm.1, ...), custom_call_target="tpu_custom_call" | custom-call | flops 939524096 | bytes 3407872 | tf_op jit(solution)/shard_map/pallas_call | solution.py:235
  4.3 3.0 %collective-permute-start.3 = (bf16[512,128]{1,0:T(8,128)(2,1)S(1)}, bf16[512,128]{1,0:T(8,128)(2,1)S(1)}, u32[]{:S(2)}, u32[]{:S(2)}) collective-permute-start(bf16[512,128]{1,0:T(8,128)(2,1)S(1)} %get-tuple-element.34), channel_id=1, source_target_pairs={{0,1},{1,0},{2,3},{3,2},{4,5},{5,4},{6,7},{7,6},{8,9},{9,8},{10,11... | collective-permute-start | bytes 393224 | tf_op jit(solution)/shard_map/ppermute | solution.py:232
  7.3 1.5 %collective-permute-start.4 = (bf16[512,128]{1,0:T(8,128)(2,1)S(1)}, bf16[512,128]{1,0:T(8,128)(2,1)S(1)}, u32[]{:S(2)}, u32[]{:S(2)}) collective-permute-start(bf16[512,128]{1,0:T(8,128)(2,1)S(1)} %get-tuple-element.35), channel_id=1, source_target_pairs={{0,2},{1,3},{2,0},{3,1},{4,6},{5,7},{6,4},{7,5},{8,10},{9,11},{10,... | collective-permute-start | bytes 393224 | tf_op jit(solution)/shard_map/ppermute | solution.py:232
  8.8 0.0 collective-permute-start.5
  8.8 2.3 %shard_map.83 = (bf16[1024,512]{1,0:T(8,128)(2,1)S(1)}, bf16[32,1024]{1,0:T(8,128)(2,1)S(1)}) custom-call(bf16[1024,512]{1,0:T(8,128)(2,1)S(1)} %get-tuple-element.28.sides_ref, bf16[1024,1024]{1,0:T(8,128)(2,1)S(1)} %get-tuple-element.25.inverse_ref, bf16[1024,1024]{1,0:T(8,128)(2,1)S(1)} %get-tuple-element.29.gather_ref, ...), custom_call_target="tpu_custom_call" | custom-call | flops 2147483648 | bytes 4194304 | tf_op jit(solution)/shard_map/pallas_call | solution.py:248
  11.1 3.0 %collective-permute-start.2 = (bf16[32,1024]{1,0:T(8,128)(2,1)S(1)}, bf16[32,1024]{1,0:T(8,128)(2,1)S(1)}, u32[]{:S(2)}, u32[]{:S(2)}) collective-permute-start(bf16[32,1024]{1,0:T(8,128)(2,1)S(1)} %get-tuple-element.32.rest_0_), channel_id=1, source_target_pairs={{0,3},{1,2},{2,1},{3,0},{4,7},{5,6},{6,5},{7,4},{8,11},{9,10},{10,... | collective-permute-start | bytes 196616 | tf_op jit(solution)/shard_map/ppermute | solution.py:232
  14.1 0.5 %collective-permute-start.1 = (bf16[32,1024]{1,0:T(8,128)(2,1)S(1)}, bf16[32,1024]{1,0:T(8,128)(2,1)S(1)}, u32[]{:S(2)}, u32[]{:S(2)}) collective-permute-start(bf16[32,1024]{1,0:T(8,128)(2,1)S(1)} %get-tuple-element.32.rest_0_), channel_id=1, source_target_pairs={{0,2},{1,3},{2,0},{3,1},{4,6},{5,7},{6,4},{7,5},{8,10},{9,11},{10,... | collective-permute-start | bytes 196616 | tf_op jit(solution)/shard_map/ppermute | solution.py:232
  14.6 0.0 collective-permute-done.3.rest_0_.rest_1_
  14.6 0.2 collective-permute-start
  14.8 1.8 %collective-permute-done.4.rest_1_.rest_2_ = bf16[512,128]{1,0:T(8,128)(2,1)S(1)} collective-permute-done((bf16[512,128]{1,0:T(8,128)(2,1)S(1)}, bf16[512,128]{1,0:T(8,128)(2,1)S(1)}, u32[]{:S(2)}, u32[]{:S(2)}) %collective-permute-start.4) | collective-permute-done | bytes 131104 | tf_op jit(solution)/shard_map/ppermute | solution.py:232
  16.6 0.0 collective-permute-done.5.rest_2_.rest_3_
  16.6 0.7 %shard_map.85 = (f32[128,512]{1,0:T(8,128)S(1)}, bf16[128,128]{1,0:T(8,128)(2,1)S(1)}) custom-call(bf16[1024,512]{1,0:T(8,128)(2,1)S(1)} %get-tuple-element.31.after.applied_ref, bf16[768,128]{1,0:T(8,128)(2,1)S(1)} %get-tuple-element.33.own_ref.rest_0_, bf16[512,128]{1,0:T(8,128)(2,1)S(1)} %collective-permute-done.3.rest_0_.rest_1_, ...), custom_call_target="tpu_custom_call" | custom-call | flops 83886080 | bytes 262144 | tf_op jit(solution)/shard_map/pallas_call | solution.py:256
  17.2 3.0 %collective-permute-start.11 = (bf16[128,128]{1,0:T(8,128)(2,1)S(1)}, bf16[128,128]{1,0:T(8,128)(2,1)S(1)}, u32[]{:S(2)}, u32[]{:S(2)}) collective-permute-start(bf16[128,128]{1,0:T(8,128)(2,1)S(1)} %get-tuple-element.38.rest_4_), channel_id=1, source_target_pairs={{0,24},{4,28},{8,16},{12,20},{16,8},{20,12},{24,0},{28,4},{1,25},{... | collective-permute-start | bytes 98312 | tf_op jit(solution)/shard_map/ppermute | solution.py:232
  20.2 0.0 collective-permute-start.9
  20.2 0.0 collective-permute-done.2.rest_3_
  20.2 1.5 %collective-permute-start.7 = (bf16[128,128]{1,0:T(8,128)(2,1)S(1)}, bf16[128,128]{1,0:T(8,128)(2,1)S(1)}, u32[]{:S(2)}, u32[]{:S(2)}) collective-permute-start(bf16[128,128]{1,0:T(8,128)(2,1)S(1)} %get-tuple-element.38.rest_4_), channel_id=1, source_target_pairs={{0,8},{4,12},{8,0},{12,4},{16,24},{20,28},{24,16},{28,20},{1,9},{5... | collective-permute-start | bytes 98312 | tf_op jit(solution)/shard_map/ppermute | solution.py:232
  21.7 0.0 collective-permute-done.1.rest_2_
  21.7 0.0 collective-permute-start.6
  21.7 1.4 %collective-permute-done.11.rest_10_ = bf16[128,128]{1,0:T(8,128)(2,1)S(1)} collective-permute-done((bf16[128,128]{1,0:T(8,128)(2,1)S(1)}, bf16[128,128]{1,0:T(8,128)(2,1)S(1)}, u32[]{:S(2)}, u32[]{:S(2)}) %collective-permute-start.11) | collective-permute-done | bytes 32800 | tf_op jit(solution)/shard_map/ppermute | solution.py:232
  23.1 0.0 collective-permute-start.12
  23.1 1.9 %collective-permute-done.9.rest_8_ = bf16[128,128]{1,0:T(8,128)(2,1)S(1)} collective-permute-done((bf16[128,128]{1,0:T(8,128)(2,1)S(1)}, bf16[128,128]{1,0:T(8,128)(2,1)S(1)}, u32[]{:S(2)}, u32[]{:S(2)}) %collective-permute-start.9) | collective-permute-done | bytes 32800 | tf_op jit(solution)/shard_map/ppermute | solution.py:232
  25.0 0.0 collective-permute-start.10
  25.0 0.0 collective-permute-done.7.rest_6_
  25.0 0.5 %collective-permute-start.8 = (bf16[128,128]{1,0:T(8,128)(2,1)S(1)}, bf16[128,128]{1,0:T(8,128)(2,1)S(1)}, u32[]{:S(2)}, u32[]{:S(2)}) collective-permute-start(bf16[128,128]{1,0:T(8,128)(2,1)S(1)} %collective-permute-done.7.rest_6_), channel_id=1, source_target_pairs={{0,4},{4,0},{8,12},{12,8},{16,20},{20,16},{24,28},{28,24},{1,5},{5... | collective-permute-start | bytes 98312 | tf_op jit(solution)/shard_map/ppermute | solution.py:232
  25.5 0.0 collective-permute-done.rest_1_
  25.5 0.1 shard_map.84.rows_ref
  25.7 0.0 collective-permute-done.6.rest_5_
  25.7 0.0 collective-permute-done.12.rest_11_
  25.7 0.6 %collective-permute-done.10.rest_9_ = bf16[128,128]{1,0:T(8,128)(2,1)S(1)} collective-permute-done((bf16[128,128]{1,0:T(8,128)(2,1)S(1)}, bf16[128,128]{1,0:T(8,128)(2,1)S(1)}, u32[]{:S(2)}, u32[]{:S(2)}) %collective-permute-start.10) | collective-permute-done | bytes 32800 | tf_op jit(solution)/shard_map/ppermute | solution.py:232
  26.2 0.2 collective-permute-done.8.rest_7_
  26.4 0.4 %shard_map.86 = (bf16[128,128]{1,0:T(8,128)(2,1)S(1)}, bf16[128,128]{1,0:T(8,128)(2,1)S(1)}, bf16[128,128]{1,0:T(8,128)(2,1)S(1)}, bf16[128,128]{1,0:T(8,128)(2,1)S(1)}) custom-call(bf16[128,1024]{1,0:T(8,128)(2,1)S(1)} %shard_map.84.rows_ref, f32[128,512]{1,0:T(8,128)S(1)} %get-tuple-element.37.level_ref, ...), custom_call_target="tpu_custom_call" | custom-call | flops 50331648 | bytes 262144 | tf_op jit(solution)/shard_map/pallas_call | solution.py:275
  26.8 1.2 %collective-permute-start.13 = (bf16[128,128]{1,0:T(8,128)(2,1)S(1)}, bf16[128,128]{1,0:T(8,128)(2,1)S(1)}, u32[]{:S(2)}, u32[]{:S(2)}) collective-permute-start(bf16[128,128]{1,0:T(8,128)(2,1)S(1)} %get-tuple-element.42), channel_id=1, source_target_pairs={{0,1},{1,0},{2,3},{3,2},{4,5},{5,4},{6,7},{7,6},{8,9},{9,8},{10,11... | collective-permute-start | bytes 98312 | tf_op jit(solution)/shard_map/ppermute | solution.py:232
  28.0 1.8 %collective-permute-start.14 = (bf16[128,128]{1,0:T(8,128)(2,1)S(1)}, bf16[128,128]{1,0:T(8,128)(2,1)S(1)}, u32[]{:S(2)}, u32[]{:S(2)}) collective-permute-start(bf16[128,128]{1,0:T(8,128)(2,1)S(1)} %get-tuple-element.43), channel_id=1, source_target_pairs={{0,2},{1,3},{2,0},{3,1},{4,6},{5,7},{6,4},{7,5},{8,10},{9,11},{10,... | collective-permute-start | bytes 98312 | tf_op jit(solution)/shard_map/ppermute | solution.py:232
  29.8 1.4 %collective-permute-start.15 = (bf16[128,128]{1,0:T(8,128)(2,1)S(1)}, bf16[128,128]{1,0:T(8,128)(2,1)S(1)}, u32[]{:S(2)}, u32[]{:S(2)}) collective-permute-start(bf16[128,128]{1,0:T(8,128)(2,1)S(1)} %get-tuple-element.44), channel_id=1, source_target_pairs={{0,3},{1,2},{2,1},{3,0},{4,7},{5,6},{6,5},{7,4},{8,11},{9,10},{10,... | collective-permute-start | bytes 98312 | tf_op jit(solution)/shard_map/ppermute | solution.py:232
  31.2 2.3 %shard_map.87 = (bf16[1024,512]{1,0:T(8,128)(2,1)S(1)}, bf16[1024,128]{1,0:T(8,128)(2,1)S(1)}) custom-call(bf16[1024,1024]{1,0:T(8,128)(2,1)S(1)} %get-tuple-element.25.inverse_ref, bf16[1024,1024]{1,0:T(8,128)(2,1)S(1)} %get-tuple-element.26.placed_ref, bf16[1024,256]{1,0:T(8,128)(2,1)S(1)} %get-tuple-element.27.pair_ref, ...), custom_call_target="tpu_custom_call" | custom-call | flops 1879048192 | bytes 4194304 | tf_op jit(solution)/shard_map/pallas_call | solution.py:283
  33.5 0.0 collective-permute-done.13.rest_1_
  33.5 0.0 collective-permute-done.14.rest_2_
  33.5 1.1 %collective-permute-done.15.rest_3_ = bf16[128,128]{1,0:T(8,128)(2,1)S(1)} collective-permute-done((bf16[128,128]{1,0:T(8,128)(2,1)S(1)}, bf16[128,128]{1,0:T(8,128)(2,1)S(1)}, u32[]{:S(2)}, u32[]{:S(2)}) %collective-permute-start.15) | collective-permute-done | bytes 32800 | tf_op jit(solution)/shard_map/ppermute | solution.py:232
  34.6 1.2 %shard_map.88 = bf16[1024,512]{1,0:T(8,128)(2,1)} custom-call(bf16[1024,512]{1,0:T(8,128)(2,1)S(1)} %get-tuple-element.40.applied_ref, bf16[1024,128]{1,0:T(8,128)(2,1)S(1)} %get-tuple-element.41.down_ref, bf16[128,128]{1,0:T(8,128)(2,1)S(1)} %get-tuple-element.39.after.rest_0_, bf16[128,128]{1,0:T(8,128)(2,1)S(1)} %collective-permute-done.13.rest_1_, ...), custom_call_target="tpu_custom_call" | custom-call | flops 134217728 | bytes 2097152 | tf_op jit(solution)/shard_map/pallas_call | solution.py:290
Async XLA Ops:
  4.3 10.3 %collective-permute-start.3 = (bf16[512,128]{1,0:T(8,128)(2,1)S(1)}, bf16[512,128]{1,0:T(8,128)(2,1)S(1)}, u32[]{:S(2)}, u32[]{:S(2)}) collective-permute-start(bf16[512,128]{1,0:T(8,128)(2,1)S(1)} %get-tuple-element.34), channel_id=1, source_target_pairs={{0,1},{1,0},{2,3},{3,2},{4,5},{5,4},{6,7},{7,6},{8,9},{9,8},{10,11... | collective-permute-start | bytes 393224 | tf_op jit(solution)/shard_map/ppermute | solution.py:232
  7.3 9.3 %collective-permute-start.4 = (bf16[512,128]{1,0:T(8,128)(2,1)S(1)}, bf16[512,128]{1,0:T(8,128)(2,1)S(1)}, u32[]{:S(2)}, u32[]{:S(2)}) collective-permute-start(bf16[512,128]{1,0:T(8,128)(2,1)S(1)} %get-tuple-element.35), channel_id=1, source_target_pairs={{0,2},{1,3},{2,0},{3,1},{4,6},{5,7},{6,4},{7,5},{8,10},{9,11},{10,... | collective-permute-start | bytes 393224 | tf_op jit(solution)/shard_map/ppermute | solution.py:232
  8.8 7.7 %collective-permute-start.5 = (bf16[512,128]{1,0:T(8,128)(2,1)S(1)}, bf16[512,128]{1,0:T(8,128)(2,1)S(1)}, u32[]{:S(2)}, u32[]{:S(2)}) collective-permute-start(bf16[512,128]{1,0:T(8,128)(2,1)S(1)} %get-tuple-element.36), channel_id=1, source_target_pairs={{0,3},{1,2},{2,1},{3,0},{4,7},{5,6},{6,5},{7,4},{8,11},{9,10},{10,... | collective-permute-start | bytes 393224 | tf_op jit(solution)/shard_map/ppermute | solution.py:232
  11.1 9.1 %collective-permute-start.2 = (bf16[32,1024]{1,0:T(8,128)(2,1)S(1)}, bf16[32,1024]{1,0:T(8,128)(2,1)S(1)}, u32[]{:S(2)}, u32[]{:S(2)}) collective-permute-start(bf16[32,1024]{1,0:T(8,128)(2,1)S(1)} %get-tuple-element.32.rest_0_), channel_id=1, source_target_pairs={{0,3},{1,2},{2,1},{3,0},{4,7},{5,6},{6,5},{7,4},{8,11},{9,10},{10,... | collective-permute-start | bytes 196616 | tf_op jit(solution)/shard_map/ppermute | solution.py:232
  14.1 7.6 %collective-permute-start.1 = (bf16[32,1024]{1,0:T(8,128)(2,1)S(1)}, bf16[32,1024]{1,0:T(8,128)(2,1)S(1)}, u32[]{:S(2)}, u32[]{:S(2)}) collective-permute-start(bf16[32,1024]{1,0:T(8,128)(2,1)S(1)} %get-tuple-element.32.rest_0_), channel_id=1, source_target_pairs={{0,2},{1,3},{2,0},{3,1},{4,6},{5,7},{6,4},{7,5},{8,10},{9,11},{10,... | collective-permute-start | bytes 196616 | tf_op jit(solution)/shard_map/ppermute | solution.py:232
  14.6 10.9 %collective-permute-start = (bf16[32,1024]{1,0:T(8,128)(2,1)S(1)}, bf16[32,1024]{1,0:T(8,128)(2,1)S(1)}, u32[]{:S(2)}, u32[]{:S(2)}) collective-permute-start(bf16[32,1024]{1,0:T(8,128)(2,1)S(1)} %get-tuple-element.32.rest_0_), channel_id=1, source_target_pairs={{0,1},{1,0},{2,3},{3,2},{4,5},{5,4},{6,7},{7,6},{8,9},{9,8},{10,11... | collective-permute-start | bytes 196616 | tf_op jit(solution)/shard_map/ppermute | solution.py:232
  17.2 5.8 %collective-permute-start.11 = (bf16[128,128]{1,0:T(8,128)(2,1)S(1)}, bf16[128,128]{1,0:T(8,128)(2,1)S(1)}, u32[]{:S(2)}, u32[]{:S(2)}) collective-permute-start(bf16[128,128]{1,0:T(8,128)(2,1)S(1)} %get-tuple-element.38.rest_4_), channel_id=1, source_target_pairs={{0,24},{4,28},{8,16},{12,20},{16,8},{20,12},{24,0},{28,4},{1,25},{... | collective-permute-start | bytes 98312 | tf_op jit(solution)/shard_map/ppermute | solution.py:232
  20.2 4.8 %collective-permute-start.9 = (bf16[128,128]{1,0:T(8,128)(2,1)S(1)}, bf16[128,128]{1,0:T(8,128)(2,1)S(1)}, u32[]{:S(2)}, u32[]{:S(2)}) collective-permute-start(bf16[128,128]{1,0:T(8,128)(2,1)S(1)} %get-tuple-element.38.rest_4_), channel_id=1, source_target_pairs={{0,16},{4,20},{8,24},{12,28},{16,0},{20,4},{24,8},{28,12},{1,17},{... | collective-permute-start | bytes 98312 | tf_op jit(solution)/shard_map/ppermute | solution.py:232
  20.2 4.8 %collective-permute-start.7 = (bf16[128,128]{1,0:T(8,128)(2,1)S(1)}, bf16[128,128]{1,0:T(8,128)(2,1)S(1)}, u32[]{:S(2)}, u32[]{:S(2)}) collective-permute-start(bf16[128,128]{1,0:T(8,128)(2,1)S(1)} %get-tuple-element.38.rest_4_), channel_id=1, source_target_pairs={{0,8},{4,12},{8,0},{12,4},{16,24},{20,28},{24,16},{28,20},{1,9},{5... | collective-permute-start | bytes 98312 | tf_op jit(solution)/shard_map/ppermute | solution.py:232
  21.7 3.9 %collective-permute-start.6 = (bf16[128,128]{1,0:T(8,128)(2,1)S(1)}, bf16[128,128]{1,0:T(8,128)(2,1)S(1)}, u32[]{:S(2)}, u32[]{:S(2)}) collective-permute-start(bf16[128,128]{1,0:T(8,128)(2,1)S(1)} %get-tuple-element.38.rest_4_), channel_id=1, source_target_pairs={{0,4},{4,0},{8,12},{12,8},{16,20},{20,16},{24,28},{28,24},{1,5},{5... | collective-permute-start | bytes 98312 | tf_op jit(solution)/shard_map/ppermute | solution.py:232
  23.1 2.6 %collective-permute-start.12 = (bf16[128,128]{1,0:T(8,128)(2,1)S(1)}, bf16[128,128]{1,0:T(8,128)(2,1)S(1)}, u32[]{:S(2)}, u32[]{:S(2)}) collective-permute-start(bf16[128,128]{1,0:T(8,128)(2,1)S(1)} %collective-permute-done.11.rest_10_), channel_id=1, source_target_pairs={{0,4},{4,0},{8,12},{12,8},{16,20},{20,16},{24,28},{28,24},{1,5},{5... | collective-permute-start | bytes 98312 | tf_op jit(solution)/shard_map/ppermute | solution.py:232
  25.0 1.2 %collective-permute-start.10 = (bf16[128,128]{1,0:T(8,128)(2,1)S(1)}, bf16[128,128]{1,0:T(8,128)(2,1)S(1)}, u32[]{:S(2)}, u32[]{:S(2)}) collective-permute-start(bf16[128,128]{1,0:T(8,128)(2,1)S(1)} %collective-permute-done.9.rest_8_), channel_id=1, source_target_pairs={{0,4},{4,0},{8,12},{12,8},{16,20},{20,16},{24,28},{28,24},{1,5},{5... | collective-permute-start | bytes 98312 | tf_op jit(solution)/shard_map/ppermute | solution.py:232
  25.0 1.4 %collective-permute-start.8 = (bf16[128,128]{1,0:T(8,128)(2,1)S(1)}, bf16[128,128]{1,0:T(8,128)(2,1)S(1)}, u32[]{:S(2)}, u32[]{:S(2)}) collective-permute-start(bf16[128,128]{1,0:T(8,128)(2,1)S(1)} %collective-permute-done.7.rest_6_), channel_id=1, source_target_pairs={{0,4},{4,0},{8,12},{12,8},{16,20},{20,16},{24,28},{28,24},{1,5},{5... | collective-permute-start | bytes 98312 | tf_op jit(solution)/shard_map/ppermute | solution.py:232
  26.8 6.7 %collective-permute-start.13 = (bf16[128,128]{1,0:T(8,128)(2,1)S(1)}, bf16[128,128]{1,0:T(8,128)(2,1)S(1)}, u32[]{:S(2)}, u32[]{:S(2)}) collective-permute-start(bf16[128,128]{1,0:T(8,128)(2,1)S(1)} %get-tuple-element.42), channel_id=1, source_target_pairs={{0,1},{1,0},{2,3},{3,2},{4,5},{5,4},{6,7},{7,6},{8,9},{9,8},{10,11... | collective-permute-start | bytes 98312 | tf_op jit(solution)/shard_map/ppermute | solution.py:232
  28.0 5.5 %collective-permute-start.14 = (bf16[128,128]{1,0:T(8,128)(2,1)S(1)}, bf16[128,128]{1,0:T(8,128)(2,1)S(1)}, u32[]{:S(2)}, u32[]{:S(2)}) collective-permute-start(bf16[128,128]{1,0:T(8,128)(2,1)S(1)} %get-tuple-element.43), channel_id=1, source_target_pairs={{0,2},{1,3},{2,0},{3,1},{4,6},{5,7},{6,4},{7,5},{8,10},{9,11},{10,... | collective-permute-start | bytes 98312 | tf_op jit(solution)/shard_map/ppermute | solution.py:232
  29.8 4.8 %collective-permute-start.15 = (bf16[128,128]{1,0:T(8,128)(2,1)S(1)}, bf16[128,128]{1,0:T(8,128)(2,1)S(1)}, u32[]{:S(2)}, u32[]{:S(2)}) collective-permute-start(bf16[128,128]{1,0:T(8,128)(2,1)S(1)} %get-tuple-element.44), channel_id=1, source_target_pairs={{0,3},{1,2},{2,1},{3,0},{4,7},{5,6},{6,5},{7,4},{8,11},{9,10},{10,... | collective-permute-start | bytes 98312 | tf_op jit(solution)/shard_map/ppermute | solution.py:232

commit v5 on v4

--- a/solution.py
+++ b/solution.py
@@ -69,8 +69,8 @@
     n, order_hbm, skel_hbm, sides_hbm, inverse_hbm, basis_hbm, core_hbm, transfer_hbm, top_hbm, *rest
 ):
     messages, own_ref = rest[: n - 1], rest[n - 1]
-    sides_ref, inverse_ref, gather_ref, placed_ref, pair_ref, top_ref = rest[n : n + 6]
-    order_ref, skel_ref, basis_ref, core_ref, transfer_ref, coeffs, sems = rest[n + 6 :]
+    sides_ref, inverse_ref, gather_ref, pair_ref, top_ref, order_ref = rest[n : n + 6]
+    skel_ref, basis_ref, core_ref, transfer_ref, coeffs, sems = rest[n + 6 :]
     me = lax.axis_index("ba")
     points, rank = basis_ref.shape
     rows = points // PIECES
@@ -85,7 +85,6 @@
         copy.wait()
     pair_ref[...] = basis_pair(skel_ref[...], basis_ref[...])
     gather_ref[...] = order_columns(order_ref[...], points)
-    placed_ref[...] = order_rows(order_ref[...], points)
     both = None
     for j in range(PIECES):
         copies[3 + j].wait()
@@ -118,37 +117,41 @@
     top_out[...] = top_ref[...]
 
 
-def down_kernel(inverse_ref, placed_ref, pair_ref, applied_ref, after, applied_out, down_ref):
+def down_kernel(inverse_ref, order_ref, pair_ref, applied_ref, after, applied_out, down_ref):
     del after
-    rank = down_ref.shape[1]
+    points, rank = down_ref.shape
+    placed = order_rows(order_ref[...], points)
     both = dot(inverse_ref[...], pair_ref[...])
     down = (both[:, :rank] + both[:, rank:]).astype(BF)
-    applied_out[...] = dot(placed_ref[...], applied_ref[...]).astype(BF)
-    down_ref[...] = dot(placed_ref[...], down).astype(BF)
+    applied_out[...] = dot(placed, applied_ref[...]).astype(BF)
+    down_ref[...] = dot(placed, down).astype(BF)
 
 
 def group_kernel(n, rank, after, own_ref, *rest):
     del after
     messages, (level_ref, group_ref) = rest[: n - 1], rest[n - 1 :]
     share = level_ref.shape[0]
-    core = {}
-    for k in range(n):
-        at = share + rank
-        for m in range(n) if k == 0 else [k] + partners(n, k):
-            core[k, m] = own_ref[at : at + rank, :] if k == 0 else messages[k - 1][at : at + rank, :]
-            at += rank
+    messages = messages[::-1]
     coeffs = [msg[0:share, :] for msg in (own_ref,) + messages]
     transfers = [msg[share : share + rank, :] for msg in (own_ref,) + messages]
-    total = None
-    for k in range(n):
-        level = None
-        for m in range(n):
-            term = dot(coeffs[m], core[m, k]) if (m, k) in core else dot(coeffs[m], core[k, m], NT)
-            level = term if level is None else level + term
-        level_ref[:, k * rank : (k + 1) * rank] = level
-        rest_of = (coeffs[k].astype(F32) - level).astype(BF)
-        term = dot(rest_of, transfers[k])
-        total = term if total is None else total + term
+    level = [None] * n
+
+    def add(k, term):
+        level[k] = term if level[k] is None else level[k] + term
+
+    for k in range(n):
+        msg = own_ref if k == 0 else messages[k - 1]
+        which = list(range(n)) if k == 0 else [k] + partners(n, k)
+        blocks = [msg[share + rank * (j + 1) : share + rank * (j + 2), :] for j in range(len(which))]
+        wide = dot(coeffs[k], jnp.concatenate(blocks, axis=1))
+        for j, m in enumerate(which):
+            add(m, wide[:, j * rank : (j + 1) * rank])
+        if len(which) > 1:
+            others = jnp.concatenate([coeffs[m] for m in which[1:]], axis=1)
+            add(k, dot(others, jnp.concatenate(blocks[1:], axis=1), NT))
+    level_ref[...] = jnp.concatenate(level, axis=1)
+    rest_of = [(coeffs[k].astype(F32) - level[k]).astype(BF) for k in range(n)]
+    total = dot(jnp.concatenate(rest_of, axis=1), jnp.concatenate(transfers, axis=0))
     group_ref[...] = total.astype(BF)
 
 
@@ -232,14 +235,13 @@
         return lax.ppermute(array, axis, [(i, i ^ k) for i in range(size)])
 
     sizes = [share + rank * (2 + len(partners(n, k))) for k in range(1, n)] + [share + rank * (n + 1)]
-    *messages, own, sides_held, inverse_held, gather, placed, pair, top_held = call(
+    *messages, own, sides_held, inverse_held, gather, pair, top_held, order_held = call(
         functools.partial(front_kernel, n),
         [shape((size, rank)) for size in sizes]
         + [shape(sides.shape), shape(inverse.shape)]
-        + [shape((points, points))] * 2
-        + [shape((points, 2 * rank)), shape(top.shape)],
+        + [shape((points, points)), shape((points, 2 * rank)), shape(top.shape), shape(order.shape, order.dtype)],
         [hbm] * 8,
-        scratch=[like(x) for x in (order, skel, basis, core, transfer)]
+        scratch=[like(x) for x in (skel, basis, core, transfer)]
         + [pltpu.VMEM((cols, rank), BF), pltpu.SemaphoreType.DMA((7 + PIECES,))],
         flops=2 * rank * points * (3 * points + cols),
         moved=2 * points * (points + cols + rank),
@@ -259,7 +261,7 @@
         [unread] + [vmem] * n,
         flops=2 * share * n * rank * (n + 1) * rank,
         moved=4 * share * n * rank,
-    )(applied, own, *received)
+    )(applied, own, *received[::-1])
     pieces = {0: group}
     for m in range(2, groups, 2):
         pieces[m] = swap(group, "aa", m)
@@ -286,7 +288,7 @@
         [vmem] * 4 + [unread],
         flops=2 * points * points * (3 * rank + cols),
         moved=2 * points * (points + 2 * cols),
-    )(inverse_held, placed, pair, applied, corrections[0])
+    )(inverse_held, order_held, pair, applied, corrections[0])
     return call(
         functools.partial(final_kernel, n),
         shape((points, cols)),

time: 36 us -> 34.3 us (0.953)
  Pallas kernels: 11.4 us -> 10.2 us
  starting transfers between devices: 17.5 us -> 16.7 us
    pallas_call x1, Pallas kernels: 4.27 us -> 3.35 us  [shards(): call(functools.partial(front_kernel, n), [shape((size, rank)) for size in...]
    ppermute x16, starting transfers between devices: 17.5 us -> 16.7 us  [swap(): return lax.ppermute(array, axis, [(i, i ^ k) for i in range(size)])]
  transfers between devices with their start and end apart: 16 -> 16, of which waited for: 6 -> 7; matrix products, arithmetic and copies ran while one was open for 0% -> 0% of each run, Pallas kernels for 15% -> 15%
where the time goes in v5:
time: 34.3 us; the launch traced here: 34.1 us
  starting transfers between devices  16.7 us (49%)
  Pallas kernels  10.2 us (30%)
  waiting for transfers between devices  7.14 us (21%)
    ppermute x16, starting transfers between devices, swap(): return lax.ppermute(array, axis, [(i, i ^ k) for i in range(size)])  16.7 us
    ppermute x16, waiting for transfers between devices, swap(): return lax.ppermute(array, axis, [(i, i ^ k) for i in range(size)])  7.14 us
    pallas_call x1, Pallas kernels, shards(): call(functools.partial(front_kernel, n), [shape((size, rank)) for size in...  3.35 us
    pallas_call x1, Pallas kernels, shards(): call(applied_kernel, [shape((points, cols)), shape(top.shape)], [vmem] *...  2.33 us
    pallas_call x1, Pallas kernels, shards(): call(down_kernel, [shape((points, cols)), shape((points, rank))], [vmem]...  2.33 us
    pallas_call x1, Pallas kernels, shards(): call(functools.partial(final_kernel, n), shape((points, cols)), [vmem] *...  1.24 us
  transfers between devices with their start and end apart: 16, of which 7 were waited for; matrix products, arithmetic and copies ran while one was open for 0% of the time, Pallas kernels for 15%

profile of v5, /device:TPU:0, one launch (start us, length us, event | category | flops | bytes accessed | tf_op | source)
XLA Modules:
  0.0 34.1 jit_solution(9132505060564994853)
XLA Ops:
  0.0 3.4 %shard_map.82 = (bf16[512,128]{1,0:T(8,128)(2,1)S(1)}, bf16[512,128]{1,0:T(8,128)(2,1)S(1)}, bf16[512,128]{1,0:T(8,128)(2,1)S(1)}, bf16[768,128]{1,0:T(8,128)(2,...) custom-call(s32[1,1024]{1,0:T(1,128)} %order_hbm.1, ...), custom_call_target="tpu_custom_call" | custom-call | flops 939524096 | bytes 3407872 | tf_op jit(solution)/shard_map/pallas_call | solution.py:238
  3.4 4.0 %collective-permute-start.3 = (bf16[512,128]{1,0:T(8,128)(2,1)S(1)}, bf16[512,128]{1,0:T(8,128)(2,1)S(1)}, u32[]{:S(2)}, u32[]{:S(2)}) collective-permute-start(bf16[512,128]{1,0:T(8,128)(2,1)S(1)} %get-tuple-element.34), channel_id=1, source_target_pairs={{0,3},{1,2},{2,1},{3,0},{4,7},{5,6},{6,5},{7,4},{8,11},{9,10},{10,... | collective-permute-start | bytes 393224 | tf_op jit(solution)/shard_map/ppermute | solution.py:235
  7.3 0.5 %collective-permute-start.4 = (bf16[512,128]{1,0:T(8,128)(2,1)S(1)}, bf16[512,128]{1,0:T(8,128)(2,1)S(1)}, u32[]{:S(2)}, u32[]{:S(2)}) collective-permute-start(bf16[512,128]{1,0:T(8,128)(2,1)S(1)} %get-tuple-element.35), channel_id=1, source_target_pairs={{0,2},{1,3},{2,0},{3,1},{4,6},{5,7},{6,4},{7,5},{8,10},{9,11},{10,... | collective-permute-start | bytes 393224 | tf_op jit(solution)/shard_map/ppermute | solution.py:235
  7.8 0.2 collective-permute-start.5
  8.0 2.3 %shard_map.83 = (bf16[1024,512]{1,0:T(8,128)(2,1)S(1)}, bf16[32,1024]{1,0:T(8,128)(2,1)S(1)}) custom-call(bf16[1024,512]{1,0:T(8,128)(2,1)S(1)} %get-tuple-element.28.sides_ref, bf16[1024,1024]{1,0:T(8,128)(2,1)S(1)} %get-tuple-element.25.inverse_ref, bf16[1024,1024]{1,0:T(8,128)(2,1)S(1)} %get-tuple-element.29.gather_ref, ...), custom_call_target="tpu_custom_call" | custom-call | flops 2147483648 | bytes 4194304 | tf_op jit(solution)/shard_map/pallas_call | solution.py:250
  10.3 2.9 %collective-permute-start.2 = (bf16[32,1024]{1,0:T(8,128)(2,1)S(1)}, bf16[32,1024]{1,0:T(8,128)(2,1)S(1)}, u32[]{:S(2)}, u32[]{:S(2)}) collective-permute-start(bf16[32,1024]{1,0:T(8,128)(2,1)S(1)} %get-tuple-element.32.rest_0_), channel_id=1, source_target_pairs={{0,3},{1,2},{2,1},{3,0},{4,7},{5,6},{6,5},{7,4},{8,11},{9,10},{10,... | collective-permute-start | bytes 196616 | tf_op jit(solution)/shard_map/ppermute | solution.py:235
  13.2 0.5 %collective-permute-start.1 = (bf16[32,1024]{1,0:T(8,128)(2,1)S(1)}, bf16[32,1024]{1,0:T(8,128)(2,1)S(1)}, u32[]{:S(2)}, u32[]{:S(2)}) collective-permute-start(bf16[32,1024]{1,0:T(8,128)(2,1)S(1)} %get-tuple-element.32.rest_0_), channel_id=1, source_target_pairs={{0,2},{1,3},{2,0},{3,1},{4,6},{5,7},{6,4},{7,5},{8,10},{9,11},{10,... | collective-permute-start | bytes 196616 | tf_op jit(solution)/shard_map/ppermute | solution.py:235
  13.7 0.0 collective-permute-done.3.rest_0_.rest_3_
  13.7 0.2 collective-permute-start
  13.9 0.3 collective-permute-done.4.rest_1_.rest_2_
  14.2 0.2 collective-permute-done.5.rest_2_.rest_1_
  14.4 0.4 %shard_map.85 = (f32[128,512]{1,0:T(8,128)S(1)}, bf16[128,128]{1,0:T(8,128)(2,1)S(1)}) custom-call(bf16[1024,512]{1,0:T(8,128)(2,1)S(1)} %get-tuple-element.31.after.applied_ref, bf16[768,128]{1,0:T(8,128)(2,1)S(1)} %get-tuple-element.33.own_ref.rest_0_, bf16[512,128]{1,0:T(8,128)(2,1)S(1)} %collective-permute-done.3.rest_0_.rest_3_, ...), custom_call_target="tpu_custom_call" | custom-call | flops 83886080 | bytes 262144 | tf_op jit(solution)/shard_map/pallas_call | solution.py:258
  14.8 3.7 %collective-permute-start.11 = (bf16[128,128]{1,0:T(8,128)(2,1)S(1)}, bf16[128,128]{1,0:T(8,128)(2,1)S(1)}, u32[]{:S(2)}, u32[]{:S(2)}) collective-permute-start(bf16[128,128]{1,0:T(8,128)(2,1)S(1)} %get-tuple-element.38.rest_4_), channel_id=1, source_target_pairs={{0,24},{4,28},{8,16},{12,20},{16,8},{20,12},{24,0},{28,4},{1,25},{... | collective-permute-start | bytes 98312 | tf_op jit(solution)/shard_map/ppermute | solution.py:235
  18.5 0.0 collective-permute-start.9
  18.5 0.0 collective-permute-done.2.rest_3_
  18.5 0.7 %collective-permute-start.7 = (bf16[128,128]{1,0:T(8,128)(2,1)S(1)}, bf16[128,128]{1,0:T(8,128)(2,1)S(1)}, u32[]{:S(2)}, u32[]{:S(2)}) collective-permute-start(bf16[128,128]{1,0:T(8,128)(2,1)S(1)} %get-tuple-element.38.rest_4_), channel_id=1, source_target_pairs={{0,8},{4,12},{8,0},{12,4},{16,24},{20,28},{24,16},{28,20},{1,9},{5... | collective-permute-start | bytes 98312 | tf_op jit(solution)/shard_map/ppermute | solution.py:235
  19.3 0.0 collective-permute-done.1.rest_2_
  19.3 0.0 collective-permute-start.6
  19.3 1.3 %collective-permute-done.11.rest_10_ = bf16[128,128]{1,0:T(8,128)(2,1)S(1)} collective-permute-done((bf16[128,128]{1,0:T(8,128)(2,1)S(1)}, bf16[128,128]{1,0:T(8,128)(2,1)S(1)}, u32[]{:S(2)}, u32[]{:S(2)}) %collective-permute-start.11) | collective-permute-done | bytes 32800 | tf_op jit(solution)/shard_map/ppermute | solution.py:235
  20.6 0.0 collective-permute-start.12
  20.6 2.7 %collective-permute-done.9.rest_8_ = bf16[128,128]{1,0:T(8,128)(2,1)S(1)} collective-permute-done((bf16[128,128]{1,0:T(8,128)(2,1)S(1)}, bf16[128,128]{1,0:T(8,128)(2,1)S(1)}, u32[]{:S(2)}, u32[]{:S(2)}) %collective-permute-start.9) | collective-permute-done | bytes 32800 | tf_op jit(solution)/shard_map/ppermute | solution.py:235
  23.3 0.0 collective-permute-start.10
  23.3 0.0 collective-permute-done.7.rest_6_
  23.3 0.5 %collective-permute-start.8 = (bf16[128,128]{1,0:T(8,128)(2,1)S(1)}, bf16[128,128]{1,0:T(8,128)(2,1)S(1)}, u32[]{:S(2)}, u32[]{:S(2)}) collective-permute-start(bf16[128,128]{1,0:T(8,128)(2,1)S(1)} %collective-permute-done.7.rest_6_), channel_id=1, source_target_pairs={{0,4},{4,0},{8,12},{12,8},{16,20},{20,16},{24,28},{28,24},{1,5},{5... | collective-permute-start | bytes 98312 | tf_op jit(solution)/shard_map/ppermute | solution.py:235
  23.9 0.0 collective-permute-done.rest_1_
  23.9 0.1 shard_map.84.rows_ref
  24.0 0.0 collective-permute-done.6.rest_5_
  24.0 0.0 collective-permute-done.12.rest_11_
  24.0 0.6 %collective-permute-done.10.rest_9_ = bf16[128,128]{1,0:T(8,128)(2,1)S(1)} collective-permute-done((bf16[128,128]{1,0:T(8,128)(2,1)S(1)}, bf16[128,128]{1,0:T(8,128)(2,1)S(1)}, u32[]{:S(2)}, u32[]{:S(2)}) %collective-permute-start.10) | collective-permute-done | bytes 32800 | tf_op jit(solution)/shard_map/ppermute | solution.py:235
  24.5 0.2 collective-permute-done.8.rest_7_
  24.7 0.4 %shard_map.86 = (bf16[128,128]{1,0:T(8,128)(2,1)S(1)}, bf16[128,128]{1,0:T(8,128)(2,1)S(1)}, bf16[128,128]{1,0:T(8,128)(2,1)S(1)}, bf16[128,128]{1,0:T(8,128)(2,1)S(1)}) custom-call(bf16[128,1024]{1,0:T(8,128)(2,1)S(1)} %shard_map.84.rows_ref, f32[128,512]{1,0:T(8,128)S(1)} %get-tuple-element.37.level_ref, ...), custom_call_target="tpu_custom_call" | custom-call | flops 50331648 | bytes 262144 | tf_op jit(solution)/shard_map/pallas_call | solution.py:277
  25.1 1.6 %collective-permute-start.13 = (bf16[128,128]{1,0:T(8,128)(2,1)S(1)}, bf16[128,128]{1,0:T(8,128)(2,1)S(1)}, u32[]{:S(2)}, u32[]{:S(2)}) collective-permute-start(bf16[128,128]{1,0:T(8,128)(2,1)S(1)} %get-tuple-element.42), channel_id=1, source_target_pairs={{0,1},{1,0},{2,3},{3,2},{4,5},{5,4},{6,7},{7,6},{8,9},{9,8},{10,11... | collective-permute-start | bytes 98312 | tf_op jit(solution)/shard_map/ppermute | solution.py:235
  26.8 1.3 %collective-permute-start.14 = (bf16[128,128]{1,0:T(8,128)(2,1)S(1)}, bf16[128,128]{1,0:T(8,128)(2,1)S(1)}, u32[]{:S(2)}, u32[]{:S(2)}) collective-permute-start(bf16[128,128]{1,0:T(8,128)(2,1)S(1)} %get-tuple-element.43), channel_id=1, source_target_pairs={{0,2},{1,3},{2,0},{3,1},{4,6},{5,7},{6,4},{7,5},{8,10},{9,11},{10,... | collective-permute-start | bytes 98312 | tf_op jit(solution)/shard_map/ppermute | solution.py:235
  28.1 0.6 %collective-permute-start.15 = (bf16[128,128]{1,0:T(8,128)(2,1)S(1)}, bf16[128,128]{1,0:T(8,128)(2,1)S(1)}, u32[]{:S(2)}, u32[]{:S(2)}) collective-permute-start(bf16[128,128]{1,0:T(8,128)(2,1)S(1)} %get-tuple-element.44), channel_id=1, source_target_pairs={{0,3},{1,2},{2,1},{3,0},{4,7},{5,6},{6,5},{7,4},{8,11},{9,10},{10,... | collective-permute-start | bytes 98312 | tf_op jit(solution)/shard_map/ppermute | solution.py:235
  28.7 2.3 %shard_map.87 = (bf16[1024,512]{1,0:T(8,128)(2,1)S(1)}, bf16[1024,128]{1,0:T(8,128)(2,1)S(1)}) custom-call(bf16[1024,1024]{1,0:T(8,128)(2,1)S(1)} %get-tuple-element.25.inverse_ref, s32[1,1024]{1,0:T(1,128)S(1)} %get-tuple-element.26.order_ref, bf16[1024,256]{1,0:T(8,128)(2,1)S(1)} %get-tuple-element.27.pair_ref, ...), custom_call_target="tpu_custom_call" | custom-call | flops 1879048192 | bytes 4194304 | tf_op jit(solution)/shard_map/pallas_call | solution.py:285
  31.0 0.0 collective-permute-done.13.rest_1_
  31.0 0.0 collective-permute-done.14.rest_2_
  31.1 1.8 %collective-permute-done.15.rest_3_ = bf16[128,128]{1,0:T(8,128)(2,1)S(1)} collective-permute-done((bf16[128,128]{1,0:T(8,128)(2,1)S(1)}, bf16[128,128]{1,0:T(8,128)(2,1)S(1)}, u32[]{:S(2)}, u32[]{:S(2)}) %collective-permute-start.15) | collective-permute-done | bytes 32800 | tf_op jit(solution)/shard_map/ppermute | solution.py:235
  32.9 1.2 %shard_map.88 = bf16[1024,512]{1,0:T(8,128)(2,1)} custom-call(bf16[1024,512]{1,0:T(8,128)(2,1)S(1)} %get-tuple-element.40.applied_ref, bf16[1024,128]{1,0:T(8,128)(2,1)S(1)} %get-tuple-element.41.down_ref, bf16[128,128]{1,0:T(8,128)(2,1)S(1)} %get-tuple-element.39.after.rest_0_, bf16[128,128]{1,0:T(8,128)(2,1)S(1)} %collective-permute-done.13.rest_1_, ...), custom_call_target="tpu_custom_call" | custom-call | flops 134217728 | bytes 2097152 | tf_op jit(solution)/shard_map/pallas_call | solution.py:292
Async XLA Ops:
  3.4 10.4 %collective-permute-start.3 = (bf16[512,128]{1,0:T(8,128)(2,1)S(1)}, bf16[512,128]{1,0:T(8,128)(2,1)S(1)}, u32[]{:S(2)}, u32[]{:S(2)}) collective-permute-start(bf16[512,128]{1,0:T(8,128)(2,1)S(1)} %get-tuple-element.34), channel_id=1, source_target_pairs={{0,3},{1,2},{2,1},{3,0},{4,7},{5,6},{6,5},{7,4},{8,11},{9,10},{10,... | collective-permute-start | bytes 393224 | tf_op jit(solution)/shard_map/ppermute | solution.py:235
  7.3 6.8 %collective-permute-start.4 = (bf16[512,128]{1,0:T(8,128)(2,1)S(1)}, bf16[512,128]{1,0:T(8,128)(2,1)S(1)}, u32[]{:S(2)}, u32[]{:S(2)}) collective-permute-start(bf16[512,128]{1,0:T(8,128)(2,1)S(1)} %get-tuple-element.35), channel_id=1, source_target_pairs={{0,2},{1,3},{2,0},{3,1},{4,6},{5,7},{6,4},{7,5},{8,10},{9,11},{10,... | collective-permute-start | bytes 393224 | tf_op jit(solution)/shard_map/ppermute | solution.py:235
  7.8 6.6 %collective-permute-start.5 = (bf16[512,128]{1,0:T(8,128)(2,1)S(1)}, bf16[512,128]{1,0:T(8,128)(2,1)S(1)}, u32[]{:S(2)}, u32[]{:S(2)}) collective-permute-start(bf16[512,128]{1,0:T(8,128)(2,1)S(1)} %get-tuple-element.36), channel_id=1, source_target_pairs={{0,1},{1,0},{2,3},{3,2},{4,5},{5,4},{6,7},{7,6},{8,9},{9,8},{10,11... | collective-permute-start | bytes 393224 | tf_op jit(solution)/shard_map/ppermute | solution.py:235
  10.3 8.2 %collective-permute-start.2 = (bf16[32,1024]{1,0:T(8,128)(2,1)S(1)}, bf16[32,1024]{1,0:T(8,128)(2,1)S(1)}, u32[]{:S(2)}, u32[]{:S(2)}) collective-permute-start(bf16[32,1024]{1,0:T(8,128)(2,1)S(1)} %get-tuple-element.32.rest_0_), channel_id=1, source_target_pairs={{0,3},{1,2},{2,1},{3,0},{4,7},{5,6},{6,5},{7,4},{8,11},{9,10},{10,... | collective-permute-start | bytes 196616 | tf_op jit(solution)/shard_map/ppermute | solution.py:235
  13.2 6.0 %collective-permute-start.1 = (bf16[32,1024]{1,0:T(8,128)(2,1)S(1)}, bf16[32,1024]{1,0:T(8,128)(2,1)S(1)}, u32[]{:S(2)}, u32[]{:S(2)}) collective-permute-start(bf16[32,1024]{1,0:T(8,128)(2,1)S(1)} %get-tuple-element.32.rest_0_), channel_id=1, source_target_pairs={{0,2},{1,3},{2,0},{3,1},{4,6},{5,7},{6,4},{7,5},{8,10},{9,11},{10,... | collective-permute-start | bytes 196616 | tf_op jit(solution)/shard_map/ppermute | solution.py:235
  13.7 10.1 %collective-permute-start = (bf16[32,1024]{1,0:T(8,128)(2,1)S(1)}, bf16[32,1024]{1,0:T(8,128)(2,1)S(1)}, u32[]{:S(2)}, u32[]{:S(2)}) collective-permute-start(bf16[32,1024]{1,0:T(8,128)(2,1)S(1)} %get-tuple-element.32.rest_0_), channel_id=1, source_target_pairs={{0,1},{1,0},{2,3},{3,2},{4,5},{5,4},{6,7},{7,6},{8,9},{9,8},{10,11... | collective-permute-start | bytes 196616 | tf_op jit(solution)/shard_map/ppermute | solution.py:235
  14.8 5.8 %collective-permute-start.11 = (bf16[128,128]{1,0:T(8,128)(2,1)S(1)}, bf16[128,128]{1,0:T(8,128)(2,1)S(1)}, u32[]{:S(2)}, u32[]{:S(2)}) collective-permute-start(bf16[128,128]{1,0:T(8,128)(2,1)S(1)} %get-tuple-element.38.rest_4_), channel_id=1, source_target_pairs={{0,24},{4,28},{8,16},{12,20},{16,8},{20,12},{24,0},{28,4},{1,25},{... | collective-permute-start | bytes 98312 | tf_op jit(solution)/shard_map/ppermute | solution.py:235
  18.5 4.8 %collective-permute-start.9 = (bf16[128,128]{1,0:T(8,128)(2,1)S(1)}, bf16[128,128]{1,0:T(8,128)(2,1)S(1)}, u32[]{:S(2)}, u32[]{:S(2)}) collective-permute-start(bf16[128,128]{1,0:T(8,128)(2,1)S(1)} %get-tuple-element.38.rest_4_), channel_id=1, source_target_pairs={{0,16},{4,20},{8,24},{12,28},{16,0},{20,4},{24,8},{28,12},{1,17},{... | collective-permute-start | bytes 98312 | tf_op jit(solution)/shard_map/ppermute | solution.py:235
  18.5 4.8 %collective-permute-start.7 = (bf16[128,128]{1,0:T(8,128)(2,1)S(1)}, bf16[128,128]{1,0:T(8,128)(2,1)S(1)}, u32[]{:S(2)}, u32[]{:S(2)}) collective-permute-start(bf16[128,128]{1,0:T(8,128)(2,1)S(1)} %get-tuple-element.38.rest_4_), channel_id=1, source_target_pairs={{0,8},{4,12},{8,0},{12,4},{16,24},{20,28},{24,16},{28,20},{1,9},{5... | collective-permute-start | bytes 98312 | tf_op jit(solution)/shard_map/ppermute | solution.py:235
  19.3 4.7 %collective-permute-start.6 = (bf16[128,128]{1,0:T(8,128)(2,1)S(1)}, bf16[128,128]{1,0:T(8,128)(2,1)S(1)}, u32[]{:S(2)}, u32[]{:S(2)}) collective-permute-start(bf16[128,128]{1,0:T(8,128)(2,1)S(1)} %get-tuple-element.38.rest_4_), channel_id=1, source_target_pairs={{0,4},{4,0},{8,12},{12,8},{16,20},{20,16},{24,28},{28,24},{1,5},{5... | collective-permute-start | bytes 98312 | tf_op jit(solution)/shard_map/ppermute | solution.py:235
  20.6 3.4 %collective-permute-start.12 = (bf16[128,128]{1,0:T(8,128)(2,1)S(1)}, bf16[128,128]{1,0:T(8,128)(2,1)S(1)}, u32[]{:S(2)}, u32[]{:S(2)}) collective-permute-start(bf16[128,128]{1,0:T(8,128)(2,1)S(1)} %collective-permute-done.11.rest_10_), channel_id=1, source_target_pairs={{0,4},{4,0},{8,12},{12,8},{16,20},{20,16},{24,28},{28,24},{1,5},{5... | collective-permute-start | bytes 98312 | tf_op jit(solution)/shard_map/ppermute | solution.py:235
  23.3 1.2 %collective-permute-start.10 = (bf16[128,128]{1,0:T(8,128)(2,1)S(1)}, bf16[128,128]{1,0:T(8,128)(2,1)S(1)}, u32[]{:S(2)}, u32[]{:S(2)}) collective-permute-start(bf16[128,128]{1,0:T(8,128)(2,1)S(1)} %collective-permute-done.9.rest_8_), channel_id=1, source_target_pairs={{0,4},{4,0},{8,12},{12,8},{16,20},{20,16},{24,28},{28,24},{1,5},{5... | collective-permute-start | bytes 98312 | tf_op jit(solution)/shard_map/ppermute | solution.py:235
  23.3 1.4 %collective-permute-start.8 = (bf16[128,128]{1,0:T(8,128)(2,1)S(1)}, bf16[128,128]{1,0:T(8,128)(2,1)S(1)}, u32[]{:S(2)}, u32[]{:S(2)}) collective-permute-start(bf16[128,128]{1,0:T(8,128)(2,1)S(1)} %collective-permute-done.7.rest_6_), channel_id=1, source_target_pairs={{0,4},{4,0},{8,12},{12,8},{16,20},{20,16},{24,28},{28,24},{1,5},{5... | collective-permute-start | bytes 98312 | tf_op jit(solution)/shard_map/ppermute | solution.py:235
  25.1 5.9 %collective-permute-start.13 = (bf16[128,128]{1,0:T(8,128)(2,1)S(1)}, bf16[128,128]{1,0:T(8,128)(2,1)S(1)}, u32[]{:S(2)}, u32[]{:S(2)}) collective-permute-start(bf16[128,128]{1,0:T(8,128)(2,1)S(1)} %get-tuple-element.42), channel_id=1, source_target_pairs={{0,1},{1,0},{2,3},{3,2},{4,5},{5,4},{6,7},{7,6},{8,9},{9,8},{10,11... | collective-permute-start | bytes 98312 | tf_op jit(solution)/shard_map/ppermute | solution.py:235
  26.8 4.3 %collective-permute-start.14 = (bf16[128,128]{1,0:T(8,128)(2,1)S(1)}, bf16[128,128]{1,0:T(8,128)(2,1)S(1)}, u32[]{:S(2)}, u32[]{:S(2)}) collective-permute-start(bf16[128,128]{1,0:T(8,128)(2,1)S(1)} %get-tuple-element.43), channel_id=1, source_target_pairs={{0,2},{1,3},{2,0},{3,1},{4,6},{5,7},{6,4},{7,5},{8,10},{9,11},{10,... | collective-permute-start | bytes 98312 | tf_op jit(solution)/shard_map/ppermute | solution.py:235
  28.1 4.8 %collective-permute-start.15 = (bf16[128,128]{1,0:T(8,128)(2,1)S(1)}, bf16[128,128]{1,0:T(8,128)(2,1)S(1)}, u32[]{:S(2)}, u32[]{:S(2)}) collective-permute-start(bf16[128,128]{1,0:T(8,128)(2,1)S(1)} %get-tuple-element.44), channel_id=1, source_target_pairs={{0,3},{1,2},{2,1},{3,0},{4,7},{5,6},{6,5},{7,4},{8,11},{9,10},{10,... | collective-permute-start | bytes 98312 | tf_op jit(solution)/shard_map/ppermute | solution.py:235

commit v6 on v5

--- a/solution.py
+++ b/solution.py
@@ -111,10 +111,14 @@
             at += rank
 
 
-def applied_kernel(sides_ref, inverse_ref, gather_ref, top_ref, applied_ref, top_out):
-    ordered = dot(gather_ref[...], sides_ref[...]).astype(BF)
-    applied_ref[...] = dot(inverse_ref[...], ordered).astype(BF)
+def ordered_kernel(sides_ref, gather_ref, top_ref, ordered_ref, top_out):
+    ordered_ref[...] = dot(gather_ref[...], sides_ref[...]).astype(BF)
     top_out[...] = top_ref[...]
+
+
+def applied_kernel(inverse_ref, ordered_ref, group_ref, applied_ref, group_out):
+    applied_ref[...] = dot(inverse_ref[...], ordered_ref[...]).astype(BF)
+    group_out[...] = group_ref[...]
 
 
 def down_kernel(inverse_ref, order_ref, pair_ref, applied_ref, after, applied_out, down_ref):
@@ -247,13 +251,13 @@
         moved=2 * points * (points + cols + rank),
     )(*far(order, skel, sides, inverse, basis, core, transfer, top))
     received = [swap(messages[k - 1], "ba", k) for k in range(1, n)]
-    applied, top_held = call(
-        applied_kernel,
+    ordered, top_held = call(
+        ordered_kernel,
         [shape((points, cols)), shape(top.shape)],
-        [vmem] * 4,
-        flops=4 * points * points * cols,
+        [vmem] * 3,
+        flops=2 * points * points * cols,
         moved=2 * points * (points + 2 * cols),
-    )(sides_held, inverse_held, gather, top_held)
+    )(sides_held, gather, top_held)
     tops = [top_held] + [swap(top_held, "ba", k) for k in range(1, n)]
     level, group = call(
         functools.partial(group_kernel, n, rank),
@@ -261,12 +265,19 @@
         [unread] + [vmem] * n,
         flops=2 * share * n * rank * (n + 1) * rank,
         moved=4 * share * n * rank,
-    )(applied, own, *received[::-1])
+    )(ordered, own, *received[::-1])
+    applied, group_held = call(
+        applied_kernel,
+        [shape((points, cols)), shape((share, rank))],
+        [vmem] * 3,
+        flops=2 * points * points * cols,
+        moved=2 * points * (points + 2 * cols),
+    )(inverse_held, ordered, group)
     pieces = {0: group}
     for m in range(2, groups, 2):
         pieces[m] = swap(group, "aa", m)
     for m in range(0, groups, 2):
-        pieces[m + 1] = swap(pieces[m], "aa", 1)
+        pieces[m + 1] = swap(pieces[m] if m else group_held, "aa", 1)
     rows = call(
         functools.partial(top_rows_kernel, n, groups),
         shape((rank, groups * rank)),

time: 34.3 us -> 34.5 us (level)
  starting transfers between devices: 16.7 us -> 17.8 us
  waiting for transfers between devices: 7.14 us -> 6.14 us
    ppermute x16, starting transfers between devices: 16.7 us -> 17.8 us  [swap(): return lax.ppermute(array, axis, [(i, i ^ k) for i in range(size)])]
    ppermute x16, waiting for transfers between devices: 7.14 us -> 6.14 us  [swap(): return lax.ppermute(array, axis, [(i, i ^ k) for i in range(size)])]
    pallas_call x1 -> x2, Pallas kernels: 2.33 us -> 2.49 us  [the longest x1 1.25 us: shards(): call(ordered_kernel, [shape((points, cols)), shape(top.shape)], [vmem] *...]
  transfers between devices with their start and end apart: 16 -> 16, of which waited for: 7 -> 7; matrix products, arithmetic and copies ran while one was open for 0% -> 0% of each run, Pallas kernels for 15% -> 16%
where the time goes in v6:
time: 34.5 us; the launch traced here: 34.4 us
  starting transfers between devices  17.8 us (52%)
  Pallas kernels  10.4 us (30%)
  waiting for transfers between devices  6.14 us (18%)
    ppermute x16, starting transfers between devices, swap(): return lax.ppermute(array, axis, [(i, i ^ k) for i in range(size)])  17.8 us
    ppermute x16, waiting for transfers between devices, swap(): return lax.ppermute(array, axis, [(i, i ^ k) for i in range(size)])  6.14 us
    pallas_call x1, Pallas kernels, shards(): call(functools.partial(front_kernel, n), [shape((size, rank)) for size in...  3.35 us
    pallas_call x1, Pallas kernels, shards(): call(down_kernel, [shape((points, cols)), shape((points, rank))], [vmem]...  2.32 us
    pallas_call x1, Pallas kernels, shards(): call(ordered_kernel, [shape((points, cols)), shape(top.shape)], [vmem] *...  1.25 us
    pallas_call x1, Pallas kernels, shards(): call(applied_kernel, [shape((points, cols)), shape((share, rank))], [vmem...  1.25 us
    pallas_call x1, Pallas kernels, shards(): call(functools.partial(final_kernel, n), shape((points, cols)), [vmem] *...  1.24 us
  transfers between devices with their start and end apart: 16, of which 7 were waited for; matrix products, arithmetic and copies ran while one was open for 0% of the time, Pallas kernels for 16%

profile of v6, /device:TPU:0, one launch (start us, length us, event | category | flops | bytes accessed | tf_op | source)
XLA Modules:
  0.0 34.4 jit_solution(17745207285185469552)
XLA Ops:
  0.0 3.4 %shard_map.82 = (bf16[512,128]{1,0:T(8,128)(2,1)S(1)}, bf16[512,128]{1,0:T(8,128)(2,1)S(1)}, bf16[512,128]{1,0:T(8,128)(2,1)S(1)}, bf16[768,128]{1,0:T(8,128)(2,...) custom-call(s32[1,1024]{1,0:T(1,128)} %order_hbm.1, ...), custom_call_target="tpu_custom_call" | custom-call | flops 939524096 | bytes 3407872 | tf_op jit(solution)/shard_map/pallas_call | solution.py:242
  3.4 4.0 %collective-permute-start = (bf16[512,128]{1,0:T(8,128)(2,1)S(1)}, bf16[512,128]{1,0:T(8,128)(2,1)S(1)}, u32[]{:S(2)}, u32[]{:S(2)}) collective-permute-start(bf16[512,128]{1,0:T(8,128)(2,1)S(1)} %get-tuple-element.35), channel_id=1, source_target_pairs={{0,3},{1,2},{2,1},{3,0},{4,7},{5,6},{6,5},{7,4},{8,11},{9,10},{10,... | collective-permute-start | bytes 393224 | tf_op jit(solution)/shard_map/ppermute | solution.py:239
  7.3 0.5 %collective-permute-start.1 = (bf16[512,128]{1,0:T(8,128)(2,1)S(1)}, bf16[512,128]{1,0:T(8,128)(2,1)S(1)}, u32[]{:S(2)}, u32[]{:S(2)}) collective-permute-start(bf16[512,128]{1,0:T(8,128)(2,1)S(1)} %get-tuple-element.36), channel_id=1, source_target_pairs={{0,2},{1,3},{2,0},{3,1},{4,6},{5,7},{6,4},{7,5},{8,10},{9,11},{10,... | collective-permute-start | bytes 393224 | tf_op jit(solution)/shard_map/ppermute | solution.py:239
  7.8 0.1 collective-permute-start.2
  8.0 1.2 %shard_map.83 = (bf16[1024,512]{1,0:T(8,128)(2,1)S(1)}, bf16[32,1024]{1,0:T(8,128)(2,1)S(1)}) custom-call(bf16[1024,512]{1,0:T(8,128)(2,1)S(1)} %get-tuple-element.30.sides_ref, bf16[1024,1024]{1,0:T(8,128)(2,1)S(1)} %get-tuple-element.31.gather_ref, bf16[32,1024]{1,0:T(8,128)(2,1)S(1)} %get-tuple-element.32.top_ref), custom_call_target="tpu_custom_call" | custom-call | flops 1073741824 | bytes 4194304 | tf_op jit(solution)/shard_map/pallas_call | solution.py:254
  9.2 2.9 %collective-permute-start.5 = (bf16[32,1024]{1,0:T(8,128)(2,1)S(1)}, bf16[32,1024]{1,0:T(8,128)(2,1)S(1)}, u32[]{:S(2)}, u32[]{:S(2)}) collective-permute-start(bf16[32,1024]{1,0:T(8,128)(2,1)S(1)} %get-tuple-element.40.rest_0_), channel_id=1, source_target_pairs={{0,3},{1,2},{2,1},{3,0},{4,7},{5,6},{6,5},{7,4},{8,11},{9,10},{10,... | collective-permute-start | bytes 196616 | tf_op jit(solution)/shard_map/ppermute | solution.py:239
  12.2 0.5 %collective-permute-start.4 = (bf16[32,1024]{1,0:T(8,128)(2,1)S(1)}, bf16[32,1024]{1,0:T(8,128)(2,1)S(1)}, u32[]{:S(2)}, u32[]{:S(2)}) collective-permute-start(bf16[32,1024]{1,0:T(8,128)(2,1)S(1)} %get-tuple-element.40.rest_0_), channel_id=1, source_target_pairs={{0,2},{1,3},{2,0},{3,1},{4,6},{5,7},{6,4},{7,5},{8,10},{9,11},{10,... | collective-permute-start | bytes 196616 | tf_op jit(solution)/shard_map/ppermute | solution.py:239
  12.7 0.0 collective-permute-done.rest_0_.rest_3_
  12.7 1.0 %collective-permute-start.3 = (bf16[32,1024]{1,0:T(8,128)(2,1)S(1)}, bf16[32,1024]{1,0:T(8,128)(2,1)S(1)}, u32[]{:S(2)}, u32[]{:S(2)}) collective-permute-start(bf16[32,1024]{1,0:T(8,128)(2,1)S(1)} %get-tuple-element.40.rest_0_), channel_id=1, source_target_pairs={{0,1},{1,0},{2,3},{3,2},{4,5},{5,4},{6,7},{7,6},{8,9},{9,8},{10,11... | collective-permute-start | bytes 196616 | tf_op jit(solution)/shard_map/ppermute | solution.py:239
  13.7 0.8 %collective-permute-done.1.rest_1_.rest_2_ = bf16[512,128]{1,0:T(8,128)(2,1)S(1)} collective-permute-done((bf16[512,128]{1,0:T(8,128)(2,1)S(1)}, bf16[512,128]{1,0:T(8,128)(2,1)S(1)}, u32[]{:S(2)}, u32[]{:S(2)}) %collective-permute-start.1) | collective-permute-done | bytes 131104 | tf_op jit(solution)/shard_map/ppermute | solution.py:239
  14.5 0.6 %collective-permute-done.2.rest_2_.rest_1_ = bf16[512,128]{1,0:T(8,128)(2,1)S(1)} collective-permute-done((bf16[512,128]{1,0:T(8,128)(2,1)S(1)}, bf16[512,128]{1,0:T(8,128)(2,1)S(1)}, u32[]{:S(2)}, u32[]{:S(2)}) %collective-permute-start.2) | collective-permute-done | bytes 131104 | tf_op jit(solution)/shard_map/ppermute | solution.py:239
  15.0 0.4 %shard_map.84 = (f32[128,512]{1,0:T(8,128)S(1)}, bf16[128,128]{1,0:T(8,128)(2,1)S(1)}) custom-call(bf16[1024,512]{1,0:T(8,128)(2,1)S(1)} %get-tuple-element.33.after.ordered_ref, bf16[768,128]{1,0:T(8,128)(2,1)S(1)} %get-tuple-element.34.own_ref.rest_0_, bf16[512,128]{1,0:T(8,128)(2,1)S(1)} %collective-permute-done.rest_0_.rest_3_, ...), custom_call_target="tpu_custom_call" | custom-call | flops 83886080 | bytes 262144 | tf_op jit(solution)/shard_map/pallas_call | solution.py:262
  15.5 3.7 %collective-permute-start.11 = (bf16[128,128]{1,0:T(8,128)(2,1)S(1)}, bf16[128,128]{1,0:T(8,128)(2,1)S(1)}, u32[]{:S(2)}, u32[]{:S(2)}) collective-permute-start(bf16[128,128]{1,0:T(8,128)(2,1)S(1)} %get-tuple-element.38.group_ref.rest_4_), channel_id=1, source_target_pairs={{0,24},{4,28},{8,16},{12,20},{16,8},{20,12},{24,0},{28,4},{1,25},{... | collective-permute-start | bytes 98312 | tf_op jit(solution)/shard_map/ppermute | solution.py:239
  19.2 0.0 collective-permute-start.9
  19.2 0.0 collective-permute-done.5.rest_3_
  19.2 0.8 %collective-permute-start.7 = (bf16[128,128]{1,0:T(8,128)(2,1)S(1)}, bf16[128,128]{1,0:T(8,128)(2,1)S(1)}, u32[]{:S(2)}, u32[]{:S(2)}) collective-permute-start(bf16[128,128]{1,0:T(8,128)(2,1)S(1)} %get-tuple-element.38.group_ref.rest_4_), channel_id=1, source_target_pairs={{0,8},{4,12},{8,0},{12,4},{16,24},{20,28},{24,16},{28,20},{1,9},{5... | collective-permute-start | bytes 98312 | tf_op jit(solution)/shard_map/ppermute | solution.py:239
  19.9 1.2 %shard_map.85 = (bf16[1024,512]{1,0:T(8,128)(2,1)S(1)}, bf16[128,128]{1,0:T(8,128)(2,1)S(1)}) custom-call(bf16[1024,1024]{1,0:T(8,128)(2,1)S(1)} %get-tuple-element.27.inverse_ref, bf16[1024,512]{1,0:T(8,128)(2,1)S(1)} %get-tuple-element.33.after.ordered_ref, bf16[128,128]{1,0:T(8,128)(2,1)S(1)} %get-tuple-element.38.group_ref.rest_4_), custom_call_target="tpu_custom_call" | custom-call | flops 1073741824 | bytes 4194304 | tf_op jit(solution)/shard_map/pallas_call | solution.py:269
  21.2 0.0 collective-permute-done.4.rest_2_
  21.2 0.1 collective-permute-start.6
  21.3 0.4 %collective-permute-done.11.rest_10_ = bf16[128,128]{1,0:T(8,128)(2,1)S(1)} collective-permute-done((bf16[128,128]{1,0:T(8,128)(2,1)S(1)}, bf16[128,128]{1,0:T(8,128)(2,1)S(1)}, u32[]{:S(2)}, u32[]{:S(2)}) %collective-permute-start.11) | collective-permute-done | bytes 32800 | tf_op jit(solution)/shard_map/ppermute | solution.py:239
  21.6 0.1 collective-permute-start.12
  21.8 2.2 %collective-permute-done.9.rest_8_ = bf16[128,128]{1,0:T(8,128)(2,1)S(1)} collective-permute-done((bf16[128,128]{1,0:T(8,128)(2,1)S(1)}, bf16[128,128]{1,0:T(8,128)(2,1)S(1)}, u32[]{:S(2)}, u32[]{:S(2)}) %collective-permute-start.9) | collective-permute-done | bytes 32800 | tf_op jit(solution)/shard_map/ppermute | solution.py:239
  24.0 0.0 collective-permute-start.10
  24.0 0.0 collective-permute-done.7.rest_6_
  24.0 0.5 %collective-permute-start.8 = (bf16[128,128]{1,0:T(8,128)(2,1)S(1)}, bf16[128,128]{1,0:T(8,128)(2,1)S(1)}, u32[]{:S(2)}, u32[]{:S(2)}) collective-permute-start(bf16[128,128]{1,0:T(8,128)(2,1)S(1)} %collective-permute-done.7.rest_6_), channel_id=1, source_target_pairs={{0,4},{4,0},{8,12},{12,8},{16,20},{20,16},{24,28},{28,24},{1,5},{5... | collective-permute-start | bytes 98312 | tf_op jit(solution)/shard_map/ppermute | solution.py:239
  24.5 0.0 collective-permute-done.3.rest_1_
  24.5 0.1 shard_map.86.rows_ref
  24.6 0.0 collective-permute-done.6.rest_5_
  24.6 0.0 collective-permute-done.12.rest_11_
  24.6 0.6 %collective-permute-done.10.rest_9_ = bf16[128,128]{1,0:T(8,128)(2,1)S(1)} collective-permute-done((bf16[128,128]{1,0:T(8,128)(2,1)S(1)}, bf16[128,128]{1,0:T(8,128)(2,1)S(1)}, u32[]{:S(2)}, u32[]{:S(2)}) %collective-permute-start.10) | collective-permute-done | bytes 32800 | tf_op jit(solution)/shard_map/ppermute | solution.py:239
  25.2 0.2 collective-permute-done.8.rest_7_
  25.4 0.4 %shard_map.87 = (bf16[128,128]{1,0:T(8,128)(2,1)S(1)}, bf16[128,128]{1,0:T(8,128)(2,1)S(1)}, bf16[128,128]{1,0:T(8,128)(2,1)S(1)}, bf16[128,128]{1,0:T(8,128)(2,1)S(1)}) custom-call(bf16[128,1024]{1,0:T(8,128)(2,1)S(1)} %shard_map.86.rows_ref, f32[128,512]{1,0:T(8,128)S(1)} %get-tuple-element.41.level_ref, ...), custom_call_target="tpu_custom_call" | custom-call | flops 50331648 | bytes 262144 | tf_op jit(solution)/shard_map/pallas_call | solution.py:288
  25.8 1.5 %collective-permute-start.13 = (bf16[128,128]{1,0:T(8,128)(2,1)S(1)}, bf16[128,128]{1,0:T(8,128)(2,1)S(1)}, u32[]{:S(2)}, u32[]{:S(2)}) collective-permute-start(bf16[128,128]{1,0:T(8,128)(2,1)S(1)} %get-tuple-element.46), channel_id=1, source_target_pairs={{0,1},{1,0},{2,3},{3,2},{4,5},{5,4},{6,7},{7,6},{8,9},{9,8},{10,11... | collective-permute-start | bytes 98312 | tf_op jit(solution)/shard_map/ppermute | solution.py:239
  27.3 1.0 %collective-permute-start.14 = (bf16[128,128]{1,0:T(8,128)(2,1)S(1)}, bf16[128,128]{1,0:T(8,128)(2,1)S(1)}, u32[]{:S(2)}, u32[]{:S(2)}) collective-permute-start(bf16[128,128]{1,0:T(8,128)(2,1)S(1)} %get-tuple-element.47), channel_id=1, source_target_pairs={{0,2},{1,3},{2,0},{3,1},{4,6},{5,7},{6,4},{7,5},{8,10},{9,11},{10,... | collective-permute-start | bytes 98312 | tf_op jit(solution)/shard_map/ppermute | solution.py:239
  28.3 1.0 %collective-permute-start.15 = (bf16[128,128]{1,0:T(8,128)(2,1)S(1)}, bf16[128,128]{1,0:T(8,128)(2,1)S(1)}, u32[]{:S(2)}, u32[]{:S(2)}) collective-permute-start(bf16[128,128]{1,0:T(8,128)(2,1)S(1)} %get-tuple-element.48), channel_id=1, source_target_pairs={{0,3},{1,2},{2,1},{3,0},{4,7},{5,6},{6,5},{7,4},{8,11},{9,10},{10,... | collective-permute-start | bytes 98312 | tf_op jit(solution)/shard_map/ppermute | solution.py:239
  29.3 2.3 %shard_map.88 = (bf16[1024,512]{1,0:T(8,128)(2,1)S(1)}, bf16[1024,128]{1,0:T(8,128)(2,1)S(1)}) custom-call(bf16[1024,1024]{1,0:T(8,128)(2,1)S(1)} %get-tuple-element.27.inverse_ref, s32[1,1024]{1,0:T(1,128)S(1)} %get-tuple-element.28.order_ref, bf16[1024,256]{1,0:T(8,128)(2,1)S(1)} %get-tuple-element.29.pair_ref, ...), custom_call_target="tpu_custom_call" | custom-call | flops 1879048192 | bytes 4194304 | tf_op jit(solution)/shard_map/pallas_call | solution.py:296
  31.7 0.0 collective-permute-done.13.rest_1_
  31.7 0.0 collective-permute-done.14.rest_2_
  31.7 1.5 %collective-permute-done.15.rest_3_ = bf16[128,128]{1,0:T(8,128)(2,1)S(1)} collective-permute-done((bf16[128,128]{1,0:T(8,128)(2,1)S(1)}, bf16[128,128]{1,0:T(8,128)(2,1)S(1)}, u32[]{:S(2)}, u32[]{:S(2)}) %collective-permute-start.15) | collective-permute-done | bytes 32800 | tf_op jit(solution)/shard_map/ppermute | solution.py:239
  33.1 1.2 %shard_map.89 = bf16[1024,512]{1,0:T(8,128)(2,1)} custom-call(bf16[1024,512]{1,0:T(8,128)(2,1)S(1)} %get-tuple-element.44.applied_ref, bf16[1024,128]{1,0:T(8,128)(2,1)S(1)} %get-tuple-element.45.down_ref, bf16[128,128]{1,0:T(8,128)(2,1)S(1)} %get-tuple-element.43.after.rest_0_, bf16[128,128]{1,0:T(8,128)(2,1)S(1)} %collective-permute-done.13.rest_1_, ...), custom_call_target="tpu_custom_call" | custom-call | flops 134217728 | bytes 2097152 | tf_op jit(solution)/shard_map/pallas_call | solution.py:303
Async XLA Ops:
  3.4 9.3 %collective-permute-start = (bf16[512,128]{1,0:T(8,128)(2,1)S(1)}, bf16[512,128]{1,0:T(8,128)(2,1)S(1)}, u32[]{:S(2)}, u32[]{:S(2)}) collective-permute-start(bf16[512,128]{1,0:T(8,128)(2,1)S(1)} %get-tuple-element.35), channel_id=1, source_target_pairs={{0,3},{1,2},{2,1},{3,0},{4,7},{5,6},{6,5},{7,4},{8,11},{9,10},{10,... | collective-permute-start | bytes 393224 | tf_op jit(solution)/shard_map/ppermute | solution.py:239
  7.3 7.1 %collective-permute-start.1 = (bf16[512,128]{1,0:T(8,128)(2,1)S(1)}, bf16[512,128]{1,0:T(8,128)(2,1)S(1)}, u32[]{:S(2)}, u32[]{:S(2)}) collective-permute-start(bf16[512,128]{1,0:T(8,128)(2,1)S(1)} %get-tuple-element.36), channel_id=1, source_target_pairs={{0,2},{1,3},{2,0},{3,1},{4,6},{5,7},{6,4},{7,5},{8,10},{9,11},{10,... | collective-permute-start | bytes 393224 | tf_op jit(solution)/shard_map/ppermute | solution.py:239
  7.8 7.2 %collective-permute-start.2 = (bf16[512,128]{1,0:T(8,128)(2,1)S(1)}, bf16[512,128]{1,0:T(8,128)(2,1)S(1)}, u32[]{:S(2)}, u32[]{:S(2)}) collective-permute-start(bf16[512,128]{1,0:T(8,128)(2,1)S(1)} %get-tuple-element.37), channel_id=1, source_target_pairs={{0,1},{1,0},{2,3},{3,2},{4,5},{5,4},{6,7},{7,6},{8,9},{9,8},{10,11... | collective-permute-start | bytes 393224 | tf_op jit(solution)/shard_map/ppermute | solution.py:239
  9.2 9.9 %collective-permute-start.5 = (bf16[32,1024]{1,0:T(8,128)(2,1)S(1)}, bf16[32,1024]{1,0:T(8,128)(2,1)S(1)}, u32[]{:S(2)}, u32[]{:S(2)}) collective-permute-start(bf16[32,1024]{1,0:T(8,128)(2,1)S(1)} %get-tuple-element.40.rest_0_), channel_id=1, source_target_pairs={{0,3},{1,2},{2,1},{3,0},{4,7},{5,6},{6,5},{7,4},{8,11},{9,10},{10,... | collective-permute-start | bytes 196616 | tf_op jit(solution)/shard_map/ppermute | solution.py:239
  12.2 9.0 %collective-permute-start.4 = (bf16[32,1024]{1,0:T(8,128)(2,1)S(1)}, bf16[32,1024]{1,0:T(8,128)(2,1)S(1)}, u32[]{:S(2)}, u32[]{:S(2)}) collective-permute-start(bf16[32,1024]{1,0:T(8,128)(2,1)S(1)} %get-tuple-element.40.rest_0_), channel_id=1, source_target_pairs={{0,2},{1,3},{2,0},{3,1},{4,6},{5,7},{6,4},{7,5},{8,10},{9,11},{10,... | collective-permute-start | bytes 196616 | tf_op jit(solution)/shard_map/ppermute | solution.py:239
  12.7 11.8 %collective-permute-start.3 = (bf16[32,1024]{1,0:T(8,128)(2,1)S(1)}, bf16[32,1024]{1,0:T(8,128)(2,1)S(1)}, u32[]{:S(2)}, u32[]{:S(2)}) collective-permute-start(bf16[32,1024]{1,0:T(8,128)(2,1)S(1)} %get-tuple-element.40.rest_0_), channel_id=1, source_target_pairs={{0,1},{1,0},{2,3},{3,2},{4,5},{5,4},{6,7},{7,6},{8,9},{9,8},{10,11... | collective-permute-start | bytes 196616 | tf_op jit(solution)/shard_map/ppermute | solution.py:239
  15.5 6.2 %collective-permute-start.11 = (bf16[128,128]{1,0:T(8,128)(2,1)S(1)}, bf16[128,128]{1,0:T(8,128)(2,1)S(1)}, u32[]{:S(2)}, u32[]{:S(2)}) collective-permute-start(bf16[128,128]{1,0:T(8,128)(2,1)S(1)} %get-tuple-element.38.group_ref.rest_4_), channel_id=1, source_target_pairs={{0,24},{4,28},{8,16},{12,20},{16,8},{20,12},{24,0},{28,4},{1,25},{... | collective-permute-start | bytes 98312 | tf_op jit(solution)/shard_map/ppermute | solution.py:239
  19.2 4.8 %collective-permute-start.9 = (bf16[128,128]{1,0:T(8,128)(2,1)S(1)}, bf16[128,128]{1,0:T(8,128)(2,1)S(1)}, u32[]{:S(2)}, u32[]{:S(2)}) collective-permute-start(bf16[128,128]{1,0:T(8,128)(2,1)S(1)} %get-tuple-element.38.group_ref.rest_4_), channel_id=1, source_target_pairs={{0,16},{4,20},{8,24},{12,28},{16,0},{20,4},{24,8},{28,12},{1,17},{... | collective-permute-start | bytes 98312 | tf_op jit(solution)/shard_map/ppermute | solution.py:239
  19.2 4.8 %collective-permute-start.7 = (bf16[128,128]{1,0:T(8,128)(2,1)S(1)}, bf16[128,128]{1,0:T(8,128)(2,1)S(1)}, u32[]{:S(2)}, u32[]{:S(2)}) collective-permute-start(bf16[128,128]{1,0:T(8,128)(2,1)S(1)} %get-tuple-element.38.group_ref.rest_4_), channel_id=1, source_target_pairs={{0,8},{4,12},{8,0},{12,4},{16,24},{20,28},{24,16},{28,20},{1,9},{5... | collective-permute-start | bytes 98312 | tf_op jit(solution)/shard_map/ppermute | solution.py:239
  21.2 3.4 %collective-permute-start.6 = (bf16[128,128]{1,0:T(8,128)(2,1)S(1)}, bf16[128,128]{1,0:T(8,128)(2,1)S(1)}, u32[]{:S(2)}, u32[]{:S(2)}) collective-permute-start(bf16[128,128]{1,0:T(8,128)(2,1)S(1)} %get-tuple-element.42), channel_id=1, source_target_pairs={{0,4},{4,0},{8,12},{12,8},{16,20},{20,16},{24,28},{28,24},{1,5},{5... | collective-permute-start | bytes 98312 | tf_op jit(solution)/shard_map/ppermute | solution.py:239
  21.6 3.0 %collective-permute-start.12 = (bf16[128,128]{1,0:T(8,128)(2,1)S(1)}, bf16[128,128]{1,0:T(8,128)(2,1)S(1)}, u32[]{:S(2)}, u32[]{:S(2)}) collective-permute-start(bf16[128,128]{1,0:T(8,128)(2,1)S(1)} %collective-permute-done.11.rest_10_), channel_id=1, source_target_pairs={{0,4},{4,0},{8,12},{12,8},{16,20},{20,16},{24,28},{28,24},{1,5},{5... | collective-permute-start | bytes 98312 | tf_op jit(solution)/shard_map/ppermute | solution.py:239
  24.0 1.2 %collective-permute-start.10 = (bf16[128,128]{1,0:T(8,128)(2,1)S(1)}, bf16[128,128]{1,0:T(8,128)(2,1)S(1)}, u32[]{:S(2)}, u32[]{:S(2)}) collective-permute-start(bf16[128,128]{1,0:T(8,128)(2,1)S(1)} %collective-permute-done.9.rest_8_), channel_id=1, source_target_pairs={{0,4},{4,0},{8,12},{12,8},{16,20},{20,16},{24,28},{28,24},{1,5},{5... | collective-permute-start | bytes 98312 | tf_op jit(solution)/shard_map/ppermute | solution.py:239
  24.0 1.4 %collective-permute-start.8 = (bf16[128,128]{1,0:T(8,128)(2,1)S(1)}, bf16[128,128]{1,0:T(8,128)(2,1)S(1)}, u32[]{:S(2)}, u32[]{:S(2)}) collective-permute-start(bf16[128,128]{1,0:T(8,128)(2,1)S(1)} %collective-permute-done.7.rest_6_), channel_id=1, source_target_pairs={{0,4},{4,0},{8,12},{12,8},{16,20},{20,16},{24,28},{28,24},{1,5},{5... | collective-permute-start | bytes 98312 | tf_op jit(solution)/shard_map/ppermute | solution.py:239
  25.8 5.9 %collective-permute-start.13 = (bf16[128,128]{1,0:T(8,128)(2,1)S(1)}, bf16[128,128]{1,0:T(8,128)(2,1)S(1)}, u32[]{:S(2)}, u32[]{:S(2)}) collective-permute-start(bf16[128,128]{1,0:T(8,128)(2,1)S(1)} %get-tuple-element.46), channel_id=1, source_target_pairs={{0,1},{1,0},{2,3},{3,2},{4,5},{5,4},{6,7},{7,6},{8,9},{9,8},{10,11... | collective-permute-start | bytes 98312 | tf_op jit(solution)/shard_map/ppermute | solution.py:239
  27.3 4.4 %collective-permute-start.14 = (bf16[128,128]{1,0:T(8,128)(2,1)S(1)}, bf16[128,128]{1,0:T(8,128)(2,1)S(1)}, u32[]{:S(2)}, u32[]{:S(2)}) collective-permute-start(bf16[128,128]{1,0:T(8,128)(2,1)S(1)} %get-tuple-element.47), channel_id=1, source_target_pairs={{0,2},{1,3},{2,0},{3,1},{4,6},{5,7},{6,4},{7,5},{8,10},{9,11},{10,... | collective-permute-start | bytes 98312 | tf_op jit(solution)/shard_map/ppermute | solution.py:239
  28.3 4.8 %collective-permute-start.15 = (bf16[128,128]{1,0:T(8,128)(2,1)S(1)}, bf16[128,128]{1,0:T(8,128)(2,1)S(1)}, u32[]{:S(2)}, u32[]{:S(2)}) collective-permute-start(bf16[128,128]{1,0:T(8,128)(2,1)S(1)} %get-tuple-element.48), channel_id=1, source_target_pairs={{0,3},{1,2},{2,1},{3,0},{4,7},{5,6},{6,5},{7,4},{8,11},{9,10},{10,... | collective-permute-start | bytes 98312 | tf_op jit(solution)/shard_map/ppermute | solution.py:239

commit v7 on v6

--- a/solution.py
+++ b/solution.py
@@ -65,55 +65,47 @@
 PIECES = 4
 
 
-def front_kernel(
-    n, order_hbm, skel_hbm, sides_hbm, inverse_hbm, basis_hbm, core_hbm, transfer_hbm, top_hbm, *rest
-):
+def pack_kernel(n, core_hbm, transfer_hbm, top_hbm, *rest):
     messages, own_ref = rest[: n - 1], rest[n - 1]
-    sides_ref, inverse_ref, gather_ref, pair_ref, top_ref, order_ref = rest[n : n + 6]
-    skel_ref, basis_ref, core_ref, transfer_ref, coeffs, sems = rest[n + 6 :]
+    core_ref, transfer_ref, top_ref, sems = rest[n:]
+    me = lax.axis_index("ba")
+    rank = transfer_ref.shape[0]
+    for copy in fetch([(core_hbm, core_ref), (transfer_hbm, transfer_ref), (top_hbm, top_ref)], sems):
+        copy.wait()
+    transfer = transfer_ref[...].astype(BF)
+    groups = top_ref.shape[1] // rank
+    top = top_ref[...].astype(F32)
+    top = jnp.concatenate([top[:, g * rank : (g + 1) * rank] for g in range(groups)], axis=0).astype(BF)
+    for k in range(n):
+        out = own_ref if k == 0 else messages[k - 1]
+        out[0:rank, :] = transfer
+        at = rank
+        for m in range(n) if k == 0 else [0] + [k ^ m for m in partners(n, k)]:
+            out[at : at + rank, :] = core_ref[:, pl.ds(pl.multiple_of((me ^ m) * rank, rank), rank)]
+            at += rank
+        out[at:, :] = top
+
+
+def front_kernel(n, order_ref, skel_ref, sides_ref, inverse_ref, basis_ref, after, *rest):
+    del after
+    outs, (gather_ref, pair_ref, coeffs) = rest[:n], rest[n:]
     me = lax.axis_index("ba")
     points, rank = basis_ref.shape
-    rows = points // PIECES
-    copies = fetch(
-        [(skel_hbm, skel_ref), (basis_hbm, basis_ref), (order_hbm, order_ref)]
-        + list(zip(pieces_of(inverse_hbm, PIECES), pieces_of(inverse_ref, PIECES)))
-        + [(sides_hbm, sides_ref), (core_hbm, core_ref), (transfer_hbm, transfer_ref), (top_hbm, top_ref)],
-        sems,
-    )
-    share = coeffs.shape[0] // n
-    for copy in copies[:3]:
-        copy.wait()
-    pair_ref[...] = basis_pair(skel_ref[...], basis_ref[...])
-    gather_ref[...] = order_columns(order_ref[...], points)
-    both = None
-    for j in range(PIECES):
-        copies[3 + j].wait()
-        at = slice(j * rows, (j + 1) * rows)
-        part = dot(pair_ref[at, :], inverse_ref[at, :], TN)
-        both = part if both is None else both + part
+    share = outs[0].shape[0]
+    pair = basis_pair(skel_ref[...], basis_ref[...])
+    both = dot(pair, inverse_ref[...], TN)
+    gather = order_columns(order_ref[...], points)
     up = (both[:rank] + both[rank:]).astype(BF)
-    up = dot(up, gather_ref[...]).astype(BF)
-    for copy in copies[3 + PIECES :]:
-        copy.wait()
+    up = dot(up, gather).astype(BF)
     coeffs[...] = dot(up, sides_ref[...]).T.astype(BF)
-    transfer = transfer_ref[...].astype(BF)
-
-    def block(m):
-        return core_ref[:, pl.ds(pl.multiple_of((me ^ m) * rank, rank), rank)]
-
-    for k in range(n):
-        out = own_ref if k == 0 else messages[k - 1]
-        out[0:share, :] = coeffs[pl.ds(pl.multiple_of((me ^ k) * share, share), share), :]
-        out[share : share + rank, :] = transfer
-        at = share + rank
-        for m in range(n) if k == 0 else [0] + [k ^ m for m in partners(n, k)]:
-            out[at : at + rank, :] = block(m)
-            at += rank
-
-
-def ordered_kernel(sides_ref, gather_ref, top_ref, ordered_ref, top_out):
+    for k in range(n):
+        outs[k][...] = coeffs[pl.ds(pl.multiple_of((me ^ k) * share, share), share), :]
+    gather_ref[...] = gather
+    pair_ref[...] = pair
+
+
+def ordered_kernel(sides_ref, gather_ref, ordered_ref):
     ordered_ref[...] = dot(gather_ref[...], sides_ref[...]).astype(BF)
-    top_out[...] = top_ref[...]
 
 
 def applied_kernel(inverse_ref, ordered_ref, group_ref, applied_ref, group_out):
@@ -131,22 +123,19 @@
     down_ref[...] = dot(placed, down).astype(BF)
 
 
-def group_kernel(n, rank, after, own_ref, *rest):
+def group_kernel(n, rank, after, *rest):
     del after
-    messages, (level_ref, group_ref) = rest[: n - 1], rest[n - 1 :]
-    share = level_ref.shape[0]
-    messages = messages[::-1]
-    coeffs = [msg[0:share, :] for msg in (own_ref,) + messages]
-    transfers = [msg[share : share + rank, :] for msg in (own_ref,) + messages]
+    pieces, messages, (level_ref, group_ref) = rest[:n][::-1], rest[n : 2 * n][::-1], rest[2 * n :]
+    coeffs = [piece[...] for piece in pieces]
+    transfers = [msg[0:rank, :] for msg in messages]
     level = [None] * n
 
     def add(k, term):
         level[k] = term if level[k] is None else level[k] + term
 
     for k in range(n):
-        msg = own_ref if k == 0 else messages[k - 1]
         which = list(range(n)) if k == 0 else [k] + partners(n, k)
-        blocks = [msg[share + rank * (j + 1) : share + rank * (j + 2), :] for j in range(len(which))]
+        blocks = [messages[k][rank * (j + 1) : rank * (j + 2), :] for j in range(len(which))]
         wide = dot(coeffs[k], jnp.concatenate(blocks, axis=1))
         for j, m in enumerate(which):
             add(m, wide[:, j * rank : (j + 1) * rank])
@@ -160,13 +149,17 @@
 
 
 def top_rows_kernel(n, groups, *rest):
-    tops, (rows_ref, held) = rest[:n], rest[n:]
+    messages, (rows_ref, held) = rest[:n], rest[n:]
     me = lax.axis_index("ba")
     mine = lax.axis_index("aa")
-    part = tops[0].shape[0]
     rank = rows_ref.shape[0]
-    for k in range(n):
-        held[pl.ds(pl.multiple_of((me ^ k) * part, part), part), :] = tops[k][...].astype(F32)
+    part = rank // n
+    for k in range(n):
+        tail = messages[k][messages[k].shape[0] - groups * part :, :].astype(F32)
+        for g in range(groups):
+            held[pl.ds(pl.multiple_of((me ^ k) * part, part), part), g * rank : (g + 1) * rank] = tail[
+                g * part : (g + 1) * part
+            ]
     for m in range(groups):
         rows_ref[:, m * rank : (m + 1) * rank] = held[
             :, pl.ds(pl.multiple_of((mine ^ m) * rank, rank), rank)
@@ -175,11 +168,10 @@
 
 def top_kernel(n, groups, rows_ref, level_ref, *rest):
     messages, pieces, outs = rest[:n], rest[n : n + groups], rest[n + groups :]
-    share = level_ref.shape[0]
     rank = rows_ref.shape[0]
     stacked = jnp.concatenate([piece[...] for piece in pieces], axis=1)
     top = dot(stacked, rows_ref[...], NT).astype(BF)
-    transfers = jnp.concatenate([msg[share : share + rank, :] for msg in messages], axis=0)
+    transfers = jnp.concatenate([msg[0:rank, :] for msg in messages], axis=0)
     correction = (level_ref[...] + dot(top, transfers, NT)).astype(BF)
     for k in range(n):
         outs[k][...] = correction[:, k * rank : (k + 1) * rank]
@@ -238,60 +230,66 @@
         size = {"aa": groups, "ba": n}[axis]
         return lax.ppermute(array, axis, [(i, i ^ k) for i in range(size)])
 
-    sizes = [share + rank * (2 + len(partners(n, k))) for k in range(1, n)] + [share + rank * (n + 1)]
-    *messages, own, sides_held, inverse_held, gather, pair, top_held, order_held = call(
+    tail = groups * top.shape[0]
+    sizes = [rank * (2 + len(partners(n, k))) + tail for k in range(1, n)] + [rank * (n + 1) + tail]
+    *messages, own = call(
+        functools.partial(pack_kernel, n),
+        [shape((size, rank)) for size in sizes],
+        [hbm] * 3,
+        scratch=[like(x) for x in (core, transfer, top)] + [pltpu.SemaphoreType.DMA((3,))],
+        flops=16 * points * points * points,
+        moved=16 * points * (points + cols + rank),
+    )(*far(core, transfer, top))
+    received = [own] + [swap(messages[k - 1], "ba", k) for k in range(1, n)]
+    *coeffs, gather, pair = call(
         functools.partial(front_kernel, n),
-        [shape((size, rank)) for size in sizes]
-        + [shape(sides.shape), shape(inverse.shape)]
-        + [shape((points, points)), shape((points, 2 * rank)), shape(top.shape), shape(order.shape, order.dtype)],
-        [hbm] * 8,
-        scratch=[like(x) for x in (skel, basis, core, transfer)]
-        + [pltpu.VMEM((cols, rank), BF), pltpu.SemaphoreType.DMA((7 + PIECES,))],
+        [shape((share, rank))] * n + [shape((points, points)), shape((points, 2 * rank))],
+        [vmem] * 5 + [unread],
+        scratch=[pltpu.VMEM((cols, rank), BF)],
         flops=2 * rank * points * (3 * points + cols),
         moved=2 * points * (points + cols + rank),
-    )(*far(order, skel, sides, inverse, basis, core, transfer, top))
-    received = [swap(messages[k - 1], "ba", k) for k in range(1, n)]
-    ordered, top_held = call(
+    )(order, skel, sides, inverse, basis, own)
+    coeffs = [coeffs[0]] + [swap(coeffs[k], "ba", k) for k in range(1, n)]
+    ordered = call(
         ordered_kernel,
-        [shape((points, cols)), shape(top.shape)],
-        [vmem] * 3,
+        shape((points, cols)),
+        [vmem] * 2,
         flops=2 * points * points * cols,
         moved=2 * points * (points + 2 * cols),
-    )(sides_held, gather, top_held)
-    tops = [top_held] + [swap(top_held, "ba", k) for k in range(1, n)]
+    )(sides, gather)
+    rows = call(
+        functools.partial(top_rows_kernel, n, groups),
+        shape((rank, groups * rank)),
+        [vmem] * n,
+        scratch=[pltpu.VMEM((rank, groups * rank), F32)],
+        moved=4 * rank * groups * rank,
+    )(*received)
     level, group = call(
         functools.partial(group_kernel, n, rank),
         [shape((share, n * rank), F32), shape((share, rank))],
-        [unread] + [vmem] * n,
+        [unread] + [vmem] * (2 * n),
         flops=2 * share * n * rank * (n + 1) * rank,
         moved=4 * share * n * rank,
-    )(ordered, own, *received[::-1])
+    )(ordered, *coeffs[::-1], *received[::-1])
     applied, group_held = call(
         applied_kernel,
         [shape((points, cols)), shape((share, rank))],
         [vmem] * 3,
         flops=2 * points * points * cols,
         moved=2 * points * (points + 2 * cols),
-    )(inverse_held, ordered, group)
+    )(inverse, ordered, group)
     pieces = {0: group}
     for m in range(2, groups, 2):
         pieces[m] = swap(group, "aa", m)
     for m in range(0, groups, 2):
         pieces[m + 1] = swap(pieces[m] if m else group_held, "aa", 1)
-    rows = call(
-        functools.partial(top_rows_kernel, n, groups),
-        shape((rank, groups * rank)),
-        [vmem] * n,
-        scratch=[pltpu.VMEM((rank, groups * rank), F32)],
-        moved=4 * rank * groups * rank,
-    )(*tops)
     corrections = call(
         functools.partial(top_kernel, n, groups),
         [shape((share, rank))] * n,
         [vmem] * (2 + n + groups),
         flops=2 * share * rank * (groups + n) * rank,
         moved=4 * share * n * rank,
-    )(rows, level, own, *received, *[pieces[m] for m in range(groups)])
+    )(rows, level, *received, *[pieces[m] for m in range(groups)])
     back = [corrections[0]] + [swap(corrections[k], "ba", k) for k in range(1, n)]
     applied, down = call(
         down_kernel,
@@ -299,7 +297,7 @@
         [vmem] * 4 + [unread],
         flops=2 * points * points * (3 * rank + cols),
         moved=2 * points * (points + 2 * cols),
-    )(inverse_held, order_held, pair, applied, corrections[0])
+    )(inverse, order, pair, applied, corrections[0])
     return call(
         functools.partial(final_kernel, n),
         shape((points, cols)),

time: 34.5 us -> 37.7 us (1.093)
  waiting for transfers between devices: 6.14 us -> 8.65 us
  starting transfers between devices: 17.8 us -> 18.8 us
  Pallas kernels: 10.4 us -> 9.89 us
    ppermute x16, waiting for transfers between devices: 6.14 us -> 8.65 us  [swap(): return lax.ppermute(array, axis, [(i, i ^ k) for i in range(size)])]
    ppermute x16, starting transfers between devices: 17.8 us -> 18.8 us  [swap(): return lax.ppermute(array, axis, [(i, i ^ k) for i in range(size)])]
    pallas_call x2 -> x3, Pallas kernels: 4.6 us -> 4.11 us  [the longest x1 1.68 us: shards(): call(functools.partial(front_kernel, n), [shape((share, rank))] * n + [sh...]
  transfers between devices with their start and end apart: 16 -> 16, of which waited for: 7 -> 6; matrix products, arithmetic and copies ran while one was open for 0% -> 0% of each run, Pallas kernels for 16% -> 18%
where the time goes in v7:
time: 37.7 us; the launch traced here: 37.5 us
  starting transfers between devices  18.8 us (50%)
  Pallas kernels  9.89 us (26%)
  waiting for transfers between devices  8.65 us (23%)
    ppermute x16, starting transfers between devices, swap(): return lax.ppermute(array, axis, [(i, i ^ k) for i in range(size)])  18.8 us
    ppermute x16, waiting for transfers between devices, swap(): return lax.ppermute(array, axis, [(i, i ^ k) for i in range(size)])  8.65 us
    pallas_call x1, Pallas kernels, shards(): call(down_kernel, [shape((points, cols)), shape((points, rank))], [vmem]...  2.32 us
    pallas_call x1, Pallas kernels, shards(): call(functools.partial(front_kernel, n), [shape((share, rank))] * n + [sh...  1.68 us
    pallas_call x1, Pallas kernels, shards(): call(applied_kernel, [shape((points, cols)), shape((share, rank))], [vmem...  1.24 us
    pallas_call x1, Pallas kernels, shards(): call(functools.partial(final_kernel, n), shape((points, cols)), [vmem] *...  1.24 us
    pallas_call x1, Pallas kernels, shards(): call(ordered_kernel, shape((points, cols)), [vmem] * 2, flops=2 * points...  1.24 us
    pallas_call x1, Pallas kernels, shards(): call(functools.partial(pack_kernel, n), [shape((size, rank)) for size in...  1.2 us
  transfers between devices with their start and end apart: 16, of which 6 were waited for; matrix products, arithmetic and copies ran while one was open for 0% of the time, Pallas kernels for 18%

profile of v7, /device:TPU:0, one launch (start us, length us, event | category | flops | bytes accessed | tf_op | source)
XLA Modules:
  0.0 37.5 jit_solution(1226638124611320221)
XLA Ops:
  0.0 0.0 copy-start.4
  0.0 0.0 copy-start.1
  0.0 1.2 %shard_map.82 = (bf16[640,128]{1,0:T(8,128)(2,1)S(1)}, bf16[640,128]{1,0:T(8,128)(2,1)S(1)}, bf16[640,128]{1,0:T(8,128)(2,1)S(1)}, bf16[896,128]{1,0:T(8,128)(2,1)S(1)}) custom-call(bf16[128,512]{1,0:T(8,128)(2,1)} %core_hbm.1, f32[128,128]{1,0:T(8,128)} %transfer_hbm.1, bf16[32,1024]{1,0:T(8,128)(2,1)} %top_hbm.1), custom_call_target="tpu_custom_call" | custom-call | flops 17179869184 | bytes 27262976 | tf_op jit(solution)/shard_map/pallas_call | solution.py:235
  1.2 4.0 %collective-permute-start.3 = (bf16[640,128]{1,0:T(8,128)(2,1)S(1)}, bf16[640,128]{1,0:T(8,128)(2,1)S(1)}, u32[]{:S(2)}, u32[]{:S(2)}) collective-permute-start(bf16[640,128]{1,0:T(8,128)(2,1)S(1)} %get-tuple-element.32), channel_id=1, source_target_pairs={{0,3},{1,2},{2,1},{3,0},{4,7},{5,6},{6,5},{7,4},{8,11},{9,10},{10,... | collective-permute-start | bytes 491528 | tf_op jit(solution)/shard_map/ppermute | solution.py:231
  5.2 0.5 %collective-permute-start.4 = (bf16[640,128]{1,0:T(8,128)(2,1)S(1)}, bf16[640,128]{1,0:T(8,128)(2,1)S(1)}, u32[]{:S(2)}, u32[]{:S(2)}) collective-permute-start(bf16[640,128]{1,0:T(8,128)(2,1)S(1)} %get-tuple-element.33), channel_id=1, source_target_pairs={{0,2},{1,3},{2,0},{3,1},{4,6},{5,7},{6,4},{7,5},{8,10},{9,11},{10,... | collective-permute-start | bytes 491528 | tf_op jit(solution)/shard_map/ppermute | solution.py:231
  5.7 0.1 collective-permute-start.5
  5.8 0.0 copy-done.4
  5.8 0.0 copy-done.1
  5.8 0.0 copy-done.2
  5.8 0.0 copy-done
  5.9 0.0 copy-done.3
  5.9 1.7 %shard_map.83 = (bf16[128,128]{1,0:T(8,128)(2,1)S(1)}, bf16[128,128]{1,0:T(8,128)(2,1)S(1)}, bf16[128,128]{1,0:T(8,128)(2,1)S(1)}, bf16[128,128]{1,0:T(8,128)(2,...) custom-call(s32[1,1024]{1,0:T(1,128)S(1)} %copy-done.3, s32[1,128]{1,0:T(1,128)S(1)} %copy-done.4, ...), custom_call_target="tpu_custom_call" | custom-call | flops 939524096 | bytes 3407872 | tf_op jit(solution)/shard_map/pallas_call | solution.py:244
  7.5 2.9 %collective-permute-start = (bf16[128,128]{1,0:T(8,128)(2,1)S(1)}, bf16[128,128]{1,0:T(8,128)(2,1)S(1)}, u32[]{:S(2)}, u32[]{:S(2)}) collective-permute-start(bf16[128,128]{1,0:T(8,128)(2,1)S(1)} %get-tuple-element.28), channel_id=1, source_target_pairs={{0,3},{1,2},{2,1},{3,0},{4,7},{5,6},{6,5},{7,4},{8,11},{9,10},{10,... | collective-permute-start | bytes 98312 | tf_op jit(solution)/shard_map/ppermute | solution.py:231
  10.5 0.5 %collective-permute-start.1 = (bf16[128,128]{1,0:T(8,128)(2,1)S(1)}, bf16[128,128]{1,0:T(8,128)(2,1)S(1)}, u32[]{:S(2)}, u32[]{:S(2)}) collective-permute-start(bf16[128,128]{1,0:T(8,128)(2,1)S(1)} %get-tuple-element.29), channel_id=1, source_target_pairs={{0,2},{1,3},{2,0},{3,1},{4,6},{5,7},{6,4},{7,5},{8,10},{9,11},{10,... | collective-permute-start | bytes 98312 | tf_op jit(solution)/shard_map/ppermute | solution.py:231
  11.0 2.7 %collective-permute-done.rest_0_ = bf16[128,128]{1,0:T(8,128)(2,1)S(1)} collective-permute-done((bf16[128,128]{1,0:T(8,128)(2,1)S(1)}, bf16[128,128]{1,0:T(8,128)(2,1)S(1)}, u32[]{:S(2)}, u32[]{:S(2)}) %collective-permute-start) | collective-permute-done | bytes 32800 | tf_op jit(solution)/shard_map/ppermute | solution.py:231
  13.7 1.7 %collective-permute-start.2 = (bf16[128,128]{1,0:T(8,128)(2,1)S(1)}, bf16[128,128]{1,0:T(8,128)(2,1)S(1)}, u32[]{:S(2)}, u32[]{:S(2)}) collective-permute-start(bf16[128,128]{1,0:T(8,128)(2,1)S(1)} %get-tuple-element.30), channel_id=1, source_target_pairs={{0,1},{1,0},{2,3},{3,2},{4,5},{5,4},{6,7},{7,6},{8,9},{9,8},{10,11... | collective-permute-start | bytes 98312 | tf_op jit(solution)/shard_map/ppermute | solution.py:231
  15.4 1.2 %shard_map.84.after.ordered_ref = bf16[1024,512]{1,0:T(8,128)(2,1)S(1)} custom-call(bf16[1024,512]{1,0:T(8,128)(2,1)S(1)} %copy-done, bf16[1024,1024]{1,0:T(8,128)(2,1)S(1)} %get-tuple-element.27.gather_ref), custom_call_target="tpu_custom_call" | custom-call | flops 1073741824 | bytes 4194304 | tf_op jit(solution)/shard_map/pallas_call | solution.py:253
  16.7 0.0 collective-permute-done.1.rest_1_
  16.7 0.9 %collective-permute-done.2.rest_2_ = bf16[128,128]{1,0:T(8,128)(2,1)S(1)} collective-permute-done((bf16[128,128]{1,0:T(8,128)(2,1)S(1)}, bf16[128,128]{1,0:T(8,128)(2,1)S(1)}, u32[]{:S(2)}, u32[]{:S(2)}) %collective-permute-start.2) | collective-permute-done | bytes 32800 | tf_op jit(solution)/shard_map/ppermute | solution.py:231
  17.6 0.0 collective-permute-done.3.rest_4_.rest_3_
  17.6 0.0 collective-permute-done.4.rest_5_.rest_2_
  17.6 0.0 collective-permute-done.5.rest_6_.rest_1_
  17.6 0.4 %shard_map.85 = (f32[128,512]{1,0:T(8,128)S(1)}, bf16[128,128]{1,0:T(8,128)(2,1)S(1)}) custom-call(bf16[1024,512]{1,0:T(8,128)(2,1)S(1)} %shard_map.84.after.ordered_ref, bf16[128,128]{1,0:T(8,128)(2,1)S(1)} %collective-permute-done.rest_0_, bf16[128,128]{1,0:T(8,128)(2,1)S(1)} %collective-permute-done.1.rest_1_, ...), custom_call_target="tpu_custom_call" | custom-call | flops 83886080 | bytes 262144 | tf_op jit(solution)/shard_map/pallas_call | solution.py:267
  18.1 2.9 %collective-permute-start.9 = (bf16[128,128]{1,0:T(8,128)(2,1)S(1)}, bf16[128,128]{1,0:T(8,128)(2,1)S(1)}, u32[]{:S(2)}, u32[]{:S(2)}) collective-permute-start(bf16[128,128]{1,0:T(8,128)(2,1)S(1)} %get-tuple-element.35.group_ref.rest_4_), channel_id=1, source_target_pairs={{0,16},{4,20},{8,24},{12,28},{16,0},{20,4},{24,8},{28,12},{1,17},{... | collective-permute-start | bytes 98312 | tf_op jit(solution)/shard_map/ppermute | solution.py:231
  20.9 1.3 %collective-permute-start.11 = (bf16[128,128]{1,0:T(8,128)(2,1)S(1)}, bf16[128,128]{1,0:T(8,128)(2,1)S(1)}, u32[]{:S(2)}, u32[]{:S(2)}) collective-permute-start(bf16[128,128]{1,0:T(8,128)(2,1)S(1)} %get-tuple-element.35.group_ref.rest_4_), channel_id=1, source_target_pairs={{0,24},{4,28},{8,16},{12,20},{16,8},{20,12},{24,0},{28,4},{1,25},{... | collective-permute-start | bytes 98312 | tf_op jit(solution)/shard_map/ppermute | solution.py:231
  22.3 0.2 collective-permute-start.7
  22.5 1.2 %shard_map.86 = (bf16[1024,512]{1,0:T(8,128)(2,1)S(1)}, bf16[128,128]{1,0:T(8,128)(2,1)S(1)}) custom-call(bf16[1024,1024]{1,0:T(8,128)(2,1)S(1)} %copy-done.1, bf16[1024,512]{1,0:T(8,128)(2,1)S(1)} %shard_map.84.after.ordered_ref, bf16[128,128]{1,0:T(8,128)(2,1)S(1)} %get-tuple-element.35.group_ref.rest_4_), custom_call_target="tpu_custom_call" | custom-call | flops 1073741824 | bytes 4194304 | tf_op jit(solution)/shard_map/pallas_call | solution.py:274
  23.8 0.1 collective-permute-start.6
  23.8 0.0 collective-permute-done.9.rest_8_
  23.9 0.5 %collective-permute-start.10 = (bf16[128,128]{1,0:T(8,128)(2,1)S(1)}, bf16[128,128]{1,0:T(8,128)(2,1)S(1)}, u32[]{:S(2)}, u32[]{:S(2)}) collective-permute-start(bf16[128,128]{1,0:T(8,128)(2,1)S(1)} %collective-permute-done.9.rest_8_), channel_id=1, source_target_pairs={{0,4},{4,0},{8,12},{12,8},{16,20},{20,16},{24,28},{28,24},{1,5},{5... | collective-permute-start | bytes 98312 | tf_op jit(solution)/shard_map/ppermute | solution.py:231
  24.3 2.3 %collective-permute-done.11.rest_10_ = bf16[128,128]{1,0:T(8,128)(2,1)S(1)} collective-permute-done((bf16[128,128]{1,0:T(8,128)(2,1)S(1)}, bf16[128,128]{1,0:T(8,128)(2,1)S(1)}, u32[]{:S(2)}, u32[]{:S(2)}) %collective-permute-start.11) | collective-permute-done | bytes 32800 | tf_op jit(solution)/shard_map/ppermute | solution.py:231
  26.6 0.0 collective-permute-start.12
  26.7 0.0 collective-permute-done.7.rest_6_
  26.7 0.5 %collective-permute-start.8 = (bf16[128,128]{1,0:T(8,128)(2,1)S(1)}, bf16[128,128]{1,0:T(8,128)(2,1)S(1)}, u32[]{:S(2)}, u32[]{:S(2)}) collective-permute-start(bf16[128,128]{1,0:T(8,128)(2,1)S(1)} %collective-permute-done.7.rest_6_), channel_id=1, source_target_pairs={{0,4},{4,0},{8,12},{12,8},{16,20},{20,16},{24,28},{28,24},{1,5},{5... | collective-permute-start | bytes 98312 | tf_op jit(solution)/shard_map/ppermute | solution.py:231
  27.2 0.1 shard_map.87.rows_ref
  27.3 0.0 collective-permute-done.6.rest_5_
  27.3 0.0 collective-permute-done.10.rest_9_
  27.3 0.6 %collective-permute-done.12.rest_11_ = bf16[128,128]{1,0:T(8,128)(2,1)S(1)} collective-permute-done((bf16[128,128]{1,0:T(8,128)(2,1)S(1)}, bf16[128,128]{1,0:T(8,128)(2,1)S(1)}, u32[]{:S(2)}, u32[]{:S(2)}) %collective-permute-start.12) | collective-permute-done | bytes 32800 | tf_op jit(solution)/shard_map/ppermute | solution.py:231
  27.9 0.2 collective-permute-done.8.rest_7_
  28.0 0.4 %shard_map.88 = (bf16[128,128]{1,0:T(8,128)(2,1)S(1)}, bf16[128,128]{1,0:T(8,128)(2,1)S(1)}, bf16[128,128]{1,0:T(8,128)(2,1)S(1)}, bf16[128,128]{1,0:T(8,128)(2,1)S(1)}) custom-call(bf16[128,1024]{1,0:T(8,128)(2,1)S(1)} %shard_map.87.rows_ref, f32[128,512]{1,0:T(8,128)S(1)} %get-tuple-element.37.level_ref, ...), custom_call_target="tpu_custom_call" | custom-call | flops 50331648 | bytes 262144 | tf_op jit(solution)/shard_map/pallas_call | solution.py:286
  28.4 1.6 %collective-permute-start.13 = (bf16[128,128]{1,0:T(8,128)(2,1)S(1)}, bf16[128,128]{1,0:T(8,128)(2,1)S(1)}, u32[]{:S(2)}, u32[]{:S(2)}) collective-permute-start(bf16[128,128]{1,0:T(8,128)(2,1)S(1)} %get-tuple-element.42), channel_id=1, source_target_pairs={{0,1},{1,0},{2,3},{3,2},{4,5},{5,4},{6,7},{7,6},{8,9},{9,8},{10,11... | collective-permute-start | bytes 98312 | tf_op jit(solution)/shard_map/ppermute | solution.py:231
  30.0 1.4 %collective-permute-start.14 = (bf16[128,128]{1,0:T(8,128)(2,1)S(1)}, bf16[128,128]{1,0:T(8,128)(2,1)S(1)}, u32[]{:S(2)}, u32[]{:S(2)}) collective-permute-start(bf16[128,128]{1,0:T(8,128)(2,1)S(1)} %get-tuple-element.43), channel_id=1, source_target_pairs={{0,2},{1,3},{2,0},{3,1},{4,6},{5,7},{6,4},{7,5},{8,10},{9,11},{10,... | collective-permute-start | bytes 98312 | tf_op jit(solution)/shard_map/ppermute | solution.py:231
  31.5 0.5 %collective-permute-start.15 = (bf16[128,128]{1,0:T(8,128)(2,1)S(1)}, bf16[128,128]{1,0:T(8,128)(2,1)S(1)}, u32[]{:S(2)}, u32[]{:S(2)}) collective-permute-start(bf16[128,128]{1,0:T(8,128)(2,1)S(1)} %get-tuple-element.44), channel_id=1, source_target_pairs={{0,3},{1,2},{2,1},{3,0},{4,7},{5,6},{6,5},{7,4},{8,11},{9,10},{10,... | collective-permute-start | bytes 98312 | tf_op jit(solution)/shard_map/ppermute | solution.py:231
  32.0 2.3 %shard_map.89 = (bf16[1024,512]{1,0:T(8,128)(2,1)S(1)}, bf16[1024,128]{1,0:T(8,128)(2,1)S(1)}) custom-call(bf16[1024,1024]{1,0:T(8,128)(2,1)S(1)} %copy-done.1, s32[1,1024]{1,0:T(1,128)S(1)} %copy-done.3, bf16[1024,256]{1,0:T(8,128)(2,1)S(1)} %get-tuple-element.26.pair_ref, bf16[1024,512]{1,0:T(8,128)(2,1)S(1)} %get-tuple-element.36.applied_ref, ...), custom_call_target="tpu_custom_call" | custom-call | flops 1879048192 | bytes 4194304 | tf_op jit(solution)/shard_map/pallas_call | solution.py:294
  34.3 0.0 collective-permute-done.13.rest_1_
  34.3 0.0 collective-permute-done.14.rest_2_
  34.4 1.9 %collective-permute-done.15.rest_3_ = bf16[128,128]{1,0:T(8,128)(2,1)S(1)} collective-permute-done((bf16[128,128]{1,0:T(8,128)(2,1)S(1)}, bf16[128,128]{1,0:T(8,128)(2,1)S(1)}, u32[]{:S(2)}, u32[]{:S(2)}) %collective-permute-start.15) | collective-permute-done | bytes 32800 | tf_op jit(solution)/shard_map/ppermute | solution.py:231
  36.3 1.2 %shard_map.90 = bf16[1024,512]{1,0:T(8,128)(2,1)} custom-call(bf16[1024,512]{1,0:T(8,128)(2,1)S(1)} %get-tuple-element.40.applied_ref, bf16[1024,128]{1,0:T(8,128)(2,1)S(1)} %get-tuple-element.41.down_ref, bf16[128,128]{1,0:T(8,128)(2,1)S(1)} %get-tuple-element.39.after.rest_0_, bf16[128,128]{1,0:T(8,128)(2,1)S(1)} %collective-permute-done.13.rest_1_, ...), custom_call_target="tpu_custom_call" | custom-call | flops 134217728 | bytes 2097152 | tf_op jit(solution)/shard_map/pallas_call | solution.py:301
  (3 shorter events, 0.0 us)
Async XLA Ops:
  0.0 5.8 %copy-start.4 = (s32[1,128]{1,0:T(1,128)S(1)}, s32[1,128]{1,0:T(1,128)}, u32[]{:S(2)}) copy-start(s32[1,128]{1,0:T(1,128)} %skel_ref.1) | copy-start | bytes 1540
  0.0 5.8 %copy-start.1 = (bf16[1024,1024]{1,0:T(8,128)(2,1)S(1)}, bf16[1024,1024]{1,0:T(8,128)(2,1)}, u32[]{:S(2)}) copy-start(bf16[1024,1024]{1,0:T(8,128)(2,1)} %inverse_ref.5) | copy-start | bytes 6291460
  0.0 5.8 %copy-start.2 = (bf16[1024,128]{1,0:T(8,128)(2,1)S(1)}, bf16[1024,128]{1,0:T(8,128)(2,1)}, u32[]{:S(2)}) copy-start(bf16[1024,128]{1,0:T(8,128)(2,1)} %basis_ref.1) | copy-start | bytes 786436
  0.0 5.8 %copy-start = (bf16[1024,512]{1,0:T(8,128)(2,1)S(1)}, bf16[1024,512]{1,0:T(8,128)(2,1)}, u32[]{:S(2)}) copy-start(bf16[1024,512]{1,0:T(8,128)(2,1)} %sides_ref.3) | copy-start | bytes 3145732
  0.0 5.8 %copy-start.3 = (s32[1,1024]{1,0:T(1,128)S(1)}, s32[1,1024]{1,0:T(1,128)}, u32[]{:S(2)}) copy-start(s32[1,1024]{1,0:T(1,128)} %order_ref.3) | copy-start | bytes 12292
  1.2 16.4 %collective-permute-start.3 = (bf16[640,128]{1,0:T(8,128)(2,1)S(1)}, bf16[640,128]{1,0:T(8,128)(2,1)S(1)}, u32[]{:S(2)}, u32[]{:S(2)}) collective-permute-start(bf16[640,128]{1,0:T(8,128)(2,1)S(1)} %get-tuple-element.32), channel_id=1, source_target_pairs={{0,3},{1,2},{2,1},{3,0},{4,7},{5,6},{6,5},{7,4},{8,11},{9,10},{10,... | collective-permute-start | bytes 491528 | tf_op jit(solution)/shard_map/ppermute | solution.py:231
  5.2 12.4 %collective-permute-start.4 = (bf16[640,128]{1,0:T(8,128)(2,1)S(1)}, bf16[640,128]{1,0:T(8,128)(2,1)S(1)}, u32[]{:S(2)}, u32[]{:S(2)}) collective-permute-start(bf16[640,128]{1,0:T(8,128)(2,1)S(1)} %get-tuple-element.33), channel_id=1, source_target_pairs={{0,2},{1,3},{2,0},{3,1},{4,6},{5,7},{6,4},{7,5},{8,10},{9,11},{10,... | collective-permute-start | bytes 491528 | tf_op jit(solution)/shard_map/ppermute | solution.py:231
  5.7 11.9 %collective-permute-start.5 = (bf16[640,128]{1,0:T(8,128)(2,1)S(1)}, bf16[640,128]{1,0:T(8,128)(2,1)S(1)}, u32[]{:S(2)}, u32[]{:S(2)}) collective-permute-start(bf16[640,128]{1,0:T(8,128)(2,1)S(1)} %get-tuple-element.34), channel_id=1, source_target_pairs={{0,1},{1,0},{2,3},{3,2},{4,5},{5,4},{6,7},{7,6},{8,9},{9,8},{10,11... | collective-permute-start | bytes 491528 | tf_op jit(solution)/shard_map/ppermute | solution.py:231
  7.5 6.2 %collective-permute-start = (bf16[128,128]{1,0:T(8,128)(2,1)S(1)}, bf16[128,128]{1,0:T(8,128)(2,1)S(1)}, u32[]{:S(2)}, u32[]{:S(2)}) collective-permute-start(bf16[128,128]{1,0:T(8,128)(2,1)S(1)} %get-tuple-element.28), channel_id=1, source_target_pairs={{0,3},{1,2},{2,1},{3,0},{4,7},{5,6},{6,5},{7,4},{8,11},{9,10},{10,... | collective-permute-start | bytes 98312 | tf_op jit(solution)/shard_map/ppermute | solution.py:231
  10.5 6.2 %collective-permute-start.1 = (bf16[128,128]{1,0:T(8,128)(2,1)S(1)}, bf16[128,128]{1,0:T(8,128)(2,1)S(1)}, u32[]{:S(2)}, u32[]{:S(2)}) collective-permute-start(bf16[128,128]{1,0:T(8,128)(2,1)S(1)} %get-tuple-element.29), channel_id=1, source_target_pairs={{0,2},{1,3},{2,0},{3,1},{4,6},{5,7},{6,4},{7,5},{8,10},{9,11},{10,... | collective-permute-start | bytes 98312 | tf_op jit(solution)/shard_map/ppermute | solution.py:231
  13.7 3.9 %collective-permute-start.2 = (bf16[128,128]{1,0:T(8,128)(2,1)S(1)}, bf16[128,128]{1,0:T(8,128)(2,1)S(1)}, u32[]{:S(2)}, u32[]{:S(2)}) collective-permute-start(bf16[128,128]{1,0:T(8,128)(2,1)S(1)} %get-tuple-element.30), channel_id=1, source_target_pairs={{0,1},{1,0},{2,3},{3,2},{4,5},{5,4},{6,7},{7,6},{8,9},{9,8},{10,11... | collective-permute-start | bytes 98312 | tf_op jit(solution)/shard_map/ppermute | solution.py:231
  18.1 5.8 %collective-permute-start.9 = (bf16[128,128]{1,0:T(8,128)(2,1)S(1)}, bf16[128,128]{1,0:T(8,128)(2,1)S(1)}, u32[]{:S(2)}, u32[]{:S(2)}) collective-permute-start(bf16[128,128]{1,0:T(8,128)(2,1)S(1)} %get-tuple-element.35.group_ref.rest_4_), channel_id=1, source_target_pairs={{0,16},{4,20},{8,24},{12,28},{16,0},{20,4},{24,8},{28,12},{1,17},{... | collective-permute-start | bytes 98312 | tf_op jit(solution)/shard_map/ppermute | solution.py:231
  20.9 5.7 %collective-permute-start.11 = (bf16[128,128]{1,0:T(8,128)(2,1)S(1)}, bf16[128,128]{1,0:T(8,128)(2,1)S(1)}, u32[]{:S(2)}, u32[]{:S(2)}) collective-permute-start(bf16[128,128]{1,0:T(8,128)(2,1)S(1)} %get-tuple-element.35.group_ref.rest_4_), channel_id=1, source_target_pairs={{0,24},{4,28},{8,16},{12,20},{16,8},{20,12},{24,0},{28,4},{1,25},{... | collective-permute-start | bytes 98312 | tf_op jit(solution)/shard_map/ppermute | solution.py:231
  22.3 4.4 %collective-permute-start.7 = (bf16[128,128]{1,0:T(8,128)(2,1)S(1)}, bf16[128,128]{1,0:T(8,128)(2,1)S(1)}, u32[]{:S(2)}, u32[]{:S(2)}) collective-permute-start(bf16[128,128]{1,0:T(8,128)(2,1)S(1)} %get-tuple-element.35.group_ref.rest_4_), channel_id=1, source_target_pairs={{0,8},{4,12},{8,0},{12,4},{16,24},{20,28},{24,16},{28,20},{1,9},{5... | collective-permute-start | bytes 98312 | tf_op jit(solution)/shard_map/ppermute | solution.py:231
  23.8 3.5 %collective-permute-start.6 = (bf16[128,128]{1,0:T(8,128)(2,1)S(1)}, bf16[128,128]{1,0:T(8,128)(2,1)S(1)}, u32[]{:S(2)}, u32[]{:S(2)}) collective-permute-start(bf16[128,128]{1,0:T(8,128)(2,1)S(1)} %get-tuple-element.38), channel_id=1, source_target_pairs={{0,4},{4,0},{8,12},{12,8},{16,20},{20,16},{24,28},{28,24},{1,5},{5... | collective-permute-start | bytes 98312 | tf_op jit(solution)/shard_map/ppermute | solution.py:231
  23.9 3.4 %collective-permute-start.10 = (bf16[128,128]{1,0:T(8,128)(2,1)S(1)}, bf16[128,128]{1,0:T(8,128)(2,1)S(1)}, u32[]{:S(2)}, u32[]{:S(2)}) collective-permute-start(bf16[128,128]{1,0:T(8,128)(2,1)S(1)} %collective-permute-done.9.rest_8_), channel_id=1, source_target_pairs={{0,4},{4,0},{8,12},{12,8},{16,20},{20,16},{24,28},{28,24},{1,5},{5... | collective-permute-start | bytes 98312 | tf_op jit(solution)/shard_map/ppermute | solution.py:231
  26.6 1.2 %collective-permute-start.12 = (bf16[128,128]{1,0:T(8,128)(2,1)S(1)}, bf16[128,128]{1,0:T(8,128)(2,1)S(1)}, u32[]{:S(2)}, u32[]{:S(2)}) collective-permute-start(bf16[128,128]{1,0:T(8,128)(2,1)S(1)} %collective-permute-done.11.rest_10_), channel_id=1, source_target_pairs={{0,4},{4,0},{8,12},{12,8},{16,20},{20,16},{24,28},{28,24},{1,5},{5... | collective-permute-start | bytes 98312 | tf_op jit(solution)/shard_map/ppermute | solution.py:231
  26.7 1.4 %collective-permute-start.8 = (bf16[128,128]{1,0:T(8,128)(2,1)S(1)}, bf16[128,128]{1,0:T(8,128)(2,1)S(1)}, u32[]{:S(2)}, u32[]{:S(2)}) collective-permute-start(bf16[128,128]{1,0:T(8,128)(2,1)S(1)} %collective-permute-done.7.rest_6_), channel_id=1, source_target_pairs={{0,4},{4,0},{8,12},{12,8},{16,20},{20,16},{24,28},{28,24},{1,5},{5... | collective-permute-start | bytes 98312 | tf_op jit(solution)/shard_map/ppermute | solution.py:231
  28.4 5.9 %collective-permute-start.13 = (bf16[128,128]{1,0:T(8,128)(2,1)S(1)}, bf16[128,128]{1,0:T(8,128)(2,1)S(1)}, u32[]{:S(2)}, u32[]{:S(2)}) collective-permute-start(bf16[128,128]{1,0:T(8,128)(2,1)S(1)} %get-tuple-element.42), channel_id=1, source_target_pairs={{0,1},{1,0},{2,3},{3,2},{4,5},{5,4},{6,7},{7,6},{8,9},{9,8},{10,11... | collective-permute-start | bytes 98312 | tf_op jit(solution)/shard_map/ppermute | solution.py:231
  30.0 4.3 %collective-permute-start.14 = (bf16[128,128]{1,0:T(8,128)(2,1)S(1)}, bf16[128,128]{1,0:T(8,128)(2,1)S(1)}, u32[]{:S(2)}, u32[]{:S(2)}) collective-permute-start(bf16[128,128]{1,0:T(8,128)(2,1)S(1)} %get-tuple-element.43), channel_id=1, source_target_pairs={{0,2},{1,3},{2,0},{3,1},{4,6},{5,7},{6,4},{7,5},{8,10},{9,11},{10,... | collective-permute-start | bytes 98312 | tf_op jit(solution)/shard_map/ppermute | solution.py:231
  31.5 4.8 %collective-permute-start.15 = (bf16[128,128]{1,0:T(8,128)(2,1)S(1)}, bf16[128,128]{1,0:T(8,128)(2,1)S(1)}, u32[]{:S(2)}, u32[]{:S(2)}) collective-permute-start(bf16[128,128]{1,0:T(8,128)(2,1)S(1)} %get-tuple-element.44), channel_id=1, source_target_pairs={{0,3},{1,2},{2,1},{3,0},{4,7},{5,6},{6,5},{7,4},{8,11},{9,10},{10,... | collective-permute-start | bytes 98312 | tf_op jit(solution)/shard_map/ppermute | solution.py:231

commit v8 on v5

--- a/solution.py
+++ b/solution.py
@@ -129,7 +129,11 @@
 
 def group_kernel(n, rank, after, own_ref, *rest):
     del after
-    messages, (level_ref, group_ref) = rest[: n - 1], rest[n - 1 :]
+    messages, rest = rest[: n - 1], rest[n - 1 :]
+    passed = (len(rest) - 2) // 2
+    tops, (level_ref, group_ref), tops_out = rest[:passed], rest[passed : passed + 2], rest[passed + 2 :]
+    for top_ref, top_out in zip(tops, tops_out):
+        top_out[...] = top_ref[...]
     share = level_ref.shape[0]
     messages = messages[::-1]
     coeffs = [msg[0:share, :] for msg in (own_ref,) + messages]
@@ -254,14 +258,21 @@
         flops=4 * points * points * cols,
         moved=2 * points * (points + 2 * cols),
     )(sides_held, inverse_held, gather, top_held)
-    tops = [top_held] + [swap(top_held, "ba", k) for k in range(1, n)]
-    level, group = call(
+    direct = [1 << j for j in range(n.bit_length() - 1)]
+    tops = {k: swap(top_held, "ba", k) for k in direct} | {0: top_held}
+    level, group, *passed = call(
         functools.partial(group_kernel, n, rank),
-        [shape((share, n * rank), F32), shape((share, rank))],
-        [unread] + [vmem] * n,
+        [shape((share, n * rank), F32), shape((share, rank))] + [shape(top.shape)] * len(direct[:-1]),
+        [unread] + [vmem] * (n + len(direct[:-1])),
         flops=2 * share * n * rank * (n + 1) * rank,
         moved=4 * share * n * rank,
-    )(applied, own, *received[::-1])
+    )(applied, own, *received[::-1], *[tops[k] for k in direct[:-1]])
+    tops |= dict(zip(direct[:-1], passed))
+    for k in range(n):
+        if k not in tops:
+            high = 1 << (k.bit_length() - 1)
+            tops[k] = swap(tops[k ^ high], "ba", high)
+    tops = [tops[k] for k in range(n)]
     pieces = {0: group}
     for m in range(2, groups, 2):
         pieces[m] = swap(group, "aa", m)
@@ -272,7 +283,7 @@
         shape((rank, groups * rank)),
         [vmem] * n,
         scratch=[pltpu.VMEM((rank, groups * rank), F32)],
-        moved=4 * rank * groups * rank,
+        moved=rank,
     )(*tops)
     corrections = call(
         functools.partial(top_kernel, n, groups),

time: 34.3 us -> 35.9 us (1.047)
  starting transfers between devices: 16.7 us -> 18.2 us
    ppermute x16, starting transfers between devices: 16.7 us -> 18.2 us  [swap(): return lax.ppermute(array, axis, [(i, i ^ k) for i in range(size)])]
  transfers between devices with their start and end apart: 16 -> 16, of which waited for: 7 -> 6; matrix products, arithmetic and copies ran while one was open for 0% -> 0% of each run, Pallas kernels for 15% -> 15%
where the time goes in v8:
time: 35.9 us; the launch traced here: 35.7 us
  starting transfers between devices  18.2 us (51%)
  Pallas kernels  10.2 us (28%)
  waiting for transfers between devices  7.18 us (20%)
    ppermute x16, starting transfers between devices, swap(): return lax.ppermute(array, axis, [(i, i ^ k) for i in range(size)])  18.2 us
    ppermute x16, waiting for transfers between devices, swap(): return lax.ppermute(array, axis, [(i, i ^ k) for i in range(size)])  7.18 us
    pallas_call x1, Pallas kernels, shards(): call(functools.partial(front_kernel, n), [shape((size, rank)) for size in...  3.35 us
    pallas_call x1, Pallas kernels, shards(): call(applied_kernel, [shape((points, cols)), shape(top.shape)], [vmem] *...  2.33 us
    pallas_call x1, Pallas kernels, shards(): call(down_kernel, [shape((points, cols)), shape((points, rank))], [vmem]...  2.32 us
    pallas_call x1, Pallas kernels, shards(): call(functools.partial(final_kernel, n), shape((points, cols)), [vmem] *...  1.24 us
  transfers between devices with their start and end apart: 16, of which 6 were waited for; matrix products, arithmetic and copies ran while one was open for 0% of the time, Pallas kernels for 15%

profile of v8, /device:TPU:0, one launch (start us, length us, event | category | flops | bytes accessed | tf_op | source)
XLA Modules:
  0.0 35.7 jit_solution(11427937573896220345)
XLA Ops:
  0.0 3.4 %shard_map.82 = (bf16[512,128]{1,0:T(8,128)(2,1)S(1)}, bf16[512,128]{1,0:T(8,128)(2,1)S(1)}, bf16[512,128]{1,0:T(8,128)(2,1)S(1)}, bf16[768,128]{1,0:T(8,128)(2,...) custom-call(s32[1,1024]{1,0:T(1,128)} %order_hbm.1, ...), custom_call_target="tpu_custom_call" | custom-call | flops 939524096 | bytes 3407872 | tf_op jit(solution)/shard_map/pallas_call | solution.py:242
  3.4 4.0 %collective-permute-start = (bf16[512,128]{1,0:T(8,128)(2,1)S(1)}, bf16[512,128]{1,0:T(8,128)(2,1)S(1)}, u32[]{:S(2)}, u32[]{:S(2)}) collective-permute-start(bf16[512,128]{1,0:T(8,128)(2,1)S(1)} %get-tuple-element.35), channel_id=1, source_target_pairs={{0,3},{1,2},{2,1},{3,0},{4,7},{5,6},{6,5},{7,4},{8,11},{9,10},{10,... | collective-permute-start | bytes 393224 | tf_op jit(solution)/shard_map/ppermute | solution.py:239
  7.3 0.5 %collective-permute-start.1 = (bf16[512,128]{1,0:T(8,128)(2,1)S(1)}, bf16[512,128]{1,0:T(8,128)(2,1)S(1)}, u32[]{:S(2)}, u32[]{:S(2)}) collective-permute-start(bf16[512,128]{1,0:T(8,128)(2,1)S(1)} %get-tuple-element.36), channel_id=1, source_target_pairs={{0,2},{1,3},{2,0},{3,1},{4,6},{5,7},{6,4},{7,5},{8,10},{9,11},{10,... | collective-permute-start | bytes 393224 | tf_op jit(solution)/shard_map/ppermute | solution.py:239
  7.8 0.2 collective-permute-start.2
  8.0 2.3 %shard_map.83 = (bf16[1024,512]{1,0:T(8,128)(2,1)S(1)}, bf16[32,1024]{1,0:T(8,128)(2,1)S(1)}) custom-call(bf16[1024,512]{1,0:T(8,128)(2,1)S(1)} %get-tuple-element.29.sides_ref, bf16[1024,1024]{1,0:T(8,128)(2,1)S(1)} %get-tuple-element.26.inverse_ref, bf16[1024,1024]{1,0:T(8,128)(2,1)S(1)} %get-tuple-element.30.gather_ref, ...), custom_call_target="tpu_custom_call" | custom-call | flops 2147483648 | bytes 4194304 | tf_op jit(solution)/shard_map/pallas_call | solution.py:254
  10.3 1.9 %collective-permute-start.3 = (bf16[32,1024]{1,0:T(8,128)(2,1)S(1)}, bf16[32,1024]{1,0:T(8,128)(2,1)S(1)}, u32[]{:S(2)}, u32[]{:S(2)}) collective-permute-start(bf16[32,1024]{1,0:T(8,128)(2,1)S(1)} %get-tuple-element.33.rest_0_), channel_id=1, source_target_pairs={{0,1},{1,0},{2,3},{3,2},{4,5},{5,4},{6,7},{7,6},{8,9},{9,8},{10,11... | collective-permute-start | bytes 196616 | tf_op jit(solution)/shard_map/ppermute | solution.py:239
  12.2 1.5 %collective-permute-start.4 = (bf16[32,1024]{1,0:T(8,128)(2,1)S(1)}, bf16[32,1024]{1,0:T(8,128)(2,1)S(1)}, u32[]{:S(2)}, u32[]{:S(2)}) collective-permute-start(bf16[32,1024]{1,0:T(8,128)(2,1)S(1)} %get-tuple-element.33.rest_0_), channel_id=1, source_target_pairs={{0,2},{1,3},{2,0},{3,1},{4,6},{5,7},{6,4},{7,5},{8,10},{9,11},{10,... | collective-permute-start | bytes 196616 | tf_op jit(solution)/shard_map/ppermute | solution.py:239
  13.8 1.5 %collective-permute-done.3.rest_3_ = bf16[32,1024]{1,0:T(8,128)(2,1)S(1)} collective-permute-done((bf16[32,1024]{1,0:T(8,128)(2,1)S(1)}, bf16[32,1024]{1,0:T(8,128)(2,1)S(1)}, u32[]{:S(2)}, u32[]{:S(2)}) %collective-permute-start.3) | collective-permute-done | bytes 65568 | tf_op jit(solution)/shard_map/ppermute | solution.py:239
  15.3 0.0 collective-permute-done.rest_0_.rest_3_
  15.3 0.0 collective-permute-done.1.rest_1_.rest_2_
  15.3 0.0 collective-permute-done.2.rest_2_.rest_1_
  15.3 0.4 %shard_map.84 = (f32[128,512]{1,0:T(8,128)S(1)}, bf16[128,128]{1,0:T(8,128)(2,1)S(1)}, bf16[32,1024]{1,0:T(8,128)(2,1)S(1)}) custom-call(bf16[1024,512]{1,0:T(8,128)(2,1)S(1)} %get-tuple-element.32.after.applied_ref, bf16[768,128]{1,0:T(8,128)(2,1)S(1)} %get-tuple-element.34.own_ref.rest_0_, bf16[512,128]{1,0:T(8,128)(2,1)S(1)} %collective-permute-done.rest_0_.rest_3_, ...), custom_call_target="tpu_custom_call" | custom-call | flops 83886080 | bytes 262144 | tf_op jit(solution)/shard_map/pallas_call | solution.py:263
  15.7 3.7 %collective-permute-start.11 = (bf16[128,128]{1,0:T(8,128)(2,1)S(1)}, bf16[128,128]{1,0:T(8,128)(2,1)S(1)}, u32[]{:S(2)}, u32[]{:S(2)}) collective-permute-start(bf16[128,128]{1,0:T(8,128)(2,1)S(1)} %get-tuple-element.40.rest_4_), channel_id=1, source_target_pairs={{0,24},{4,28},{8,16},{12,20},{16,8},{20,12},{24,0},{28,4},{1,25},{... | collective-permute-start | bytes 98312 | tf_op jit(solution)/shard_map/ppermute | solution.py:239
  19.4 1.3 %collective-permute-start.5 = (bf16[32,1024]{1,0:T(8,128)(2,1)S(1)}, bf16[32,1024]{1,0:T(8,128)(2,1)S(1)}, u32[]{:S(2)}, u32[]{:S(2)}) collective-permute-start(bf16[32,1024]{1,0:T(8,128)(2,1)S(1)} %get-tuple-element.38.rest_1_), channel_id=1, source_target_pairs={{0,2},{1,3},{2,0},{3,1},{4,6},{5,7},{6,4},{7,5},{8,10},{9,11},{10,... | collective-permute-start | bytes 196616 | tf_op jit(solution)/shard_map/ppermute | solution.py:239
  20.7 0.0 collective-permute-start.9
  20.7 0.8 %collective-permute-start.7 = (bf16[128,128]{1,0:T(8,128)(2,1)S(1)}, bf16[128,128]{1,0:T(8,128)(2,1)S(1)}, u32[]{:S(2)}, u32[]{:S(2)}) collective-permute-start(bf16[128,128]{1,0:T(8,128)(2,1)S(1)} %get-tuple-element.40.rest_4_), channel_id=1, source_target_pairs={{0,8},{4,12},{8,0},{12,4},{16,24},{20,28},{24,16},{28,20},{1,9},{5... | collective-permute-start | bytes 98312 | tf_op jit(solution)/shard_map/ppermute | solution.py:239
  21.5 0.0 collective-permute-done.4.rest_2_
  21.5 0.0 collective-permute-start.6
  21.5 0.2 collective-permute-done.11.rest_10_
  21.6 0.3 collective-permute-start.12
  22.0 3.5 %collective-permute-done.9.rest_8_ = bf16[128,128]{1,0:T(8,128)(2,1)S(1)} collective-permute-done((bf16[128,128]{1,0:T(8,128)(2,1)S(1)}, bf16[128,128]{1,0:T(8,128)(2,1)S(1)}, u32[]{:S(2)}, u32[]{:S(2)}) %collective-permute-start.9) | collective-permute-done | bytes 32800 | tf_op jit(solution)/shard_map/ppermute | solution.py:239
  25.5 0.0 collective-permute-start.10
  25.5 0.0 collective-permute-done.7.rest_6_
  25.5 0.5 %collective-permute-start.8 = (bf16[128,128]{1,0:T(8,128)(2,1)S(1)}, bf16[128,128]{1,0:T(8,128)(2,1)S(1)}, u32[]{:S(2)}, u32[]{:S(2)}) collective-permute-start(bf16[128,128]{1,0:T(8,128)(2,1)S(1)} %collective-permute-done.7.rest_6_), channel_id=1, source_target_pairs={{0,4},{4,0},{8,12},{12,8},{16,20},{20,16},{24,28},{28,24},{1,5},{5... | collective-permute-start | bytes 98312 | tf_op jit(solution)/shard_map/ppermute | solution.py:239
  26.0 0.0 collective-permute-done.5.rest_3_
  26.0 0.1 shard_map.85.rows_ref
  26.1 0.0 collective-permute-done.6.rest_5_
  26.1 0.0 collective-permute-done.12.rest_11_
  26.2 0.6 %collective-permute-done.10.rest_9_ = bf16[128,128]{1,0:T(8,128)(2,1)S(1)} collective-permute-done((bf16[128,128]{1,0:T(8,128)(2,1)S(1)}, bf16[128,128]{1,0:T(8,128)(2,1)S(1)}, u32[]{:S(2)}, u32[]{:S(2)}) %collective-permute-start.10) | collective-permute-done | bytes 32800 | tf_op jit(solution)/shard_map/ppermute | solution.py:239
  26.7 0.2 collective-permute-done.8.rest_7_
  26.9 0.4 %shard_map.86 = (bf16[128,128]{1,0:T(8,128)(2,1)S(1)}, bf16[128,128]{1,0:T(8,128)(2,1)S(1)}, bf16[128,128]{1,0:T(8,128)(2,1)S(1)}, bf16[128,128]{1,0:T(8,128)(2,1)S(1)}) custom-call(bf16[128,1024]{1,0:T(8,128)(2,1)S(1)} %shard_map.85.rows_ref, f32[128,512]{1,0:T(8,128)S(1)} %get-tuple-element.39.level_ref, ...), custom_call_target="tpu_custom_call" | custom-call | flops 50331648 | bytes 262144 | tf_op jit(solution)/shard_map/pallas_call | solution.py:288
  27.3 1.6 %collective-permute-start.13 = (bf16[128,128]{1,0:T(8,128)(2,1)S(1)}, bf16[128,128]{1,0:T(8,128)(2,1)S(1)}, u32[]{:S(2)}, u32[]{:S(2)}) collective-permute-start(bf16[128,128]{1,0:T(8,128)(2,1)S(1)} %get-tuple-element.44), channel_id=1, source_target_pairs={{0,1},{1,0},{2,3},{3,2},{4,5},{5,4},{6,7},{7,6},{8,9},{9,8},{10,11... | collective-permute-start | bytes 98312 | tf_op jit(solution)/shard_map/ppermute | solution.py:239
  28.9 0.8 %collective-permute-start.14 = (bf16[128,128]{1,0:T(8,128)(2,1)S(1)}, bf16[128,128]{1,0:T(8,128)(2,1)S(1)}, u32[]{:S(2)}, u32[]{:S(2)}) collective-permute-start(bf16[128,128]{1,0:T(8,128)(2,1)S(1)} %get-tuple-element.45), channel_id=1, source_target_pairs={{0,2},{1,3},{2,0},{3,1},{4,6},{5,7},{6,4},{7,5},{8,10},{9,11},{10,... | collective-permute-start | bytes 98312 | tf_op jit(solution)/shard_map/ppermute | solution.py:239
  29.7 1.2 %collective-permute-start.15 = (bf16[128,128]{1,0:T(8,128)(2,1)S(1)}, bf16[128,128]{1,0:T(8,128)(2,1)S(1)}, u32[]{:S(2)}, u32[]{:S(2)}) collective-permute-start(bf16[128,128]{1,0:T(8,128)(2,1)S(1)} %get-tuple-element.46), channel_id=1, source_target_pairs={{0,3},{1,2},{2,1},{3,0},{4,7},{5,6},{6,5},{7,4},{8,11},{9,10},{10,... | collective-permute-start | bytes 98312 | tf_op jit(solution)/shard_map/ppermute | solution.py:239
  30.9 2.3 %shard_map.87 = (bf16[1024,512]{1,0:T(8,128)(2,1)S(1)}, bf16[1024,128]{1,0:T(8,128)(2,1)S(1)}) custom-call(bf16[1024,1024]{1,0:T(8,128)(2,1)S(1)} %get-tuple-element.26.inverse_ref, s32[1,1024]{1,0:T(1,128)S(1)} %get-tuple-element.27.order_ref, bf16[1024,256]{1,0:T(8,128)(2,1)S(1)} %get-tuple-element.28.pair_ref, ...), custom_call_target="tpu_custom_call" | custom-call | flops 1879048192 | bytes 4194304 | tf_op jit(solution)/shard_map/pallas_call | solution.py:296
  33.2 0.0 collective-permute-done.13.rest_1_
  33.2 0.0 collective-permute-done.14.rest_2_
  33.2 1.3 %collective-permute-done.15.rest_3_ = bf16[128,128]{1,0:T(8,128)(2,1)S(1)} collective-permute-done((bf16[128,128]{1,0:T(8,128)(2,1)S(1)}, bf16[128,128]{1,0:T(8,128)(2,1)S(1)}, u32[]{:S(2)}, u32[]{:S(2)}) %collective-permute-start.15) | collective-permute-done | bytes 32800 | tf_op jit(solution)/shard_map/ppermute | solution.py:239
  34.5 1.2 %shard_map.88 = bf16[1024,512]{1,0:T(8,128)(2,1)} custom-call(bf16[1024,512]{1,0:T(8,128)(2,1)S(1)} %get-tuple-element.42.applied_ref, bf16[1024,128]{1,0:T(8,128)(2,1)S(1)} %get-tuple-element.43.down_ref, bf16[128,128]{1,0:T(8,128)(2,1)S(1)} %get-tuple-element.41.after.rest_0_, bf16[128,128]{1,0:T(8,128)(2,1)S(1)} %collective-permute-done.13.rest_1_, ...), custom_call_target="tpu_custom_call" | custom-call | flops 134217728 | bytes 2097152 | tf_op jit(solution)/shard_map/pallas_call | solution.py:303
Async XLA Ops:
  3.4 11.9 %collective-permute-start = (bf16[512,128]{1,0:T(8,128)(2,1)S(1)}, bf16[512,128]{1,0:T(8,128)(2,1)S(1)}, u32[]{:S(2)}, u32[]{:S(2)}) collective-permute-start(bf16[512,128]{1,0:T(8,128)(2,1)S(1)} %get-tuple-element.35), channel_id=1, source_target_pairs={{0,3},{1,2},{2,1},{3,0},{4,7},{5,6},{6,5},{7,4},{8,11},{9,10},{10,... | collective-permute-start | bytes 393224 | tf_op jit(solution)/shard_map/ppermute | solution.py:239
  7.3 8.0 %collective-permute-start.1 = (bf16[512,128]{1,0:T(8,128)(2,1)S(1)}, bf16[512,128]{1,0:T(8,128)(2,1)S(1)}, u32[]{:S(2)}, u32[]{:S(2)}) collective-permute-start(bf16[512,128]{1,0:T(8,128)(2,1)S(1)} %get-tuple-element.36), channel_id=1, source_target_pairs={{0,2},{1,3},{2,0},{3,1},{4,6},{5,7},{6,4},{7,5},{8,10},{9,11},{10,... | collective-permute-start | bytes 393224 | tf_op jit(solution)/shard_map/ppermute | solution.py:239
  7.8 7.5 %collective-permute-start.2 = (bf16[512,128]{1,0:T(8,128)(2,1)S(1)}, bf16[512,128]{1,0:T(8,128)(2,1)S(1)}, u32[]{:S(2)}, u32[]{:S(2)}) collective-permute-start(bf16[512,128]{1,0:T(8,128)(2,1)S(1)} %get-tuple-element.37), channel_id=1, source_target_pairs={{0,1},{1,0},{2,3},{3,2},{4,5},{5,4},{6,7},{7,6},{8,9},{9,8},{10,11... | collective-permute-start | bytes 393224 | tf_op jit(solution)/shard_map/ppermute | solution.py:239
  10.3 5.0 %collective-permute-start.3 = (bf16[32,1024]{1,0:T(8,128)(2,1)S(1)}, bf16[32,1024]{1,0:T(8,128)(2,1)S(1)}, u32[]{:S(2)}, u32[]{:S(2)}) collective-permute-start(bf16[32,1024]{1,0:T(8,128)(2,1)S(1)} %get-tuple-element.33.rest_0_), channel_id=1, source_target_pairs={{0,1},{1,0},{2,3},{3,2},{4,5},{5,4},{6,7},{7,6},{8,9},{9,8},{10,11... | collective-permute-start | bytes 196616 | tf_op jit(solution)/shard_map/ppermute | solution.py:239
  12.2 9.2 %collective-permute-start.4 = (bf16[32,1024]{1,0:T(8,128)(2,1)S(1)}, bf16[32,1024]{1,0:T(8,128)(2,1)S(1)}, u32[]{:S(2)}, u32[]{:S(2)}) collective-permute-start(bf16[32,1024]{1,0:T(8,128)(2,1)S(1)} %get-tuple-element.33.rest_0_), channel_id=1, source_target_pairs={{0,2},{1,3},{2,0},{3,1},{4,6},{5,7},{6,4},{7,5},{8,10},{9,11},{10,... | collective-permute-start | bytes 196616 | tf_op jit(solution)/shard_map/ppermute | solution.py:239
  15.7 5.9 %collective-permute-start.11 = (bf16[128,128]{1,0:T(8,128)(2,1)S(1)}, bf16[128,128]{1,0:T(8,128)(2,1)S(1)}, u32[]{:S(2)}, u32[]{:S(2)}) collective-permute-start(bf16[128,128]{1,0:T(8,128)(2,1)S(1)} %get-tuple-element.40.rest_4_), channel_id=1, source_target_pairs={{0,24},{4,28},{8,16},{12,20},{16,8},{20,12},{24,0},{28,4},{1,25},{... | collective-permute-start | bytes 98312 | tf_op jit(solution)/shard_map/ppermute | solution.py:239
  19.4 6.6 %collective-permute-start.5 = (bf16[32,1024]{1,0:T(8,128)(2,1)S(1)}, bf16[32,1024]{1,0:T(8,128)(2,1)S(1)}, u32[]{:S(2)}, u32[]{:S(2)}) collective-permute-start(bf16[32,1024]{1,0:T(8,128)(2,1)S(1)} %get-tuple-element.38.rest_1_), channel_id=1, source_target_pairs={{0,2},{1,3},{2,0},{3,1},{4,6},{5,7},{6,4},{7,5},{8,10},{9,11},{10,... | collective-permute-start | bytes 196616 | tf_op jit(solution)/shard_map/ppermute | solution.py:239
  20.7 4.8 %collective-permute-start.9 = (bf16[128,128]{1,0:T(8,128)(2,1)S(1)}, bf16[128,128]{1,0:T(8,128)(2,1)S(1)}, u32[]{:S(2)}, u32[]{:S(2)}) collective-permute-start(bf16[128,128]{1,0:T(8,128)(2,1)S(1)} %get-tuple-element.40.rest_4_), channel_id=1, source_target_pairs={{0,16},{4,20},{8,24},{12,28},{16,0},{20,4},{24,8},{28,12},{1,17},{... | collective-permute-start | bytes 98312 | tf_op jit(solution)/shard_map/ppermute | solution.py:239
  20.7 4.8 %collective-permute-start.7 = (bf16[128,128]{1,0:T(8,128)(2,1)S(1)}, bf16[128,128]{1,0:T(8,128)(2,1)S(1)}, u32[]{:S(2)}, u32[]{:S(2)}) collective-permute-start(bf16[128,128]{1,0:T(8,128)(2,1)S(1)} %get-tuple-element.40.rest_4_), channel_id=1, source_target_pairs={{0,8},{4,12},{8,0},{12,4},{16,24},{20,28},{24,16},{28,20},{1,9},{5... | collective-permute-start | bytes 98312 | tf_op jit(solution)/shard_map/ppermute | solution.py:239
  21.5 4.7 %collective-permute-start.6 = (bf16[128,128]{1,0:T(8,128)(2,1)S(1)}, bf16[128,128]{1,0:T(8,128)(2,1)S(1)}, u32[]{:S(2)}, u32[]{:S(2)}) collective-permute-start(bf16[128,128]{1,0:T(8,128)(2,1)S(1)} %get-tuple-element.40.rest_4_), channel_id=1, source_target_pairs={{0,4},{4,0},{8,12},{12,8},{16,20},{20,16},{24,28},{28,24},{1,5},{5... | collective-permute-start | bytes 98312 | tf_op jit(solution)/shard_map/ppermute | solution.py:239
  21.6 4.5 %collective-permute-start.12 = (bf16[128,128]{1,0:T(8,128)(2,1)S(1)}, bf16[128,128]{1,0:T(8,128)(2,1)S(1)}, u32[]{:S(2)}, u32[]{:S(2)}) collective-permute-start(bf16[128,128]{1,0:T(8,128)(2,1)S(1)} %collective-permute-done.11.rest_10_), channel_id=1, source_target_pairs={{0,4},{4,0},{8,12},{12,8},{16,20},{20,16},{24,28},{28,24},{1,5},{5... | collective-permute-start | bytes 98312 | tf_op jit(solution)/shard_map/ppermute | solution.py:239
  25.5 1.2 %collective-permute-start.10 = (bf16[128,128]{1,0:T(8,128)(2,1)S(1)}, bf16[128,128]{1,0:T(8,128)(2,1)S(1)}, u32[]{:S(2)}, u32[]{:S(2)}) collective-permute-start(bf16[128,128]{1,0:T(8,128)(2,1)S(1)} %collective-permute-done.9.rest_8_), channel_id=1, source_target_pairs={{0,4},{4,0},{8,12},{12,8},{16,20},{20,16},{24,28},{28,24},{1,5},{5... | collective-permute-start | bytes 98312 | tf_op jit(solution)/shard_map/ppermute | solution.py:239
  25.5 1.4 %collective-permute-start.8 = (bf16[128,128]{1,0:T(8,128)(2,1)S(1)}, bf16[128,128]{1,0:T(8,128)(2,1)S(1)}, u32[]{:S(2)}, u32[]{:S(2)}) collective-permute-start(bf16[128,128]{1,0:T(8,128)(2,1)S(1)} %collective-permute-done.7.rest_6_), channel_id=1, source_target_pairs={{0,4},{4,0},{8,12},{12,8},{16,20},{20,16},{24,28},{28,24},{1,5},{5... | collective-permute-start | bytes 98312 | tf_op jit(solution)/shard_map/ppermute | solution.py:239
  27.3 5.9 %collective-permute-start.13 = (bf16[128,128]{1,0:T(8,128)(2,1)S(1)}, bf16[128,128]{1,0:T(8,128)(2,1)S(1)}, u32[]{:S(2)}, u32[]{:S(2)}) collective-permute-start(bf16[128,128]{1,0:T(8,128)(2,1)S(1)} %get-tuple-element.44), channel_id=1, source_target_pairs={{0,1},{1,0},{2,3},{3,2},{4,5},{5,4},{6,7},{7,6},{8,9},{9,8},{10,11... | collective-permute-start | bytes 98312 | tf_op jit(solution)/shard_map/ppermute | solution.py:239
  28.9 4.3 %collective-permute-start.14 = (bf16[128,128]{1,0:T(8,128)(2,1)S(1)}, bf16[128,128]{1,0:T(8,128)(2,1)S(1)}, u32[]{:S(2)}, u32[]{:S(2)}) collective-permute-start(bf16[128,128]{1,0:T(8,128)(2,1)S(1)} %get-tuple-element.45), channel_id=1, source_target_pairs={{0,2},{1,3},{2,0},{3,1},{4,6},{5,7},{6,4},{7,5},{8,10},{9,11},{10,... | collective-permute-start | bytes 98312 | tf_op jit(solution)/shard_map/ppermute | solution.py:239
  29.7 4.8 %collective-permute-start.15 = (bf16[128,128]{1,0:T(8,128)(2,1)S(1)}, bf16[128,128]{1,0:T(8,128)(2,1)S(1)}, u32[]{:S(2)}, u32[]{:S(2)}) collective-permute-start(bf16[128,128]{1,0:T(8,128)(2,1)S(1)} %get-tuple-element.46), channel_id=1, source_target_pairs={{0,3},{1,2},{2,1},{3,0},{4,7},{5,6},{6,5},{7,4},{8,11},{9,10},{10,... | collective-permute-start | bytes 98312 | tf_op jit(solution)/shard_map/ppermute | solution.py:239

commit v9 on v7

--- a/solution.py
+++ b/solution.py
@@ -149,7 +149,8 @@
 
 
 def top_rows_kernel(n, groups, *rest):
-    messages, (rows_ref, held) = rest[:n], rest[n:]
+    messages, (coeffs_ref, coeffs_out, rows_ref, held) = rest[:n], rest[n:]
+    coeffs_out[...] = coeffs_ref[...]
     me = lax.axis_index("ba")
     mine = lax.axis_index("aa")
     rank = rows_ref.shape[0]
@@ -249,6 +250,13 @@
         flops=2 * rank * points * (3 * points + cols),
         moved=2 * points * (points + cols + rank),
     )(order, skel, sides, inverse, basis, own)
+    coeffs[1], rows = call(
+        functools.partial(top_rows_kernel, n, groups),
+        [shape((share, rank)), shape((rank, groups * rank))],
+        [vmem] * (n + 1),
+        scratch=[pltpu.VMEM((rank, groups * rank), F32)],
+        moved=4 * rank * groups * rank,
+    )(*received, coeffs[1])
     coeffs = [coeffs[0]] + [swap(coeffs[k], "ba", k) for k in range(1, n)]
     ordered = call(
         ordered_kernel,
@@ -257,13 +265,6 @@
         flops=2 * points * points * cols,
         moved=2 * points * (points + 2 * cols),
     )(sides, gather)
-    rows = call(
-        functools.partial(top_rows_kernel, n, groups),
-        shape((rank, groups * rank)),
-        [vmem] * n,
-        scratch=[pltpu.VMEM((rank, groups * rank), F32)],
-        moved=4 * rank * groups * rank,
-    )(*received)
     level, group = call(
         functools.partial(group_kernel, n, rank),
         [shape((share, n * rank), F32), shape((share, rank))],

time: 37.7 us -> 38.8 us (1.029)
  waiting for transfers between devices: 8.65 us -> 11 us
  starting transfers between devices: 18.8 us -> 17.6 us
    ppermute x16, waiting for transfers between devices: 8.65 us -> 11 us  [swap(): return lax.ppermute(array, axis, [(i, i ^ k) for i in range(size)])]
    ppermute x16, starting transfers between devices: 18.8 us -> 17.6 us  [swap(): return lax.ppermute(array, axis, [(i, i ^ k) for i in range(size)])]
  transfers between devices with their start and end apart: 16 -> 16, of which waited for: 6 -> 6; matrix products, arithmetic and copies ran while one was open for 0% -> 0% of each run, Pallas kernels for 18% -> 17%
where the time goes in v9:
time: 38.8 us; the launch traced here: 38.6 us
  starting transfers between devices  17.6 us (45%)
  waiting for transfers between devices  11 us (28%)
  Pallas kernels  9.89 us (25%)
    ppermute x16, starting transfers between devices, swap(): return lax.ppermute(array, axis, [(i, i ^ k) for i in range(size)])  17.6 us
    ppermute x16, waiting for transfers between devices, swap(): return lax.ppermute(array, axis, [(i, i ^ k) for i in range(size)])  11 us
    pallas_call x1, Pallas kernels, shards(): call(down_kernel, [shape((points, cols)), shape((points, rank))], [vmem]...  2.32 us
    pallas_call x1, Pallas kernels, shards(): call(functools.partial(front_kernel, n), [shape((share, rank))] * n + [sh...  1.69 us
    pallas_call x1, Pallas kernels, shards(): call(applied_kernel, [shape((points, cols)), shape((share, rank))], [vmem...  1.24 us
    pallas_call x1, Pallas kernels, shards(): call(functools.partial(final_kernel, n), shape((points, cols)), [vmem] *...  1.24 us
    pallas_call x1, Pallas kernels, shards(): call(ordered_kernel, shape((points, cols)), [vmem] * 2, flops=2 * points...  1.24 us
    pallas_call x1, Pallas kernels, shards(): call(functools.partial(pack_kernel, n), [shape((size, rank)) for size in...  1.2 us
  transfers between devices with their start and end apart: 16, of which 6 were waited for; matrix products, arithmetic and copies ran while one was open for 0% of the time, Pallas kernels for 17%

profile of v9, /device:TPU:0, one launch (start us, length us, event | category | flops | bytes accessed | tf_op | source)
XLA Modules:
  0.0 38.6 jit_solution(16015716278276615715)
XLA Ops:
  0.0 0.0 copy-start.1
  0.0 0.0 copy-start.3
  0.0 1.2 %shard_map.82 = (bf16[640,128]{1,0:T(8,128)(2,1)S(1)}, bf16[640,128]{1,0:T(8,128)(2,1)S(1)}, bf16[640,128]{1,0:T(8,128)(2,1)S(1)}, bf16[896,128]{1,0:T(8,128)(2,1)S(1)}) custom-call(bf16[128,512]{1,0:T(8,128)(2,1)} %core_hbm.1, f32[128,128]{1,0:T(8,128)} %transfer_hbm.1, bf16[32,1024]{1,0:T(8,128)(2,1)} %top_hbm.1), custom_call_target="tpu_custom_call" | custom-call | flops 17179869184 | bytes 27262976 | tf_op jit(solution)/shard_map/pallas_call | solution.py:236
  1.2 3.0 %collective-permute-start.2 = (bf16[640,128]{1,0:T(8,128)(2,1)S(1)}, bf16[640,128]{1,0:T(8,128)(2,1)S(1)}, u32[]{:S(2)}, u32[]{:S(2)}) collective-permute-start(bf16[640,128]{1,0:T(8,128)(2,1)S(1)} %get-tuple-element.32), channel_id=1, source_target_pairs={{0,1},{1,0},{2,3},{3,2},{4,5},{5,4},{6,7},{7,6},{8,9},{9,8},{10,11... | collective-permute-start | bytes 491528 | tf_op jit(solution)/shard_map/ppermute | solution.py:232
  4.2 1.5 %collective-permute-start.3 = (bf16[640,128]{1,0:T(8,128)(2,1)S(1)}, bf16[640,128]{1,0:T(8,128)(2,1)S(1)}, u32[]{:S(2)}, u32[]{:S(2)}) collective-permute-start(bf16[640,128]{1,0:T(8,128)(2,1)S(1)} %get-tuple-element.33), channel_id=1, source_target_pairs={{0,2},{1,3},{2,0},{3,1},{4,6},{5,7},{6,4},{7,5},{8,10},{9,11},{10,... | collective-permute-start | bytes 491528 | tf_op jit(solution)/shard_map/ppermute | solution.py:232
  5.8 0.0 collective-permute-start.4
  5.8 0.0 copy-done.1
  5.8 0.0 copy-done.3
  5.8 0.0 copy-done.4
  5.8 0.0 copy-done
  5.8 0.0 copy-done.2
  5.8 1.7 %shard_map.83 = (bf16[128,128]{1,0:T(8,128)(2,1)S(1)}, bf16[128,128]{1,0:T(8,128)(2,1)S(1)}, bf16[128,128]{1,0:T(8,128)(2,1)S(1)}, bf16[128,128]{1,0:T(8,128)(2,...) custom-call(s32[1,1024]{1,0:T(1,128)S(1)} %copy-done.3, s32[1,128]{1,0:T(1,128)S(1)} %copy-done.4, ...), custom_call_target="tpu_custom_call" | custom-call | flops 939524096 | bytes 3407872 | tf_op jit(solution)/shard_map/pallas_call | solution.py:245
  7.5 3.0 %collective-permute-start = (bf16[128,128]{1,0:T(8,128)(2,1)S(1)}, bf16[128,128]{1,0:T(8,128)(2,1)S(1)}, u32[]{:S(2)}, u32[]{:S(2)}) collective-permute-start(bf16[128,128]{1,0:T(8,128)(2,1)S(1)} %get-tuple-element.30), channel_id=1, source_target_pairs={{0,3},{1,2},{2,1},{3,0},{4,7},{5,6},{6,5},{7,4},{8,11},{9,10},{10,... | collective-permute-start | bytes 98312 | tf_op jit(solution)/shard_map/ppermute | solution.py:232
  10.5 0.5 %collective-permute-start.1 = (bf16[128,128]{1,0:T(8,128)(2,1)S(1)}, bf16[128,128]{1,0:T(8,128)(2,1)S(1)}, u32[]{:S(2)}, u32[]{:S(2)}) collective-permute-start(bf16[128,128]{1,0:T(8,128)(2,1)S(1)} %get-tuple-element.31), channel_id=1, source_target_pairs={{0,2},{1,3},{2,0},{3,1},{4,6},{5,7},{6,4},{7,5},{8,10},{9,11},{10,... | collective-permute-start | bytes 98312 | tf_op jit(solution)/shard_map/ppermute | solution.py:232
  11.0 0.0 collective-permute-done.2.rest_1_.rest_6_
  11.0 3.2 %collective-permute-done.3.rest_2_.rest_5_ = bf16[640,128]{1,0:T(8,128)(2,1)S(1)} collective-permute-done((bf16[640,128]{1,0:T(8,128)(2,1)S(1)}, bf16[640,128]{1,0:T(8,128)(2,1)S(1)}, u32[]{:S(2)}, u32[]{:S(2)}) %collective-permute-start.3) | collective-permute-done | bytes 163872 | tf_op jit(solution)/shard_map/ppermute | solution.py:232
  14.2 0.0 collective-permute-done.4.rest_3_.rest_4_
  14.2 0.1 shard_map.85
  14.3 1.0 %collective-permute-start.5 = (bf16[128,128]{1,0:T(8,128)(2,1)S(1)}, bf16[128,128]{1,0:T(8,128)(2,1)S(1)}, u32[]{:S(2)}, u32[]{:S(2)}) collective-permute-start(bf16[128,128]{1,0:T(8,128)(2,1)S(1)} %get-tuple-element.36), channel_id=1, source_target_pairs={{0,1},{1,0},{2,3},{3,2},{4,5},{5,4},{6,7},{7,6},{8,9},{9,8},{10,11... | collective-permute-start | bytes 98312 | tf_op jit(solution)/shard_map/ppermute | solution.py:232
  15.3 1.2 %shard_map.84.after.ordered_ref = bf16[1024,512]{1,0:T(8,128)(2,1)S(1)} custom-call(bf16[1024,512]{1,0:T(8,128)(2,1)S(1)} %copy-done, bf16[1024,1024]{1,0:T(8,128)(2,1)S(1)} %get-tuple-element.29.gather_ref), custom_call_target="tpu_custom_call" | custom-call | flops 1073741824 | bytes 4194304 | tf_op jit(solution)/shard_map/pallas_call | solution.py:261
  16.5 0.0 collective-permute-done.rest_0_
  16.5 0.0 collective-permute-done.1.rest_1_
  16.5 1.8 %collective-permute-done.5.rest_2_ = bf16[128,128]{1,0:T(8,128)(2,1)S(1)} collective-permute-done((bf16[128,128]{1,0:T(8,128)(2,1)S(1)}, bf16[128,128]{1,0:T(8,128)(2,1)S(1)}, u32[]{:S(2)}, u32[]{:S(2)}) %collective-permute-start.5) | collective-permute-done | bytes 32800 | tf_op jit(solution)/shard_map/ppermute | solution.py:232
  18.3 0.4 %shard_map.86 = (f32[128,512]{1,0:T(8,128)S(1)}, bf16[128,128]{1,0:T(8,128)(2,1)S(1)}) custom-call(bf16[1024,512]{1,0:T(8,128)(2,1)S(1)} %shard_map.84.after.ordered_ref, bf16[128,128]{1,0:T(8,128)(2,1)S(1)} %collective-permute-done.rest_0_, bf16[128,128]{1,0:T(8,128)(2,1)S(1)} %collective-permute-done.1.rest_1_, ...), custom_call_target="tpu_custom_call" | custom-call | flops 83886080 | bytes 262144 | tf_op jit(solution)/shard_map/pallas_call | solution.py:268
  18.7 1.6 %collective-permute-start.7 = (bf16[128,128]{1,0:T(8,128)(2,1)S(1)}, bf16[128,128]{1,0:T(8,128)(2,1)S(1)}, u32[]{:S(2)}, u32[]{:S(2)}) collective-permute-start(bf16[128,128]{1,0:T(8,128)(2,1)S(1)} %get-tuple-element.38.group_ref.rest_4_), channel_id=1, source_target_pairs={{0,8},{4,12},{8,0},{12,4},{16,24},{20,28},{24,16},{28,20},{1,9},{5... | collective-permute-start | bytes 98312 | tf_op jit(solution)/shard_map/ppermute | solution.py:232
  20.4 2.6 %collective-permute-start.9 = (bf16[128,128]{1,0:T(8,128)(2,1)S(1)}, bf16[128,128]{1,0:T(8,128)(2,1)S(1)}, u32[]{:S(2)}, u32[]{:S(2)}) collective-permute-start(bf16[128,128]{1,0:T(8,128)(2,1)S(1)} %get-tuple-element.38.group_ref.rest_4_), channel_id=1, source_target_pairs={{0,16},{4,20},{8,24},{12,28},{16,0},{20,4},{24,8},{28,12},{1,17},{... | collective-permute-start | bytes 98312 | tf_op jit(solution)/shard_map/ppermute | solution.py:232
  23.0 0.2 collective-permute-start.11
  23.2 1.2 %shard_map.87 = (bf16[1024,512]{1,0:T(8,128)(2,1)S(1)}, bf16[128,128]{1,0:T(8,128)(2,1)S(1)}) custom-call(bf16[1024,1024]{1,0:T(8,128)(2,1)S(1)} %copy-done.1, bf16[1024,512]{1,0:T(8,128)(2,1)S(1)} %shard_map.84.after.ordered_ref, bf16[128,128]{1,0:T(8,128)(2,1)S(1)} %get-tuple-element.38.group_ref.rest_4_), custom_call_target="tpu_custom_call" | custom-call | flops 1073741824 | bytes 4194304 | tf_op jit(solution)/shard_map/pallas_call | solution.py:275
  24.4 0.1 collective-permute-start.6
  24.5 0.0 collective-permute-done.7.rest_6_
  24.5 0.5 %collective-permute-start.8 = (bf16[128,128]{1,0:T(8,128)(2,1)S(1)}, bf16[128,128]{1,0:T(8,128)(2,1)S(1)}, u32[]{:S(2)}, u32[]{:S(2)}) collective-permute-start(bf16[128,128]{1,0:T(8,128)(2,1)S(1)} %collective-permute-done.7.rest_6_), channel_id=1, source_target_pairs={{0,4},{4,0},{8,12},{12,8},{16,20},{20,16},{24,28},{28,24},{1,5},{5... | collective-permute-start | bytes 98312 | tf_op jit(solution)/shard_map/ppermute | solution.py:232
  25.0 0.4 %collective-permute-done.9.rest_8_ = bf16[128,128]{1,0:T(8,128)(2,1)S(1)} collective-permute-done((bf16[128,128]{1,0:T(8,128)(2,1)S(1)}, bf16[128,128]{1,0:T(8,128)(2,1)S(1)}, u32[]{:S(2)}, u32[]{:S(2)}) %collective-permute-start.9) | collective-permute-done | bytes 32800 | tf_op jit(solution)/shard_map/ppermute | solution.py:232
  25.4 0.0 collective-permute-start.10
  25.5 3.2 %collective-permute-done.11.rest_10_ = bf16[128,128]{1,0:T(8,128)(2,1)S(1)} collective-permute-done((bf16[128,128]{1,0:T(8,128)(2,1)S(1)}, bf16[128,128]{1,0:T(8,128)(2,1)S(1)}, u32[]{:S(2)}, u32[]{:S(2)}) %collective-permute-start.11) | collective-permute-done | bytes 32800 | tf_op jit(solution)/shard_map/ppermute | solution.py:232
  28.7 0.0 collective-permute-start.12
  28.7 0.0 collective-permute-done.6.rest_5_
  28.7 0.0 collective-permute-done.8.rest_7_
  28.7 0.0 collective-permute-done.10.rest_9_
  28.7 1.2 %collective-permute-done.12.rest_11_ = bf16[128,128]{1,0:T(8,128)(2,1)S(1)} collective-permute-done((bf16[128,128]{1,0:T(8,128)(2,1)S(1)}, bf16[128,128]{1,0:T(8,128)(2,1)S(1)}, u32[]{:S(2)}, u32[]{:S(2)}) %collective-permute-start.12) | collective-permute-done | bytes 32800 | tf_op jit(solution)/shard_map/ppermute | solution.py:232
  29.9 0.4 %shard_map.88 = (bf16[128,128]{1,0:T(8,128)(2,1)S(1)}, bf16[128,128]{1,0:T(8,128)(2,1)S(1)}, bf16[128,128]{1,0:T(8,128)(2,1)S(1)}, bf16[128,128]{1,0:T(8,128)(2,1)S(1)}) custom-call(bf16[128,1024]{1,0:T(8,128)(2,1)S(1)} %get-tuple-element.40.rows_ref, f32[128,512]{1,0:T(8,128)S(1)} %get-tuple-element.41.level_ref, ...), custom_call_target="tpu_custom_call" | custom-call | flops 50331648 | bytes 262144 | tf_op jit(solution)/shard_map/pallas_call | solution.py:287
  30.3 1.0 %collective-permute-start.13 = (bf16[128,128]{1,0:T(8,128)(2,1)S(1)}, bf16[128,128]{1,0:T(8,128)(2,1)S(1)}, u32[]{:S(2)}, u32[]{:S(2)}) collective-permute-start(bf16[128,128]{1,0:T(8,128)(2,1)S(1)} %get-tuple-element.46), channel_id=1, source_target_pairs={{0,1},{1,0},{2,3},{3,2},{4,5},{5,4},{6,7},{7,6},{8,9},{9,8},{10,11... | collective-permute-start | bytes 98312 | tf_op jit(solution)/shard_map/ppermute | solution.py:232
  31.3 1.3 %collective-permute-start.14 = (bf16[128,128]{1,0:T(8,128)(2,1)S(1)}, bf16[128,128]{1,0:T(8,128)(2,1)S(1)}, u32[]{:S(2)}, u32[]{:S(2)}) collective-permute-start(bf16[128,128]{1,0:T(8,128)(2,1)S(1)} %get-tuple-element.47), channel_id=1, source_target_pairs={{0,2},{1,3},{2,0},{3,1},{4,6},{5,7},{6,4},{7,5},{8,10},{9,11},{10,... | collective-permute-start | bytes 98312 | tf_op jit(solution)/shard_map/ppermute | solution.py:232
  32.6 1.3 %collective-permute-start.15 = (bf16[128,128]{1,0:T(8,128)(2,1)S(1)}, bf16[128,128]{1,0:T(8,128)(2,1)S(1)}, u32[]{:S(2)}, u32[]{:S(2)}) collective-permute-start(bf16[128,128]{1,0:T(8,128)(2,1)S(1)} %get-tuple-element.48), channel_id=1, source_target_pairs={{0,3},{1,2},{2,1},{3,0},{4,7},{5,6},{6,5},{7,4},{8,11},{9,10},{10,... | collective-permute-start | bytes 98312 | tf_op jit(solution)/shard_map/ppermute | solution.py:232
  33.9 2.3 %shard_map.89 = (bf16[1024,512]{1,0:T(8,128)(2,1)S(1)}, bf16[1024,128]{1,0:T(8,128)(2,1)S(1)}) custom-call(bf16[1024,1024]{1,0:T(8,128)(2,1)S(1)} %copy-done.1, s32[1,1024]{1,0:T(1,128)S(1)} %copy-done.3, bf16[1024,256]{1,0:T(8,128)(2,1)S(1)} %get-tuple-element.28.pair_ref, bf16[1024,512]{1,0:T(8,128)(2,1)S(1)} %get-tuple-element.39.applied_ref, ...), custom_call_target="tpu_custom_call" | custom-call | flops 1879048192 | bytes 4194304 | tf_op jit(solution)/shard_map/pallas_call | solution.py:295
  36.2 0.0 collective-permute-done.13.rest_1_
  36.2 0.0 collective-permute-done.14.rest_2_
  36.2 1.2 %collective-permute-done.15.rest_3_ = bf16[128,128]{1,0:T(8,128)(2,1)S(1)} collective-permute-done((bf16[128,128]{1,0:T(8,128)(2,1)S(1)}, bf16[128,128]{1,0:T(8,128)(2,1)S(1)}, u32[]{:S(2)}, u32[]{:S(2)}) %collective-permute-start.15) | collective-permute-done | bytes 32800 | tf_op jit(solution)/shard_map/ppermute | solution.py:232
  37.4 1.2 %shard_map.90 = bf16[1024,512]{1,0:T(8,128)(2,1)} custom-call(bf16[1024,512]{1,0:T(8,128)(2,1)S(1)} %get-tuple-element.44.applied_ref, bf16[1024,128]{1,0:T(8,128)(2,1)S(1)} %get-tuple-element.45.down_ref, bf16[128,128]{1,0:T(8,128)(2,1)S(1)} %get-tuple-element.43.after.rest_0_, bf16[128,128]{1,0:T(8,128)(2,1)S(1)} %collective-permute-done.13.rest_1_, ...), custom_call_target="tpu_custom_call" | custom-call | flops 134217728 | bytes 2097152 | tf_op jit(solution)/shard_map/pallas_call | solution.py:302
  (3 shorter events, 0.0 us)
Async XLA Ops:
  0.0 5.8 %copy-start.1 = (bf16[1024,1024]{1,0:T(8,128)(2,1)S(1)}, bf16[1024,1024]{1,0:T(8,128)(2,1)}, u32[]{:S(2)}) copy-start(bf16[1024,1024]{1,0:T(8,128)(2,1)} %inverse_ref.5) | copy-start | bytes 6291460
  0.0 5.8 %copy-start.3 = (s32[1,1024]{1,0:T(1,128)S(1)}, s32[1,1024]{1,0:T(1,128)}, u32[]{:S(2)}) copy-start(s32[1,1024]{1,0:T(1,128)} %order_ref.3) | copy-start | bytes 12292
  0.0 5.8 %copy-start.4 = (s32[1,128]{1,0:T(1,128)S(1)}, s32[1,128]{1,0:T(1,128)}, u32[]{:S(2)}) copy-start(s32[1,128]{1,0:T(1,128)} %skel_ref.1) | copy-start | bytes 1540
  0.0 5.8 %copy-start = (bf16[1024,512]{1,0:T(8,128)(2,1)S(1)}, bf16[1024,512]{1,0:T(8,128)(2,1)}, u32[]{:S(2)}) copy-start(bf16[1024,512]{1,0:T(8,128)(2,1)} %sides_ref.3) | copy-start | bytes 3145732
  0.0 5.8 %copy-start.2 = (bf16[1024,128]{1,0:T(8,128)(2,1)S(1)}, bf16[1024,128]{1,0:T(8,128)(2,1)}, u32[]{:S(2)}) copy-start(bf16[1024,128]{1,0:T(8,128)(2,1)} %basis_ref.1) | copy-start | bytes 786436
  1.2 9.8 %collective-permute-start.2 = (bf16[640,128]{1,0:T(8,128)(2,1)S(1)}, bf16[640,128]{1,0:T(8,128)(2,1)S(1)}, u32[]{:S(2)}, u32[]{:S(2)}) collective-permute-start(bf16[640,128]{1,0:T(8,128)(2,1)S(1)} %get-tuple-element.32), channel_id=1, source_target_pairs={{0,1},{1,0},{2,3},{3,2},{4,5},{5,4},{6,7},{7,6},{8,9},{9,8},{10,11... | collective-permute-start | bytes 491528 | tf_op jit(solution)/shard_map/ppermute | solution.py:232
  4.2 10.0 %collective-permute-start.3 = (bf16[640,128]{1,0:T(8,128)(2,1)S(1)}, bf16[640,128]{1,0:T(8,128)(2,1)S(1)}, u32[]{:S(2)}, u32[]{:S(2)}) collective-permute-start(bf16[640,128]{1,0:T(8,128)(2,1)S(1)} %get-tuple-element.33), channel_id=1, source_target_pairs={{0,2},{1,3},{2,0},{3,1},{4,6},{5,7},{6,4},{7,5},{8,10},{9,11},{10,... | collective-permute-start | bytes 491528 | tf_op jit(solution)/shard_map/ppermute | solution.py:232
  5.8 8.4 %collective-permute-start.4 = (bf16[640,128]{1,0:T(8,128)(2,1)S(1)}, bf16[640,128]{1,0:T(8,128)(2,1)S(1)}, u32[]{:S(2)}, u32[]{:S(2)}) collective-permute-start(bf16[640,128]{1,0:T(8,128)(2,1)S(1)} %get-tuple-element.34), channel_id=1, source_target_pairs={{0,3},{1,2},{2,1},{3,0},{4,7},{5,6},{6,5},{7,4},{8,11},{9,10},{10,... | collective-permute-start | bytes 491528 | tf_op jit(solution)/shard_map/ppermute | solution.py:232
  7.5 9.0 %collective-permute-start = (bf16[128,128]{1,0:T(8,128)(2,1)S(1)}, bf16[128,128]{1,0:T(8,128)(2,1)S(1)}, u32[]{:S(2)}, u32[]{:S(2)}) collective-permute-start(bf16[128,128]{1,0:T(8,128)(2,1)S(1)} %get-tuple-element.30), channel_id=1, source_target_pairs={{0,3},{1,2},{2,1},{3,0},{4,7},{5,6},{6,5},{7,4},{8,11},{9,10},{10,... | collective-permute-start | bytes 98312 | tf_op jit(solution)/shard_map/ppermute | solution.py:232
  10.5 6.1 %collective-permute-start.1 = (bf16[128,128]{1,0:T(8,128)(2,1)S(1)}, bf16[128,128]{1,0:T(8,128)(2,1)S(1)}, u32[]{:S(2)}, u32[]{:S(2)}) collective-permute-start(bf16[128,128]{1,0:T(8,128)(2,1)S(1)} %get-tuple-element.31), channel_id=1, source_target_pairs={{0,2},{1,3},{2,0},{3,1},{4,6},{5,7},{6,4},{7,5},{8,10},{9,11},{10,... | collective-permute-start | bytes 98312 | tf_op jit(solution)/shard_map/ppermute | solution.py:232
  14.3 4.0 %collective-permute-start.5 = (bf16[128,128]{1,0:T(8,128)(2,1)S(1)}, bf16[128,128]{1,0:T(8,128)(2,1)S(1)}, u32[]{:S(2)}, u32[]{:S(2)}) collective-permute-start(bf16[128,128]{1,0:T(8,128)(2,1)S(1)} %get-tuple-element.36), channel_id=1, source_target_pairs={{0,1},{1,0},{2,3},{3,2},{4,5},{5,4},{6,7},{7,6},{8,9},{9,8},{10,11... | collective-permute-start | bytes 98312 | tf_op jit(solution)/shard_map/ppermute | solution.py:232
  18.7 5.8 %collective-permute-start.7 = (bf16[128,128]{1,0:T(8,128)(2,1)S(1)}, bf16[128,128]{1,0:T(8,128)(2,1)S(1)}, u32[]{:S(2)}, u32[]{:S(2)}) collective-permute-start(bf16[128,128]{1,0:T(8,128)(2,1)S(1)} %get-tuple-element.38.group_ref.rest_4_), channel_id=1, source_target_pairs={{0,8},{4,12},{8,0},{12,4},{16,24},{20,28},{24,16},{28,20},{1,9},{5... | collective-permute-start | bytes 98312 | tf_op jit(solution)/shard_map/ppermute | solution.py:232
  20.4 5.1 %collective-permute-start.9 = (bf16[128,128]{1,0:T(8,128)(2,1)S(1)}, bf16[128,128]{1,0:T(8,128)(2,1)S(1)}, u32[]{:S(2)}, u32[]{:S(2)}) collective-permute-start(bf16[128,128]{1,0:T(8,128)(2,1)S(1)} %get-tuple-element.38.group_ref.rest_4_), channel_id=1, source_target_pairs={{0,16},{4,20},{8,24},{12,28},{16,0},{20,4},{24,8},{28,12},{1,17},{... | collective-permute-start | bytes 98312 | tf_op jit(solution)/shard_map/ppermute | solution.py:232
  23.0 5.7 %collective-permute-start.11 = (bf16[128,128]{1,0:T(8,128)(2,1)S(1)}, bf16[128,128]{1,0:T(8,128)(2,1)S(1)}, u32[]{:S(2)}, u32[]{:S(2)}) collective-permute-start(bf16[128,128]{1,0:T(8,128)(2,1)S(1)} %get-tuple-element.38.group_ref.rest_4_), channel_id=1, source_target_pairs={{0,24},{4,28},{8,16},{12,20},{16,8},{20,12},{24,0},{28,4},{1,25},{... | collective-permute-start | bytes 98312 | tf_op jit(solution)/shard_map/ppermute | solution.py:232
  24.4 4.3 %collective-permute-start.6 = (bf16[128,128]{1,0:T(8,128)(2,1)S(1)}, bf16[128,128]{1,0:T(8,128)(2,1)S(1)}, u32[]{:S(2)}, u32[]{:S(2)}) collective-permute-start(bf16[128,128]{1,0:T(8,128)(2,1)S(1)} %get-tuple-element.42), channel_id=1, source_target_pairs={{0,4},{4,0},{8,12},{12,8},{16,20},{20,16},{24,28},{28,24},{1,5},{5... | collective-permute-start | bytes 98312 | tf_op jit(solution)/shard_map/ppermute | solution.py:232
  24.5 4.2 %collective-permute-start.8 = (bf16[128,128]{1,0:T(8,128)(2,1)S(1)}, bf16[128,128]{1,0:T(8,128)(2,1)S(1)}, u32[]{:S(2)}, u32[]{:S(2)}) collective-permute-start(bf16[128,128]{1,0:T(8,128)(2,1)S(1)} %collective-permute-done.7.rest_6_), channel_id=1, source_target_pairs={{0,4},{4,0},{8,12},{12,8},{16,20},{20,16},{24,28},{28,24},{1,5},{5... | collective-permute-start | bytes 98312 | tf_op jit(solution)/shard_map/ppermute | solution.py:232
  25.4 3.3 %collective-permute-start.10 = (bf16[128,128]{1,0:T(8,128)(2,1)S(1)}, bf16[128,128]{1,0:T(8,128)(2,1)S(1)}, u32[]{:S(2)}, u32[]{:S(2)}) collective-permute-start(bf16[128,128]{1,0:T(8,128)(2,1)S(1)} %collective-permute-done.9.rest_8_), channel_id=1, source_target_pairs={{0,4},{4,0},{8,12},{12,8},{16,20},{20,16},{24,28},{28,24},{1,5},{5... | collective-permute-start | bytes 98312 | tf_op jit(solution)/shard_map/ppermute | solution.py:232
  28.7 1.2 %collective-permute-start.12 = (bf16[128,128]{1,0:T(8,128)(2,1)S(1)}, bf16[128,128]{1,0:T(8,128)(2,1)S(1)}, u32[]{:S(2)}, u32[]{:S(2)}) collective-permute-start(bf16[128,128]{1,0:T(8,128)(2,1)S(1)} %collective-permute-done.11.rest_10_), channel_id=1, source_target_pairs={{0,4},{4,0},{8,12},{12,8},{16,20},{20,16},{24,28},{28,24},{1,5},{5... | collective-permute-start | bytes 98312 | tf_op jit(solution)/shard_map/ppermute | solution.py:232
  30.3 5.9 %collective-permute-start.13 = (bf16[128,128]{1,0:T(8,128)(2,1)S(1)}, bf16[128,128]{1,0:T(8,128)(2,1)S(1)}, u32[]{:S(2)}, u32[]{:S(2)}) collective-permute-start(bf16[128,128]{1,0:T(8,128)(2,1)S(1)} %get-tuple-element.46), channel_id=1, source_target_pairs={{0,1},{1,0},{2,3},{3,2},{4,5},{5,4},{6,7},{7,6},{8,9},{9,8},{10,11... | collective-permute-start | bytes 98312 | tf_op jit(solution)/shard_map/ppermute | solution.py:232
  31.3 4.9 %collective-permute-start.14 = (bf16[128,128]{1,0:T(8,128)(2,1)S(1)}, bf16[128,128]{1,0:T(8,128)(2,1)S(1)}, u32[]{:S(2)}, u32[]{:S(2)}) collective-permute-start(bf16[128,128]{1,0:T(8,128)(2,1)S(1)} %get-tuple-element.47), channel_id=1, source_target_pairs={{0,2},{1,3},{2,0},{3,1},{4,6},{5,7},{6,4},{7,5},{8,10},{9,11},{10,... | collective-permute-start | bytes 98312 | tf_op jit(solution)/shard_map/ppermute | solution.py:232
  32.6 4.8 %collective-permute-start.15 = (bf16[128,128]{1,0:T(8,128)(2,1)S(1)}, bf16[128,128]{1,0:T(8,128)(2,1)S(1)}, u32[]{:S(2)}, u32[]{:S(2)}) collective-permute-start(bf16[128,128]{1,0:T(8,128)(2,1)S(1)} %get-tuple-element.48), channel_id=1, source_target_pairs={{0,3},{1,2},{2,1},{3,0},{4,7},{5,6},{6,5},{7,4},{8,11},{9,10},{10,... | collective-permute-start | bytes 98312 | tf_op jit(solution)/shard_map/ppermute | solution.py:232

commit v10 on v5

--- a/solution.py
+++ b/solution.py
@@ -182,7 +182,7 @@
 
 
 def final_kernel(n, applied_ref, down_ref, *rest):
-    pieces, (out_hbm, correction, out_ref, sems) = rest[:n], rest[n:]
+    pieces, (out_hbm, correction, out_ref, sems) = rest[:n][::-1], rest[n:]
     me = lax.axis_index("ba")
     share = pieces[0].shape[0]
     for k in range(n):
@@ -297,7 +297,7 @@
         scratch=[pltpu.VMEM((cols, rank), BF), pltpu.VMEM((points, cols), BF), pltpu.SemaphoreType.DMA((PIECES,))],
         flops=2 * points * cols * rank,
         moved=4 * points * cols,
-    )(applied, down, *back)
+    )(applied, down, *back[::-1])
 
 
 def solution(mesh):

time: 34.3 us -> 33.5 us (0.977)
  waiting for transfers between devices: 7.14 us -> 6.39 us
    ppermute x16, waiting for transfers between devices: 7.14 us -> 6.39 us  [swap(): return lax.ppermute(array, axis, [(i, i ^ k) for i in range(size)])]
  transfers between devices with their start and end apart: 16 -> 16, of which waited for: 7 -> 8; matrix products, arithmetic and copies ran while one was open for 0% -> 0% of each run, Pallas kernels for 15% -> 16%
where the time goes in v10:
time: 33.5 us; the launch traced here: 33.4 us
  starting transfers between devices  16.7 us (50%)
  Pallas kernels  10.2 us (30%)
  waiting for transfers between devices  6.39 us (19%)
    ppermute x16, starting transfers between devices, swap(): return lax.ppermute(array, axis, [(i, i ^ k) for i in range(size)])  16.7 us
    ppermute x16, waiting for transfers between devices, swap(): return lax.ppermute(array, axis, [(i, i ^ k) for i in range(size)])  6.39 us
    pallas_call x1, Pallas kernels, shards(): call(functools.partial(front_kernel, n), [shape((size, rank)) for size in...  3.35 us
    pallas_call x1, Pallas kernels, shards(): call(down_kernel, [shape((points, cols)), shape((points, rank))], [vmem]...  2.33 us
    pallas_call x1, Pallas kernels, shards(): call(applied_kernel, [shape((points, cols)), shape(top.shape)], [vmem] *...  2.33 us
    pallas_call x1, Pallas kernels, shards(): call(functools.partial(final_kernel, n), shape((points, cols)), [vmem] *...  1.25 us
  transfers between devices with their start and end apart: 16, of which 8 were waited for; matrix products, arithmetic and copies ran while one was open for 0% of the time, Pallas kernels for 16%

profile of v10, /device:TPU:0, one launch (start us, length us, event | category | flops | bytes accessed | tf_op | source)
XLA Modules:
  0.0 33.4 jit_solution(967241181968030662)
XLA Ops:
  0.0 3.4 %shard_map.82 = (bf16[512,128]{1,0:T(8,128)(2,1)S(1)}, bf16[512,128]{1,0:T(8,128)(2,1)S(1)}, bf16[512,128]{1,0:T(8,128)(2,1)S(1)}, bf16[768,128]{1,0:T(8,128)(2,...) custom-call(s32[1,1024]{1,0:T(1,128)} %order_hbm.1, ...), custom_call_target="tpu_custom_call" | custom-call | flops 939524096 | bytes 3407872 | tf_op jit(solution)/shard_map/pallas_call | solution.py:238
  3.4 4.0 %collective-permute-start.3 = (bf16[512,128]{1,0:T(8,128)(2,1)S(1)}, bf16[512,128]{1,0:T(8,128)(2,1)S(1)}, u32[]{:S(2)}, u32[]{:S(2)}) collective-permute-start(bf16[512,128]{1,0:T(8,128)(2,1)S(1)} %get-tuple-element.34), channel_id=1, source_target_pairs={{0,3},{1,2},{2,1},{3,0},{4,7},{5,6},{6,5},{7,4},{8,11},{9,10},{10,... | collective-permute-start | bytes 393224 | tf_op jit(solution)/shard_map/ppermute | solution.py:235
  7.3 0.5 %collective-permute-start.4 = (bf16[512,128]{1,0:T(8,128)(2,1)S(1)}, bf16[512,128]{1,0:T(8,128)(2,1)S(1)}, u32[]{:S(2)}, u32[]{:S(2)}) collective-permute-start(bf16[512,128]{1,0:T(8,128)(2,1)S(1)} %get-tuple-element.35), channel_id=1, source_target_pairs={{0,2},{1,3},{2,0},{3,1},{4,6},{5,7},{6,4},{7,5},{8,10},{9,11},{10,... | collective-permute-start | bytes 393224 | tf_op jit(solution)/shard_map/ppermute | solution.py:235
  7.8 0.2 collective-permute-start.5
  8.0 2.3 %shard_map.83 = (bf16[1024,512]{1,0:T(8,128)(2,1)S(1)}, bf16[32,1024]{1,0:T(8,128)(2,1)S(1)}) custom-call(bf16[1024,512]{1,0:T(8,128)(2,1)S(1)} %get-tuple-element.28.sides_ref, bf16[1024,1024]{1,0:T(8,128)(2,1)S(1)} %get-tuple-element.25.inverse_ref, bf16[1024,1024]{1,0:T(8,128)(2,1)S(1)} %get-tuple-element.29.gather_ref, ...), custom_call_target="tpu_custom_call" | custom-call | flops 2147483648 | bytes 4194304 | tf_op jit(solution)/shard_map/pallas_call | solution.py:250
  10.3 2.9 %collective-permute-start.2 = (bf16[32,1024]{1,0:T(8,128)(2,1)S(1)}, bf16[32,1024]{1,0:T(8,128)(2,1)S(1)}, u32[]{:S(2)}, u32[]{:S(2)}) collective-permute-start(bf16[32,1024]{1,0:T(8,128)(2,1)S(1)} %get-tuple-element.32.rest_0_), channel_id=1, source_target_pairs={{0,3},{1,2},{2,1},{3,0},{4,7},{5,6},{6,5},{7,4},{8,11},{9,10},{10,... | collective-permute-start | bytes 196616 | tf_op jit(solution)/shard_map/ppermute | solution.py:235
  13.2 0.5 %collective-permute-start.1 = (bf16[32,1024]{1,0:T(8,128)(2,1)S(1)}, bf16[32,1024]{1,0:T(8,128)(2,1)S(1)}, u32[]{:S(2)}, u32[]{:S(2)}) collective-permute-start(bf16[32,1024]{1,0:T(8,128)(2,1)S(1)} %get-tuple-element.32.rest_0_), channel_id=1, source_target_pairs={{0,2},{1,3},{2,0},{3,1},{4,6},{5,7},{6,4},{7,5},{8,10},{9,11},{10,... | collective-permute-start | bytes 196616 | tf_op jit(solution)/shard_map/ppermute | solution.py:235
  13.7 0.0 collective-permute-done.3.rest_0_.rest_3_
  13.7 0.2 collective-permute-start
  13.9 0.3 collective-permute-done.4.rest_1_.rest_2_
  14.2 0.2 collective-permute-done.5.rest_2_.rest_1_
  14.4 0.4 %shard_map.85 = (f32[128,512]{1,0:T(8,128)S(1)}, bf16[128,128]{1,0:T(8,128)(2,1)S(1)}) custom-call(bf16[1024,512]{1,0:T(8,128)(2,1)S(1)} %get-tuple-element.31.after.applied_ref, bf16[768,128]{1,0:T(8,128)(2,1)S(1)} %get-tuple-element.33.own_ref.rest_0_, bf16[512,128]{1,0:T(8,128)(2,1)S(1)} %collective-permute-done.3.rest_0_.rest_3_, ...), custom_call_target="tpu_custom_call" | custom-call | flops 83886080 | bytes 262144 | tf_op jit(solution)/shard_map/pallas_call | solution.py:258
  14.8 3.7 %collective-permute-start.11 = (bf16[128,128]{1,0:T(8,128)(2,1)S(1)}, bf16[128,128]{1,0:T(8,128)(2,1)S(1)}, u32[]{:S(2)}, u32[]{:S(2)}) collective-permute-start(bf16[128,128]{1,0:T(8,128)(2,1)S(1)} %get-tuple-element.38.rest_4_), channel_id=1, source_target_pairs={{0,24},{4,28},{8,16},{12,20},{16,8},{20,12},{24,0},{28,4},{1,25},{... | collective-permute-start | bytes 98312 | tf_op jit(solution)/shard_map/ppermute | solution.py:235
  18.5 0.0 collective-permute-start.9
  18.5 0.0 collective-permute-done.2.rest_3_
  18.5 0.7 %collective-permute-start.7 = (bf16[128,128]{1,0:T(8,128)(2,1)S(1)}, bf16[128,128]{1,0:T(8,128)(2,1)S(1)}, u32[]{:S(2)}, u32[]{:S(2)}) collective-permute-start(bf16[128,128]{1,0:T(8,128)(2,1)S(1)} %get-tuple-element.38.rest_4_), channel_id=1, source_target_pairs={{0,8},{4,12},{8,0},{12,4},{16,24},{20,28},{24,16},{28,20},{1,9},{5... | collective-permute-start | bytes 98312 | tf_op jit(solution)/shard_map/ppermute | solution.py:235
  19.3 0.0 collective-permute-done.1.rest_2_
  19.3 0.0 collective-permute-start.6
  19.3 1.3 %collective-permute-done.11.rest_10_ = bf16[128,128]{1,0:T(8,128)(2,1)S(1)} collective-permute-done((bf16[128,128]{1,0:T(8,128)(2,1)S(1)}, bf16[128,128]{1,0:T(8,128)(2,1)S(1)}, u32[]{:S(2)}, u32[]{:S(2)}) %collective-permute-start.11) | collective-permute-done | bytes 32800 | tf_op jit(solution)/shard_map/ppermute | solution.py:235
  20.6 0.0 collective-permute-start.12
  20.6 2.7 %collective-permute-done.9.rest_8_ = bf16[128,128]{1,0:T(8,128)(2,1)S(1)} collective-permute-done((bf16[128,128]{1,0:T(8,128)(2,1)S(1)}, bf16[128,128]{1,0:T(8,128)(2,1)S(1)}, u32[]{:S(2)}, u32[]{:S(2)}) %collective-permute-start.9) | collective-permute-done | bytes 32800 | tf_op jit(solution)/shard_map/ppermute | solution.py:235
  23.3 0.0 collective-permute-start.10
  23.3 0.0 collective-permute-done.7.rest_6_
  23.3 0.5 %collective-permute-start.8 = (bf16[128,128]{1,0:T(8,128)(2,1)S(1)}, bf16[128,128]{1,0:T(8,128)(2,1)S(1)}, u32[]{:S(2)}, u32[]{:S(2)}) collective-permute-start(bf16[128,128]{1,0:T(8,128)(2,1)S(1)} %collective-permute-done.7.rest_6_), channel_id=1, source_target_pairs={{0,4},{4,0},{8,12},{12,8},{16,20},{20,16},{24,28},{28,24},{1,5},{5... | collective-permute-start | bytes 98312 | tf_op jit(solution)/shard_map/ppermute | solution.py:235
  23.9 0.0 collective-permute-done.rest_1_
  23.9 0.1 shard_map.84.rows_ref
  24.0 0.0 collective-permute-done.6.rest_5_
  24.0 0.0 collective-permute-done.12.rest_11_
  24.0 0.6 %collective-permute-done.10.rest_9_ = bf16[128,128]{1,0:T(8,128)(2,1)S(1)} collective-permute-done((bf16[128,128]{1,0:T(8,128)(2,1)S(1)}, bf16[128,128]{1,0:T(8,128)(2,1)S(1)}, u32[]{:S(2)}, u32[]{:S(2)}) %collective-permute-start.10) | collective-permute-done | bytes 32800 | tf_op jit(solution)/shard_map/ppermute | solution.py:235
  24.5 0.2 collective-permute-done.8.rest_7_
  24.7 0.4 %shard_map.86 = (bf16[128,128]{1,0:T(8,128)(2,1)S(1)}, bf16[128,128]{1,0:T(8,128)(2,1)S(1)}, bf16[128,128]{1,0:T(8,128)(2,1)S(1)}, bf16[128,128]{1,0:T(8,128)(2,1)S(1)}) custom-call(bf16[128,1024]{1,0:T(8,128)(2,1)S(1)} %shard_map.84.rows_ref, f32[128,512]{1,0:T(8,128)S(1)} %get-tuple-element.37.level_ref, ...), custom_call_target="tpu_custom_call" | custom-call | flops 50331648 | bytes 262144 | tf_op jit(solution)/shard_map/pallas_call | solution.py:277
  25.1 2.4 %collective-permute-start.13 = (bf16[128,128]{1,0:T(8,128)(2,1)S(1)}, bf16[128,128]{1,0:T(8,128)(2,1)S(1)}, u32[]{:S(2)}, u32[]{:S(2)}) collective-permute-start(bf16[128,128]{1,0:T(8,128)(2,1)S(1)} %get-tuple-element.42), channel_id=1, source_target_pairs={{0,3},{1,2},{2,1},{3,0},{4,7},{5,6},{6,5},{7,4},{8,11},{9,10},{10,... | collective-permute-start | bytes 98312 | tf_op jit(solution)/shard_map/ppermute | solution.py:235
  27.5 0.7 %collective-permute-start.14 = (bf16[128,128]{1,0:T(8,128)(2,1)S(1)}, bf16[128,128]{1,0:T(8,128)(2,1)S(1)}, u32[]{:S(2)}, u32[]{:S(2)}) collective-permute-start(bf16[128,128]{1,0:T(8,128)(2,1)S(1)} %get-tuple-element.43), channel_id=1, source_target_pairs={{0,2},{1,3},{2,0},{3,1},{4,6},{5,7},{6,4},{7,5},{8,10},{9,11},{10,... | collective-permute-start | bytes 98312 | tf_op jit(solution)/shard_map/ppermute | solution.py:235
  28.2 0.5 %collective-permute-start.15 = (bf16[128,128]{1,0:T(8,128)(2,1)S(1)}, bf16[128,128]{1,0:T(8,128)(2,1)S(1)}, u32[]{:S(2)}, u32[]{:S(2)}) collective-permute-start(bf16[128,128]{1,0:T(8,128)(2,1)S(1)} %get-tuple-element.44), channel_id=1, source_target_pairs={{0,1},{1,0},{2,3},{3,2},{4,5},{5,4},{6,7},{7,6},{8,9},{9,8},{10,11... | collective-permute-start | bytes 98312 | tf_op jit(solution)/shard_map/ppermute | solution.py:235
  28.7 2.3 %shard_map.87 = (bf16[1024,512]{1,0:T(8,128)(2,1)S(1)}, bf16[1024,128]{1,0:T(8,128)(2,1)S(1)}) custom-call(bf16[1024,1024]{1,0:T(8,128)(2,1)S(1)} %get-tuple-element.25.inverse_ref, s32[1,1024]{1,0:T(1,128)S(1)} %get-tuple-element.26.order_ref, bf16[1024,256]{1,0:T(8,128)(2,1)S(1)} %get-tuple-element.27.pair_ref, ...), custom_call_target="tpu_custom_call" | custom-call | flops 1879048192 | bytes 4194304 | tf_op jit(solution)/shard_map/pallas_call | solution.py:285
  31.0 0.0 collective-permute-done.13.rest_0_
  31.0 0.4 %collective-permute-done.14.rest_1_ = bf16[128,128]{1,0:T(8,128)(2,1)S(1)} collective-permute-done((bf16[128,128]{1,0:T(8,128)(2,1)S(1)}, bf16[128,128]{1,0:T(8,128)(2,1)S(1)}, u32[]{:S(2)}, u32[]{:S(2)}) %collective-permute-start.14) | collective-permute-done | bytes 32800 | tf_op jit(solution)/shard_map/ppermute | solution.py:235
  31.4 0.7 %collective-permute-done.15.rest_2_ = bf16[128,128]{1,0:T(8,128)(2,1)S(1)} collective-permute-done((bf16[128,128]{1,0:T(8,128)(2,1)S(1)}, bf16[128,128]{1,0:T(8,128)(2,1)S(1)}, u32[]{:S(2)}, u32[]{:S(2)}) %collective-permute-start.15) | collective-permute-done | bytes 32800 | tf_op jit(solution)/shard_map/ppermute | solution.py:235
  32.1 1.2 %shard_map.88 = bf16[1024,512]{1,0:T(8,128)(2,1)} custom-call(bf16[1024,512]{1,0:T(8,128)(2,1)S(1)} %get-tuple-element.40.applied_ref, bf16[1024,128]{1,0:T(8,128)(2,1)S(1)} %get-tuple-element.41.down_ref, bf16[128,128]{1,0:T(8,128)(2,1)S(1)} %collective-permute-done.13.rest_0_, bf16[128,128]{1,0:T(8,128)(2,1)S(1)} %collective-permute-done.14.rest_1_, ...), custom_call_target="tpu_custom_call" | custom-call | flops 134217728 | bytes 2097152 | tf_op jit(solution)/shard_map/pallas_call | solution.py:292
Async XLA Ops:
  3.4 10.4 %collective-permute-start.3 = (bf16[512,128]{1,0:T(8,128)(2,1)S(1)}, bf16[512,128]{1,0:T(8,128)(2,1)S(1)}, u32[]{:S(2)}, u32[]{:S(2)}) collective-permute-start(bf16[512,128]{1,0:T(8,128)(2,1)S(1)} %get-tuple-element.34), channel_id=1, source_target_pairs={{0,3},{1,2},{2,1},{3,0},{4,7},{5,6},{6,5},{7,4},{8,11},{9,10},{10,... | collective-permute-start | bytes 393224 | tf_op jit(solution)/shard_map/ppermute | solution.py:235
  7.3 6.8 %collective-permute-start.4 = (bf16[512,128]{1,0:T(8,128)(2,1)S(1)}, bf16[512,128]{1,0:T(8,128)(2,1)S(1)}, u32[]{:S(2)}, u32[]{:S(2)}) collective-permute-start(bf16[512,128]{1,0:T(8,128)(2,1)S(1)} %get-tuple-element.35), channel_id=1, source_target_pairs={{0,2},{1,3},{2,0},{3,1},{4,6},{5,7},{6,4},{7,5},{8,10},{9,11},{10,... | collective-permute-start | bytes 393224 | tf_op jit(solution)/shard_map/ppermute | solution.py:235
  7.8 6.6 %collective-permute-start.5 = (bf16[512,128]{1,0:T(8,128)(2,1)S(1)}, bf16[512,128]{1,0:T(8,128)(2,1)S(1)}, u32[]{:S(2)}, u32[]{:S(2)}) collective-permute-start(bf16[512,128]{1,0:T(8,128)(2,1)S(1)} %get-tuple-element.36), channel_id=1, source_target_pairs={{0,1},{1,0},{2,3},{3,2},{4,5},{5,4},{6,7},{7,6},{8,9},{9,8},{10,11... | collective-permute-start | bytes 393224 | tf_op jit(solution)/shard_map/ppermute | solution.py:235
  10.3 8.2 %collective-permute-start.2 = (bf16[32,1024]{1,0:T(8,128)(2,1)S(1)}, bf16[32,1024]{1,0:T(8,128)(2,1)S(1)}, u32[]{:S(2)}, u32[]{:S(2)}) collective-permute-start(bf16[32,1024]{1,0:T(8,128)(2,1)S(1)} %get-tuple-element.32.rest_0_), channel_id=1, source_target_pairs={{0,3},{1,2},{2,1},{3,0},{4,7},{5,6},{6,5},{7,4},{8,11},{9,10},{10,... | collective-permute-start | bytes 196616 | tf_op jit(solution)/shard_map/ppermute | solution.py:235
  13.2 6.0 %collective-permute-start.1 = (bf16[32,1024]{1,0:T(8,128)(2,1)S(1)}, bf16[32,1024]{1,0:T(8,128)(2,1)S(1)}, u32[]{:S(2)}, u32[]{:S(2)}) collective-permute-start(bf16[32,1024]{1,0:T(8,128)(2,1)S(1)} %get-tuple-element.32.rest_0_), channel_id=1, source_target_pairs={{0,2},{1,3},{2,0},{3,1},{4,6},{5,7},{6,4},{7,5},{8,10},{9,11},{10,... | collective-permute-start | bytes 196616 | tf_op jit(solution)/shard_map/ppermute | solution.py:235
  13.7 10.1 %collective-permute-start = (bf16[32,1024]{1,0:T(8,128)(2,1)S(1)}, bf16[32,1024]{1,0:T(8,128)(2,1)S(1)}, u32[]{:S(2)}, u32[]{:S(2)}) collective-permute-start(bf16[32,1024]{1,0:T(8,128)(2,1)S(1)} %get-tuple-element.32.rest_0_), channel_id=1, source_target_pairs={{0,1},{1,0},{2,3},{3,2},{4,5},{5,4},{6,7},{7,6},{8,9},{9,8},{10,11... | collective-permute-start | bytes 196616 | tf_op jit(solution)/shard_map/ppermute | solution.py:235
  14.8 5.8 %collective-permute-start.11 = (bf16[128,128]{1,0:T(8,128)(2,1)S(1)}, bf16[128,128]{1,0:T(8,128)(2,1)S(1)}, u32[]{:S(2)}, u32[]{:S(2)}) collective-permute-start(bf16[128,128]{1,0:T(8,128)(2,1)S(1)} %get-tuple-element.38.rest_4_), channel_id=1, source_target_pairs={{0,24},{4,28},{8,16},{12,20},{16,8},{20,12},{24,0},{28,4},{1,25},{... | collective-permute-start | bytes 98312 | tf_op jit(solution)/shard_map/ppermute | solution.py:235
  18.5 4.8 %collective-permute-start.9 = (bf16[128,128]{1,0:T(8,128)(2,1)S(1)}, bf16[128,128]{1,0:T(8,128)(2,1)S(1)}, u32[]{:S(2)}, u32[]{:S(2)}) collective-permute-start(bf16[128,128]{1,0:T(8,128)(2,1)S(1)} %get-tuple-element.38.rest_4_), channel_id=1, source_target_pairs={{0,16},{4,20},{8,24},{12,28},{16,0},{20,4},{24,8},{28,12},{1,17},{... | collective-permute-start | bytes 98312 | tf_op jit(solution)/shard_map/ppermute | solution.py:235
  18.5 4.8 %collective-permute-start.7 = (bf16[128,128]{1,0:T(8,128)(2,1)S(1)}, bf16[128,128]{1,0:T(8,128)(2,1)S(1)}, u32[]{:S(2)}, u32[]{:S(2)}) collective-permute-start(bf16[128,128]{1,0:T(8,128)(2,1)S(1)} %get-tuple-element.38.rest_4_), channel_id=1, source_target_pairs={{0,8},{4,12},{8,0},{12,4},{16,24},{20,28},{24,16},{28,20},{1,9},{5... | collective-permute-start | bytes 98312 | tf_op jit(solution)/shard_map/ppermute | solution.py:235
  19.3 4.7 %collective-permute-start.6 = (bf16[128,128]{1,0:T(8,128)(2,1)S(1)}, bf16[128,128]{1,0:T(8,128)(2,1)S(1)}, u32[]{:S(2)}, u32[]{:S(2)}) collective-permute-start(bf16[128,128]{1,0:T(8,128)(2,1)S(1)} %get-tuple-element.38.rest_4_), channel_id=1, source_target_pairs={{0,4},{4,0},{8,12},{12,8},{16,20},{20,16},{24,28},{28,24},{1,5},{5... | collective-permute-start | bytes 98312 | tf_op jit(solution)/shard_map/ppermute | solution.py:235
  20.6 3.4 %collective-permute-start.12 = (bf16[128,128]{1,0:T(8,128)(2,1)S(1)}, bf16[128,128]{1,0:T(8,128)(2,1)S(1)}, u32[]{:S(2)}, u32[]{:S(2)}) collective-permute-start(bf16[128,128]{1,0:T(8,128)(2,1)S(1)} %collective-permute-done.11.rest_10_), channel_id=1, source_target_pairs={{0,4},{4,0},{8,12},{12,8},{16,20},{20,16},{24,28},{28,24},{1,5},{5... | collective-permute-start | bytes 98312 | tf_op jit(solution)/shard_map/ppermute | solution.py:235
  23.3 1.2 %collective-permute-start.10 = (bf16[128,128]{1,0:T(8,128)(2,1)S(1)}, bf16[128,128]{1,0:T(8,128)(2,1)S(1)}, u32[]{:S(2)}, u32[]{:S(2)}) collective-permute-start(bf16[128,128]{1,0:T(8,128)(2,1)S(1)} %collective-permute-done.9.rest_8_), channel_id=1, source_target_pairs={{0,4},{4,0},{8,12},{12,8},{16,20},{20,16},{24,28},{28,24},{1,5},{5... | collective-permute-start | bytes 98312 | tf_op jit(solution)/shard_map/ppermute | solution.py:235
  23.3 1.4 %collective-permute-start.8 = (bf16[128,128]{1,0:T(8,128)(2,1)S(1)}, bf16[128,128]{1,0:T(8,128)(2,1)S(1)}, u32[]{:S(2)}, u32[]{:S(2)}) collective-permute-start(bf16[128,128]{1,0:T(8,128)(2,1)S(1)} %collective-permute-done.7.rest_6_), channel_id=1, source_target_pairs={{0,4},{4,0},{8,12},{12,8},{16,20},{20,16},{24,28},{28,24},{1,5},{5... | collective-permute-start | bytes 98312 | tf_op jit(solution)/shard_map/ppermute | solution.py:235
  25.1 5.9 %collective-permute-start.13 = (bf16[128,128]{1,0:T(8,128)(2,1)S(1)}, bf16[128,128]{1,0:T(8,128)(2,1)S(1)}, u32[]{:S(2)}, u32[]{:S(2)}) collective-permute-start(bf16[128,128]{1,0:T(8,128)(2,1)S(1)} %get-tuple-element.42), channel_id=1, source_target_pairs={{0,3},{1,2},{2,1},{3,0},{4,7},{5,6},{6,5},{7,4},{8,11},{9,10},{10,... | collective-permute-start | bytes 98312 | tf_op jit(solution)/shard_map/ppermute | solution.py:235
  27.5 3.9 %collective-permute-start.14 = (bf16[128,128]{1,0:T(8,128)(2,1)S(1)}, bf16[128,128]{1,0:T(8,128)(2,1)S(1)}, u32[]{:S(2)}, u32[]{:S(2)}) collective-permute-start(bf16[128,128]{1,0:T(8,128)(2,1)S(1)} %get-tuple-element.43), channel_id=1, source_target_pairs={{0,2},{1,3},{2,0},{3,1},{4,6},{5,7},{6,4},{7,5},{8,10},{9,11},{10,... | collective-permute-start | bytes 98312 | tf_op jit(solution)/shard_map/ppermute | solution.py:235
  28.2 3.9 %collective-permute-start.15 = (bf16[128,128]{1,0:T(8,128)(2,1)S(1)}, bf16[128,128]{1,0:T(8,128)(2,1)S(1)}, u32[]{:S(2)}, u32[]{:S(2)}) collective-permute-start(bf16[128,128]{1,0:T(8,128)(2,1)S(1)} %get-tuple-element.44), channel_id=1, source_target_pairs={{0,1},{1,0},{2,3},{3,2},{4,5},{5,4},{6,7},{7,6},{8,9},{9,8},{10,11... | collective-permute-start | bytes 98312 | tf_op jit(solution)/shard_map/ppermute | solution.py:235

commit v11 on v6

--- a/solution.py
+++ b/solution.py
@@ -160,7 +160,7 @@
 
 
 def top_rows_kernel(n, groups, *rest):
-    tops, (rows_ref, held) = rest[:n], rest[n:]
+    tops, (rows_ref, held) = rest[:n][::-1], rest[n:]
     me = lax.axis_index("ba")
     mine = lax.axis_index("aa")
     part = tops[0].shape[0]
@@ -186,7 +186,7 @@
 
 
 def final_kernel(n, applied_ref, down_ref, *rest):
-    pieces, (out_hbm, correction, out_ref, sems) = rest[:n], rest[n:]
+    pieces, (out_hbm, correction, out_ref, sems) = rest[:n][::-1], rest[n:]
     me = lax.axis_index("ba")
     share = pieces[0].shape[0]
     for k in range(n):
@@ -284,7 +284,7 @@
         [vmem] * n,
         scratch=[pltpu.VMEM((rank, groups * rank), F32)],
         moved=4 * rank * groups * rank,
-    )(*tops)
+    )(*tops[::-1])
     corrections = call(
         functools.partial(top_kernel, n, groups),
         [shape((share, rank))] * n,
@@ -308,7 +308,7 @@
         scratch=[pltpu.VMEM((cols, rank), BF), pltpu.VMEM((points, cols), BF), pltpu.SemaphoreType.DMA((PIECES,))],
         flops=2 * points * cols * rank,
         moved=4 * points * cols,
-    )(applied, down, *back)
+    )(applied, down, *back[::-1])
 
 
 def solution(mesh):

time: 34.5 us -> 34.1 us (0.988)
  waiting for transfers between devices: 6.14 us -> 4.37 us
  starting transfers between devices: 17.8 us -> 19.1 us
    ppermute x16, waiting for transfers between devices: 6.14 us -> 4.37 us  [swap(): return lax.ppermute(array, axis, [(i, i ^ k) for i in range(size)])]
    ppermute x16, starting transfers between devices: 17.8 us -> 19.1 us  [swap(): return lax.ppermute(array, axis, [(i, i ^ k) for i in range(size)])]
  transfers between devices with their start and end apart: 16 -> 16, of which waited for: 7 -> 5; matrix products, arithmetic and copies ran while one was open for 0% -> 0% of each run, Pallas kernels for 16% -> 16%
where the time goes in v11:
time: 34.1 us; the launch traced here: 33.9 us
  starting transfers between devices  19.1 us (56%)
  Pallas kernels  10.4 us (30%)
  waiting for transfers between devices  4.37 us (13%)
    ppermute x16, starting transfers between devices, swap(): return lax.ppermute(array, axis, [(i, i ^ k) for i in range(size)])  19.1 us
    ppermute x16, waiting for transfers between devices, swap(): return lax.ppermute(array, axis, [(i, i ^ k) for i in range(size)])  4.37 us
    pallas_call x1, Pallas kernels, shards(): call(functools.partial(front_kernel, n), [shape((size, rank)) for size in...  3.35 us
    pallas_call x1, Pallas kernels, shards(): call(down_kernel, [shape((points, cols)), shape((points, rank))], [vmem]...  2.32 us
    pallas_call x1, Pallas kernels, shards(): call(ordered_kernel, [shape((points, cols)), shape(top.shape)], [vmem] *...  1.25 us
    pallas_call x1, Pallas kernels, shards(): call(applied_kernel, [shape((points, cols)), shape((share, rank))], [vmem...  1.25 us
    pallas_call x1, Pallas kernels, shards(): call(functools.partial(final_kernel, n), shape((points, cols)), [vmem] *...  1.25 us
  transfers between devices with their start and end apart: 16, of which 5 were waited for; matrix products, arithmetic and copies ran while one was open for 0% of the time, Pallas kernels for 16%

profile of v11, /device:TPU:0, one launch (start us, length us, event | category | flops | bytes accessed | tf_op | source)
XLA Modules:
  0.0 33.9 jit_solution(17087362381233700852)
XLA Ops:
  0.0 3.4 %shard_map.82 = (bf16[512,128]{1,0:T(8,128)(2,1)S(1)}, bf16[512,128]{1,0:T(8,128)(2,1)S(1)}, bf16[512,128]{1,0:T(8,128)(2,1)S(1)}, bf16[768,128]{1,0:T(8,128)(2,...) custom-call(s32[1,1024]{1,0:T(1,128)} %order_hbm.1, ...), custom_call_target="tpu_custom_call" | custom-call | flops 939524096 | bytes 3407872 | tf_op jit(solution)/shard_map/pallas_call | solution.py:242
  3.4 4.0 %collective-permute-start = (bf16[512,128]{1,0:T(8,128)(2,1)S(1)}, bf16[512,128]{1,0:T(8,128)(2,1)S(1)}, u32[]{:S(2)}, u32[]{:S(2)}) collective-permute-start(bf16[512,128]{1,0:T(8,128)(2,1)S(1)} %get-tuple-element.35), channel_id=1, source_target_pairs={{0,3},{1,2},{2,1},{3,0},{4,7},{5,6},{6,5},{7,4},{8,11},{9,10},{10,... | collective-permute-start | bytes 393224 | tf_op jit(solution)/shard_map/ppermute | solution.py:239
  7.3 0.5 %collective-permute-start.1 = (bf16[512,128]{1,0:T(8,128)(2,1)S(1)}, bf16[512,128]{1,0:T(8,128)(2,1)S(1)}, u32[]{:S(2)}, u32[]{:S(2)}) collective-permute-start(bf16[512,128]{1,0:T(8,128)(2,1)S(1)} %get-tuple-element.36), channel_id=1, source_target_pairs={{0,2},{1,3},{2,0},{3,1},{4,6},{5,7},{6,4},{7,5},{8,10},{9,11},{10,... | collective-permute-start | bytes 393224 | tf_op jit(solution)/shard_map/ppermute | solution.py:239
  7.8 0.1 collective-permute-start.2
  8.0 1.2 %shard_map.83 = (bf16[1024,512]{1,0:T(8,128)(2,1)S(1)}, bf16[32,1024]{1,0:T(8,128)(2,1)S(1)}) custom-call(bf16[1024,512]{1,0:T(8,128)(2,1)S(1)} %get-tuple-element.30.sides_ref, bf16[1024,1024]{1,0:T(8,128)(2,1)S(1)} %get-tuple-element.31.gather_ref, bf16[32,1024]{1,0:T(8,128)(2,1)S(1)} %get-tuple-element.32.top_ref), custom_call_target="tpu_custom_call" | custom-call | flops 1073741824 | bytes 4194304 | tf_op jit(solution)/shard_map/pallas_call | solution.py:254
  9.2 2.0 %collective-permute-start.5 = (bf16[32,1024]{1,0:T(8,128)(2,1)S(1)}, bf16[32,1024]{1,0:T(8,128)(2,1)S(1)}, u32[]{:S(2)}, u32[]{:S(2)}) collective-permute-start(bf16[32,1024]{1,0:T(8,128)(2,1)S(1)} %get-tuple-element.40.rest_3_), channel_id=1, source_target_pairs={{0,1},{1,0},{2,3},{3,2},{4,5},{5,4},{6,7},{7,6},{8,9},{9,8},{10,11... | collective-permute-start | bytes 196616 | tf_op jit(solution)/shard_map/ppermute | solution.py:239
  11.2 1.5 %collective-permute-start.4 = (bf16[32,1024]{1,0:T(8,128)(2,1)S(1)}, bf16[32,1024]{1,0:T(8,128)(2,1)S(1)}, u32[]{:S(2)}, u32[]{:S(2)}) collective-permute-start(bf16[32,1024]{1,0:T(8,128)(2,1)S(1)} %get-tuple-element.40.rest_3_), channel_id=1, source_target_pairs={{0,2},{1,3},{2,0},{3,1},{4,6},{5,7},{6,4},{7,5},{8,10},{9,11},{10,... | collective-permute-start | bytes 196616 | tf_op jit(solution)/shard_map/ppermute | solution.py:239
  12.7 0.0 collective-permute-done.rest_0_.rest_3_
  12.7 1.9 %collective-permute-start.3 = (bf16[32,1024]{1,0:T(8,128)(2,1)S(1)}, bf16[32,1024]{1,0:T(8,128)(2,1)S(1)}, u32[]{:S(2)}, u32[]{:S(2)}) collective-permute-start(bf16[32,1024]{1,0:T(8,128)(2,1)S(1)} %get-tuple-element.40.rest_3_), channel_id=1, source_target_pairs={{0,3},{1,2},{2,1},{3,0},{4,7},{5,6},{6,5},{7,4},{8,11},{9,10},{10,... | collective-permute-start | bytes 196616 | tf_op jit(solution)/shard_map/ppermute | solution.py:239
  14.6 0.0 collective-permute-done.1.rest_1_.rest_2_
  14.6 0.4 %collective-permute-done.2.rest_2_.rest_1_ = bf16[512,128]{1,0:T(8,128)(2,1)S(1)} collective-permute-done((bf16[512,128]{1,0:T(8,128)(2,1)S(1)}, bf16[512,128]{1,0:T(8,128)(2,1)S(1)}, u32[]{:S(2)}, u32[]{:S(2)}) %collective-permute-start.2) | collective-permute-done | bytes 131104 | tf_op jit(solution)/shard_map/ppermute | solution.py:239
  15.0 0.4 %shard_map.84 = (f32[128,512]{1,0:T(8,128)S(1)}, bf16[128,128]{1,0:T(8,128)(2,1)S(1)}) custom-call(bf16[1024,512]{1,0:T(8,128)(2,1)S(1)} %get-tuple-element.33.after.ordered_ref, bf16[768,128]{1,0:T(8,128)(2,1)S(1)} %get-tuple-element.34.own_ref.rest_0_, bf16[512,128]{1,0:T(8,128)(2,1)S(1)} %collective-permute-done.rest_0_.rest_3_, ...), custom_call_target="tpu_custom_call" | custom-call | flops 83886080 | bytes 262144 | tf_op jit(solution)/shard_map/pallas_call | solution.py:262
  15.5 3.7 %collective-permute-start.11 = (bf16[128,128]{1,0:T(8,128)(2,1)S(1)}, bf16[128,128]{1,0:T(8,128)(2,1)S(1)}, u32[]{:S(2)}, u32[]{:S(2)}) collective-permute-start(bf16[128,128]{1,0:T(8,128)(2,1)S(1)} %get-tuple-element.38.group_ref.rest_4_), channel_id=1, source_target_pairs={{0,24},{4,28},{8,16},{12,20},{16,8},{20,12},{24,0},{28,4},{1,25},{... | collective-permute-start | bytes 98312 | tf_op jit(solution)/shard_map/ppermute | solution.py:239
  19.2 0.0 collective-permute-start.9
  19.2 0.0 collective-permute-done.5.rest_2_
  19.2 0.8 %collective-permute-start.7 = (bf16[128,128]{1,0:T(8,128)(2,1)S(1)}, bf16[128,128]{1,0:T(8,128)(2,1)S(1)}, u32[]{:S(2)}, u32[]{:S(2)}) collective-permute-start(bf16[128,128]{1,0:T(8,128)(2,1)S(1)} %get-tuple-element.38.group_ref.rest_4_), channel_id=1, source_target_pairs={{0,8},{4,12},{8,0},{12,4},{16,24},{20,28},{24,16},{28,20},{1,9},{5... | collective-permute-start | bytes 98312 | tf_op jit(solution)/shard_map/ppermute | solution.py:239
  19.9 1.2 %shard_map.85 = (bf16[1024,512]{1,0:T(8,128)(2,1)S(1)}, bf16[128,128]{1,0:T(8,128)(2,1)S(1)}) custom-call(bf16[1024,1024]{1,0:T(8,128)(2,1)S(1)} %get-tuple-element.27.inverse_ref, bf16[1024,512]{1,0:T(8,128)(2,1)S(1)} %get-tuple-element.33.after.ordered_ref, bf16[128,128]{1,0:T(8,128)(2,1)S(1)} %get-tuple-element.38.group_ref.rest_4_), custom_call_target="tpu_custom_call" | custom-call | flops 1073741824 | bytes 4194304 | tf_op jit(solution)/shard_map/pallas_call | solution.py:269
  21.2 0.0 collective-permute-done.4.rest_1_
  21.2 0.1 collective-permute-start.6
  21.3 0.0 collective-permute-done.11.rest_10_
  21.3 0.5 %collective-permute-start.12 = (bf16[128,128]{1,0:T(8,128)(2,1)S(1)}, bf16[128,128]{1,0:T(8,128)(2,1)S(1)}, u32[]{:S(2)}, u32[]{:S(2)}) collective-permute-start(bf16[128,128]{1,0:T(8,128)(2,1)S(1)} %collective-permute-done.11.rest_10_), channel_id=1, source_target_pairs={{0,4},{4,0},{8,12},{12,8},{16,20},{20,16},{24,28},{28,24},{1,5},{5... | collective-permute-start | bytes 98312 | tf_op jit(solution)/shard_map/ppermute | solution.py:239
  21.8 2.2 %collective-permute-done.9.rest_8_ = bf16[128,128]{1,0:T(8,128)(2,1)S(1)} collective-permute-done((bf16[128,128]{1,0:T(8,128)(2,1)S(1)}, bf16[128,128]{1,0:T(8,128)(2,1)S(1)}, u32[]{:S(2)}, u32[]{:S(2)}) %collective-permute-start.9) | collective-permute-done | bytes 32800 | tf_op jit(solution)/shard_map/ppermute | solution.py:239
  24.0 0.0 collective-permute-start.10
  24.0 0.0 collective-permute-done.7.rest_6_
  24.0 0.5 %collective-permute-start.8 = (bf16[128,128]{1,0:T(8,128)(2,1)S(1)}, bf16[128,128]{1,0:T(8,128)(2,1)S(1)}, u32[]{:S(2)}, u32[]{:S(2)}) collective-permute-start(bf16[128,128]{1,0:T(8,128)(2,1)S(1)} %collective-permute-done.7.rest_6_), channel_id=1, source_target_pairs={{0,4},{4,0},{8,12},{12,8},{16,20},{20,16},{24,28},{28,24},{1,5},{5... | collective-permute-start | bytes 98312 | tf_op jit(solution)/shard_map/ppermute | solution.py:239
  24.5 0.0 collective-permute-done.3.rest_0_
  24.5 0.1 shard_map.86.rows_ref
  24.6 0.0 collective-permute-done.6.rest_5_
  24.6 0.0 collective-permute-done.12.rest_11_
  24.6 0.6 %collective-permute-done.10.rest_9_ = bf16[128,128]{1,0:T(8,128)(2,1)S(1)} collective-permute-done((bf16[128,128]{1,0:T(8,128)(2,1)S(1)}, bf16[128,128]{1,0:T(8,128)(2,1)S(1)}, u32[]{:S(2)}, u32[]{:S(2)}) %collective-permute-start.10) | collective-permute-done | bytes 32800 | tf_op jit(solution)/shard_map/ppermute | solution.py:239
  25.2 0.2 collective-permute-done.8.rest_7_
  25.4 0.4 %shard_map.87 = (bf16[128,128]{1,0:T(8,128)(2,1)S(1)}, bf16[128,128]{1,0:T(8,128)(2,1)S(1)}, bf16[128,128]{1,0:T(8,128)(2,1)S(1)}, bf16[128,128]{1,0:T(8,128)(2,1)S(1)}) custom-call(bf16[128,1024]{1,0:T(8,128)(2,1)S(1)} %shard_map.86.rows_ref, f32[128,512]{1,0:T(8,128)S(1)} %get-tuple-element.41.level_ref, ...), custom_call_target="tpu_custom_call" | custom-call | flops 50331648 | bytes 262144 | tf_op jit(solution)/shard_map/pallas_call | solution.py:288
  25.8 1.5 %collective-permute-start.13 = (bf16[128,128]{1,0:T(8,128)(2,1)S(1)}, bf16[128,128]{1,0:T(8,128)(2,1)S(1)}, u32[]{:S(2)}, u32[]{:S(2)}) collective-permute-start(bf16[128,128]{1,0:T(8,128)(2,1)S(1)} %get-tuple-element.46), channel_id=1, source_target_pairs={{0,3},{1,2},{2,1},{3,0},{4,7},{5,6},{6,5},{7,4},{8,11},{9,10},{10,... | collective-permute-start | bytes 98312 | tf_op jit(solution)/shard_map/ppermute | solution.py:239
  27.3 1.5 %collective-permute-start.14 = (bf16[128,128]{1,0:T(8,128)(2,1)S(1)}, bf16[128,128]{1,0:T(8,128)(2,1)S(1)}, u32[]{:S(2)}, u32[]{:S(2)}) collective-permute-start(bf16[128,128]{1,0:T(8,128)(2,1)S(1)} %get-tuple-element.47), channel_id=1, source_target_pairs={{0,2},{1,3},{2,0},{3,1},{4,6},{5,7},{6,4},{7,5},{8,10},{9,11},{10,... | collective-permute-start | bytes 98312 | tf_op jit(solution)/shard_map/ppermute | solution.py:239
  28.8 0.6 %collective-permute-start.15 = (bf16[128,128]{1,0:T(8,128)(2,1)S(1)}, bf16[128,128]{1,0:T(8,128)(2,1)S(1)}, u32[]{:S(2)}, u32[]{:S(2)}) collective-permute-start(bf16[128,128]{1,0:T(8,128)(2,1)S(1)} %get-tuple-element.48), channel_id=1, source_target_pairs={{0,1},{1,0},{2,3},{3,2},{4,5},{5,4},{6,7},{7,6},{8,9},{9,8},{10,11... | collective-permute-start | bytes 98312 | tf_op jit(solution)/shard_map/ppermute | solution.py:239
  29.3 2.3 %shard_map.88 = (bf16[1024,512]{1,0:T(8,128)(2,1)S(1)}, bf16[1024,128]{1,0:T(8,128)(2,1)S(1)}) custom-call(bf16[1024,1024]{1,0:T(8,128)(2,1)S(1)} %get-tuple-element.27.inverse_ref, s32[1,1024]{1,0:T(1,128)S(1)} %get-tuple-element.28.order_ref, bf16[1024,256]{1,0:T(8,128)(2,1)S(1)} %get-tuple-element.29.pair_ref, ...), custom_call_target="tpu_custom_call" | custom-call | flops 1879048192 | bytes 4194304 | tf_op jit(solution)/shard_map/pallas_call | solution.py:296
  31.7 0.0 collective-permute-done.13.rest_0_
  31.7 0.0 collective-permute-done.14.rest_1_
  31.7 1.0 %collective-permute-done.15.rest_2_ = bf16[128,128]{1,0:T(8,128)(2,1)S(1)} collective-permute-done((bf16[128,128]{1,0:T(8,128)(2,1)S(1)}, bf16[128,128]{1,0:T(8,128)(2,1)S(1)}, u32[]{:S(2)}, u32[]{:S(2)}) %collective-permute-start.15) | collective-permute-done | bytes 32800 | tf_op jit(solution)/shard_map/ppermute | solution.py:239
  32.7 1.2 %shard_map.89 = bf16[1024,512]{1,0:T(8,128)(2,1)} custom-call(bf16[1024,512]{1,0:T(8,128)(2,1)S(1)} %get-tuple-element.44.applied_ref, bf16[1024,128]{1,0:T(8,128)(2,1)S(1)} %get-tuple-element.45.down_ref, bf16[128,128]{1,0:T(8,128)(2,1)S(1)} %collective-permute-done.13.rest_0_, bf16[128,128]{1,0:T(8,128)(2,1)S(1)} %collective-permute-done.14.rest_1_, ...), custom_call_target="tpu_custom_call" | custom-call | flops 134217728 | bytes 2097152 | tf_op jit(solution)/shard_map/pallas_call | solution.py:303
Async XLA Ops:
  3.4 9.4 %collective-permute-start = (bf16[512,128]{1,0:T(8,128)(2,1)S(1)}, bf16[512,128]{1,0:T(8,128)(2,1)S(1)}, u32[]{:S(2)}, u32[]{:S(2)}) collective-permute-start(bf16[512,128]{1,0:T(8,128)(2,1)S(1)} %get-tuple-element.35), channel_id=1, source_target_pairs={{0,3},{1,2},{2,1},{3,0},{4,7},{5,6},{6,5},{7,4},{8,11},{9,10},{10,... | collective-permute-start | bytes 393224 | tf_op jit(solution)/shard_map/ppermute | solution.py:239
  7.3 7.3 %collective-permute-start.1 = (bf16[512,128]{1,0:T(8,128)(2,1)S(1)}, bf16[512,128]{1,0:T(8,128)(2,1)S(1)}, u32[]{:S(2)}, u32[]{:S(2)}) collective-permute-start(bf16[512,128]{1,0:T(8,128)(2,1)S(1)} %get-tuple-element.36), channel_id=1, source_target_pairs={{0,2},{1,3},{2,0},{3,1},{4,6},{5,7},{6,4},{7,5},{8,10},{9,11},{10,... | collective-permute-start | bytes 393224 | tf_op jit(solution)/shard_map/ppermute | solution.py:239
  7.8 7.2 %collective-permute-start.2 = (bf16[512,128]{1,0:T(8,128)(2,1)S(1)}, bf16[512,128]{1,0:T(8,128)(2,1)S(1)}, u32[]{:S(2)}, u32[]{:S(2)}) collective-permute-start(bf16[512,128]{1,0:T(8,128)(2,1)S(1)} %get-tuple-element.37), channel_id=1, source_target_pairs={{0,1},{1,0},{2,3},{3,2},{4,5},{5,4},{6,7},{7,6},{8,9},{9,8},{10,11... | collective-permute-start | bytes 393224 | tf_op jit(solution)/shard_map/ppermute | solution.py:239
  9.2 9.9 %collective-permute-start.5 = (bf16[32,1024]{1,0:T(8,128)(2,1)S(1)}, bf16[32,1024]{1,0:T(8,128)(2,1)S(1)}, u32[]{:S(2)}, u32[]{:S(2)}) collective-permute-start(bf16[32,1024]{1,0:T(8,128)(2,1)S(1)} %get-tuple-element.40.rest_3_), channel_id=1, source_target_pairs={{0,1},{1,0},{2,3},{3,2},{4,5},{5,4},{6,7},{7,6},{8,9},{9,8},{10,11... | collective-permute-start | bytes 196616 | tf_op jit(solution)/shard_map/ppermute | solution.py:239
  11.2 10.0 %collective-permute-start.4 = (bf16[32,1024]{1,0:T(8,128)(2,1)S(1)}, bf16[32,1024]{1,0:T(8,128)(2,1)S(1)}, u32[]{:S(2)}, u32[]{:S(2)}) collective-permute-start(bf16[32,1024]{1,0:T(8,128)(2,1)S(1)} %get-tuple-element.40.rest_3_), channel_id=1, source_target_pairs={{0,2},{1,3},{2,0},{3,1},{4,6},{5,7},{6,4},{7,5},{8,10},{9,11},{10,... | collective-permute-start | bytes 196616 | tf_op jit(solution)/shard_map/ppermute | solution.py:239
  12.7 11.8 %collective-permute-start.3 = (bf16[32,1024]{1,0:T(8,128)(2,1)S(1)}, bf16[32,1024]{1,0:T(8,128)(2,1)S(1)}, u32[]{:S(2)}, u32[]{:S(2)}) collective-permute-start(bf16[32,1024]{1,0:T(8,128)(2,1)S(1)} %get-tuple-element.40.rest_3_), channel_id=1, source_target_pairs={{0,3},{1,2},{2,1},{3,0},{4,7},{5,6},{6,5},{7,4},{8,11},{9,10},{10,... | collective-permute-start | bytes 196616 | tf_op jit(solution)/shard_map/ppermute | solution.py:239
  15.5 5.8 %collective-permute-start.11 = (bf16[128,128]{1,0:T(8,128)(2,1)S(1)}, bf16[128,128]{1,0:T(8,128)(2,1)S(1)}, u32[]{:S(2)}, u32[]{:S(2)}) collective-permute-start(bf16[128,128]{1,0:T(8,128)(2,1)S(1)} %get-tuple-element.38.group_ref.rest_4_), channel_id=1, source_target_pairs={{0,24},{4,28},{8,16},{12,20},{16,8},{20,12},{24,0},{28,4},{1,25},{... | collective-permute-start | bytes 98312 | tf_op jit(solution)/shard_map/ppermute | solution.py:239
  19.2 4.8 %collective-permute-start.9 = (bf16[128,128]{1,0:T(8,128)(2,1)S(1)}, bf16[128,128]{1,0:T(8,128)(2,1)S(1)}, u32[]{:S(2)}, u32[]{:S(2)}) collective-permute-start(bf16[128,128]{1,0:T(8,128)(2,1)S(1)} %get-tuple-element.38.group_ref.rest_4_), channel_id=1, source_target_pairs={{0,16},{4,20},{8,24},{12,28},{16,0},{20,4},{24,8},{28,12},{1,17},{... | collective-permute-start | bytes 98312 | tf_op jit(solution)/shard_map/ppermute | solution.py:239
  19.2 4.8 %collective-permute-start.7 = (bf16[128,128]{1,0:T(8,128)(2,1)S(1)}, bf16[128,128]{1,0:T(8,128)(2,1)S(1)}, u32[]{:S(2)}, u32[]{:S(2)}) collective-permute-start(bf16[128,128]{1,0:T(8,128)(2,1)S(1)} %get-tuple-element.38.group_ref.rest_4_), channel_id=1, source_target_pairs={{0,8},{4,12},{8,0},{12,4},{16,24},{20,28},{24,16},{28,20},{1,9},{5... | collective-permute-start | bytes 98312 | tf_op jit(solution)/shard_map/ppermute | solution.py:239
  21.2 3.4 %collective-permute-start.6 = (bf16[128,128]{1,0:T(8,128)(2,1)S(1)}, bf16[128,128]{1,0:T(8,128)(2,1)S(1)}, u32[]{:S(2)}, u32[]{:S(2)}) collective-permute-start(bf16[128,128]{1,0:T(8,128)(2,1)S(1)} %get-tuple-element.42), channel_id=1, source_target_pairs={{0,4},{4,0},{8,12},{12,8},{16,20},{20,16},{24,28},{28,24},{1,5},{5... | collective-permute-start | bytes 98312 | tf_op jit(solution)/shard_map/ppermute | solution.py:239
  21.3 3.3 %collective-permute-start.12 = (bf16[128,128]{1,0:T(8,128)(2,1)S(1)}, bf16[128,128]{1,0:T(8,128)(2,1)S(1)}, u32[]{:S(2)}, u32[]{:S(2)}) collective-permute-start(bf16[128,128]{1,0:T(8,128)(2,1)S(1)} %collective-permute-done.11.rest_10_), channel_id=1, source_target_pairs={{0,4},{4,0},{8,12},{12,8},{16,20},{20,16},{24,28},{28,24},{1,5},{5... | collective-permute-start | bytes 98312 | tf_op jit(solution)/shard_map/ppermute | solution.py:239
  24.0 1.2 %collective-permute-start.10 = (bf16[128,128]{1,0:T(8,128)(2,1)S(1)}, bf16[128,128]{1,0:T(8,128)(2,1)S(1)}, u32[]{:S(2)}, u32[]{:S(2)}) collective-permute-start(bf16[128,128]{1,0:T(8,128)(2,1)S(1)} %collective-permute-done.9.rest_8_), channel_id=1, source_target_pairs={{0,4},{4,0},{8,12},{12,8},{16,20},{20,16},{24,28},{28,24},{1,5},{5... | collective-permute-start | bytes 98312 | tf_op jit(solution)/shard_map/ppermute | solution.py:239
  24.0 1.4 %collective-permute-start.8 = (bf16[128,128]{1,0:T(8,128)(2,1)S(1)}, bf16[128,128]{1,0:T(8,128)(2,1)S(1)}, u32[]{:S(2)}, u32[]{:S(2)}) collective-permute-start(bf16[128,128]{1,0:T(8,128)(2,1)S(1)} %collective-permute-done.7.rest_6_), channel_id=1, source_target_pairs={{0,4},{4,0},{8,12},{12,8},{16,20},{20,16},{24,28},{28,24},{1,5},{5... | collective-permute-start | bytes 98312 | tf_op jit(solution)/shard_map/ppermute | solution.py:239
  25.8 5.9 %collective-permute-start.13 = (bf16[128,128]{1,0:T(8,128)(2,1)S(1)}, bf16[128,128]{1,0:T(8,128)(2,1)S(1)}, u32[]{:S(2)}, u32[]{:S(2)}) collective-permute-start(bf16[128,128]{1,0:T(8,128)(2,1)S(1)} %get-tuple-element.46), channel_id=1, source_target_pairs={{0,3},{1,2},{2,1},{3,0},{4,7},{5,6},{6,5},{7,4},{8,11},{9,10},{10,... | collective-permute-start | bytes 98312 | tf_op jit(solution)/shard_map/ppermute | solution.py:239
  27.3 4.4 %collective-permute-start.14 = (bf16[128,128]{1,0:T(8,128)(2,1)S(1)}, bf16[128,128]{1,0:T(8,128)(2,1)S(1)}, u32[]{:S(2)}, u32[]{:S(2)}) collective-permute-start(bf16[128,128]{1,0:T(8,128)(2,1)S(1)} %get-tuple-element.47), channel_id=1, source_target_pairs={{0,2},{1,3},{2,0},{3,1},{4,6},{5,7},{6,4},{7,5},{8,10},{9,11},{10,... | collective-permute-start | bytes 98312 | tf_op jit(solution)/shard_map/ppermute | solution.py:239
  28.8 3.9 %collective-permute-start.15 = (bf16[128,128]{1,0:T(8,128)(2,1)S(1)}, bf16[128,128]{1,0:T(8,128)(2,1)S(1)}, u32[]{:S(2)}, u32[]{:S(2)}) collective-permute-start(bf16[128,128]{1,0:T(8,128)(2,1)S(1)} %get-tuple-element.48), channel_id=1, source_target_pairs={{0,1},{1,0},{2,3},{3,2},{4,5},{5,4},{6,7},{7,6},{8,9},{9,8},{10,11... | collective-permute-start | bytes 98312 | tf_op jit(solution)/shard_map/ppermute | solution.py:239

commit v12 on v10

--- a/solution.py
+++ b/solution.py
@@ -19,8 +19,7 @@
 
 
 def partners(n, k):
-    half = (n - 2) // 2
-    return [(k - 1 + j) % (n - 1) + 1 for j in range(1, half + 1)]
+    return [m for m in range(1, n) if (m.bit_count(), -m) > (k.bit_count(), -k)]
 
 
 def column_of(row, count):

time: 33.5 us -> 35 us (1.045)
  starting transfers between devices: 16.7 us -> 17.5 us
  waiting for transfers between devices: 6.39 us -> 7.09 us
    ppermute x16, starting transfers between devices: 16.7 us -> 17.5 us  [swap(): return lax.ppermute(array, axis, [(i, i ^ k) for i in range(size)])]
    ppermute x16, waiting for transfers between devices: 6.39 us -> 7.09 us  [swap(): return lax.ppermute(array, axis, [(i, i ^ k) for i in range(size)])]
  transfers between devices with their start and end apart: 16 -> 16, of which waited for: 8 -> 7; matrix products, arithmetic and copies ran while one was open for 0% -> 0% of each run, Pallas kernels for 16% -> 15%
where the time goes in v12:
time: 35 us; the launch traced here: 34.9 us
  starting transfers between devices  17.5 us (50%)
  Pallas kernels  10.2 us (29%)
  waiting for transfers between devices  7.09 us (20%)
    ppermute x16, starting transfers between devices, swap(): return lax.ppermute(array, axis, [(i, i ^ k) for i in range(size)])  17.5 us
    ppermute x16, waiting for transfers between devices, swap(): return lax.ppermute(array, axis, [(i, i ^ k) for i in range(size)])  7.09 us
    pallas_call x1, Pallas kernels, shards(): call(functools.partial(front_kernel, n), [shape((size, rank)) for size in...  3.35 us
    pallas_call x1, Pallas kernels, shards(): call(applied_kernel, [shape((points, cols)), shape(top.shape)], [vmem] *...  2.33 us
    pallas_call x1, Pallas kernels, shards(): call(down_kernel, [shape((points, cols)), shape((points, rank))], [vmem]...  2.33 us
    pallas_call x1, Pallas kernels, shards(): call(functools.partial(final_kernel, n), shape((points, cols)), [vmem] *...  1.24 us
  transfers between devices with their start and end apart: 16, of which 7 were waited for; matrix products, arithmetic and copies ran while one was open for 0% of the time, Pallas kernels for 15%

profile of v12, /device:TPU:0, one launch (start us, length us, event | category | flops | bytes accessed | tf_op | source)
XLA Modules:
  0.0 34.9 jit_solution(1570454023502339139)
XLA Ops:
  0.0 3.4 %shard_map.82 = (bf16[512,128]{1,0:T(8,128)(2,1)S(1)}, bf16[640,128]{1,0:T(8,128)(2,1)S(1)}, bf16[384,128]{1,0:T(8,128)(2,1)S(1)}, bf16[768,128]{1,0:T(8,128)(2,...) custom-call(s32[1,1024]{1,0:T(1,128)} %order_hbm.1, ...), custom_call_target="tpu_custom_call" | custom-call | flops 939524096 | bytes 3407872 | tf_op jit(solution)/shard_map/pallas_call | solution.py:237
  3.4 4.0 %collective-permute-start.3 = (bf16[384,128]{1,0:T(8,128)(2,1)S(1)}, bf16[384,128]{1,0:T(8,128)(2,1)S(1)}, u32[]{:S(2)}, u32[]{:S(2)}) collective-permute-start(bf16[384,128]{1,0:T(8,128)(2,1)S(1)} %get-tuple-element.34), channel_id=1, source_target_pairs={{0,3},{1,2},{2,1},{3,0},{4,7},{5,6},{6,5},{7,4},{8,11},{9,10},{10,... | collective-permute-start | bytes 294920 | tf_op jit(solution)/shard_map/ppermute | solution.py:234
  7.3 0.5 %collective-permute-start.5 = (bf16[512,128]{1,0:T(8,128)(2,1)S(1)}, bf16[512,128]{1,0:T(8,128)(2,1)S(1)}, u32[]{:S(2)}, u32[]{:S(2)}) collective-permute-start(bf16[512,128]{1,0:T(8,128)(2,1)S(1)} %get-tuple-element.36), channel_id=1, source_target_pairs={{0,1},{1,0},{2,3},{3,2},{4,5},{5,4},{6,7},{7,6},{8,9},{9,8},{10,11... | collective-permute-start | bytes 393224 | tf_op jit(solution)/shard_map/ppermute | solution.py:234
  7.9 0.1 collective-permute-start.4
  8.0 2.3 %shard_map.83 = (bf16[1024,512]{1,0:T(8,128)(2,1)S(1)}, bf16[32,1024]{1,0:T(8,128)(2,1)S(1)}) custom-call(bf16[1024,512]{1,0:T(8,128)(2,1)S(1)} %get-tuple-element.28.sides_ref, bf16[1024,1024]{1,0:T(8,128)(2,1)S(1)} %get-tuple-element.25.inverse_ref, bf16[1024,1024]{1,0:T(8,128)(2,1)S(1)} %get-tuple-element.29.gather_ref, ...), custom_call_target="tpu_custom_call" | custom-call | flops 2147483648 | bytes 4194304 | tf_op jit(solution)/shard_map/pallas_call | solution.py:249
  10.3 2.9 %collective-permute-start.2 = (bf16[32,1024]{1,0:T(8,128)(2,1)S(1)}, bf16[32,1024]{1,0:T(8,128)(2,1)S(1)}, u32[]{:S(2)}, u32[]{:S(2)}) collective-permute-start(bf16[32,1024]{1,0:T(8,128)(2,1)S(1)} %get-tuple-element.32.rest_0_), channel_id=1, source_target_pairs={{0,3},{1,2},{2,1},{3,0},{4,7},{5,6},{6,5},{7,4},{8,11},{9,10},{10,... | collective-permute-start | bytes 196616 | tf_op jit(solution)/shard_map/ppermute | solution.py:234
  13.2 0.5 %collective-permute-start.1 = (bf16[32,1024]{1,0:T(8,128)(2,1)S(1)}, bf16[32,1024]{1,0:T(8,128)(2,1)S(1)}, u32[]{:S(2)}, u32[]{:S(2)}) collective-permute-start(bf16[32,1024]{1,0:T(8,128)(2,1)S(1)} %get-tuple-element.32.rest_0_), channel_id=1, source_target_pairs={{0,2},{1,3},{2,0},{3,1},{4,6},{5,7},{6,4},{7,5},{8,10},{9,11},{10,... | collective-permute-start | bytes 196616 | tf_op jit(solution)/shard_map/ppermute | solution.py:234
  13.7 0.0 collective-permute-done.3.rest_0_.rest_3_
  13.7 0.2 collective-permute-start
  13.9 0.0 collective-permute-done.5.rest_2_.rest_1_
  13.9 0.6 %collective-permute-done.4.rest_1_.rest_2_ = bf16[640,128]{1,0:T(8,128)(2,1)S(1)} collective-permute-done((bf16[640,128]{1,0:T(8,128)(2,1)S(1)}, bf16[640,128]{1,0:T(8,128)(2,1)S(1)}, u32[]{:S(2)}, u32[]{:S(2)}) %collective-permute-start.4) | collective-permute-done | bytes 163872 | tf_op jit(solution)/shard_map/ppermute | solution.py:234
  14.5 0.4 %shard_map.85 = (f32[128,512]{1,0:T(8,128)S(1)}, bf16[128,128]{1,0:T(8,128)(2,1)S(1)}) custom-call(bf16[1024,512]{1,0:T(8,128)(2,1)S(1)} %get-tuple-element.31.after.applied_ref, bf16[768,128]{1,0:T(8,128)(2,1)S(1)} %get-tuple-element.33.own_ref.rest_0_, bf16[384,128]{1,0:T(8,128)(2,1)S(1)} %collective-permute-done.3.rest_0_.rest_3_, ...), custom_call_target="tpu_custom_call" | custom-call | flops 83886080 | bytes 262144 | tf_op jit(solution)/shard_map/pallas_call | solution.py:257
  14.9 4.1 %collective-permute-start.11 = (bf16[128,128]{1,0:T(8,128)(2,1)S(1)}, bf16[128,128]{1,0:T(8,128)(2,1)S(1)}, u32[]{:S(2)}, u32[]{:S(2)}) collective-permute-start(bf16[128,128]{1,0:T(8,128)(2,1)S(1)} %get-tuple-element.38.rest_4_), channel_id=1, source_target_pairs={{0,24},{4,28},{8,16},{12,20},{16,8},{20,12},{24,0},{28,4},{1,25},{... | collective-permute-start | bytes 98312 | tf_op jit(solution)/shard_map/ppermute | solution.py:234
  19.0 0.0 collective-permute-start.9
  19.0 0.0 collective-permute-done.2.rest_3_
  19.1 0.6 %collective-permute-start.7 = (bf16[128,128]{1,0:T(8,128)(2,1)S(1)}, bf16[128,128]{1,0:T(8,128)(2,1)S(1)}, u32[]{:S(2)}, u32[]{:S(2)}) collective-permute-start(bf16[128,128]{1,0:T(8,128)(2,1)S(1)} %get-tuple-element.38.rest_4_), channel_id=1, source_target_pairs={{0,8},{4,12},{8,0},{12,4},{16,24},{20,28},{24,16},{28,20},{1,9},{5... | collective-permute-start | bytes 98312 | tf_op jit(solution)/shard_map/ppermute | solution.py:234
  19.7 0.0 collective-permute-done.1.rest_2_
  19.7 0.0 collective-permute-start.6
  19.7 1.3 %collective-permute-done.11.rest_10_ = bf16[128,128]{1,0:T(8,128)(2,1)S(1)} collective-permute-done((bf16[128,128]{1,0:T(8,128)(2,1)S(1)}, bf16[128,128]{1,0:T(8,128)(2,1)S(1)}, u32[]{:S(2)}, u32[]{:S(2)}) %collective-permute-start.11) | collective-permute-done | bytes 32800 | tf_op jit(solution)/shard_map/ppermute | solution.py:234
  21.0 0.0 collective-permute-start.12
  21.0 2.8 %collective-permute-done.9.rest_8_ = bf16[128,128]{1,0:T(8,128)(2,1)S(1)} collective-permute-done((bf16[128,128]{1,0:T(8,128)(2,1)S(1)}, bf16[128,128]{1,0:T(8,128)(2,1)S(1)}, u32[]{:S(2)}, u32[]{:S(2)}) %collective-permute-start.9) | collective-permute-done | bytes 32800 | tf_op jit(solution)/shard_map/ppermute | solution.py:234
  23.9 0.0 collective-permute-start.10
  23.9 0.0 collective-permute-done.7.rest_6_
  23.9 0.5 %collective-permute-start.8 = (bf16[128,128]{1,0:T(8,128)(2,1)S(1)}, bf16[128,128]{1,0:T(8,128)(2,1)S(1)}, u32[]{:S(2)}, u32[]{:S(2)}) collective-permute-start(bf16[128,128]{1,0:T(8,128)(2,1)S(1)} %collective-permute-done.7.rest_6_), channel_id=1, source_target_pairs={{0,4},{4,0},{8,12},{12,8},{16,20},{20,16},{24,28},{28,24},{1,5},{5... | collective-permute-start | bytes 98312 | tf_op jit(solution)/shard_map/ppermute | solution.py:234
  24.4 0.0 collective-permute-done.rest_1_
  24.4 0.1 shard_map.84.rows_ref
  24.5 0.0 collective-permute-done.6.rest_5_
  24.5 0.0 collective-permute-done.12.rest_11_
  24.5 0.6 %collective-permute-done.10.rest_9_ = bf16[128,128]{1,0:T(8,128)(2,1)S(1)} collective-permute-done((bf16[128,128]{1,0:T(8,128)(2,1)S(1)}, bf16[128,128]{1,0:T(8,128)(2,1)S(1)}, u32[]{:S(2)}, u32[]{:S(2)}) %collective-permute-start.10) | collective-permute-done | bytes 32800 | tf_op jit(solution)/shard_map/ppermute | solution.py:234
  25.1 0.2 collective-permute-done.8.rest_7_
  25.2 0.4 %shard_map.86 = (bf16[128,128]{1,0:T(8,128)(2,1)S(1)}, bf16[128,128]{1,0:T(8,128)(2,1)S(1)}, bf16[128,128]{1,0:T(8,128)(2,1)S(1)}, bf16[128,128]{1,0:T(8,128)(2,1)S(1)}) custom-call(bf16[128,1024]{1,0:T(8,128)(2,1)S(1)} %shard_map.84.rows_ref, f32[128,512]{1,0:T(8,128)S(1)} %get-tuple-element.37.level_ref, ...), custom_call_target="tpu_custom_call" | custom-call | flops 50331648 | bytes 262144 | tf_op jit(solution)/shard_map/pallas_call | solution.py:276
  25.7 2.8 %collective-permute-start.13 = (bf16[128,128]{1,0:T(8,128)(2,1)S(1)}, bf16[128,128]{1,0:T(8,128)(2,1)S(1)}, u32[]{:S(2)}, u32[]{:S(2)}) collective-permute-start(bf16[128,128]{1,0:T(8,128)(2,1)S(1)} %get-tuple-element.42), channel_id=1, source_target_pairs={{0,3},{1,2},{2,1},{3,0},{4,7},{5,6},{6,5},{7,4},{8,11},{9,10},{10,... | collective-permute-start | bytes 98312 | tf_op jit(solution)/shard_map/ppermute | solution.py:234
  28.5 1.3 %collective-permute-start.14 = (bf16[128,128]{1,0:T(8,128)(2,1)S(1)}, bf16[128,128]{1,0:T(8,128)(2,1)S(1)}, u32[]{:S(2)}, u32[]{:S(2)}) collective-permute-start(bf16[128,128]{1,0:T(8,128)(2,1)S(1)} %get-tuple-element.43), channel_id=1, source_target_pairs={{0,2},{1,3},{2,0},{3,1},{4,6},{5,7},{6,4},{7,5},{8,10},{9,11},{10,... | collective-permute-start | bytes 98312 | tf_op jit(solution)/shard_map/ppermute | solution.py:234
  29.7 0.0 collective-permute-start.15
  29.7 2.3 %shard_map.87 = (bf16[1024,512]{1,0:T(8,128)(2,1)S(1)}, bf16[1024,128]{1,0:T(8,128)(2,1)S(1)}) custom-call(bf16[1024,1024]{1,0:T(8,128)(2,1)S(1)} %get-tuple-element.25.inverse_ref, s32[1,1024]{1,0:T(1,128)S(1)} %get-tuple-element.26.order_ref, bf16[1024,256]{1,0:T(8,128)(2,1)S(1)} %get-tuple-element.27.pair_ref, ...), custom_call_target="tpu_custom_call" | custom-call | flops 1879048192 | bytes 4194304 | tf_op jit(solution)/shard_map/pallas_call | solution.py:284
  32.0 0.0 collective-permute-done.13.rest_0_
  32.1 0.3 collective-permute-done.14.rest_1_
  32.4 1.3 %collective-permute-done.15.rest_2_ = bf16[128,128]{1,0:T(8,128)(2,1)S(1)} collective-permute-done((bf16[128,128]{1,0:T(8,128)(2,1)S(1)}, bf16[128,128]{1,0:T(8,128)(2,1)S(1)}, u32[]{:S(2)}, u32[]{:S(2)}) %collective-permute-start.15) | collective-permute-done | bytes 32800 | tf_op jit(solution)/shard_map/ppermute | solution.py:234
  33.6 1.2 %shard_map.88 = bf16[1024,512]{1,0:T(8,128)(2,1)} custom-call(bf16[1024,512]{1,0:T(8,128)(2,1)S(1)} %get-tuple-element.40.applied_ref, bf16[1024,128]{1,0:T(8,128)(2,1)S(1)} %get-tuple-element.41.down_ref, bf16[128,128]{1,0:T(8,128)(2,1)S(1)} %collective-permute-done.13.rest_0_, bf16[128,128]{1,0:T(8,128)(2,1)S(1)} %collective-permute-done.14.rest_1_, ...), custom_call_target="tpu_custom_call" | custom-call | flops 134217728 | bytes 2097152 | tf_op jit(solution)/shard_map/pallas_call | solution.py:291
Async XLA Ops:
  3.4 10.4 %collective-permute-start.3 = (bf16[384,128]{1,0:T(8,128)(2,1)S(1)}, bf16[384,128]{1,0:T(8,128)(2,1)S(1)}, u32[]{:S(2)}, u32[]{:S(2)}) collective-permute-start(bf16[384,128]{1,0:T(8,128)(2,1)S(1)} %get-tuple-element.34), channel_id=1, source_target_pairs={{0,3},{1,2},{2,1},{3,0},{4,7},{5,6},{6,5},{7,4},{8,11},{9,10},{10,... | collective-permute-start | bytes 294920 | tf_op jit(solution)/shard_map/ppermute | solution.py:234
  7.3 6.5 %collective-permute-start.5 = (bf16[512,128]{1,0:T(8,128)(2,1)S(1)}, bf16[512,128]{1,0:T(8,128)(2,1)S(1)}, u32[]{:S(2)}, u32[]{:S(2)}) collective-permute-start(bf16[512,128]{1,0:T(8,128)(2,1)S(1)} %get-tuple-element.36), channel_id=1, source_target_pairs={{0,1},{1,0},{2,3},{3,2},{4,5},{5,4},{6,7},{7,6},{8,9},{9,8},{10,11... | collective-permute-start | bytes 393224 | tf_op jit(solution)/shard_map/ppermute | solution.py:234
  7.9 6.6 %collective-permute-start.4 = (bf16[640,128]{1,0:T(8,128)(2,1)S(1)}, bf16[640,128]{1,0:T(8,128)(2,1)S(1)}, u32[]{:S(2)}, u32[]{:S(2)}) collective-permute-start(bf16[640,128]{1,0:T(8,128)(2,1)S(1)} %get-tuple-element.35), channel_id=1, source_target_pairs={{0,2},{1,3},{2,0},{3,1},{4,6},{5,7},{6,4},{7,5},{8,10},{9,11},{10,... | collective-permute-start | bytes 491528 | tf_op jit(solution)/shard_map/ppermute | solution.py:234
  10.3 8.7 %collective-permute-start.2 = (bf16[32,1024]{1,0:T(8,128)(2,1)S(1)}, bf16[32,1024]{1,0:T(8,128)(2,1)S(1)}, u32[]{:S(2)}, u32[]{:S(2)}) collective-permute-start(bf16[32,1024]{1,0:T(8,128)(2,1)S(1)} %get-tuple-element.32.rest_0_), channel_id=1, source_target_pairs={{0,3},{1,2},{2,1},{3,0},{4,7},{5,6},{6,5},{7,4},{8,11},{9,10},{10,... | collective-permute-start | bytes 196616 | tf_op jit(solution)/shard_map/ppermute | solution.py:234
  13.2 6.5 %collective-permute-start.1 = (bf16[32,1024]{1,0:T(8,128)(2,1)S(1)}, bf16[32,1024]{1,0:T(8,128)(2,1)S(1)}, u32[]{:S(2)}, u32[]{:S(2)}) collective-permute-start(bf16[32,1024]{1,0:T(8,128)(2,1)S(1)} %get-tuple-element.32.rest_0_), channel_id=1, source_target_pairs={{0,2},{1,3},{2,0},{3,1},{4,6},{5,7},{6,4},{7,5},{8,10},{9,11},{10,... | collective-permute-start | bytes 196616 | tf_op jit(solution)/shard_map/ppermute | solution.py:234
  13.7 10.7 %collective-permute-start = (bf16[32,1024]{1,0:T(8,128)(2,1)S(1)}, bf16[32,1024]{1,0:T(8,128)(2,1)S(1)}, u32[]{:S(2)}, u32[]{:S(2)}) collective-permute-start(bf16[32,1024]{1,0:T(8,128)(2,1)S(1)} %get-tuple-element.32.rest_0_), channel_id=1, source_target_pairs={{0,1},{1,0},{2,3},{3,2},{4,5},{5,4},{6,7},{7,6},{8,9},{9,8},{10,11... | collective-permute-start | bytes 196616 | tf_op jit(solution)/shard_map/ppermute | solution.py:234
  14.9 6.1 %collective-permute-start.11 = (bf16[128,128]{1,0:T(8,128)(2,1)S(1)}, bf16[128,128]{1,0:T(8,128)(2,1)S(1)}, u32[]{:S(2)}, u32[]{:S(2)}) collective-permute-start(bf16[128,128]{1,0:T(8,128)(2,1)S(1)} %get-tuple-element.38.rest_4_), channel_id=1, source_target_pairs={{0,24},{4,28},{8,16},{12,20},{16,8},{20,12},{24,0},{28,4},{1,25},{... | collective-permute-start | bytes 98312 | tf_op jit(solution)/shard_map/ppermute | solution.py:234
  19.0 4.8 %collective-permute-start.9 = (bf16[128,128]{1,0:T(8,128)(2,1)S(1)}, bf16[128,128]{1,0:T(8,128)(2,1)S(1)}, u32[]{:S(2)}, u32[]{:S(2)}) collective-permute-start(bf16[128,128]{1,0:T(8,128)(2,1)S(1)} %get-tuple-element.38.rest_4_), channel_id=1, source_target_pairs={{0,16},{4,20},{8,24},{12,28},{16,0},{20,4},{24,8},{28,12},{1,17},{... | collective-permute-start | bytes 98312 | tf_op jit(solution)/shard_map/ppermute | solution.py:234
  19.1 4.8 %collective-permute-start.7 = (bf16[128,128]{1,0:T(8,128)(2,1)S(1)}, bf16[128,128]{1,0:T(8,128)(2,1)S(1)}, u32[]{:S(2)}, u32[]{:S(2)}) collective-permute-start(bf16[128,128]{1,0:T(8,128)(2,1)S(1)} %get-tuple-element.38.rest_4_), channel_id=1, source_target_pairs={{0,8},{4,12},{8,0},{12,4},{16,24},{20,28},{24,16},{28,20},{1,9},{5... | collective-permute-start | bytes 98312 | tf_op jit(solution)/shard_map/ppermute | solution.py:234
  19.7 4.8 %collective-permute-start.6 = (bf16[128,128]{1,0:T(8,128)(2,1)S(1)}, bf16[128,128]{1,0:T(8,128)(2,1)S(1)}, u32[]{:S(2)}, u32[]{:S(2)}) collective-permute-start(bf16[128,128]{1,0:T(8,128)(2,1)S(1)} %get-tuple-element.38.rest_4_), channel_id=1, source_target_pairs={{0,4},{4,0},{8,12},{12,8},{16,20},{20,16},{24,28},{28,24},{1,5},{5... | collective-permute-start | bytes 98312 | tf_op jit(solution)/shard_map/ppermute | solution.py:234
  21.0 3.5 %collective-permute-start.12 = (bf16[128,128]{1,0:T(8,128)(2,1)S(1)}, bf16[128,128]{1,0:T(8,128)(2,1)S(1)}, u32[]{:S(2)}, u32[]{:S(2)}) collective-permute-start(bf16[128,128]{1,0:T(8,128)(2,1)S(1)} %collective-permute-done.11.rest_10_), channel_id=1, source_target_pairs={{0,4},{4,0},{8,12},{12,8},{16,20},{20,16},{24,28},{28,24},{1,5},{5... | collective-permute-start | bytes 98312 | tf_op jit(solution)/shard_map/ppermute | solution.py:234
  23.9 1.2 %collective-permute-start.10 = (bf16[128,128]{1,0:T(8,128)(2,1)S(1)}, bf16[128,128]{1,0:T(8,128)(2,1)S(1)}, u32[]{:S(2)}, u32[]{:S(2)}) collective-permute-start(bf16[128,128]{1,0:T(8,128)(2,1)S(1)} %collective-permute-done.9.rest_8_), channel_id=1, source_target_pairs={{0,4},{4,0},{8,12},{12,8},{16,20},{20,16},{24,28},{28,24},{1,5},{5... | collective-permute-start | bytes 98312 | tf_op jit(solution)/shard_map/ppermute | solution.py:234
  23.9 1.4 %collective-permute-start.8 = (bf16[128,128]{1,0:T(8,128)(2,1)S(1)}, bf16[128,128]{1,0:T(8,128)(2,1)S(1)}, u32[]{:S(2)}, u32[]{:S(2)}) collective-permute-start(bf16[128,128]{1,0:T(8,128)(2,1)S(1)} %collective-permute-done.7.rest_6_), channel_id=1, source_target_pairs={{0,4},{4,0},{8,12},{12,8},{16,20},{20,16},{24,28},{28,24},{1,5},{5... | collective-permute-start | bytes 98312 | tf_op jit(solution)/shard_map/ppermute | solution.py:234
  25.7 6.4 %collective-permute-start.13 = (bf16[128,128]{1,0:T(8,128)(2,1)S(1)}, bf16[128,128]{1,0:T(8,128)(2,1)S(1)}, u32[]{:S(2)}, u32[]{:S(2)}) collective-permute-start(bf16[128,128]{1,0:T(8,128)(2,1)S(1)} %get-tuple-element.42), channel_id=1, source_target_pairs={{0,3},{1,2},{2,1},{3,0},{4,7},{5,6},{6,5},{7,4},{8,11},{9,10},{10,... | collective-permute-start | bytes 98312 | tf_op jit(solution)/shard_map/ppermute | solution.py:234
  28.5 3.9 %collective-permute-start.14 = (bf16[128,128]{1,0:T(8,128)(2,1)S(1)}, bf16[128,128]{1,0:T(8,128)(2,1)S(1)}, u32[]{:S(2)}, u32[]{:S(2)}) collective-permute-start(bf16[128,128]{1,0:T(8,128)(2,1)S(1)} %get-tuple-element.43), channel_id=1, source_target_pairs={{0,2},{1,3},{2,0},{3,1},{4,6},{5,7},{6,4},{7,5},{8,10},{9,11},{10,... | collective-permute-start | bytes 98312 | tf_op jit(solution)/shard_map/ppermute | solution.py:234
  29.7 3.9 %collective-permute-start.15 = (bf16[128,128]{1,0:T(8,128)(2,1)S(1)}, bf16[128,128]{1,0:T(8,128)(2,1)S(1)}, u32[]{:S(2)}, u32[]{:S(2)}) collective-permute-start(bf16[128,128]{1,0:T(8,128)(2,1)S(1)} %get-tuple-element.44), channel_id=1, source_target_pairs={{0,1},{1,0},{2,3},{3,2},{4,5},{5,4},{6,7},{7,6},{8,9},{9,8},{10,11... | collective-permute-start | bytes 98312 | tf_op jit(solution)/shard_map/ppermute | solution.py:234

commit v13 on v10

--- a/solution.py
+++ b/solution.py
@@ -117,14 +117,18 @@
     top_out[...] = top_ref[...]
 
 
-def down_kernel(inverse_ref, order_ref, pair_ref, applied_ref, after, applied_out, down_ref):
+def down_kernel(inverse_ref, pair_ref, group_ref, down_ref, group_out):
+    rank = down_ref.shape[1]
+    both = dot(inverse_ref[...], pair_ref[...])
+    down_ref[...] = (both[:, :rank] + both[:, rank:]).astype(BF)
+    group_out[...] = group_ref[...]
+
+
+def place_kernel(order_ref, applied_ref, down_ref, after, applied_out, down_out):
     del after
-    points, rank = down_ref.shape
-    placed = order_rows(order_ref[...], points)
-    both = dot(inverse_ref[...], pair_ref[...])
-    down = (both[:, :rank] + both[:, rank:]).astype(BF)
+    placed = order_rows(order_ref[...], applied_ref.shape[0])
     applied_out[...] = dot(placed, applied_ref[...]).astype(BF)
-    down_ref[...] = dot(placed, down).astype(BF)
+    down_out[...] = dot(placed, down_ref[...]).astype(BF)
 
 
 def group_kernel(n, rank, after, own_ref, *rest):
@@ -262,11 +266,18 @@
         flops=2 * share * n * rank * (n + 1) * rank,
         moved=4 * share * n * rank,
     )(applied, own, *received[::-1])
+    down, group_held = call(
+        down_kernel,
+        [shape((points, rank)), shape((share, rank))],
+        [vmem] * 3,
+        flops=4 * points * points * rank,
+        moved=2 * points * (points + 2 * rank),
+    )(inverse_held, pair, group)
     pieces = {0: group}
     for m in range(2, groups, 2):
         pieces[m] = swap(group, "aa", m)
     for m in range(0, groups, 2):
-        pieces[m + 1] = swap(pieces[m], "aa", 1)
+        pieces[m + 1] = swap(pieces[m] if m else group_held, "aa", 1)
     rows = call(
         functools.partial(top_rows_kernel, n, groups),
         shape((rank, groups * rank)),
@@ -283,12 +294,12 @@
     )(rows, level, own, *received, *[pieces[m] for m in range(groups)])
     back = [corrections[0]] + [swap(corrections[k], "ba", k) for k in range(1, n)]
     applied, down = call(
-        down_kernel,
+        place_kernel,
         [shape((points, cols)), shape((points, rank))],
-        [vmem] * 4 + [unread],
-        flops=2 * points * points * (3 * rank + cols),
+        [vmem] * 3 + [unread],
+        flops=2 * points * points * (rank + cols),
         moved=2 * points * (points + 2 * cols),
-    )(inverse_held, order_held, pair, applied, corrections[0])
+    )(order_held, applied, down, corrections[0])
     return call(
         functools.partial(final_kernel, n),
         shape((points, cols)),

time: 33.5 us -> 33.5 us (level)
    pallas_call x1 -> x2, Pallas kernels: 2.33 us -> 2.5 us  [the longest x1 1.79 us: shards(): call(place_kernel, [shape((points, cols)), shape((points, rank))], [vmem]...]
where the time goes in v13:
time: 33.5 us; the launch traced here: 33.4 us
  starting transfers between devices  16.8 us (50%)
  Pallas kernels  10.4 us (31%)
  waiting for transfers between devices  6.12 us (18%)
    ppermute x16, starting transfers between devices, swap(): return lax.ppermute(array, axis, [(i, i ^ k) for i in range(size)])  16.8 us
    ppermute x16, waiting for transfers between devices, swap(): return lax.ppermute(array, axis, [(i, i ^ k) for i in range(size)])  6.12 us
    pallas_call x1, Pallas kernels, shards(): call(functools.partial(front_kernel, n), [shape((size, rank)) for size in...  3.35 us
    pallas_call x1, Pallas kernels, shards(): call(applied_kernel, [shape((points, cols)), shape(top.shape)], [vmem] *...  2.33 us
    pallas_call x1, Pallas kernels, shards(): call(place_kernel, [shape((points, cols)), shape((points, rank))], [vmem]...  1.79 us
    pallas_call x1, Pallas kernels, shards(): call(functools.partial(final_kernel, n), shape((points, cols)), [vmem] *...  1.25 us
    pallas_call x1, Pallas kernels, shards(): call(down_kernel, [shape((points, rank)), shape((share, rank))], [vmem] *...  0.71 us
  transfers between devices with their start and end apart: 16, of which 8 were waited for; matrix products, arithmetic and copies ran while one was open for 0% of the time, Pallas kernels for 16%

profile of v13, /device:TPU:0, one launch (start us, length us, event | category | flops | bytes accessed | tf_op | source)
XLA Modules:
  0.0 33.4 jit_solution(382813057667218537)
XLA Ops:
  0.0 3.4 %shard_map.82 = (bf16[512,128]{1,0:T(8,128)(2,1)S(1)}, bf16[512,128]{1,0:T(8,128)(2,1)S(1)}, bf16[512,128]{1,0:T(8,128)(2,1)S(1)}, bf16[768,128]{1,0:T(8,128)(2,...) custom-call(s32[1,1024]{1,0:T(1,128)} %order_hbm.1, ...), custom_call_target="tpu_custom_call" | custom-call | flops 939524096 | bytes 3407872 | tf_op jit(solution)/shard_map/pallas_call | solution.py:242
  3.4 4.0 %collective-permute-start = (bf16[512,128]{1,0:T(8,128)(2,1)S(1)}, bf16[512,128]{1,0:T(8,128)(2,1)S(1)}, u32[]{:S(2)}, u32[]{:S(2)}) collective-permute-start(bf16[512,128]{1,0:T(8,128)(2,1)S(1)} %get-tuple-element.35), channel_id=1, source_target_pairs={{0,3},{1,2},{2,1},{3,0},{4,7},{5,6},{6,5},{7,4},{8,11},{9,10},{10,... | collective-permute-start | bytes 393224 | tf_op jit(solution)/shard_map/ppermute | solution.py:239
  7.3 0.5 %collective-permute-start.1 = (bf16[512,128]{1,0:T(8,128)(2,1)S(1)}, bf16[512,128]{1,0:T(8,128)(2,1)S(1)}, u32[]{:S(2)}, u32[]{:S(2)}) collective-permute-start(bf16[512,128]{1,0:T(8,128)(2,1)S(1)} %get-tuple-element.36), channel_id=1, source_target_pairs={{0,2},{1,3},{2,0},{3,1},{4,6},{5,7},{6,4},{7,5},{8,10},{9,11},{10,... | collective-permute-start | bytes 393224 | tf_op jit(solution)/shard_map/ppermute | solution.py:239
  7.8 0.1 collective-permute-start.2
  8.0 2.3 %shard_map.83 = (bf16[1024,512]{1,0:T(8,128)(2,1)S(1)}, bf16[32,1024]{1,0:T(8,128)(2,1)S(1)}) custom-call(bf16[1024,512]{1,0:T(8,128)(2,1)S(1)} %get-tuple-element.28.sides_ref, bf16[1024,1024]{1,0:T(8,128)(2,1)S(1)} %get-tuple-element.29.inverse_ref, bf16[1024,1024]{1,0:T(8,128)(2,1)S(1)} %get-tuple-element.30.gather_ref, ...), custom_call_target="tpu_custom_call" | custom-call | flops 2147483648 | bytes 4194304 | tf_op jit(solution)/shard_map/pallas_call | solution.py:254
  10.3 2.9 %collective-permute-start.5 = (bf16[32,1024]{1,0:T(8,128)(2,1)S(1)}, bf16[32,1024]{1,0:T(8,128)(2,1)S(1)}, u32[]{:S(2)}, u32[]{:S(2)}) collective-permute-start(bf16[32,1024]{1,0:T(8,128)(2,1)S(1)} %get-tuple-element.40.rest_0_), channel_id=1, source_target_pairs={{0,3},{1,2},{2,1},{3,0},{4,7},{5,6},{6,5},{7,4},{8,11},{9,10},{10,... | collective-permute-start | bytes 196616 | tf_op jit(solution)/shard_map/ppermute | solution.py:239
  13.2 0.5 %collective-permute-start.4 = (bf16[32,1024]{1,0:T(8,128)(2,1)S(1)}, bf16[32,1024]{1,0:T(8,128)(2,1)S(1)}, u32[]{:S(2)}, u32[]{:S(2)}) collective-permute-start(bf16[32,1024]{1,0:T(8,128)(2,1)S(1)} %get-tuple-element.40.rest_0_), channel_id=1, source_target_pairs={{0,2},{1,3},{2,0},{3,1},{4,6},{5,7},{6,4},{7,5},{8,10},{9,11},{10,... | collective-permute-start | bytes 196616 | tf_op jit(solution)/shard_map/ppermute | solution.py:239
  13.7 0.0 collective-permute-done.rest_0_.rest_3_
  13.7 0.1 collective-permute-start.3
  13.9 0.3 collective-permute-done.1.rest_1_.rest_2_
  14.2 0.2 collective-permute-done.2.rest_2_.rest_1_
  14.4 0.4 %shard_map.84 = (f32[128,512]{1,0:T(8,128)S(1)}, bf16[128,128]{1,0:T(8,128)(2,1)S(1)}) custom-call(bf16[1024,512]{1,0:T(8,128)(2,1)S(1)} %get-tuple-element.32.after.applied_ref, bf16[768,128]{1,0:T(8,128)(2,1)S(1)} %get-tuple-element.34.own_ref.rest_0_, bf16[512,128]{1,0:T(8,128)(2,1)S(1)} %collective-permute-done.rest_0_.rest_3_, ...), custom_call_target="tpu_custom_call" | custom-call | flops 83886080 | bytes 262144 | tf_op jit(solution)/shard_map/pallas_call | solution.py:262
  14.8 3.7 %collective-permute-start.11 = (bf16[128,128]{1,0:T(8,128)(2,1)S(1)}, bf16[128,128]{1,0:T(8,128)(2,1)S(1)}, u32[]{:S(2)}, u32[]{:S(2)}) collective-permute-start(bf16[128,128]{1,0:T(8,128)(2,1)S(1)} %get-tuple-element.38.group_ref.rest_4_), channel_id=1, source_target_pairs={{0,24},{4,28},{8,16},{12,20},{16,8},{20,12},{24,0},{28,4},{1,25},{... | collective-permute-start | bytes 98312 | tf_op jit(solution)/shard_map/ppermute | solution.py:239
  18.5 0.0 collective-permute-start.9
  18.5 0.0 collective-permute-done.5.rest_3_
  18.5 0.8 %collective-permute-start.7 = (bf16[128,128]{1,0:T(8,128)(2,1)S(1)}, bf16[128,128]{1,0:T(8,128)(2,1)S(1)}, u32[]{:S(2)}, u32[]{:S(2)}) collective-permute-start(bf16[128,128]{1,0:T(8,128)(2,1)S(1)} %get-tuple-element.38.group_ref.rest_4_), channel_id=1, source_target_pairs={{0,8},{4,12},{8,0},{12,4},{16,24},{20,28},{24,16},{28,20},{1,9},{5... | collective-permute-start | bytes 98312 | tf_op jit(solution)/shard_map/ppermute | solution.py:239
  19.3 0.7 %shard_map.85 = (bf16[1024,128]{1,0:T(8,128)(2,1)S(1)}, bf16[128,128]{1,0:T(8,128)(2,1)S(1)}) custom-call(bf16[1024,1024]{1,0:T(8,128)(2,1)S(1)} %get-tuple-element.29.inverse_ref, bf16[1024,256]{1,0:T(8,128)(2,1)S(1)} %get-tuple-element.33.pair_ref, bf16[128,128]{1,0:T(8,128)(2,1)S(1)} %get-tuple-element.38.group_ref.rest_4_), custom_call_target="tpu_custom_call" | custom-call | flops 536870912 | bytes 2621440 | tf_op jit(solution)/shard_map/pallas_call | solution.py:269
  20.0 0.0 collective-permute-done.4.rest_2_
  20.0 0.1 collective-permute-start.6
  20.1 0.5 %collective-permute-done.11.rest_10_ = bf16[128,128]{1,0:T(8,128)(2,1)S(1)} collective-permute-done((bf16[128,128]{1,0:T(8,128)(2,1)S(1)}, bf16[128,128]{1,0:T(8,128)(2,1)S(1)}, u32[]{:S(2)}, u32[]{:S(2)}) %collective-permute-start.11) | collective-permute-done | bytes 32800 | tf_op jit(solution)/shard_map/ppermute | solution.py:239
  20.6 0.0 collective-permute-start.12
  20.6 2.7 %collective-permute-done.9.rest_8_ = bf16[128,128]{1,0:T(8,128)(2,1)S(1)} collective-permute-done((bf16[128,128]{1,0:T(8,128)(2,1)S(1)}, bf16[128,128]{1,0:T(8,128)(2,1)S(1)}, u32[]{:S(2)}, u32[]{:S(2)}) %collective-permute-start.9) | collective-permute-done | bytes 32800 | tf_op jit(solution)/shard_map/ppermute | solution.py:239
  23.3 0.0 collective-permute-start.10
  23.3 0.0 collective-permute-done.7.rest_6_
  23.3 0.5 %collective-permute-start.8 = (bf16[128,128]{1,0:T(8,128)(2,1)S(1)}, bf16[128,128]{1,0:T(8,128)(2,1)S(1)}, u32[]{:S(2)}, u32[]{:S(2)}) collective-permute-start(bf16[128,128]{1,0:T(8,128)(2,1)S(1)} %collective-permute-done.7.rest_6_), channel_id=1, source_target_pairs={{0,4},{4,0},{8,12},{12,8},{16,20},{20,16},{24,28},{28,24},{1,5},{5... | collective-permute-start | bytes 98312 | tf_op jit(solution)/shard_map/ppermute | solution.py:239
  23.9 0.0 collective-permute-done.3.rest_1_
  23.9 0.1 shard_map.86.rows_ref
  24.0 0.0 collective-permute-done.6.rest_5_
  24.0 0.0 collective-permute-done.12.rest_11_
  24.0 0.6 %collective-permute-done.10.rest_9_ = bf16[128,128]{1,0:T(8,128)(2,1)S(1)} collective-permute-done((bf16[128,128]{1,0:T(8,128)(2,1)S(1)}, bf16[128,128]{1,0:T(8,128)(2,1)S(1)}, u32[]{:S(2)}, u32[]{:S(2)}) %collective-permute-start.10) | collective-permute-done | bytes 32800 | tf_op jit(solution)/shard_map/ppermute | solution.py:239
  24.5 0.2 collective-permute-done.8.rest_7_
  24.7 0.4 %shard_map.87 = (bf16[128,128]{1,0:T(8,128)(2,1)S(1)}, bf16[128,128]{1,0:T(8,128)(2,1)S(1)}, bf16[128,128]{1,0:T(8,128)(2,1)S(1)}, bf16[128,128]{1,0:T(8,128)(2,1)S(1)}) custom-call(bf16[128,1024]{1,0:T(8,128)(2,1)S(1)} %shard_map.86.rows_ref, f32[128,512]{1,0:T(8,128)S(1)} %get-tuple-element.41.level_ref, ...), custom_call_target="tpu_custom_call" | custom-call | flops 50331648 | bytes 262144 | tf_op jit(solution)/shard_map/pallas_call | solution.py:288
  25.1 2.4 %collective-permute-start.13 = (bf16[128,128]{1,0:T(8,128)(2,1)S(1)}, bf16[128,128]{1,0:T(8,128)(2,1)S(1)}, u32[]{:S(2)}, u32[]{:S(2)}) collective-permute-start(bf16[128,128]{1,0:T(8,128)(2,1)S(1)} %get-tuple-element.46), channel_id=1, source_target_pairs={{0,3},{1,2},{2,1},{3,0},{4,7},{5,6},{6,5},{7,4},{8,11},{9,10},{10,... | collective-permute-start | bytes 98312 | tf_op jit(solution)/shard_map/ppermute | solution.py:239
  27.5 0.7 %collective-permute-start.14 = (bf16[128,128]{1,0:T(8,128)(2,1)S(1)}, bf16[128,128]{1,0:T(8,128)(2,1)S(1)}, u32[]{:S(2)}, u32[]{:S(2)}) collective-permute-start(bf16[128,128]{1,0:T(8,128)(2,1)S(1)} %get-tuple-element.47), channel_id=1, source_target_pairs={{0,2},{1,3},{2,0},{3,1},{4,6},{5,7},{6,4},{7,5},{8,10},{9,11},{10,... | collective-permute-start | bytes 98312 | tf_op jit(solution)/shard_map/ppermute | solution.py:239
  28.2 0.5 %collective-permute-start.15 = (bf16[128,128]{1,0:T(8,128)(2,1)S(1)}, bf16[128,128]{1,0:T(8,128)(2,1)S(1)}, u32[]{:S(2)}, u32[]{:S(2)}) collective-permute-start(bf16[128,128]{1,0:T(8,128)(2,1)S(1)} %get-tuple-element.48), channel_id=1, source_target_pairs={{0,1},{1,0},{2,3},{3,2},{4,5},{5,4},{6,7},{7,6},{8,9},{9,8},{10,11... | collective-permute-start | bytes 98312 | tf_op jit(solution)/shard_map/ppermute | solution.py:239
  28.7 1.8 %shard_map.88 = (bf16[1024,512]{1,0:T(8,128)(2,1)S(1)}, bf16[1024,128]{1,0:T(8,128)(2,1)S(1)}) custom-call(s32[1,1024]{1,0:T(1,128)S(1)} %get-tuple-element.27.order_ref, bf16[1024,512]{1,0:T(8,128)(2,1)S(1)} %get-tuple-element.32.after.applied_ref, bf16[1024,128]{1,0:T(8,128)(2,1)S(1)} %get-tuple-element.39.down_ref, ...), custom_call_target="tpu_custom_call" | custom-call | flops 1342177280 | bytes 4194304 | tf_op jit(solution)/shard_map/pallas_call | solution.py:296
  30.5 0.0 collective-permute-done.13.rest_0_
  30.5 0.9 %collective-permute-done.14.rest_1_ = bf16[128,128]{1,0:T(8,128)(2,1)S(1)} collective-permute-done((bf16[128,128]{1,0:T(8,128)(2,1)S(1)}, bf16[128,128]{1,0:T(8,128)(2,1)S(1)}, u32[]{:S(2)}, u32[]{:S(2)}) %collective-permute-start.14) | collective-permute-done | bytes 32800 | tf_op jit(solution)/shard_map/ppermute | solution.py:239
  31.4 0.7 %collective-permute-done.15.rest_2_ = bf16[128,128]{1,0:T(8,128)(2,1)S(1)} collective-permute-done((bf16[128,128]{1,0:T(8,128)(2,1)S(1)}, bf16[128,128]{1,0:T(8,128)(2,1)S(1)}, u32[]{:S(2)}, u32[]{:S(2)}) %collective-permute-start.15) | collective-permute-done | bytes 32800 | tf_op jit(solution)/shard_map/ppermute | solution.py:239
  32.1 1.2 %shard_map.89 = bf16[1024,512]{1,0:T(8,128)(2,1)} custom-call(bf16[1024,512]{1,0:T(8,128)(2,1)S(1)} %get-tuple-element.44.applied_ref, bf16[1024,128]{1,0:T(8,128)(2,1)S(1)} %get-tuple-element.45.down_ref, bf16[128,128]{1,0:T(8,128)(2,1)S(1)} %collective-permute-done.13.rest_0_, bf16[128,128]{1,0:T(8,128)(2,1)S(1)} %collective-permute-done.14.rest_1_, ...), custom_call_target="tpu_custom_call" | custom-call | flops 134217728 | bytes 2097152 | tf_op jit(solution)/shard_map/pallas_call | solution.py:303
Async XLA Ops:
  3.4 10.4 %collective-permute-start = (bf16[512,128]{1,0:T(8,128)(2,1)S(1)}, bf16[512,128]{1,0:T(8,128)(2,1)S(1)}, u32[]{:S(2)}, u32[]{:S(2)}) collective-permute-start(bf16[512,128]{1,0:T(8,128)(2,1)S(1)} %get-tuple-element.35), channel_id=1, source_target_pairs={{0,3},{1,2},{2,1},{3,0},{4,7},{5,6},{6,5},{7,4},{8,11},{9,10},{10,... | collective-permute-start | bytes 393224 | tf_op jit(solution)/shard_map/ppermute | solution.py:239
  7.3 6.8 %collective-permute-start.1 = (bf16[512,128]{1,0:T(8,128)(2,1)S(1)}, bf16[512,128]{1,0:T(8,128)(2,1)S(1)}, u32[]{:S(2)}, u32[]{:S(2)}) collective-permute-start(bf16[512,128]{1,0:T(8,128)(2,1)S(1)} %get-tuple-element.36), channel_id=1, source_target_pairs={{0,2},{1,3},{2,0},{3,1},{4,6},{5,7},{6,4},{7,5},{8,10},{9,11},{10,... | collective-permute-start | bytes 393224 | tf_op jit(solution)/shard_map/ppermute | solution.py:239
  7.8 6.6 %collective-permute-start.2 = (bf16[512,128]{1,0:T(8,128)(2,1)S(1)}, bf16[512,128]{1,0:T(8,128)(2,1)S(1)}, u32[]{:S(2)}, u32[]{:S(2)}) collective-permute-start(bf16[512,128]{1,0:T(8,128)(2,1)S(1)} %get-tuple-element.37), channel_id=1, source_target_pairs={{0,1},{1,0},{2,3},{3,2},{4,5},{5,4},{6,7},{7,6},{8,9},{9,8},{10,11... | collective-permute-start | bytes 393224 | tf_op jit(solution)/shard_map/ppermute | solution.py:239
  10.3 8.2 %collective-permute-start.5 = (bf16[32,1024]{1,0:T(8,128)(2,1)S(1)}, bf16[32,1024]{1,0:T(8,128)(2,1)S(1)}, u32[]{:S(2)}, u32[]{:S(2)}) collective-permute-start(bf16[32,1024]{1,0:T(8,128)(2,1)S(1)} %get-tuple-element.40.rest_0_), channel_id=1, source_target_pairs={{0,3},{1,2},{2,1},{3,0},{4,7},{5,6},{6,5},{7,4},{8,11},{9,10},{10,... | collective-permute-start | bytes 196616 | tf_op jit(solution)/shard_map/ppermute | solution.py:239
  13.2 6.8 %collective-permute-start.4 = (bf16[32,1024]{1,0:T(8,128)(2,1)S(1)}, bf16[32,1024]{1,0:T(8,128)(2,1)S(1)}, u32[]{:S(2)}, u32[]{:S(2)}) collective-permute-start(bf16[32,1024]{1,0:T(8,128)(2,1)S(1)} %get-tuple-element.40.rest_0_), channel_id=1, source_target_pairs={{0,2},{1,3},{2,0},{3,1},{4,6},{5,7},{6,4},{7,5},{8,10},{9,11},{10,... | collective-permute-start | bytes 196616 | tf_op jit(solution)/shard_map/ppermute | solution.py:239
  13.7 10.1 %collective-permute-start.3 = (bf16[32,1024]{1,0:T(8,128)(2,1)S(1)}, bf16[32,1024]{1,0:T(8,128)(2,1)S(1)}, u32[]{:S(2)}, u32[]{:S(2)}) collective-permute-start(bf16[32,1024]{1,0:T(8,128)(2,1)S(1)} %get-tuple-element.40.rest_0_), channel_id=1, source_target_pairs={{0,1},{1,0},{2,3},{3,2},{4,5},{5,4},{6,7},{7,6},{8,9},{9,8},{10,11... | collective-permute-start | bytes 196616 | tf_op jit(solution)/shard_map/ppermute | solution.py:239
  14.8 5.8 %collective-permute-start.11 = (bf16[128,128]{1,0:T(8,128)(2,1)S(1)}, bf16[128,128]{1,0:T(8,128)(2,1)S(1)}, u32[]{:S(2)}, u32[]{:S(2)}) collective-permute-start(bf16[128,128]{1,0:T(8,128)(2,1)S(1)} %get-tuple-element.38.group_ref.rest_4_), channel_id=1, source_target_pairs={{0,24},{4,28},{8,16},{12,20},{16,8},{20,12},{24,0},{28,4},{1,25},{... | collective-permute-start | bytes 98312 | tf_op jit(solution)/shard_map/ppermute | solution.py:239
  18.5 4.8 %collective-permute-start.9 = (bf16[128,128]{1,0:T(8,128)(2,1)S(1)}, bf16[128,128]{1,0:T(8,128)(2,1)S(1)}, u32[]{:S(2)}, u32[]{:S(2)}) collective-permute-start(bf16[128,128]{1,0:T(8,128)(2,1)S(1)} %get-tuple-element.38.group_ref.rest_4_), channel_id=1, source_target_pairs={{0,16},{4,20},{8,24},{12,28},{16,0},{20,4},{24,8},{28,12},{1,17},{... | collective-permute-start | bytes 98312 | tf_op jit(solution)/shard_map/ppermute | solution.py:239
  18.5 4.8 %collective-permute-start.7 = (bf16[128,128]{1,0:T(8,128)(2,1)S(1)}, bf16[128,128]{1,0:T(8,128)(2,1)S(1)}, u32[]{:S(2)}, u32[]{:S(2)}) collective-permute-start(bf16[128,128]{1,0:T(8,128)(2,1)S(1)} %get-tuple-element.38.group_ref.rest_4_), channel_id=1, source_target_pairs={{0,8},{4,12},{8,0},{12,4},{16,24},{20,28},{24,16},{28,20},{1,9},{5... | collective-permute-start | bytes 98312 | tf_op jit(solution)/shard_map/ppermute | solution.py:239
  20.0 4.0 %collective-permute-start.6 = (bf16[128,128]{1,0:T(8,128)(2,1)S(1)}, bf16[128,128]{1,0:T(8,128)(2,1)S(1)}, u32[]{:S(2)}, u32[]{:S(2)}) collective-permute-start(bf16[128,128]{1,0:T(8,128)(2,1)S(1)} %get-tuple-element.42), channel_id=1, source_target_pairs={{0,4},{4,0},{8,12},{12,8},{16,20},{20,16},{24,28},{28,24},{1,5},{5... | collective-permute-start | bytes 98312 | tf_op jit(solution)/shard_map/ppermute | solution.py:239
  20.6 3.4 %collective-permute-start.12 = (bf16[128,128]{1,0:T(8,128)(2,1)S(1)}, bf16[128,128]{1,0:T(8,128)(2,1)S(1)}, u32[]{:S(2)}, u32[]{:S(2)}) collective-permute-start(bf16[128,128]{1,0:T(8,128)(2,1)S(1)} %collective-permute-done.11.rest_10_), channel_id=1, source_target_pairs={{0,4},{4,0},{8,12},{12,8},{16,20},{20,16},{24,28},{28,24},{1,5},{5... | collective-permute-start | bytes 98312 | tf_op jit(solution)/shard_map/ppermute | solution.py:239
  23.3 1.2 %collective-permute-start.10 = (bf16[128,128]{1,0:T(8,128)(2,1)S(1)}, bf16[128,128]{1,0:T(8,128)(2,1)S(1)}, u32[]{:S(2)}, u32[]{:S(2)}) collective-permute-start(bf16[128,128]{1,0:T(8,128)(2,1)S(1)} %collective-permute-done.9.rest_8_), channel_id=1, source_target_pairs={{0,4},{4,0},{8,12},{12,8},{16,20},{20,16},{24,28},{28,24},{1,5},{5... | collective-permute-start | bytes 98312 | tf_op jit(solution)/shard_map/ppermute | solution.py:239
  23.3 1.4 %collective-permute-start.8 = (bf16[128,128]{1,0:T(8,128)(2,1)S(1)}, bf16[128,128]{1,0:T(8,128)(2,1)S(1)}, u32[]{:S(2)}, u32[]{:S(2)}) collective-permute-start(bf16[128,128]{1,0:T(8,128)(2,1)S(1)} %collective-permute-done.7.rest_6_), channel_id=1, source_target_pairs={{0,4},{4,0},{8,12},{12,8},{16,20},{20,16},{24,28},{28,24},{1,5},{5... | collective-permute-start | bytes 98312 | tf_op jit(solution)/shard_map/ppermute | solution.py:239
  25.1 5.4 %collective-permute-start.13 = (bf16[128,128]{1,0:T(8,128)(2,1)S(1)}, bf16[128,128]{1,0:T(8,128)(2,1)S(1)}, u32[]{:S(2)}, u32[]{:S(2)}) collective-permute-start(bf16[128,128]{1,0:T(8,128)(2,1)S(1)} %get-tuple-element.46), channel_id=1, source_target_pairs={{0,3},{1,2},{2,1},{3,0},{4,7},{5,6},{6,5},{7,4},{8,11},{9,10},{10,... | collective-permute-start | bytes 98312 | tf_op jit(solution)/shard_map/ppermute | solution.py:239
  27.5 3.9 %collective-permute-start.14 = (bf16[128,128]{1,0:T(8,128)(2,1)S(1)}, bf16[128,128]{1,0:T(8,128)(2,1)S(1)}, u32[]{:S(2)}, u32[]{:S(2)}) collective-permute-start(bf16[128,128]{1,0:T(8,128)(2,1)S(1)} %get-tuple-element.47), channel_id=1, source_target_pairs={{0,2},{1,3},{2,0},{3,1},{4,6},{5,7},{6,4},{7,5},{8,10},{9,11},{10,... | collective-permute-start | bytes 98312 | tf_op jit(solution)/shard_map/ppermute | solution.py:239
  28.2 3.9 %collective-permute-start.15 = (bf16[128,128]{1,0:T(8,128)(2,1)S(1)}, bf16[128,128]{1,0:T(8,128)(2,1)S(1)}, u32[]{:S(2)}, u32[]{:S(2)}) collective-permute-start(bf16[128,128]{1,0:T(8,128)(2,1)S(1)} %get-tuple-element.48), channel_id=1, source_target_pairs={{0,1},{1,0},{2,3},{3,2},{4,5},{5,4},{6,7},{7,6},{8,9},{9,8},{10,11... | collective-permute-start | bytes 98312 | tf_op jit(solution)/shard_map/ppermute | solution.py:239
